TPU v7x, 32 devices: a whole 2x2x4 slice. The times are simulated.
32 devices in a mesh: tok: 32 (over z, y, x, core).
Axes of the slice: x: 2, y: 2, z: 4, core: 2. Of those that a mesh axis runs over, the one named last changes fastest.
Arguments:
- tokens: bfloat16 [16384, 1536], P('tok'), may hold values from -6 to 6
- cotangent: bfloat16 [16384, 1536], P('tok'), may hold values from -6 to 6
- attn_gain: bfloat16 [1536], P('tok'), may hold values from 0.5 to 1.5
- ffn_gain: bfloat16 [1536], P('tok'), may hold values from 0.5 to 1.5
- w_query: bfloat16 [1536, 1536], P('tok'), may hold values from -0.15625 to 0.15625
- w_key: bfloat16 [1536, 128], P('tok'), may hold values from -0.15625 to 0.15625
- w_value: bfloat16 [1536, 128], P('tok'), may hold values from -0.15625 to 0.15625
- w_out: bfloat16 [1536, 1536], P('tok'), may hold values from -1.25 to 1.25
- w_gate: bfloat16 [1536, 4608], P('tok'), may hold values from -0.15625 to 0.15625
- w_up: bfloat16 [1536, 4608], P('tok'), may hold values from -0.15625 to 0.15625
- w_down: bfloat16 [1536, 4608], P('tok'), may hold values from -0.09375 to 0.09375
- segments: int32 [16384], replicated, may hold values from 0 to 81, as said below
- positions: int32 [16384], P('tok'), may hold values from 0 to 3998, as said below
Outputs:
- output: bfloat16 [16384, 1536], P('tok')
- grad_tokens: bfloat16 [16384, 1536], P('tok')
- grad_attn_gain: float32 [1536], P('tok')
- grad_ffn_gain: float32 [1536], P('tok')
- grad_query: float32 [1536, 1536], P('tok')
- grad_key: float32 [1536, 128], P('tok')
- grad_value: float32 [1536, 128], P('tok')
- grad_out: float32 [1536, 1536], P('tok')
- grad_gate: float32 [1536, 4608], P('tok')
- grad_up: float32 [1536, 4608], P('tok')
- grad_down: float32 [1536, 4608], P('tok')
Inputs may be any that keep to these rules, and one draw needn't show every extreme that they name: `segments`: segment numbers never fall along the tokens; one number marks one document of the one packed sequence of 16384 tokens; documents hold 200 to 2000 tokens, except the last, which the sequence's end cuts. Within a document positions rise by one per token; each document starts at 0, except the first, which may start later.
All inputs are finite; a program needn't handle non-finite values.
Results may differ from a plain program's by a relative error of at most 0.015.
Values may be sent and summed in bfloat16 or wider, within the bound.
A program may use at most 384 MiB of HBM per device.

v0:
```python
import jax
import jax.numpy as jnp
from jax import lax
from jax.sharding import PartitionSpec as P

HQ = 12
HD = 128
WINDOW = 1024
MICRO = 2


EPSILON = 1e-06


def passed_along(array, axis, by):
    size = lax.axis_size(axis)
    pairs = [(i, i + by) for i in range(size) if 0 <= i + by < size]
    return lax.ppermute(array, axis, pairs)


def rms_norm(values, scales):
    return values * lax.rsqrt(jnp.mean(values * values, axis=-1, keepdims=True) + EPSILON) * scales


def angle_table(positions, head_size):
    frequency = 10000.0 ** (-jnp.arange(head_size // 2, dtype=jnp.float32) * 2.0 / head_size)
    return positions.astype(jnp.float32)[:, None] * frequency[None, :]


def rotate(values, angles):
    half_size = values.shape[-1] // 2
    cosine = jnp.cos(angles)[:, None, :]
    sine_part = jnp.sin(angles)[:, None, :]
    former = values[..., :half_size]
    latter = values[..., half_size:]
    return jnp.concatenate(
        [former * cosine - latter * sine_part, latter * cosine + former * sine_part], axis=-1
    )


def outer_sum(left_side, right_side):
    return lax.dot_general(
        left_side, right_side, (((0,), (0,)), ((), ())), preferred_element_type=jnp.float32
    )


def by_rows(left_side, right_side):
    return lax.dot_general(
        left_side, right_side, (((1,), (1,)), ((), ())), preferred_element_type=jnp.float32
    )


def gelu_product(gate, up_part):
    return jax.nn.gelu(gate, approximate=True) * up_part


def on_device(
    tokens,
    cotangent,
    attn_gain,
    ffn_gain,
    w_query,
    w_key,
    w_value,
    w_out,
    w_gate,
    w_up,
    w_down,
    segments,
    positions,
):
    token_count = tokens.shape[0]
    batch_rows = token_count // MICRO
    tail_rows = min(token_count, WINDOW)
    hop_count = WINDOW // tail_rows
    key_rows = WINDOW + batch_rows
    head_size = HD
    heads_all = HQ
    scale = head_size ** (-0.5)
    device = lax.axis_index("tok")
    inputs = tokens.astype(jnp.float32)
    angles = angle_table(positions, head_size)
    padded_segments = jnp.concatenate([jnp.full((WINDOW,), -1, jnp.int32), segments])
    key_segments = lax.dynamic_slice_in_dim(
        padded_segments, device * token_count, WINDOW + token_count
    )
    query_segments = lax.dynamic_slice_in_dim(segments, device * token_count, token_count)
    offsets = jnp.arange(key_rows)[None, :] - jnp.arange(batch_rows)[:, None]
    in_window = (offsets > 0) & (offsets <= WINDOW)

    def scores_of(query_rot, key_block, allowed):
        raw = jnp.einsum("qhd,kd->hqk", query_rot, key_block, preferred_element_type=jnp.float32)
        return jnp.where(allowed[None], raw * scale, -jnp.inf)

    saved = []
    outputs = []
    for batch in range(MICRO):
        gain_one, gain_two, query_w, key_w, value_w, out_w, gate_w, up_w, down_w = (
            lax.all_gather(attn_gain, "tok", axis=0, tiled=True),
            lax.all_gather(ffn_gain, "tok", axis=0, tiled=True),
            lax.all_gather(w_query, "tok", axis=0, tiled=True),
            lax.all_gather(w_key, "tok", axis=0, tiled=True),
            lax.all_gather(w_value, "tok", axis=0, tiled=True),
            lax.all_gather(w_out, "tok", axis=0, tiled=True),
            lax.all_gather(w_gate, "tok", axis=0, tiled=True),
            lax.all_gather(w_up, "tok", axis=0, tiled=True),
            lax.all_gather(w_down, "tok", axis=0, tiled=True),
        )
        if batch == 0:
            normed = rms_norm(inputs, gain_one.astype(jnp.float32)).astype(jnp.bfloat16)
            keys_new = rotate(
                jnp.dot(normed, key_w, preferred_element_type=jnp.float32)[:, None, :], angles
            )[:, 0]
            values_new = jnp.dot(normed, value_w, preferred_element_type=jnp.float32)
            key_value = jnp.concatenate(
                [keys_new.astype(jnp.bfloat16), values_new.astype(jnp.bfloat16)], axis=1
            )
            received = []
            for hop in range(hop_count, 0, -1):
                received.append(passed_along(key_value, "tok", hop))
            all_keys = jnp.concatenate(received + [key_value], axis=0)
        start = batch * batch_rows
        stop = start + batch_rows
        query_rot = rotate(
            jnp.dot(normed[start:stop], query_w, preferred_element_type=jnp.float32).reshape(
                batch_rows, heads_all, head_size
            ),
            angles[start:stop],
        ).astype(jnp.bfloat16)
        key_block = all_keys[start : start + key_rows]
        allowed = in_window & (
            query_segments[start:stop][:, None] == key_segments[start : start + key_rows][None, :]
        )
        scores = scores_of(query_rot, key_block[:, :head_size], allowed)
        top = jnp.max(scores, axis=-1, keepdims=True)
        expo = jnp.exp(scores - top)
        total = jnp.sum(expo, axis=-1, keepdims=True)
        log_total = top + jnp.log(total)
        probs_low = (expo / total).astype(jnp.bfloat16)
        mixed = jnp.einsum(
            "hqk,kd->qhd", probs_low, key_block[:, head_size:], preferred_element_type=jnp.float32
        )
        mixed_low = mixed.reshape(batch_rows, heads_all * head_size).astype(jnp.bfloat16)
        middle = inputs[start:stop] + by_rows(mixed_low, out_w)
        normed_two = rms_norm(middle, gain_two.astype(jnp.float32)).astype(jnp.bfloat16)
        gate = jnp.dot(normed_two, gate_w, preferred_element_type=jnp.float32)
        up_part = jnp.dot(normed_two, up_w, preferred_element_type=jnp.float32)
        hidden = gelu_product(gate, up_part).astype(jnp.bfloat16)
        result = middle + by_rows(hidden, down_w)
        outputs.append(result.astype(jnp.bfloat16))
        saved.append(
            (query_rot, log_total, mixed_low, middle, normed_two, gate, up_part, hidden, allowed)
        )
    key_grads = jnp.zeros((WINDOW + token_count, 2 * head_size), jnp.float32)
    normed_grads = [None] * MICRO
    middle_grads = [None] * MICRO
    totals = None
    for batch in range(MICRO - 1, -1, -1):
        gain_one, gain_two, query_w, key_w, value_w, out_w, gate_w, up_w, down_w = (
            lax.all_gather(attn_gain, "tok", axis=0, tiled=True),
            lax.all_gather(ffn_gain, "tok", axis=0, tiled=True),
            lax.all_gather(w_query, "tok", axis=0, tiled=True),
            lax.all_gather(w_key, "tok", axis=0, tiled=True),
            lax.all_gather(w_value, "tok", axis=0, tiled=True),
            lax.all_gather(w_out, "tok", axis=0, tiled=True),
            lax.all_gather(w_gate, "tok", axis=0, tiled=True),
            lax.all_gather(w_up, "tok", axis=0, tiled=True),
            lax.all_gather(w_down, "tok", axis=0, tiled=True),
        )
        query_rot, log_total, mixed_low, middle, normed_two, gate, up_part, hidden, allowed = saved[
            batch
        ]
        start = batch * batch_rows
        stop = start + batch_rows
        key_block = all_keys[start : start + key_rows]
        down_cot = cotangent[start:stop]
        grad_down_w = outer_sum(down_cot, hidden)
        grad_hidden = jnp.dot(down_cot, down_w, preferred_element_type=jnp.float32)
        unused_value, ffn_back = jax.vjp(gelu_product, gate, up_part)
        grad_gate, grad_up = ffn_back(grad_hidden)
        gate_low = grad_gate.astype(jnp.bfloat16)
        up_low = grad_up.astype(jnp.bfloat16)
        grad_gate_w = outer_sum(normed_two, gate_low)
        grad_up_w = outer_sum(normed_two, up_low)
        grad_normed_two = by_rows(gate_low, gate_w) + by_rows(up_low, up_w)
        unused_norm, norm_back = jax.vjp(rms_norm, middle, gain_two.astype(jnp.float32))
        grad_middle, grad_gain_two = norm_back(grad_normed_two)
        grad_middle = grad_middle + down_cot.astype(jnp.float32)
        grad_branch = grad_middle.astype(jnp.bfloat16)
        grad_out_w = outer_sum(grad_branch, mixed_low)
        grad_mixed = (
            jnp.dot(grad_branch, out_w, preferred_element_type=jnp.float32)
            .astype(jnp.bfloat16)
            .reshape(batch_rows, heads_all, head_size)
        )
        scores = scores_of(query_rot, key_block[:, :head_size], allowed)
        probs = jnp.exp(scores - log_total)
        probs_low = probs.astype(jnp.bfloat16)
        grad_probs = jnp.einsum(
            "qhd,kd->hqk", grad_mixed, key_block[:, head_size:], preferred_element_type=jnp.float32
        )
        inner_sum = jnp.sum(probs * grad_probs, axis=-1, keepdims=True)
        grad_scores = (probs * (grad_probs - inner_sum) * scale).astype(jnp.bfloat16)
        grad_queries = jnp.einsum(
            "hqk,kd->qhd", grad_scores, key_block[:, :head_size], preferred_element_type=jnp.float32
        )
        grad_keys = jnp.einsum(
            "hqk,qhd->kd", grad_scores, query_rot, preferred_element_type=jnp.float32
        )
        grad_values = jnp.einsum(
            "hqk,qhd->kd", probs_low, grad_mixed, preferred_element_type=jnp.float32
        )
        key_grads = key_grads.at[start : start + key_rows].add(
            jnp.concatenate([grad_keys, grad_values], axis=1)
        )
        query_low = (
            rotate(grad_queries, -angles[start:stop])
            .reshape(batch_rows, heads_all * head_size)
            .astype(jnp.bfloat16)
        )
        grad_query_w = outer_sum(normed[start:stop], query_low)
        normed_grads[batch] = by_rows(query_low, query_w)
        middle_grads[batch] = grad_middle
        parts = (grad_gain_two, grad_query_w, grad_out_w, grad_gate_w, grad_up_w, grad_down_w)
        totals = parts if totals is None else jax.tree.map(jnp.add, totals, parts)
    shares = key_grads[WINDOW:]
    for hop in range(1, hop_count + 1):
        first_row = (hop_count - hop) * tail_rows
        returned = passed_along(
            key_grads[first_row : first_row + tail_rows].astype(jnp.bfloat16), "tok", -hop
        ).astype(jnp.float32)
        shares = shares.at[token_count - tail_rows :].add(returned)
    key_low = rotate(shares[:, None, :head_size], -angles)[:, 0].astype(jnp.bfloat16)
    value_low = shares[:, head_size:].astype(jnp.bfloat16)
    grad_key_w = outer_sum(normed, key_low)
    grad_value_w = outer_sum(normed, value_low)
    grad_normed = (
        jnp.concatenate(normed_grads, axis=0)
        + by_rows(key_low, key_w)
        + by_rows(value_low, value_w)
    )
    unused_first, first_back = jax.vjp(rms_norm, inputs, gain_one.astype(jnp.float32))
    grad_inputs, grad_gain_one = first_back(grad_normed)
    grad_tokens = (jnp.concatenate(middle_grads, axis=0) + grad_inputs).astype(jnp.bfloat16)
    gain_two_sum, query_sum, out_sum, gate_sum, up_sum, down_sum = totals
    summed = (
        lax.psum_scatter(grad_gain_one, "tok", scatter_dimension=0, tiled=True),
        lax.psum_scatter(gain_two_sum, "tok", scatter_dimension=0, tiled=True),
        lax.psum_scatter(query_sum, "tok", scatter_dimension=0, tiled=True),
        lax.psum_scatter(grad_key_w, "tok", scatter_dimension=0, tiled=True),
        lax.psum_scatter(grad_value_w, "tok", scatter_dimension=0, tiled=True),
        lax.psum_scatter(out_sum, "tok", scatter_dimension=0, tiled=True),
        lax.psum_scatter(gate_sum, "tok", scatter_dimension=0, tiled=True),
        lax.psum_scatter(up_sum, "tok", scatter_dimension=0, tiled=True),
        lax.psum_scatter(down_sum, "tok", scatter_dimension=0, tiled=True),
    )
    return (
        jnp.concatenate(outputs, axis=0),
        grad_tokens,
        summed[0],
        summed[1],
        summed[2],
        summed[3],
        summed[4],
        summed[5],
        summed[6],
        summed[7],
        summed[8],
    )


def solution(mesh):
    in_specs = (
        P("tok", None),
        P("tok", None),
        P("tok"),
        P("tok"),
        P("tok", None),
        P("tok", None),
        P("tok", None),
        P("tok", None),
        P("tok", None),
        P("tok", None),
        P("tok", None),
        P(),
        P("tok"),
    )
    out_specs = (
        P("tok", None),
        P("tok", None),
        P("tok"),
        P("tok"),
        P("tok", None),
        P("tok", None),
        P("tok", None),
        P("tok", None),
        P("tok", None),
        P("tok", None),
        P("tok", None),
    )
    return jax.shard_map(
        on_device, mesh=mesh, in_specs=in_specs, out_specs=out_specs, check_vma=False
    )
```

profile of v0, /device:TPU:0, one launch (start us, length us, event | category | flops | bytes accessed | tf_op | source)
XLA Modules:
  0.0 1996.8 jit_solution(6181165232666433269)
XLA Ops:
  12.3 42.2 %all-reduce.7 = (bf16[1536]{0:T(1024)(128)(2,1)S(1)}, bf16[1536]{0:T(1024)(128)(2,1)S(1)}) all-reduce(bf16[1536]{0:T(1024)(128)(2,1)S(1)} %dynamic-update-slice.10, bf16[1536]{0:T(1024)(128)(2,1)S(1)} %dynamic-update-slice.11), channel_id=1, replica_groups=mesh['tok'=32] {'tok'}, use_global_device_ids=true, to_apply=%add.2 | all-reduce | flops 3072 | bytes 12288
  55.2 42.6 %all_gather.19 = bf16[1536,128]{1,0:T(8,128)(2,1)S(1)} all-gather(bf16[48,128]{1,0:T(8,128)(2,1)} %param.30), channel_id=1, replica_groups=mesh['tok'=32] {'tok'}, dimensions={0}, use_global_device_ids=true | all-gather | bytes 405504 | tf_op jit(solution)/shard_map/all_gather | solution.py:102
  100.5 38.5 %all_gather.20 = bf16[1536,128]{1,0:T(8,128)(2,1)S(1)} all-gather(bf16[48,128]{1,0:T(8,128)(2,1)S(1)} %copy-done.73), channel_id=1, replica_groups=mesh['tok'=32] {'tok'}, dimensions={0}, use_global_device_ids=true | all-gather | bytes 405504 | tf_op jit(solution)/shard_map/all_gather | solution.py:103
  141.8 3.1 collective-permute-start.1
  144.8 3.5 collective-permute-start
  159.2 4.3 fusion.63
  166.4 2.8 copy.164
  169.2 4.3 fusion.66
  176.4 2.8 copy.162
  181.2 7.1 fusion.127
  188.3 7.5 fusion.8
  195.8 7.7 fusion.57
  203.7 5.0 multiply_reduce_fusion.8
  210.4 7.2 fusion.126
  217.6 7.8 fusion.9
  225.3 7.5 fusion.56
  235.7 16.8 all-gather.10.cloned.1.call-done
  252.5 10.5 fusion.128
  262.9 93.7 %all-gather.12.cloned.1.call-done = bf16[1536,4608]{1,0:T(8,128)(2,1)} async-done(((bf16[48,4608]{1,0:T(8,128)(2,1)}), bf16[1536,4608]{1,0:T(8,128)(2,1)}) %all-gather.12.cloned.1.call-update) | async-done | bytes 14155792 | tf_op jit(solution)/shard_map/all_gather | solution.py:106
  356.6 10.7 fusion.129
  367.3 93.5 %all-gather.14.cloned.1.call-done = bf16[1536,4608]{1,0:T(8,128)(2,1)} async-done(((bf16[48,4608]{1,0:T(8,128)(2,1)}), bf16[1536,4608]{1,0:T(8,128)(2,1)}) %all-gather.14.cloned.1.call-update) | async-done | bytes 14155792 | tf_op jit(solution)/shard_map/all_gather | solution.py:107
  460.7 14.7 multiply_convert_fusion.1
  475.4 9.1 fusion.132
  484.6 12.8 multiply_reduce_fusion.3
  497.4 7.3 fusion.130
  504.7 7.3 fusion.131
  512.0 11.3 multiply_convert_fusion
  523.3 9.1 fusion.133
  532.4 17.0 multiply_reduce_fusion.4
  549.4 3.2 fusion.52
  552.6 5.7 convolution_convert_fusion
  560.6 9.1 fusion.84
  569.7 9.1 fusion.49
  578.8 26.1 %fusion.54 = f32[256,12,128]{0,2,1:T(8,128)} fusion(f32[1280,256,12]{1,0,2:T(8,128)} %fusion.84, f32[12,256,1280]{1,2,0:T(8,128)} %get-tuple-element.171, f32[12,256]{1,0:T(8,128)S(1)} %log_add_fusion, bf16[1536,256]{0,1:T(8,128)(2,1)} %maximum_maximum_fusion), kind=kOutput, calls=%fused_computation.108 | convolution fusion | flops 1034162432 | bytes 64847872 | tf_op jit(solution)/shard_map/hqk,kd->qhd/dot_general | solution.py:204
  604.9 26.8 %fusion.44 = f32[1280,128]{0,1:T(8,128)} fusion(f32[1280,256,12]{1,0,2:T(8,128)} %fusion.84, f32[12,256,1280]{1,2,0:T(8,128)} %get-tuple-element.171, f32[12,256]{1,0:T(8,128)S(1)} %log_add_fusion, bf16[256,12,64]{2,0,1:T(8,128)(2,1)} %copy-done.37, bf16[256,12,64]{2,0,1:T(8,128)(2,1)} %copy-done.36), kind=kOutput, calls=%fused_computation.85 | convolution fusion | flops 1035735296 | bytes 32911360 | tf_op jit(solution)/shard_map/hqk,qhd->kd/dot_general | solution.py:207
  631.8 4.6 convolution_convert_fusion.1
  637.8 8.7 fusion.83
  646.5 9.1 fusion.46
  655.6 26.5 %fusion.45 = f32[1280,128]{0,1:T(8,128)} fusion(f32[1280,256,12]{1,0,2:T(8,128)} %fusion.83, f32[12,256,1280]{1,2,0:T(8,128)} %get-tuple-element.173, f32[12,256]{1,0:T(8,128)S(1)} %log_add_fusion.1, bf16[256,12,64]{2,0,1:T(8,128)(2,1)} %copy-done.35, bf16[256,12,64]{2,0,1:T(8,128)(2,1)S(1)} %copy-done.34), kind=kOutput, calls=%fused_computation.86 | convolution fusion | flops 1035735296 | bytes 32911360 | tf_op jit(solution)/shard_map/hqk,qhd->kd/dot_general | solution.py:207
  688.1 6.5 collective-permute-done.3
  698.4 26.4 %fusion.55 = f32[256,12,128]{0,2,1:T(8,128)} fusion(f32[1280,256,12]{1,0,2:T(8,128)} %fusion.83, f32[12,256,1280]{1,2,0:T(8,128)} %get-tuple-element.173, f32[12,256]{1,0:T(8,128)S(1)} %log_add_fusion.1, bf16[1536,256]{0,1:T(8,128)(2,1)} %maximum_maximum_fusion), kind=kOutput, calls=%fused_computation.109 | convolution fusion | flops 1034162432 | bytes 64847872 | tf_op jit(solution)/shard_map/hqk,kd->qhd/dot_general | solution.py:204
  724.8 6.2 fusion.61
  735.2 8.8 convolution_add_fusion.3
  744.1 2.7 fusion.76
  746.8 5.0 convolution_add_fusion.2
  753.0 13.2 fusion.136
  766.2 19.4 convolution_add_fusion.1
  785.7 13.1 fusion.137
  798.8 19.5 convolution_add_fusion
  819.7 13.7 fusion.68
  833.4 19.5 add_bitcast_fusion
  852.9 27.8 %copy.160 = f32[1536,4608]{1,0:T(8,128)} copy(f32[1536,4608]{0,1:T(8,128)} %add_bitcast_fusion) | data formatting | bytes 56623104
  882.4 8.7 fusion.43
  891.2 7.6 fusion.42
  900.1 3.8 fusion.135
  903.9 3.8 fusion.134
  909.6 2.9 multiply_reduce_fusion
  912.5 41.6 %all-reduce.6 = (f32[1536]{0:T(1024)S(1)}, f32[1536]{0:T(1024)S(1)}) all-reduce(f32[1536]{0:T(1024)S(1)} %get-tuple-element.119, f32[1536]{0:T(1024)S(1)} %add.228), channel_id=2, replica_groups=mesh['tok'=32] {'tok'}, use_global_device_ids=true, to_apply=%region_13.14.clone | all-reduce | flops 3072 | bytes 24576
  955.3 4.3 fusion.41
  959.6 78.0 %reduce-scatter.10.cloned.1.call-done = f32[48,1536]{1,0:T(8,128)} async-done(((f32[1536,1536]{1,0:T(8,128)}), f32[48,1536]{1,0:T(8,128)}) %reduce-scatter.10.cloned.1.call-update) | async-done | bytes 294928 | tf_op jit(solution)/shard_map/reduce_scatter | solution.py:249
  1037.6 141.9 %reduce-scatter.16.cloned.1.call-done = f32[48,1536]{1,0:T(8,128)} async-done(((f32[1536,1536]{1,0:T(8,128)}), f32[48,1536]{1,0:T(8,128)}) %reduce-scatter.16.cloned.1.call-update) | async-done | bytes 294928 | tf_op jit(solution)/shard_map/reduce_scatter | solution.py:252
  1179.6 269.8 %reduce-scatter.18.cloned.1.call-done = f32[48,4608]{1,0:T(8,128)} async-done(((f32[1536,4608]{1,0:T(8,128)}), f32[48,4608]{1,0:T(8,128)}) %reduce-scatter.18.cloned.1.call-update) | async-done | bytes 884752 | tf_op jit(solution)/shard_map/reduce_scatter | solution.py:253
  1449.3 270.4 %reduce-scatter.20.cloned.1.call-done = f32[48,4608]{1,0:T(8,128)} async-done(((f32[1536,4608]{1,0:T(8,128)}), f32[48,4608]{1,0:T(8,128)}) %reduce-scatter.20.cloned.1.call-update) | async-done | bytes 884752 | tf_op jit(solution)/shard_map/reduce_scatter | solution.py:254
  1719.7 270.1 %reduce-scatter.22.cloned.1.call-done = f32[48,4608]{1,0:T(8,128)} async-done(((f32[1536,4608]{1,0:T(8,128)}), f32[48,4608]{1,0:T(8,128)}) %reduce-scatter.22.cloned.1.call-update) | async-done | bytes 884752
  (256 shorter events, 60.2 us)
Async XLA Ops:
  7.2 90.6 %copy-start.2 = (bf16[512,1536]{1,0:T(8,128)(2,1)S(1)}, bf16[512,1536]{1,0:T(8,128)(2,1)}, u32[]{:S(2)}) copy-start(bf16[512,1536]{1,0:T(8,128)(2,1)} %param.25) | copy-start | bytes 4718596
  7.2 152.1 %all-gather.6.cloned.1.call-start = ((), (), s32[]{:S(2)}) async-start(), calls=%async_computation.7 | async-start | bytes 4866048 | tf_op jit(solution)/shard_map/all_gather | solution.py:101
  7.9 195.7 %all-gather.8.cloned.1.call-start = ((), (), s32[]{:S(2)}) async-start(), calls=%async_computation.8 | async-start | bytes 4866048 | tf_op jit(solution)/shard_map/all_gather | solution.py:104
  8.7 243.8 %all-gather.10.cloned.1.call-start = ((), (), s32[]{:S(2)}) async-start(), calls=%async_computation.9 | async-start | bytes 14598144 | tf_op jit(solution)/shard_map/all_gather | solution.py:105
  9.4 347.2 %all-gather.12.cloned.1.call-start = ((), (), s32[]{:S(2)}) async-start(), calls=%async_computation.10 | async-start | bytes 14598144 | tf_op jit(solution)/shard_map/all_gather | solution.py:106
  10.0 450.7 %all-gather.14.cloned.1.call-start = ((), (), s32[]{:S(2)}) async-start(), calls=%async_computation.11 | async-start | bytes 14598144 | tf_op jit(solution)/shard_map/all_gather | solution.py:107
  10.6 949.1 %reduce-scatter.12.cloned.1.call-start = ((), (), s32[]{:S(2)}) async-start(), calls=%async_computation.13 | async-start | bytes 811008 | tf_op jit(solution)/shard_map/reduce_scatter | solution.py:250
  54.5 45.3 %copy-start.64 = (f32[1536]{0:T(1024)}, f32[1536]{0:T(1024)S(1)}, u32[]{:S(2)}) copy-start(f32[1536]{0:T(1024)S(1)} %convert_element_type.137) | copy-start | bytes 18436
  55.2 95.2 %copy-start.67 = (f32[512]{0:T(512)}, f32[512]{0:T(512)S(1)}, u32[]{:S(2)}) copy-start(f32[512]{0:T(512)S(1)} %convert_element_type.139) | copy-start | bytes 6148
  55.2 95.1 %copy-start.76 = (f32[64]{0:T(128)}, f32[64]{0:T(128)S(1)}, u32[]{:S(2)}) copy-start(f32[64]{0:T(128)S(1)} %multiply_power_fusion) | copy-start | bytes 772
  98.7 40.2 %copy-start.69 = (f32[512]{0:T(512)}, f32[512]{0:T(512)S(1)}, u32[]{:S(2)}) copy-start(f32[512]{0:T(512)S(1)} %fusion.105) | copy-start | bytes 6148
  99.2 70.0 %copy-start = (bf16[512,1536]{1,0:T(8,128)(2,1)}, bf16[512,1536]{1,0:T(8,128)(2,1)S(1)}, u32[]{:S(2)}) copy-start(bf16[512,1536]{1,0:T(8,128)(2,1)S(1)} %multiply_convert_fusion.4) | copy-start | bytes 4718596
  100.4 41.3 %copy-start.48 = (bf16[512,128]{0,1:T(8,128)(2,1)}, bf16[512,128]{0,1:T(8,128)(2,1)S(1)}, u32[]{:S(2)}) copy-start(bf16[512,128]{0,1:T(8,128)(2,1)S(1)} %maximum_bitcast_fusion) | copy-start | bytes 393220
  141.8 13.6 copy-start.66
  141.8 15.3 collective-permute-start.1
  144.8 12.3 collective-permute-start
  181.1 7.2 copy-start.33
  181.1 7.2 copy-start.35
  203.6 5.0 copy-start.50
  203.6 5.1 copy-start.14
  203.6 5.1 copy-start.58
  203.7 5.0 copy-start.59
  208.6 26.8 %copy-start.15 = (f32[256,1536]{1,0:T(8,128)}, f32[256,1536]{1,0:T(8,128)S(1)}, u32[]{:S(2)}) copy-start(f32[256,1536]{1,0:T(8,128)S(1)} %get-tuple-element.175) | copy-start | bytes 4718596
  209.2 8.4 copy-start.36
  209.2 8.4 copy-start.37
  217.6 15.3 slice-start
  225.3 7.5 copy-start.32
  225.3 7.5 slice-start.1
  235.7 120.9 %copy-start.8 = (bf16[256,1536]{1,0:T(8,128)(2,1)}, bf16[256,1536]{1,0:T(8,128)(2,1)S(1)}, u32[]{:S(2)}) copy-start(bf16[256,1536]{1,0:T(8,128)(2,1)S(1)} %multiply_convert_fusion.6) | copy-start | bytes 2359300
  262.9 197.8 %copy-start.11 = (bf16[512,1536]{1,0:T(8,128)(2,1)S(1)}, bf16[512,1536]{1,0:T(8,128)(2,1)}, u32[]{:S(2)}) copy-start(bf16[512,1536]{1,0:T(8,128)(2,1)} %param.26) | copy-start | bytes 4718596
  475.4 9.1 copy-start.43
  497.4 7.3 copy-start.38
  523.3 9.1 copy-start.45
  523.3 9.1 copy-start.44
  532.4 17.0 copy-start.12
  532.4 17.0 copy-start.16
  552.6 79.1 %copy-start.6 = (f32[256,1536]{1,0:T(8,128)}, f32[256,1536]{1,0:T(8,128)S(1)}, u32[]{:S(2)}) copy-start(f32[256,1536]{1,0:T(8,128)S(1)} %get-tuple-element.145) | copy-start | bytes 4718596
  552.6 191.4 %copy-start.4 = (f32[256,1536]{1,0:T(8,128)}, f32[256,1536]{1,0:T(8,128)S(1)}, u32[]{:S(2)}) copy-start(f32[256,1536]{1,0:T(8,128)S(1)} %get-tuple-element.146) | copy-start | bytes 4718596
  560.6 9.1 copy-start.10
  646.5 9.1 copy-start.34
  655.6 26.5 %copy-start.42 = (f32[1280,128]{0,1:T(8,128)S(1)}, f32[1280,128]{0,1:T(8,128)}, u32[]{:S(2)}) copy-start(f32[1280,128]{0,1:T(8,128)} %fusion.49) | copy-start | bytes 1966084
  684.2 11.3 copy-start.68
  684.2 11.3 copy-start.77
  684.2 10.4 collective-permute-start.3
  685.5 9.1 collective-permute-start.2
  686.9 9.9 copy-start.1
  698.3 261.3 %reduce-scatter.14.cloned.1.call-start = ((), (), s32[]{:S(2)}) async-start(), calls=%async_computation.14 | async-start | bytes 811008 | tf_op jit(solution)/shard_map/reduce_scatter | solution.py:251
  724.8 6.2 copy-start.27
  732.6 305.1 %reduce-scatter.10.cloned.1.call-start = ((), (), s32[]{:S(2)}) async-start(), calls=%async_computation.12 | async-start | bytes 9732096 | tf_op jit(solution)/shard_map/reduce_scatter | solution.py:249
  744.0 435.6 %reduce-scatter.16.cloned.1.call-start = ((), (), s32[]{:S(2)}) async-start(), calls=%async_computation.15 | async-start | bytes 9732096 | tf_op jit(solution)/shard_map/reduce_scatter | solution.py:252
  751.9 14.3 copy-start.9
  751.9 697.4 %reduce-scatter.18.cloned.1.call-start = ((), (), s32[]{:S(2)}) async-start(), calls=%async_computation.16 | async-start | bytes 29196288 | tf_op jit(solution)/shard_map/reduce_scatter | solution.py:253
  785.7 934.0 %reduce-scatter.20.cloned.1.call-start = ((), (), s32[]{:S(2)}) async-start(), calls=%async_computation.17 | async-start | bytes 29196288 | tf_op jit(solution)/shard_map/reduce_scatter | solution.py:254
  818.3 1171.5 %reduce-scatter.22.cloned.1.call-start = ((), (), s32[]{:S(2)}) async-start(), calls=%async_computation.18 | async-start | bytes 29196288
  882.4 8.8 copy-start.17
  882.4 8.8 copy-start.20
  891.1 7.6 copy-start.49
  891.1 8.9 copy-start.29
  900.0 3.9 copy-start.31
  903.9 3.9 copy-start.25
  903.9 3.9 copy-start.55
  903.9 3.9 copy-start.57
  909.5 45.7 %copy-start.72 = (f32[512]{0:T(512)S(1)}, f32[512]{0:T(512)}, u32[]{:S(2)}) copy-start(f32[512]{0:T(512)} %copy-done.71) | copy-start | bytes 6148
  909.5 45.7 %copy-start.5 = (f32[256,1536]{1,0:T(8,128)S(1)}, f32[256,1536]{1,0:T(8,128)}, u32[]{:S(2)}) copy-start(f32[256,1536]{1,0:T(8,128)} %copy-done.4) | copy-start | bytes 4718596
  (32 other events, 52.1 us)
Sparse Core Ops, SparseCore 0:
  10.9 68.8 all-gather.5
  82.8 62.7 all-gather.7
  148.4 103.9 all-gather.9
  255.2 101.3 all-gather.11
  359.3 101.3 all-gather.13
  698.5 97.6 reduce-scatter.11
  801.8 94.5 reduce-scatter.13
  902.9 134.7 reduce-scatter.9
  1045.1 134.3 reduce-scatter.15
  1186.4 262.8 reduce-scatter.17
  1456.3 263.3 reduce-scatter.19
  1726.6 263.1 reduce-scatter.21
where the time goes:
time: 2000 us
  waiting for transfers between devices  1240 us (62%)
  matrix products  461 us (23%)
  blocking collectives  165 us (8%)
  local copies, waits for them, and re-layouts  59.8 us (3%)
  other arithmetic  42.7 us (2%)
    unnamed x13, waiting for transfers between devices  273 us
    reduce_scatter x1, waiting for transfers between devices, on_device(): lax.psum_scatter(up_sum, 'tok', scatter_dimension=0, tiled=True)  270 us
    reduce_scatter x1, waiting for transfers between devices, on_device(): lax.psum_scatter(gate_sum, 'tok', scatter_dimension=0, tiled=True)  270 us
    reduce_scatter x1, waiting for transfers between devices, on_device(): lax.psum_scatter(out_sum, 'tok', scatter_dimension=0, tiled=True)  142 us
    dot_general x12, matrix products, outer_sum(): lax.dot_general(left_side, right_side, (((0,), (0,)), ((), ())), preferre...  124 us
    all_gather x1, waiting for transfers between devices, on_device(): lax.all_gather(w_up, 'tok', axis=0, tiled=True)  93.7 us
    all_gather x1, waiting for transfers between devices, on_device(): lax.all_gather(w_down, 'tok', axis=0, tiled=True)  93.5 us
    unnamed x2, blocking collectives  83.8 us
  transfers between devices with their start and end apart: 16, of which 9 were waited for; matrix products, arithmetic and copies ran while one was open for 16% of the time, Pallas kernels for 0%

commit v1 on v0

v1 whole, which is shorter than its diff:
```python
import functools

import jax
import jax.numpy as jnp
from jax import lax
from jax.experimental import pallas as pl
from jax.experimental.pallas import tpu as pltpu
from jax.sharding import PartitionSpec as P

HQ = 12
HD = 128
WINDOW = 1024
EPSILON = 1e-06

CORE, NEAR, SIDE, GROUP, RING = 1, 2, 4, 4, 8
LONGEST_RING = 8
LOG2E = 1.4426950408889634
LOW = jnp.bfloat16
FULL = jnp.float32
MIB = 1024 * 1024


def flip(array, bit):
    size = lax.axis_size("tok")
    return lax.ppermute(array, "tok", [(i, i ^ bit) for i in range(size)])


def around(array):
    size = lax.axis_size("tok")
    return lax.ppermute(array, "tok", [(i, (i + RING) % size) for i in range(size)])


def passed_along(array, by):
    size = lax.axis_size("tok")
    pairs = [(i, i + by) for i in range(size) if 0 <= i + by < size]
    return lax.ppermute(array, "tok", pairs)


def rms_norm(values, scales):
    return values * lax.rsqrt(jnp.mean(values * values, axis=-1, keepdims=True) + EPSILON) * scales


def outer_sum(left_side, right_side):
    return lax.dot_general(
        left_side, right_side, (((0,), (0,)), ((), ())), preferred_element_type=FULL
    )


def by_rows(left_side, right_side):
    return lax.dot_general(
        left_side, right_side, (((1,), (1,)), ((), ())), preferred_element_type=FULL
    )


def matmul(left_side, right_side):
    return jnp.dot(left_side, right_side, preferred_element_type=FULL)


def pick(array, index):
    return lax.dynamic_index_in_dim(array, index, 0, keepdims=False)


def place():
    device = lax.axis_index("tok")
    return device, device % 2, (device // 2) % 2, (device // 4) % 2, device // RING


def rows_to_group(array):
    two = jnp.concatenate([array, flip(array, NEAR)], axis=0)
    return jnp.concatenate([two, flip(two, CORE)], axis=0)


def rows_from_group(partial):
    half = partial.shape[0] // 2
    two = partial[:half].astype(FULL) + flip(partial[half:].astype(LOW), CORE).astype(FULL)
    quarter = half // 2
    return two[:quarter] + flip(two[quarter:].astype(LOW), NEAR).astype(FULL)


def slices_to_group(parts):
    _, core, near, _, _ = place()
    rows, columns = parts.shape[1:]
    mine = lax.dynamic_slice_in_dim(parts, 2 * near, 2, 0)
    theirs = flip(lax.dynamic_slice_in_dim(parts, 2 * (1 - near), 2, 0), NEAR)
    here = jnp.stack([pick(mine, core), pick(theirs, core)])
    away = flip(jnp.stack([pick(mine, 1 - core), pick(theirs, 1 - core)]), CORE)
    by_core = jnp.where(core == 0, jnp.stack([here, away], 1), jnp.stack([away, here], 1))
    by_near = jnp.where(near == 0, by_core, by_core[::-1])
    return by_near.reshape(4 * rows, columns)


def slices_from_group(block):
    _, core, near, _, _ = place()
    rows, columns = block.shape[0] // 4, block.shape[1]
    parts = block.astype(LOW).reshape(2, 2, rows, columns)
    mine, theirs = pick(parts, near), flip(pick(parts, 1 - near), NEAR)
    here = jnp.stack([pick(mine, core), pick(theirs, core)])
    away = flip(jnp.stack([pick(mine, 1 - core), pick(theirs, 1 - core)]), CORE)
    by_core = jnp.where(core == 0, jnp.stack([here, away], 1), jnp.stack([away, here], 1))
    by_near = jnp.where(near == 0, by_core, by_core[::-1])
    return by_near.reshape(4, rows, columns)


def groups_of(stride):
    size = lax.axis_size("tok")
    return [[s + stride * k for k in range(size // stride)] for s in range(stride)]


def spread(block, stages):
    size = lax.axis_size("tok")
    ring = size // RING
    if ring > LONGEST_RING:
        return lax.all_gather(
            block, "tok", axis=0, tiled=True, axis_index_groups=groups_of(stages[-1])
        )
    device, _, _, _, z = place()
    rows, columns = block.shape
    steps = RING // stages[-1]
    total = jnp.zeros((ring * steps, rows, columns), block.dtype)
    own = block
    for step in range(ring):
        chunk = lax.rem(z - step + ring, ring)
        blocks = [own]
        for bit in stages:
            stacked = jnp.stack(blocks) if len(blocks) > 1 else blocks[0][None]
            got = flip(stacked, bit)
            blocks = blocks + [got[k] for k in range(len(blocks))]
        low_bits = lax.rem(device, RING) // stages[-1]
        for k, piece in enumerate(blocks):
            mask = 0
            for j, bit in enumerate(stages):
                if (k >> j) & 1:
                    mask |= bit // stages[-1]
            index = chunk * steps + lax.bitwise_xor(low_bits, mask)
            total = lax.dynamic_update_index_in_dim(total, piece, index, 0)
        if step < ring - 1:
            own = around(own)
    return total.reshape(ring * steps * rows, columns)


def collect(partial, stages):
    size = lax.axis_size("tok")
    ring = size // RING
    if ring > LONGEST_RING:
        return lax.psum_scatter(
            partial.astype(FULL),
            "tok",
            scatter_dimension=0,
            tiled=True,
            axis_index_groups=groups_of(stages[-1]),
        )
    device, _, _, _, z = place()
    steps = RING // stages[-1]
    rows, columns = partial.shape[0] // (ring * steps), partial.shape[1]
    parts = partial.astype(LOW).reshape((ring, *([2] * len(stages)), rows, columns))

    def piece(chunk):
        held = pick(parts, chunk)
        for bit in reversed(stages):
            axis = stages.index(bit)
            own_bit = (device // bit) % 2
            keep = lax.dynamic_index_in_dim(held, own_bit, axis, keepdims=False)
            give = lax.dynamic_index_in_dim(held, 1 - own_bit, axis, keepdims=False)
            held = keep.astype(FULL) + flip(give.astype(LOW), bit).astype(FULL)
        return held

    total = piece(lax.rem(z - 1 + ring, ring))
    for step in range(1, ring):
        total = around(total.astype(LOW)).astype(FULL) + piece(lax.rem(z - 1 - step + 2 * ring, ring))
    return total


def turn(values, cosine, sine):
    return values * cosine + pltpu.roll(values, HD // 2, 1) * sine


def mask_into(bias, key_segments, query_segments, block):
    keys, queries = bias.shape
    for start in range(0, queries, block):
        offset = (
            lax.broadcasted_iota(jnp.int32, (keys, block), 0)
            - lax.broadcasted_iota(jnp.int32, (keys, block), 1)
            - start
        )
        same = key_segments[...] == query_segments[:, start : start + block]
        allowed = same & (offset > 0) & (offset <= WINDOW)
        bias[:, start : start + block] = jnp.where(allowed, 0.0, -jnp.inf)


def attend_kernel(
    block, factor, q_ref, key_ref, value_t_ref, ks_ref, qs_ref, cos_ref, sin_ref,
    rot_ref, mixed_ref, log_ref, bias,
):
    @pl.when(pl.program_id(0) == 0)
    def _():
        mask_into(bias, ks_ref, qs_ref, block)

    queries = q_ref.shape[0]
    rot_ref[...] = turn(q_ref[...], cos_ref[...], sin_ref[...]).astype(LOW)
    for start in range(0, queries, block):
        rows, span = pl.ds(start, block), pl.ds(start, WINDOW + block)
        raw = by_rows(key_ref[span, :], rot_ref[rows, :])
        score = raw * factor + bias[span, rows]
        top = jnp.max(score, axis=0, keepdims=True)
        expo = jnp.exp2(score - top)
        total = jnp.sum(expo, axis=0, keepdims=True)
        mixed_t = matmul(value_t_ref[:, span], expo.astype(LOW)) / total
        mixed_ref[rows, :] = mixed_t.T.astype(LOW)
        log_ref[0, :, rows] = top + jnp.log2(total)


def attend(raw_query, key_value, key_segments, query_segments, cosine, sine):
    queries, width = raw_query.shape
    keys = key_value.shape[0]
    heads = width // HD
    block = min(256, queries)
    head = pl.BlockSpec((queries, HD), lambda h: (0, h))
    whole = lambda shape: pl.BlockSpec(shape, lambda h: (0,) * len(shape))
    cost = 4 * width * queries * (WINDOW + block)
    return pl.pallas_call(
        functools.partial(attend_kernel, block, HD**-0.5 * LOG2E),
        grid=(heads,),
        in_specs=[
            head,
            whole((keys, HD)),
            whole((HD, keys)),
            whole((keys, 1)),
            whole((1, queries)),
            whole((queries, HD)),
            whole((queries, HD)),
        ],
        out_specs=[head, head, pl.BlockSpec((1, 1, queries), lambda h: (h, 0, 0))],
        out_shape=[
            jax.ShapeDtypeStruct((queries, width), LOW),
            jax.ShapeDtypeStruct((queries, width), LOW),
            jax.ShapeDtypeStruct((heads, 1, queries), FULL),
        ],
        scratch_shapes=[pltpu.VMEM((keys, queries), FULL)],
        compiler_params=pltpu.CompilerParams(vmem_limit_bytes=40 * MIB),
        cost_estimate=pl.CostEstimate(
            flops=4 * cost, bytes_accessed=8 * queries * width, transcendentals=0
        ),
    )(
        raw_query,
        key_value[:, :HD],
        key_value[:, HD:].T,
        key_segments[:, None],
        query_segments[None, :],
        cosine,
        sine,
    )


def attend_back_kernel(
    block, factor, rot_ref, grad_ref, mixed_ref, log_ref, key_ref, value_ref, key_t_ref, ks_ref, qs_ref,
    cos_ref, sin_ref, query_out, key_out, value_out, bias,
):
    @pl.when(pl.program_id(0) == 0)
    def _():
        mask_into(bias, ks_ref, qs_ref, block)
        key_out[...] = jnp.zeros_like(key_out)
        value_out[...] = jnp.zeros_like(value_out)

    queries = rot_ref.shape[0]
    for start in range(0, queries, block):
        rows, span = pl.ds(start, block), pl.ds(start, WINDOW + block)
        rot, grad = rot_ref[rows, :], grad_ref[rows, :]
        product = grad.astype(FULL) * mixed_ref[rows, :].astype(FULL)
        inner = jnp.sum(product.T, axis=0, keepdims=True)
        raw = by_rows(key_ref[span, :], rot)
        prob = jnp.exp2(raw * factor + (bias[span, rows] - log_ref[0, :, rows]))
        grad_prob = by_rows(value_ref[span, :], grad)
        grad_raw = (prob * (grad_prob - inner)).astype(LOW)
        value_out[span, :] += matmul(prob.astype(LOW), grad)
        key_out[span, :] += matmul(grad_raw, rot)
        back = matmul(key_t_ref[:, span], grad_raw).T * HD**-0.5
        query_out[rows, :] = turn(back, cos_ref[rows, :], -sin_ref[rows, :]).astype(LOW)


def attend_back(rot, grad, mixed, logs, key_value, key_segments, query_segments, cosine, sine):
    queries, width = rot.shape
    keys = key_value.shape[0]
    heads = width // HD
    block = min(256, queries)
    head = pl.BlockSpec((queries, HD), lambda h: (0, h))
    whole = lambda shape: pl.BlockSpec(shape, lambda h: (0,) * len(shape))
    cost = 10 * width * queries * (WINDOW + block)
    return pl.pallas_call(
        functools.partial(attend_back_kernel, block, HD**-0.5 * LOG2E),
        grid=(heads,),
        in_specs=[
            head,
            head,
            head,
            pl.BlockSpec((1, 1, queries), lambda h: (h, 0, 0)),
            whole((keys, HD)),
            whole((keys, HD)),
            whole((HD, keys)),
            whole((keys, 1)),
            whole((1, queries)),
            whole((queries, HD)),
            whole((queries, HD)),
        ],
        out_specs=[head, whole((keys, HD)), whole((keys, HD))],
        out_shape=[
            jax.ShapeDtypeStruct((queries, width), LOW),
            jax.ShapeDtypeStruct((keys, HD), FULL),
            jax.ShapeDtypeStruct((keys, HD), FULL),
        ],
        scratch_shapes=[pltpu.VMEM((keys, queries), FULL)],
        compiler_params=pltpu.CompilerParams(vmem_limit_bytes=40 * MIB),
        cost_estimate=pl.CostEstimate(
            flops=3 * cost, bytes_accessed=8 * queries * width, transcendentals=0
        ),
    )(
        rot,
        grad,
        mixed,
        logs,
        key_value[:, :HD],
        key_value[:, HD:],
        key_value[:, :HD].T,
        key_segments[:, None],
        query_segments[None, :],
        cosine,
        sine,
    )


GELU_A = 0.7978845608028654
GELU_B = 0.044715


def hidden_kernel(normed_ref, cot_ref, gate_ref, up_ref, down_ref, hidden_ref, gate_out, up_out):
    gate = matmul(normed_ref[...], gate_ref[...])
    up = matmul(normed_ref[...], up_ref[...])
    grad_hidden = matmul(cot_ref[...], down_ref[...])
    square = gate * gate
    bent = jnp.tanh(gate * (GELU_A + GELU_A * GELU_B * square))
    half = 0.5 * (1.0 + bent)
    value = gate * half
    slope = half + 0.5 * gate * (1.0 - bent * bent) * (GELU_A + 3.0 * GELU_A * GELU_B * square)
    hidden_ref[...] = (value * up).astype(LOW)
    gate_out[...] = (grad_hidden * up * slope).astype(LOW)
    up_out[...] = (grad_hidden * value).astype(LOW)


def hidden_and_grads(normed, cotangent, gate_w, up_w, down_w):
    tokens, width = normed.shape
    columns = gate_w.shape[1]
    rows, wide = min(512, tokens), 384
    token_block = pl.BlockSpec((rows, width), lambda j, i: (i, 0))
    weight_block = pl.BlockSpec((width, wide), lambda j, i: (0, j))
    out_block = pl.BlockSpec((rows, wide), lambda j, i: (i, j))
    return pl.pallas_call(
        hidden_kernel,
        grid=(columns // wide, tokens // rows),
        in_specs=[token_block, token_block, weight_block, weight_block, weight_block],
        out_specs=[out_block] * 3,
        out_shape=[jax.ShapeDtypeStruct((tokens, columns), LOW)] * 3,
        compiler_params=pltpu.CompilerParams(vmem_limit_bytes=48 * MIB),
        cost_estimate=pl.CostEstimate(
            flops=6 * tokens * width * columns,
            bytes_accessed=12 * tokens * width,
            transcendentals=tokens * columns,
        ),
    )(normed, cotangent, gate_w, up_w, down_w)


def as_column(vector):
    return jnp.pad(vector[:, None], ((0, 0), (0, HD - 1)))


def on_device(
    tokens, cotangent, attn_gain, ffn_gain, w_query, w_key, w_value, w_out, w_gate, w_up, w_down,
    segments, positions,
):
    token_count, width = tokens.shape
    own_rows, hidden_width = w_gate.shape
    slice_width = hidden_width // GROUP
    heads_width = w_query.shape[1]
    tail_rows = min(token_count, WINDOW)
    hop_count = WINDOW // tail_rows
    device = lax.axis_index("tok")
    inputs = tokens.astype(FULL)

    frequency = 10000.0 ** (-jnp.arange(HD // 2, dtype=FULL) * 2.0 / HD)
    angles = positions.astype(FULL)[:, None] * frequency[None, :]
    cosine = jnp.concatenate([jnp.cos(angles)] * 2, axis=1)
    sine_half = jnp.sin(angles)
    sine = jnp.concatenate([-sine_half, sine_half], axis=1)
    padded_segments = jnp.concatenate([jnp.full((WINDOW,), -1, jnp.int32), segments])
    key_segments = lax.dynamic_slice_in_dim(
        padded_segments, device * token_count, WINDOW + token_count
    )
    query_segments = lax.dynamic_slice_in_dim(segments, device * token_count, token_count)

    attn_pack = jnp.concatenate(
        [
            w_query,
            w_key,
            w_value,
            w_out,
            jnp.pad(
                jnp.stack([attn_gain, ffn_gain], axis=1), ((0, 0), (0, HD - 2))
            ),
        ],
        axis=1,
    )
    attn_all = spread(attn_pack, (SIDE, NEAR, CORE))
    edge = heads_width + 2 * HD
    query_w, kv_w = attn_all[:, :heads_width], attn_all[:, heads_width:edge]
    out_w = attn_all[:, edge : edge + heads_width]
    gains = attn_all[:, edge + heads_width : edge + heads_width + 2].astype(FULL)
    gain_one, gain_two = gains[:, 0], gains[:, 1]

    def sliced(weight):
        return weight.reshape(own_rows, GROUP, slice_width).transpose(1, 0, 2)

    ffn_pack = jnp.concatenate([sliced(w_gate), sliced(w_up), sliced(w_down)], axis=2)
    ffn_rows = slices_to_group(ffn_pack)
    gate_up_w = spread(ffn_rows[:, : 2 * slice_width], (SIDE,))
    down_w = spread(ffn_rows[:, 2 * slice_width :], (SIDE,))
    gate_w, up_w = gate_up_w[:, :slice_width], gate_up_w[:, slice_width:]
    cot_group = rows_to_group(cotangent)

    inverse_one = lax.rsqrt(jnp.mean(inputs * inputs, axis=-1, keepdims=True) + EPSILON)
    normed = (inputs * inverse_one * gain_one).astype(LOW)
    kv = matmul(normed, kv_w)

    def turned(values, sine_signed):
        half = HD // 2
        rolled = jnp.concatenate([values[:, half:], values[:, :half]], axis=1)
        return values * cosine + rolled * sine_signed

    key_value = jnp.concatenate([turned(kv[:, :HD], sine), kv[:, HD:]], axis=1).astype(LOW)
    received = [passed_along(key_value, hop) for hop in range(hop_count, 0, -1)]
    all_keys = jnp.concatenate(received + [key_value], axis=0)
    raw_query = matmul(normed, query_w)
    rot, mixed, logs = attend(raw_query, all_keys, key_segments, query_segments, cosine, sine)
    middle = inputs + by_rows(mixed, out_w)
    inverse_two = lax.rsqrt(jnp.mean(middle * middle, axis=-1, keepdims=True) + EPSILON)
    normed_two = (middle * inverse_two * gain_two).astype(LOW)

    normed_group = rows_to_group(normed_two)
    hidden, gate_low, up_low = hidden_and_grads(normed_group, cot_group, gate_w, up_w, down_w)
    grad_down_w = outer_sum(cot_group, hidden).astype(LOW)
    down_sum = collect(grad_down_w, (SIDE,))
    grad_normed_part = by_rows(gate_low, gate_w) + by_rows(up_low, up_w)
    grad_normed_two = rows_from_group(grad_normed_part.astype(LOW))
    gate_up_low = jnp.concatenate([gate_low, up_low], axis=1)
    grad_gate_up_w = outer_sum(normed_group, gate_up_low).astype(LOW)
    gate_up_sum = collect(grad_gate_up_w, (SIDE,))
    result = middle + rows_from_group(by_rows(hidden, down_w).astype(LOW))
    output = result.astype(LOW)

    scaled = grad_normed_two * gain_two
    grad_middle = (
        cotangent.astype(FULL)
        + inverse_two * scaled
        - middle * inverse_two**3 * jnp.mean(scaled * middle, axis=-1, keepdims=True)
    )
    gain_two_part = jnp.sum(grad_normed_two * middle * inverse_two, axis=0)
    branch = grad_middle.astype(LOW)
    grad_mixed = matmul(branch, out_w).astype(LOW)
    grad_out_w = outer_sum(branch, mixed)
    out_sum = collect(
        jnp.concatenate([grad_out_w.astype(LOW), as_column(gain_two_part.astype(LOW))], axis=1),
        (SIDE, NEAR, CORE),
    )

    query_low, key_grads, value_grads = attend_back(
        rot, grad_mixed, mixed, logs, all_keys, key_segments, query_segments, cosine, sine
    )
    grads = jnp.concatenate([key_grads * HD**-0.5, value_grads], axis=1)
    shares = grads[WINDOW:]
    for hop in range(1, hop_count + 1):
        first_row = (hop_count - hop) * tail_rows
        returned = passed_along(grads[first_row : first_row + tail_rows].astype(LOW), -hop)
        shares = shares.at[token_count - tail_rows :].add(returned.astype(FULL))
    kv_low = jnp.concatenate([turned(shares[:, :HD], -sine), shares[:, HD:]], axis=1).astype(LOW)
    grad_query_w = outer_sum(normed, query_low).astype(LOW)
    grad_kv_w = outer_sum(normed, kv_low).astype(LOW)
    grad_normed = by_rows(query_low, query_w) + by_rows(kv_low, kv_w)
    scaled_one = grad_normed * gain_one
    grad_inputs = inverse_one * scaled_one - inputs * inverse_one**3 * jnp.mean(
        scaled_one * inputs, axis=-1, keepdims=True
    )
    grad_tokens = (grad_middle + grad_inputs).astype(LOW)
    gain_one_part = jnp.sum(grad_normed * inputs * inverse_one, axis=0)
    query_sum = collect(
        jnp.concatenate([grad_query_w, grad_kv_w, as_column(gain_one_part.astype(LOW))], axis=1),
        (SIDE, NEAR, CORE),
    )

    down_parts = slices_from_group(down_sum)
    gate_up_parts = slices_from_group(gate_up_sum)

    def joined(parts):
        return parts.transpose(1, 0, 2).reshape(own_rows, hidden_width).astype(FULL)

    return (
        output,
        grad_tokens,
        query_sum[:, edge],
        out_sum[:, heads_width],
        query_sum[:, :heads_width],
        query_sum[:, heads_width : heads_width + HD],
        query_sum[:, heads_width + HD : edge],
        out_sum[:, :heads_width],
        joined(gate_up_parts[:, :, :slice_width]),
        joined(gate_up_parts[:, :, slice_width:]),
        joined(down_parts),
    )


def solution(mesh):
    rows, flat = P("tok", None), P("tok")
    return jax.shard_map(
        on_device,
        mesh=mesh,
        in_specs=(rows, rows, flat, flat, rows, rows, rows, rows, rows, rows, rows, P(), flat),
        out_specs=(rows, rows, flat, flat, rows, rows, rows, rows, rows, rows, rows),
        check_vma=False,
    )
```

time: 2000 us -> 817 us (0.41)
  waiting for transfers between devices: 1240 us -> 292 us
  matrix products: 461 us -> 105 us
  blocking collectives: 165 us -> 0 us
  starting transfers between devices: 9.6 us -> 103 us
  Pallas kernels: 0 us -> 86.7 us
  local copies, waits for them, and re-layouts: 59.8 us -> 145 us
  other arithmetic: 42.7 us -> 70 us
    reduce_scatter x6 -> x0, waiting for transfers between devices: 760 us -> none  [the longest x1 270 us: on_device(): lax.psum_scatter(up_sum, 'tok', scatter_dimension=0, tiled=True)]
    ppermute x4 -> x91, waiting for transfers between devices: 6.55 us -> 292 us  [the longest x66 187 us: flip(): return lax.ppermute(array, 'tok', [(i, i ^ bit) for i in range(size)])]
    unnamed x13 -> x0, waiting for transfers between devices: 273 us -> none
    dot_general x24 -> x3, matrix products: 253 us -> 14.5 us  [matmul(): return jnp.dot(left_side, right_side, preferred_element_type=FULL)]
    all_gather x5 -> x0, waiting for transfers between devices: 204 us -> none  [the longest x1 93.7 us: on_device(): lax.all_gather(w_up, 'tok', axis=0, tiled=True)]
    ppermute x4 -> x91, starting transfers between devices: 9.12 us -> 103 us  [the longest x66 64.9 us: flip(): return lax.ppermute(array, 'tok', [(i, i ^ bit) for i in range(size)])]
    pallas_call x0 -> x3, Pallas kernels: none -> 86.7 us  [the longest x1 36.5 us: hidden_and_grads(): pl.pallas_call(hidden_kernel, grid=(columns // wide, tokens // rows), in_...]
    unnamed x2 -> x0, blocking collectives: 83.8 us -> none
  transfers between devices with their start and end apart: 16 -> 91, of which waited for: 9 -> 38; matrix products, arithmetic and copies ran while one was open for 16% -> 32% of each run, Pallas kernels for 0% -> 6%
where the time goes in v1:
time: 817 us; the launch traced here: 805 us
  waiting for transfers between devices  292 us (36%)
  local copies, waits for them, and re-layouts  145 us (18%)
  matrix products  105 us (13%)
  starting transfers between devices  103 us (13%)
  Pallas kernels  86.7 us (11%)
  other arithmetic  70 us (9%)
    ppermute x66, waiting for transfers between devices, flip(): return lax.ppermute(array, 'tok', [(i, i ^ bit) for i in range(size)])  187 us
    ppermute x21, waiting for transfers between devices, around(): lax.ppermute(array, 'tok', [(i, (i + RING) % size) for i in range(size)])  101 us
    ppermute x66, starting transfers between devices, flip(): return lax.ppermute(array, 'tok', [(i, i ^ bit) for i in range(size)])  64.9 us
    dot_general x6, matrix products, by_rows(): lax.dot_general(left_side, right_side, (((1,), (1,)), ((), ())), preferre...  49.7 us
    dynamic_update_slice x48, local copies, waits for them, and re-layouts, spread(): total = lax.dynamic_update_index_in_dim(total, piece, index, 0)  48.6 us
    dot_general x5, matrix products, outer_sum(): lax.dot_general(left_side, right_side, (((0,), (0,)), ((), ())), preferre...  40.9 us
    pallas_call x1, Pallas kernels, hidden_and_grads(): pl.pallas_call(hidden_kernel, grid=(columns // wide, tokens // rows), in_...  36.5 us
    ppermute x21, starting transfers between devices, around(): lax.ppermute(array, 'tok', [(i, (i + RING) % size) for i in range(size)])  30.8 us
  transfers between devices with their start and end apart: 91, of which 38 were waited for; matrix products, arithmetic and copies ran while one was open for 32% of the time, Pallas kernels for 6%

profile of v1, /device:TPU:0, one launch (start us, length us, event | category | flops | bytes accessed | tf_op | source)
XLA Modules:
  0.0 805.3 jit_solution(12750144161522471235)
XLA Ops:
  7.5 2.9 collective-permute-start.21
  16.8 4.2 constant_dynamic-slice_fusion.20
  21.0 4.7 broadcast_in_dim.113
  35.0 2.7 constant_dynamic-slice_fusion.18
  45.3 29.0 %collective-permute-done.1 = bf16[2,48,3456]{2,1,0:T(8,128)(2,1)S(1)} collective-permute-done((bf16[2,48,3456]{2,1,0:T(8,128)(2,1)S(1)}, bf16[2,48,3456]{2,1,0:T(8,128)(2,1)S(1)}, u32[]{:S(2)}, u32[]{:S(2)}) %collective-permute-start.1) | collective-permute-done | bytes 663584 | tf_op jit(solution)/shard_map/ppermute | solution.py:25
  80.4 4.2 collective-permute-done.11
  87.6 2.8 broadcast_select_fusion
  90.4 15.6 %rev.9 = bf16[2,2,48,3456]{3,0,2,1:T(2,128)(2,1)} reverse(bf16[2,2,48,3456]{3,0,2,1:T(2,128)(2,1)} %broadcast_select_fusion), dimensions={0} | reverse | bytes 2654208 | tf_op jit(solution)/shard_map/rev | solution.py:88
  106.0 4.2 broadcast_select_fusion.1
  118.9 3.3 pad_maximum_fusion.2
  125.9 12.3 %collective-permute-done.13 = bf16[2,48,3456]{2,1,0:T(8,128)(2,1)S(1)} collective-permute-done((bf16[2,48,3456]{2,1,0:T(8,128)(2,1)S(1)}, bf16[2,48,3456]{2,1,0:T(8,128)(2,1)S(1)}, u32[]{:S(2)}, u32[]{:S(2)}) %collective-permute-start.13) | collective-permute-done | bytes 663584 | tf_op jit(solution)/shard_map/ppermute | solution.py:25
  143.6 5.1 collective-permute-done.32
  148.7 3.9 collective-permute-done.33
  191.4 2.8 collective-permute-start.15
  195.7 6.7 fusion.13.q_ref
  202.4 11.7 %collective-permute-start.26 = (bf16[192,2304]{1,0:T(8,128)(2,1)}, bf16[192,2304]{1,0:T(8,128)(2,1)}, u32[]{:S(2)}, u32[]{:S(2)}) collective-permute-start(bf16[192,2304]{1,0:T(8,128)(2,1)} %collective-permute-done.24), channel_id=1, source_target_pairs={{0,8},{1,9},{2,10},{3,11},{4,12},{5,13},{6,14},{7,15},{8,16},{9,17... | collective-permute-start | bytes 2654216 | tf_op jit(solution)/shard_map/ppermute | solution.py:30
  217.4 25.5 %shard_map.222 = (bf16[512,1536]{1,0:T(8,128)(2,1)S(1)}, bf16[512,1536]{1,0:T(8,128)(2,1)S(1)}, f32[12,1,512]{2,1,0:T(1,128)S(1)}) custom-call(f32[512,1536]{1,0:T(8,128)S(1)} %copy-done, bf16[1536,128]{1,0:T(8,128)(2,1)S(1)} %get-tuple-element.118.key_ref, bf16[128,1536]{1,0:T(8,128)(2,1)S(1)} %copy.112.value_t_ref, ...), custom_call_target="tpu_custom_call" | custom-call | flops 16106127360 | bytes 6291456 | tf_op jit(solution)/shard_map/pallas_call | solution.py:220
  242.9 5.8 multiply_reduce_fusion.2
  254.9 2.7 collective-permute-start.28
  264.1 14.4 %collective-permute-done.28 = bf16[192,2304]{1,0:T(8,128)(2,1)} collective-permute-done((bf16[192,2304]{1,0:T(8,128)(2,1)}, bf16[192,2304]{1,0:T(8,128)(2,1)}, u32[]{:S(2)}, u32[]{:S(2)}) %collective-permute-start.28) | collective-permute-done | bytes 884768 | tf_op jit(solution)/shard_map/ppermute | solution.py:30
  279.4 8.5 %collective-permute-done.17 = bf16[512,1536]{1,0:T(8,128)(2,1)} collective-permute-done((bf16[512,1536]{1,0:T(8,128)(2,1)}, bf16[512,1536]{1,0:T(8,128)(2,1)}, u32[]{:S(2)}, u32[]{:S(2)}) %collective-permute-start.17) | collective-permute-done | bytes 1572896 | tf_op jit(solution)/shard_map/ppermute | solution.py:25
  294.5 3.8 constant_dynamic-update-slice_fusion.29.cot_ref
  300.3 5.4 fusion.103
  305.6 6.6 pad_maximum_fusion.normed_ref
  312.2 36.5 %shard_map.223 = (bf16[2048,1152]{1,0:T(8,128)(2,1)}, bf16[2048,1152]{1,0:T(8,128)(2,1)}, bf16[2048,1152]{1,0:T(8,128)(2,1)}) custom-call(bf16[2048,1536]{1,0:T(8,128)(2,1)} %pad_maximum_fusion.normed_ref, bf16[2048,1536]{1,0:T(8,128)(2,1)} %constant_dynamic-update-slice_fusion.29.cot_ref, bf16[1536,1152]{1,0:T(8,128)(2,1)S(1)} %get-tuple-element.82.gate_ref, ...), custom_call_target="tpu_custom_call" | custom-call | flops 21743271936 | bytes 37748736 | tf_op jit(solution)/shard_map/pallas_call | solution.py:355
  348.7 12.1 %convolution_convert_fusion.1 = bf16[1536,1152]{1,0:T(8,128)(2,1)S(1)} fusion(bf16[2048,1536]{1,0:T(8,128)(2,1)} %constant_dynamic-update-slice_fusion.29.cot_ref, bf16[2048,1152]{1,0:T(8,128)(2,1)} %get-tuple-element.61), kind=kOutput, calls=%fused_computation.9 | convolution fusion | flops 7249526784 | bytes 14548992 | tf_op jit(solution)/shard_map/dot_general | solution.py:44
  366.2 11.1 %fusion.96 = f32[2048,1536]{1,0:T(8,128)} fusion(bf16[2048,1152]{1,0:T(8,128)(2,1)S(1)} %copy-done.57, bf16[1536,2304]{1,0:T(8,128)(2,1)S(1)} %bitcast.283), kind=kOutput, calls=%fused_computation.330 | convolution fusion | flops 7247757312 | bytes 20840448 | tf_op jit(solution)/shard_map/dot_general | solution.py:50
  377.3 22.0 %convolution_convert_fusion = bf16[1536,2304]{1,0:T(8,128)(2,1)} fusion(bf16[2048,1152]{1,0:T(8,128)(2,1)} %get-tuple-element.63, bf16[2048,1152]{1,0:T(8,128)(2,1)} %get-tuple-element.62, bf16[1024,1536]{1,0:T(8,128)(2,1)} %collective-permute-done.18, bf16[512,1536]{1,0:T(8,128)(2,1)} %collective-permute-done.17, bf16[512,1536]{1,0:T(8,128)(2,1)} %multiply_convert_fusion), kind=kOutput, calls=%fused_computation.3 | convolution fusion | flops 14536802304 | bytes 22806528 | tf_op jit(solution)/shard_map/dot_general | solution.py:44
  399.3 3.5 dynamic-slice_bitcast_fusion.3
  403.8 13.8 %add_convert_fusion = bf16[2048,1536]{1,0:T(8,128)(2,1)S(1)} fusion(f32[2048,1536]{1,0:T(8,128)} %fusion.96, bf16[2048,1152]{1,0:T(8,128)(2,1)} %get-tuple-element.62, bf16[1536,2304]{1,0:T(8,128)(2,1)} %bitcast.280), kind=kOutput, calls=%fused_computation | convolution fusion | flops 7254048768 | bytes 27131904 | tf_op jit(solution)/shard_map/dot_general | solution.py:50
  420.0 5.4 collective-permute-done.73
  429.1 11.2 %collective-permute-done.83 = bf16[192,1152]{1,0:T(8,128)(2,1)S(1)} collective-permute-done((bf16[192,1152]{1,0:T(8,128)(2,1)S(1)}, bf16[192,1152]{1,0:T(8,128)(2,1)S(1)}, u32[]{:S(2)}, u32[]{:S(2)}) %collective-permute-start.83) | collective-permute-done | bytes 442400 | tf_op jit(solution)/shard_map/ppermute | solution.py:30
  442.3 10.2 %convolution_convert_fusion.4 = bf16[2048,1536]{1,0:T(8,128)(2,1)S(1)} fusion(bf16[2048,1152]{1,0:T(8,128)(2,1)} %get-tuple-element.61, bf16[1536,1152]{1,0:T(8,128)(2,1)S(1)} %bitcast.311), kind=kOutput, calls=%fused_computation.12 | convolution fusion | flops 7250903040 | bytes 14548992 | tf_op jit(solution)/shard_map/dot_general | solution.py:50
  457.6 5.1 collective-permute-done.85
  468.8 11.4 %collective-permute-done.87 = bf16[192,1152]{1,0:T(8,128)(2,1)S(1)} collective-permute-done((bf16[192,1152]{1,0:T(8,128)(2,1)S(1)}, bf16[192,1152]{1,0:T(8,128)(2,1)S(1)}, u32[]{:S(2)}, u32[]{:S(2)}) %collective-permute-start.87) | collective-permute-done | bytes 442400 | tf_op jit(solution)/shard_map/ppermute | solution.py:30
  483.3 4.8 collective-permute-done.89
  488.8 9.9 %collective-permute-done.76 = bf16[192,2304]{1,0:T(8,128)(2,1)S(1)} collective-permute-done((bf16[192,2304]{1,0:T(8,128)(2,1)S(1)}, bf16[192,2304]{1,0:T(8,128)(2,1)S(1)}, u32[]{:S(2)}, u32[]{:S(2)}) %collective-permute-start.76) | collective-permute-done | bytes 884768 | tf_op jit(solution)/shard_map/ppermute | solution.py:30
  500.6 21.7 %collective-permute-done.78 = bf16[192,2304]{1,0:T(8,128)(2,1)S(1)} collective-permute-done((bf16[192,2304]{1,0:T(8,128)(2,1)S(1)}, bf16[192,2304]{1,0:T(8,128)(2,1)S(1)}, u32[]{:S(2)}, u32[]{:S(2)}) %collective-permute-start.78) | collective-permute-done | bytes 884768 | tf_op jit(solution)/shard_map/ppermute | solution.py:30
  524.5 2.8 convert_add_fusion.2
  527.9 8.0 collective-permute-done.80
  536.1 2.9 convert_add_fusion.1
  543.4 57.6 %collective-permute-done.40 = bf16[512,1536]{1,0:T(8,128)(2,1)S(1)} collective-permute-done((bf16[512,1536]{1,0:T(8,128)(2,1)S(1)}, bf16[512,1536]{1,0:T(8,128)(2,1)S(1)}, u32[]{:S(2)}, u32[]{:S(2)}) %collective-permute-start.40) | collective-permute-done | bytes 1572896 | tf_op jit(solution)/shard_map/ppermute | solution.py:25
  604.7 2.9 convolution_convert_fusion.2
  607.7 6.0 fusion.32.grad_ref
  616.3 7.6 copy.124
  623.9 3.7 constant_dynamic-slice_fusion.9
  630.9 24.7 %shard_map.224 = (bf16[512,1536]{1,0:T(8,128)(2,1)S(1)}, f32[1536,128]{1,0:T(8,128)S(1)}, f32[1536,128]{1,0:T(8,128)S(1)}) custom-call(bf16[512,1536]{1,0:T(8,128)(2,1)S(1)} %copy-done.6, bf16[512,1536]{1,0:T(8,128)(2,1)S(1)} %copy-done.4, bf16[512,1536]{1,0:T(8,128)(2,1)S(1)} %copy-done.3, f32[12,1,512]{2,1,0:T(1,128)S(1)} %get-tuple-element.65.log_ref, ...), custom_call_target="tpu_custom_call" | custom-call | flops 30198988800 | bytes 6291456 | tf_op jit(solution)/shard_map/pallas_call | solution.py:288
  658.9 3.2 convolution_convert_fusion.3
  662.1 3.8 collective-permute-start.70
  665.8 4.4 collective-permute-done.42
  673.2 7.1 fusion.27
  680.3 3.0 fusion.5
  683.2 8.5 %copy.117 = bf16[1536,1920]{1,0:T(8,128)(2,1)} copy(bf16[1536,1920]{0,1:T(8,128)(2,1)} %fusion.5) | data formatting | bytes 11796480 | tf_op jit(solution)/shard_map/concatenate | solution.py:492
  691.8 3.0 constant_dynamic-slice_fusion.15
  707.3 6.8 collective-permute-done.59
  715.9 7.5 collective-permute-done.63
  725.0 6.8 collective-permute-done.67
  733.2 6.1 collective-permute-done.71
  750.1 3.8 collective-permute-done.61
  758.2 6.8 collective-permute-done.48
  765.1 6.7 collective-permute-done.52
  777.5 5.5 collective-permute-done.49
  788.5 6.9 collective-permute-done.50
  798.6 4.3 collective-permute-done.54
  (481 shorter events, 224.0 us)
Async XLA Ops:
  7.5 27.4 %collective-permute-start.21 = (bf16[2,48,3456]{2,0,1:T(2,128)(2,1)}, bf16[2,48,3456]{2,0,1:T(2,128)(2,1)}, u32[]{:S(2)}, u32[]{:S(2)}) collective-permute-start(bf16[2,48,3456]{2,0,1:T(2,128)(2,1)} %constant_dynamic-slice_fusion.19), channel_id=1, source_target_pairs={{0,2},{1,3},{2,0},{3,1},{4,6},{5,7},{6,4},{7,5},{8,10},{9,11},{10,... | collective-permute-start | bytes 1990664 | tf_op jit(solution)/shard_map/ppermute | solution.py:25
  10.7 21.4 %collective-permute-start.3 = (bf16[48,3456]{1,0:T(8,128)(2,1)S(1)}, bf16[48,3456]{1,0:T(8,128)(2,1)S(1)}, u32[]{:S(2)}, u32[]{:S(2)}) collective-permute-start(bf16[48,3456]{1,0:T(8,128)(2,1)S(1)} %constant_dynamic-update-slice_fusion.24), channel_id=1, source_target_pairs={{0,8},{1,9},{2,10},{3,11},{4,12},{5,13},{6,14},{7,15},{8,16},{9,17... | collective-permute-start | bytes 995336 | tf_op jit(solution)/shard_map/ppermute | solution.py:30
  12.3 18.1 %collective-permute-start = (bf16[1,48,3456]{2,1,0:T(8,128)(2,1)S(1)}, bf16[1,48,3456]{2,1,0:T(8,128)(2,1)S(1)}, u32[]{:S(2)}, u32[]{:S(2)}) collective-permute-start(bf16[1,48,3456]{2,1,0:T(8,128)(2,1)S(1)} %bitcast.301), channel_id=1, source_target_pairs={{0,4},{1,5},{2,6},{3,7},{4,0},{5,1},{6,2},{7,3},{8,12},{9,13},{10,... | collective-permute-start | bytes 995336 | tf_op jit(solution)/shard_map/ppermute | solution.py:25
  13.8 101.1 %collective-permute-start.19 = (bf16[512,1536]{1,0:T(8,128)(2,1)S(1)}, bf16[512,1536]{1,0:T(8,128)(2,1)}, u32[]{:S(2)}, u32[]{:S(2)}) collective-permute-start(bf16[512,1536]{1,0:T(8,128)(2,1)S(1)} %copy-done.10), channel_id=1, source_target_pairs={{0,2},{1,3},{2,0},{3,1},{4,6},{5,7},{6,4},{7,5},{8,10},{9,11},{10,... | collective-permute-start | bytes 4718600 | tf_op jit(solution)/shard_map/ppermute | solution.py:25
  30.5 43.8 %collective-permute-start.1 = (bf16[2,48,3456]{2,1,0:T(8,128)(2,1)S(1)}, bf16[2,48,3456]{2,1,0:T(8,128)(2,1)S(1)}, u32[]{:S(2)}, u32[]{:S(2)}) collective-permute-start(bf16[2,48,3456]{2,1,0:T(8,128)(2,1)S(1)} %pad_maximum_fusion.9), channel_id=1, source_target_pairs={{0,2},{1,3},{2,0},{3,1},{4,6},{5,7},{6,4},{7,5},{8,10},{9,11},{10,... | collective-permute-start | bytes 1990664 | tf_op jit(solution)/shard_map/ppermute | solution.py:25
  39.2 46.9 %collective-permute-start.22 = (bf16[2,48,3456]{2,0,1:T(2,128)(2,1)S(1)}, bf16[2,48,3456]{2,0,1:T(2,128)(2,1)S(1)}, u32[]{:S(2)}, u32[]{:S(2)}) collective-permute-start(bf16[2,48,3456]{2,0,1:T(2,128)(2,1)S(1)} %pad_maximum_fusion.13), channel_id=1, source_target_pairs={{0,1},{1,0},{2,3},{3,2},{4,5},{5,4},{6,7},{7,6},{8,9},{9,8},{10,11... | collective-permute-start | bytes 1990664 | tf_op jit(solution)/shard_map/ppermute | solution.py:25
  41.2 70.5 %collective-permute-start.5 = (bf16[2,48,3456]{2,1,0:T(8,128)(2,1)}, bf16[2,48,3456]{2,1,0:T(8,128)(2,1)}, u32[]{:S(2)}, u32[]{:S(2)}) collective-permute-start(bf16[2,48,3456]{2,1,0:T(8,128)(2,1)} %pad_maximum_fusion.10), channel_id=1, source_target_pairs={{0,2},{1,3},{2,0},{3,1},{4,6},{5,7},{6,4},{7,5},{8,10},{9,11},{10,... | collective-permute-start | bytes 1990664 | tf_op jit(solution)/shard_map/ppermute | solution.py:25
  42.2 37.2 %collective-permute-start.8 = (bf16[1,48,3456]{2,1,0:T(8,128)(2,1)S(1)}, bf16[1,48,3456]{2,1,0:T(8,128)(2,1)S(1)}, u32[]{:S(2)}, u32[]{:S(2)}) collective-permute-start(bf16[1,48,3456]{2,1,0:T(8,128)(2,1)S(1)} %bitcast.318), channel_id=1, source_target_pairs={{0,4},{1,5},{2,6},{3,7},{4,0},{5,1},{6,2},{7,3},{8,12},{9,13},{10,... | collective-permute-start | bytes 995336 | tf_op jit(solution)/shard_map/ppermute | solution.py:25
  79.4 75.0 %collective-permute-start.2 = (bf16[4,48,3456]{2,1,0:T(8,128)(2,1)}, bf16[4,48,3456]{2,1,0:T(8,128)(2,1)}, u32[]{:S(2)}, u32[]{:S(2)}) collective-permute-start(bf16[4,48,3456]{2,1,0:T(8,128)(2,1)} %pad_maximum_fusion.4), channel_id=1, source_target_pairs={{0,1},{1,0},{2,3},{3,2},{4,5},{5,4},{6,7},{7,6},{8,9},{9,8},{10,11... | collective-permute-start | bytes 3981320 | tf_op jit(solution)/shard_map/ppermute | solution.py:25
  84.6 37.6 %collective-permute-start.9 = (bf16[2,48,3456]{2,1,0:T(8,128)(2,1)}, bf16[2,48,3456]{2,1,0:T(8,128)(2,1)}, u32[]{:S(2)}, u32[]{:S(2)}) collective-permute-start(bf16[2,48,3456]{2,1,0:T(8,128)(2,1)} %pad_maximum_fusion.11), channel_id=1, source_target_pairs={{0,2},{1,3},{2,0},{3,1},{4,6},{5,7},{6,4},{7,5},{8,10},{9,11},{10,... | collective-permute-start | bytes 1990664 | tf_op jit(solution)/shard_map/ppermute | solution.py:25
  86.1 27.7 %collective-permute-start.12 = (bf16[1,48,3456]{2,1,0:T(8,128)(2,1)}, bf16[1,48,3456]{2,1,0:T(8,128)(2,1)S(1)}, u32[]{:S(2)}, u32[]{:S(2)}) collective-permute-start(bf16[1,48,3456]{2,1,0:T(8,128)(2,1)} %bitcast.5), channel_id=1, source_target_pairs={{0,4},{1,5},{2,6},{3,7},{4,0},{5,1},{6,2},{7,3},{8,12},{9,13},{10,... | collective-permute-start | bytes 995336 | tf_op jit(solution)/shard_map/ppermute | solution.py:25
  111.6 13.2 %collective-permute-start.30 = (bf16[1,192,1152]{2,1,0:T(8,128)(2,1)S(1)}, bf16[1,192,1152]{2,1,0:T(8,128)(2,1)S(1)}, u32[]{:S(2)}, u32[]{:S(2)}) collective-permute-start(bf16[1,192,1152]{2,1,0:T(8,128)(2,1)S(1)} %get-tuple-element.104), channel_id=1, source_target_pairs={{0,4},{1,5},{2,6},{3,7},{4,0},{5,1},{6,2},{7,3},{8,12},{9,13},{10,... | collective-permute-start | bytes 1327112 | tf_op jit(solution)/shard_map/ppermute | solution.py:25
  114.9 26.7 %collective-permute-start.23 = (bf16[1,192,2304]{2,1,0:T(8,128)(2,1)S(1)}, bf16[1,192,2304]{2,1,0:T(8,128)(2,1)S(1)}, u32[]{:S(2)}, u32[]{:S(2)}) collective-permute-start(bf16[1,192,2304]{2,1,0:T(8,128)(2,1)S(1)} %get-tuple-element.106), channel_id=1, source_target_pairs={{0,4},{1,5},{2,6},{3,7},{4,0},{5,1},{6,2},{7,3},{8,12},{9,13},{10,... | collective-permute-start | bytes 2654216 | tf_op jit(solution)/shard_map/ppermute | solution.py:25
  122.3 30.4 %collective-permute-start.24 = (bf16[192,2304]{1,0:T(8,128)(2,1)S(1)}, bf16[192,2304]{1,0:T(8,128)(2,1)}, u32[]{:S(2)}, u32[]{:S(2)}) collective-permute-start(bf16[192,2304]{1,0:T(8,128)(2,1)S(1)} %get-tuple-element.105), channel_id=1, source_target_pairs={{0,8},{1,9},{2,10},{3,11},{4,12},{5,13},{6,14},{7,15},{8,16},{9,17... | collective-permute-start | bytes 2654216 | tf_op jit(solution)/shard_map/ppermute | solution.py:30
  124.8 13.4 %collective-permute-start.13 = (bf16[2,48,3456]{2,1,0:T(8,128)(2,1)S(1)}, bf16[2,48,3456]{2,1,0:T(8,128)(2,1)S(1)}, u32[]{:S(2)}, u32[]{:S(2)}) collective-permute-start(bf16[2,48,3456]{2,1,0:T(8,128)(2,1)S(1)} %pad_maximum_fusion.12), channel_id=1, source_target_pairs={{0,2},{1,3},{2,0},{3,1},{4,6},{5,7},{6,4},{7,5},{8,10},{9,11},{10,... | collective-permute-start | bytes 1990664 | tf_op jit(solution)/shard_map/ppermute | solution.py:25
  125.8 41.9 %collective-permute-start.6 = (bf16[4,48,3456]{2,1,0:T(8,128)(2,1)S(1)}, bf16[4,48,3456]{2,1,0:T(8,128)(2,1)S(1)}, u32[]{:S(2)}, u32[]{:S(2)}) collective-permute-start(bf16[4,48,3456]{2,1,0:T(8,128)(2,1)S(1)} %pad_maximum_fusion.5), channel_id=1, source_target_pairs={{0,1},{1,0},{2,3},{3,2},{4,5},{5,4},{6,7},{7,6},{8,9},{9,8},{10,11... | collective-permute-start | bytes 3981320 | tf_op jit(solution)/shard_map/ppermute | solution.py:25
  148.6 145.9 %collective-permute-start.20 = (bf16[1024,1536]{1,0:T(8,128)(2,1)}, bf16[1024,1536]{1,0:T(8,128)(2,1)}, u32[]{:S(2)}, u32[]{:S(2)}) collective-permute-start(bf16[1024,1536]{1,0:T(8,128)(2,1)} %pad_maximum_fusion.2), channel_id=1, source_target_pairs={{0,1},{1,0},{2,3},{3,2},{4,5},{5,4},{6,7},{7,6},{8,9},{9,8},{10,11... | collective-permute-start | bytes 9437192 | tf_op jit(solution)/shard_map/ppermute | solution.py:25
  152.6 24.2 %collective-permute-start.10 = (bf16[4,48,3456]{2,1,0:T(8,128)(2,1)S(1)}, bf16[4,48,3456]{2,1,0:T(8,128)(2,1)S(1)}, u32[]{:S(2)}, u32[]{:S(2)}) collective-permute-start(bf16[4,48,3456]{2,1,0:T(8,128)(2,1)S(1)} %pad_maximum_fusion.6), channel_id=1, source_target_pairs={{0,1},{1,0},{2,3},{3,2},{4,5},{5,4},{6,7},{7,6},{8,9},{9,8},{10,11... | collective-permute-start | bytes 3981320 | tf_op jit(solution)/shard_map/ppermute | solution.py:25
  152.6 31.6 %collective-permute-start.14 = (bf16[4,48,3456]{2,1,0:T(8,128)(2,1)S(1)}, bf16[4,48,3456]{2,1,0:T(8,128)(2,1)S(1)}, u32[]{:S(2)}, u32[]{:S(2)}) collective-permute-start(bf16[4,48,3456]{2,1,0:T(8,128)(2,1)S(1)} %pad_maximum_fusion.7), channel_id=1, source_target_pairs={{0,1},{1,0},{2,3},{3,2},{4,5},{5,4},{6,7},{7,6},{8,9},{9,8},{10,11... | collective-permute-start | bytes 3981320 | tf_op jit(solution)/shard_map/ppermute | solution.py:25
  154.5 22.2 %collective-permute-start.34 = (bf16[1,192,1152]{2,1,0:T(8,128)(2,1)S(1)}, bf16[1,192,1152]{2,1,0:T(8,128)(2,1)S(1)}, u32[]{:S(2)}, u32[]{:S(2)}) collective-permute-start(bf16[1,192,1152]{2,1,0:T(8,128)(2,1)S(1)} %bitcast.334), channel_id=1, source_target_pairs={{0,4},{1,5},{2,6},{3,7},{4,0},{5,1},{6,2},{7,3},{8,12},{9,13},{10,... | collective-permute-start | bytes 1327112 | tf_op jit(solution)/shard_map/ppermute | solution.py:25
  167.7 87.2 %collective-permute-start.25 = (bf16[1,192,2304]{2,1,0:T(8,128)(2,1)}, bf16[1,192,2304]{2,1,0:T(8,128)(2,1)}, u32[]{:S(2)}, u32[]{:S(2)}) collective-permute-start(bf16[1,192,2304]{2,1,0:T(8,128)(2,1)} %bitcast.16), channel_id=1, source_target_pairs={{0,4},{1,5},{2,6},{3,7},{4,0},{5,1},{6,2},{7,3},{8,12},{9,13},{10,... | collective-permute-start | bytes 2654216 | tf_op jit(solution)/shard_map/ppermute | solution.py:25
  176.7 25.7 %collective-permute-start.35 = (bf16[192,1152]{1,0:T(8,128)(2,1)S(1)}, bf16[192,1152]{1,0:T(8,128)(2,1)}, u32[]{:S(2)}, u32[]{:S(2)}) collective-permute-start(bf16[192,1152]{1,0:T(8,128)(2,1)S(1)} %collective-permute-done.33), channel_id=1, source_target_pairs={{0,8},{1,9},{2,10},{3,11},{4,12},{5,13},{6,14},{7,15},{8,16},{9,17... | collective-permute-start | bytes 1327112 | tf_op jit(solution)/shard_map/ppermute | solution.py:30
  191.4 22.7 %collective-permute-start.15 = (bf16[512,256]{1,0:T(8,128)(2,1)S(1)}, bf16[512,256]{1,0:T(8,128)(2,1)S(1)}, u32[]{:S(2)}, u32[]{:S(2)}) collective-permute-start(bf16[512,256]{1,0:T(8,128)(2,1)S(1)} %pad_maximum_fusion.17), channel_id=1, source_target_pairs={{0,2},{1,3},{2,4},{3,5},{4,6},{5,7},{6,8},{7,9},{8,10},{9,11},{10,... | collective-permute-start | bytes 786440 | tf_op jit(solution)/shard_map/ppermute | solution.py:36
  194.3 20.7 %collective-permute-start.16 = (bf16[512,256]{1,0:T(8,128)(2,1)S(1)}, bf16[512,256]{1,0:T(8,128)(2,1)S(1)}, u32[]{:S(2)}, u32[]{:S(2)}) collective-permute-start(bf16[512,256]{1,0:T(8,128)(2,1)S(1)} %pad_maximum_fusion.17), channel_id=1, source_target_pairs={{0,1},{1,2},{2,3},{3,4},{4,5},{5,6},{6,7},{7,8},{8,9},{9,10},{10,1... | collective-permute-start | bytes 786440 | tf_op jit(solution)/shard_map/ppermute | solution.py:36
  202.4 51.5 %collective-permute-start.26 = (bf16[192,2304]{1,0:T(8,128)(2,1)}, bf16[192,2304]{1,0:T(8,128)(2,1)}, u32[]{:S(2)}, u32[]{:S(2)}) collective-permute-start(bf16[192,2304]{1,0:T(8,128)(2,1)} %collective-permute-done.24), channel_id=1, source_target_pairs={{0,8},{1,9},{2,10},{3,11},{4,12},{5,13},{6,14},{7,15},{8,16},{9,17... | collective-permute-start | bytes 2654216 | tf_op jit(solution)/shard_map/ppermute | solution.py:30
  214.1 45.7 %collective-permute-start.36 = (bf16[1,192,1152]{2,1,0:T(8,128)(2,1)}, bf16[1,192,1152]{2,1,0:T(8,128)(2,1)}, u32[]{:S(2)}, u32[]{:S(2)}) collective-permute-start(bf16[1,192,1152]{2,1,0:T(8,128)(2,1)} %bitcast.23), channel_id=1, source_target_pairs={{0,4},{1,5},{2,6},{3,7},{4,0},{5,1},{6,2},{7,3},{8,12},{9,13},{10,... | collective-permute-start | bytes 1327112 | tf_op jit(solution)/shard_map/ppermute | solution.py:25
  250.4 37.5 %collective-permute-start.17 = (bf16[512,1536]{1,0:T(8,128)(2,1)}, bf16[512,1536]{1,0:T(8,128)(2,1)}, u32[]{:S(2)}, u32[]{:S(2)}) collective-permute-start(bf16[512,1536]{1,0:T(8,128)(2,1)} %multiply_convert_fusion), channel_id=1, source_target_pairs={{0,2},{1,3},{2,0},{3,1},{4,6},{5,7},{6,4},{7,5},{8,10},{9,11},{10,... | collective-permute-start | bytes 4718600 | tf_op jit(solution)/shard_map/ppermute | solution.py:25
  253.8 36.4 %collective-permute-start.27 = (bf16[1,192,2304]{2,1,0:T(8,128)(2,1)}, bf16[1,192,2304]{2,1,0:T(8,128)(2,1)}, u32[]{:S(2)}, u32[]{:S(2)}) collective-permute-start(bf16[1,192,2304]{2,1,0:T(8,128)(2,1)} %bitcast.17), channel_id=1, source_target_pairs={{0,4},{1,5},{2,6},{3,7},{4,0},{5,1},{6,2},{7,3},{8,12},{9,13},{10,... | collective-permute-start | bytes 2654216 | tf_op jit(solution)/shard_map/ppermute | solution.py:25
  254.9 23.6 %collective-permute-start.28 = (bf16[192,2304]{1,0:T(8,128)(2,1)}, bf16[192,2304]{1,0:T(8,128)(2,1)}, u32[]{:S(2)}, u32[]{:S(2)}) collective-permute-start(bf16[192,2304]{1,0:T(8,128)(2,1)} %collective-permute-done.26), channel_id=1, source_target_pairs={{0,8},{1,9},{2,10},{3,11},{4,12},{5,13},{6,14},{7,15},{8,16},{9,17... | collective-permute-start | bytes 2654216 | tf_op jit(solution)/shard_map/ppermute | solution.py:30
  278.5 20.8 %collective-permute-start.29 = (bf16[1,192,2304]{2,1,0:T(8,128)(2,1)}, bf16[1,192,2304]{2,1,0:T(8,128)(2,1)S(1)}, u32[]{:S(2)}, u32[]{:S(2)}) collective-permute-start(bf16[1,192,2304]{2,1,0:T(8,128)(2,1)} %bitcast.18), channel_id=1, source_target_pairs={{0,4},{1,5},{2,6},{3,7},{4,0},{5,1},{6,2},{7,3},{8,12},{9,13},{10,... | collective-permute-start | bytes 2654216 | tf_op jit(solution)/shard_map/ppermute | solution.py:25
  290.0 15.7 %collective-permute-start.18 = (bf16[1024,1536]{1,0:T(8,128)(2,1)S(1)}, bf16[1024,1536]{1,0:T(8,128)(2,1)}, u32[]{:S(2)}, u32[]{:S(2)}) collective-permute-start(bf16[1024,1536]{1,0:T(8,128)(2,1)S(1)} %pad_maximum_fusion.1), channel_id=1, source_target_pairs={{0,1},{1,0},{2,3},{3,2},{4,5},{5,4},{6,7},{7,6},{8,9},{9,8},{10,11... | collective-permute-start | bytes 9437192 | tf_op jit(solution)/shard_map/ppermute | solution.py:25
  362.1 55.4 %collective-permute-start.82 = (bf16[192,1152]{1,0:T(8,128)(2,1)}, bf16[192,1152]{1,0:T(8,128)(2,1)}, u32[]{:S(2)}, u32[]{:S(2)}) collective-permute-start(bf16[192,1152]{1,0:T(8,128)(2,1)} %get-tuple-element.97), channel_id=1, source_target_pairs={{0,4},{1,5},{2,6},{3,7},{4,0},{5,1},{6,2},{7,3},{8,12},{9,13},{10,... | collective-permute-start | bytes 1327112 | tf_op jit(solution)/shard_map/ppermute | solution.py:25
  363.1 65.0 %collective-permute-start.84 = (bf16[192,1152]{1,0:T(8,128)(2,1)}, bf16[192,1152]{1,0:T(8,128)(2,1)}, u32[]{:S(2)}, u32[]{:S(2)}) collective-permute-start(bf16[192,1152]{1,0:T(8,128)(2,1)} %get-tuple-element.100), channel_id=1, source_target_pairs={{0,4},{1,5},{2,6},{3,7},{4,0},{5,1},{6,2},{7,3},{8,12},{9,13},{10,... | collective-permute-start | bytes 1327112 | tf_op jit(solution)/shard_map/ppermute | solution.py:25
  364.1 92.9 %collective-permute-start.86 = (bf16[192,1152]{1,0:T(8,128)(2,1)}, bf16[192,1152]{1,0:T(8,128)(2,1)}, u32[]{:S(2)}, u32[]{:S(2)}) collective-permute-start(bf16[192,1152]{1,0:T(8,128)(2,1)} %get-tuple-element.99), channel_id=1, source_target_pairs={{0,4},{1,5},{2,6},{3,7},{4,0},{5,1},{6,2},{7,3},{8,12},{9,13},{10,... | collective-permute-start | bytes 1327112 | tf_op jit(solution)/shard_map/ppermute | solution.py:25
  365.1 101.1 %collective-permute-start.88 = (bf16[192,1152]{1,0:T(8,128)(2,1)}, bf16[192,1152]{1,0:T(8,128)(2,1)}, u32[]{:S(2)}, u32[]{:S(2)}) collective-permute-start(bf16[192,1152]{1,0:T(8,128)(2,1)} %get-tuple-element.98), channel_id=1, source_target_pairs={{0,4},{1,5},{2,6},{3,7},{4,0},{5,1},{6,2},{7,3},{8,12},{9,13},{10,... | collective-permute-start | bytes 1327112 | tf_op jit(solution)/shard_map/ppermute | solution.py:25
  402.8 22.6 %collective-permute-start.73 = (bf16[192,2304]{1,0:T(8,128)(2,1)S(1)}, bf16[192,2304]{1,0:T(8,128)(2,1)S(1)}, u32[]{:S(2)}, u32[]{:S(2)}) collective-permute-start(bf16[192,2304]{1,0:T(8,128)(2,1)S(1)} %get-tuple-element.77), channel_id=1, source_target_pairs={{0,4},{1,5},{2,6},{3,7},{4,0},{5,1},{6,2},{7,3},{8,12},{9,13},{10,... | collective-permute-start | bytes 2654216 | tf_op jit(solution)/shard_map/ppermute | solution.py:25
  417.6 47.7 %collective-permute-start.75 = (bf16[192,2304]{1,0:T(8,128)(2,1)}, bf16[192,2304]{1,0:T(8,128)(2,1)S(1)}, u32[]{:S(2)}, u32[]{:S(2)}) collective-permute-start(bf16[192,2304]{1,0:T(8,128)(2,1)} %get-tuple-element.80), channel_id=1, source_target_pairs={{0,4},{1,5},{2,6},{3,7},{4,0},{5,1},{6,2},{7,3},{8,12},{9,13},{10,... | collective-permute-start | bytes 2654216 | tf_op jit(solution)/shard_map/ppermute | solution.py:25
  425.4 14.9 %collective-permute-start.83 = (bf16[192,1152]{1,0:T(8,128)(2,1)S(1)}, bf16[192,1152]{1,0:T(8,128)(2,1)S(1)}, u32[]{:S(2)}, u32[]{:S(2)}) collective-permute-start(bf16[192,1152]{1,0:T(8,128)(2,1)S(1)} %fusion.49), channel_id=1, source_target_pairs={{0,8},{1,9},{2,10},{3,11},{4,12},{5,13},{6,14},{7,15},{8,16},{9,17... | collective-permute-start | bytes 1327112 | tf_op jit(solution)/shard_map/ppermute | solution.py:30
  428.1 37.3 %collective-permute-start.74 = (bf16[192,2304]{1,0:T(8,128)(2,1)S(1)}, bf16[192,2304]{1,0:T(8,128)(2,1)S(1)}, u32[]{:S(2)}, u32[]{:S(2)}) collective-permute-start(bf16[192,2304]{1,0:T(8,128)(2,1)S(1)} %fusion.41), channel_id=1, source_target_pairs={{0,8},{1,9},{2,10},{3,11},{4,12},{5,13},{6,14},{7,15},{8,16},{9,17... | collective-permute-start | bytes 2654216 | tf_op jit(solution)/shard_map/ppermute | solution.py:30
  441.6 21.1 %collective-permute-start.85 = (bf16[192,1152]{1,0:T(8,128)(2,1)S(1)}, bf16[192,1152]{1,0:T(8,128)(2,1)S(1)}, u32[]{:S(2)}, u32[]{:S(2)}) collective-permute-start(bf16[192,1152]{1,0:T(8,128)(2,1)S(1)} %fusion.48), channel_id=1, source_target_pairs={{0,8},{1,9},{2,10},{3,11},{4,12},{5,13},{6,14},{7,15},{8,16},{9,17... | collective-permute-start | bytes 1327112 | tf_op jit(solution)/shard_map/ppermute | solution.py:30
  457.0 31.2 %collective-permute-start.77 = (bf16[192,2304]{1,0:T(8,128)(2,1)S(1)}, bf16[192,2304]{1,0:T(8,128)(2,1)S(1)}, u32[]{:S(2)}, u32[]{:S(2)}) collective-permute-start(bf16[192,2304]{1,0:T(8,128)(2,1)S(1)} %copy-done.43), channel_id=1, source_target_pairs={{0,4},{1,5},{2,6},{3,7},{4,0},{5,1},{6,2},{7,3},{8,12},{9,13},{10,... | collective-permute-start | bytes 2654216 | tf_op jit(solution)/shard_map/ppermute | solution.py:25
  462.7 37.8 %collective-permute-start.79 = (bf16[192,2304]{1,0:T(8,128)(2,1)S(1)}, bf16[192,2304]{1,0:T(8,128)(2,1)S(1)}, u32[]{:S(2)}, u32[]{:S(2)}) collective-permute-start(bf16[192,2304]{1,0:T(8,128)(2,1)S(1)} %copy-done.42), channel_id=1, source_target_pairs={{0,4},{1,5},{2,6},{3,7},{4,0},{5,1},{6,2},{7,3},{8,12},{9,13},{10,... | collective-permute-start | bytes 2654216 | tf_op jit(solution)/shard_map/ppermute | solution.py:25
  465.3 59.2 %collective-permute-start.37 = (bf16[1024,1536]{1,0:T(8,128)(2,1)S(1)}, bf16[1024,1536]{1,0:T(8,128)(2,1)}, u32[]{:S(2)}, u32[]{:S(2)}) collective-permute-start(bf16[1024,1536]{1,0:T(8,128)(2,1)S(1)} %slice.338), channel_id=1, source_target_pairs={{0,1},{1,0},{2,3},{3,2},{4,5},{5,4},{6,7},{7,6},{8,9},{9,8},{10,11... | collective-permute-start | bytes 9437192 | tf_op jit(solution)/shard_map/ppermute | solution.py:25
  465.4 14.8 %collective-permute-start.87 = (bf16[192,1152]{1,0:T(8,128)(2,1)S(1)}, bf16[192,1152]{1,0:T(8,128)(2,1)S(1)}, u32[]{:S(2)}, u32[]{:S(2)}) collective-permute-start(bf16[192,1152]{1,0:T(8,128)(2,1)S(1)} %fusion.46), channel_id=1, source_target_pairs={{0,8},{1,9},{2,10},{3,11},{4,12},{5,13},{6,14},{7,15},{8,16},{9,17... | collective-permute-start | bytes 1327112 | tf_op jit(solution)/shard_map/ppermute | solution.py:30
  466.2 32.4 %collective-permute-start.76 = (bf16[192,2304]{1,0:T(8,128)(2,1)S(1)}, bf16[192,2304]{1,0:T(8,128)(2,1)S(1)}, u32[]{:S(2)}, u32[]{:S(2)}) collective-permute-start(bf16[192,2304]{1,0:T(8,128)(2,1)S(1)} %fusion.40), channel_id=1, source_target_pairs={{0,8},{1,9},{2,10},{3,11},{4,12},{5,13},{6,14},{7,15},{8,16},{9,17... | collective-permute-start | bytes 2654216 | tf_op jit(solution)/shard_map/ppermute | solution.py:30
  488.1 47.9 %collective-permute-start.39 = (bf16[1024,1536]{1,0:T(8,128)(2,1)}, bf16[1024,1536]{1,0:T(8,128)(2,1)}, u32[]{:S(2)}, u32[]{:S(2)}) collective-permute-start(bf16[1024,1536]{1,0:T(8,128)(2,1)} %slice.342), channel_id=1, source_target_pairs={{0,1},{1,0},{2,3},{3,2},{4,5},{5,4},{6,7},{7,6},{8,9},{9,8},{10,11... | collective-permute-start | bytes 9437192 | tf_op jit(solution)/shard_map/ppermute | solution.py:25
  499.1 23.2 %collective-permute-start.78 = (bf16[192,2304]{1,0:T(8,128)(2,1)S(1)}, bf16[192,2304]{1,0:T(8,128)(2,1)S(1)}, u32[]{:S(2)}, u32[]{:S(2)}) collective-permute-start(bf16[192,2304]{1,0:T(8,128)(2,1)S(1)} %fusion.38), channel_id=1, source_target_pairs={{0,8},{1,9},{2,10},{3,11},{4,12},{5,13},{6,14},{7,15},{8,16},{9,17... | collective-permute-start | bytes 2654216 | tf_op jit(solution)/shard_map/ppermute | solution.py:30
  522.7 13.2 %collective-permute-start.80 = (bf16[2,48,2304]{2,1,0:T(8,128)(2,1)S(1)}, bf16[2,48,2304]{2,1,0:T(8,128)(2,1)S(1)}, u32[]{:S(2)}, u32[]{:S(2)}) collective-permute-start(bf16[2,48,2304]{2,1,0:T(8,128)(2,1)S(1)} %dynamic-slice_bitcast_fusion.10), channel_id=1, source_target_pairs={{0,2},{1,3},{2,0},{3,1},{4,6},{5,7},{6,4},{7,5},{8,10},{9,11},{10,... | collective-permute-start | bytes 1327112 | tf_op jit(solution)/shard_map/ppermute | solution.py:25
  527.5 74.7 %collective-permute-start.38 = (bf16[512,1536]{1,0:T(8,128)(2,1)S(1)}, bf16[512,1536]{1,0:T(8,128)(2,1)S(1)}, u32[]{:S(2)}, u32[]{:S(2)}) collective-permute-start(bf16[512,1536]{1,0:T(8,128)(2,1)S(1)} %slice.459), channel_id=1, source_target_pairs={{0,2},{1,3},{2,0},{3,1},{4,6},{5,7},{6,4},{7,5},{8,10},{9,11},{10,... | collective-permute-start | bytes 4718600 | tf_op jit(solution)/shard_map/ppermute | solution.py:25
  539.1 61.9 %collective-permute-start.40 = (bf16[512,1536]{1,0:T(8,128)(2,1)S(1)}, bf16[512,1536]{1,0:T(8,128)(2,1)S(1)}, u32[]{:S(2)}, u32[]{:S(2)}) collective-permute-start(bf16[512,1536]{1,0:T(8,128)(2,1)S(1)} %slice.458), channel_id=1, source_target_pairs={{0,2},{1,3},{2,0},{3,1},{4,6},{5,7},{6,4},{7,5},{8,10},{9,11},{10,... | collective-permute-start | bytes 4718600 | tf_op jit(solution)/shard_map/ppermute | solution.py:25
  628.6 70.2 %collective-permute-start.58 = (bf16[2,2,48,1664]{3,2,0,1:T(8,128)(2,1)}, bf16[2,2,48,1664]{3,2,0,1:T(8,128)(2,1)}, u32[]{:S(2)}, u32[]{:S(2)}) collective-permute-start(bf16[2,2,48,1664]{3,2,0,1:T(8,128)(2,1)} %bitcast.276), channel_id=1, source_target_pairs={{0,1},{1,0},{2,3},{3,2},{4,5},{5,4},{6,7},{7,6},{8,9},{9,8},{10,11... | collective-permute-start | bytes 1916936 | tf_op jit(solution)/shard_map/ppermute | solution.py:25
  629.4 70.7 %collective-permute-start.62 = (bf16[2,2,48,1664]{3,2,0,1:T(8,128)(2,1)}, bf16[2,2,48,1664]{3,2,0,1:T(8,128)(2,1)}, u32[]{:S(2)}, u32[]{:S(2)}) collective-permute-start(bf16[2,2,48,1664]{3,2,0,1:T(8,128)(2,1)} %bitcast.275), channel_id=1, source_target_pairs={{0,1},{1,0},{2,3},{3,2},{4,5},{5,4},{6,7},{7,6},{8,9},{9,8},{10,11... | collective-permute-start | bytes 1916936 | tf_op jit(solution)/shard_map/ppermute | solution.py:25
  630.9 72.4 %collective-permute-start.66 = (bf16[2,2,48,1664]{3,2,0,1:T(8,128)(2,1)}, bf16[2,2,48,1664]{3,2,0,1:T(8,128)(2,1)}, u32[]{:S(2)}, u32[]{:S(2)}) collective-permute-start(bf16[2,2,48,1664]{3,2,0,1:T(8,128)(2,1)} %bitcast.274), channel_id=1, source_target_pairs={{0,1},{1,0},{2,3},{3,2},{4,5},{5,4},{6,7},{7,6},{8,9},{9,8},{10,11... | collective-permute-start | bytes 1916936 | tf_op jit(solution)/shard_map/ppermute | solution.py:25
  662.1 39.9 %collective-permute-start.70 = (bf16[2,2,48,1664]{3,2,1,0:T(8,128)(2,1)}, bf16[2,2,48,1664]{3,2,1,0:T(8,128)(2,1)S(1)}, u32[]{:S(2)}, u32[]{:S(2)}) collective-permute-start(bf16[2,2,48,1664]{3,2,1,0:T(8,128)(2,1)} %get-tuple-element.94), channel_id=1, source_target_pairs={{0,1},{1,0},{2,3},{3,2},{4,5},{5,4},{6,7},{7,6},{8,9},{9,8},{10,11... | collective-permute-start | bytes 1916936 | tf_op jit(solution)/shard_map/ppermute | solution.py:25
  694.8 46.1 %collective-permute-start.43 = (bf16[2,2,48,1920]{3,2,0,1:T(8,128)(2,1)S(1)}, bf16[2,2,48,1920]{3,2,0,1:T(8,128)(2,1)S(1)}, u32[]{:S(2)}, u32[]{:S(2)}) collective-permute-start(bf16[2,2,48,1920]{3,2,0,1:T(8,128)(2,1)S(1)} %bitcast.333), channel_id=1, source_target_pairs={{0,1},{1,0},{2,3},{3,2},{4,5},{5,4},{6,7},{7,6},{8,9},{9,8},{10,11... | collective-permute-start | bytes 2211848 | tf_op jit(solution)/shard_map/ppermute | solution.py:25
  698.8 42.9 %collective-permute-start.47 = (bf16[2,2,48,1920]{3,2,0,1:T(8,128)(2,1)S(1)}, bf16[2,2,48,1920]{3,2,0,1:T(8,128)(2,1)S(1)}, u32[]{:S(2)}, u32[]{:S(2)}) collective-permute-start(bf16[2,2,48,1920]{3,2,0,1:T(8,128)(2,1)S(1)} %bitcast.332), channel_id=1, source_target_pairs={{0,1},{1,0},{2,3},{3,2},{4,5},{5,4},{6,7},{7,6},{8,9},{9,8},{10,11... | collective-permute-start | bytes 2211848 | tf_op jit(solution)/shard_map/ppermute | solution.py:25
  700.2 45.2 %collective-permute-start.51 = (bf16[2,2,48,1920]{3,2,0,1:T(8,128)(2,1)S(1)}, bf16[2,2,48,1920]{3,2,0,1:T(8,128)(2,1)S(1)}, u32[]{:S(2)}, u32[]{:S(2)}) collective-permute-start(bf16[2,2,48,1920]{3,2,0,1:T(8,128)(2,1)S(1)} %bitcast.331), channel_id=1, source_target_pairs={{0,1},{1,0},{2,3},{3,2},{4,5},{5,4},{6,7},{7,6},{8,9},{9,8},{10,11... | collective-permute-start | bytes 2211848 | tf_op jit(solution)/shard_map/ppermute | solution.py:25
  702.0 41.6 %collective-permute-start.55 = (bf16[2,2,48,1920]{3,2,1,0:T(8,128)(2,1)S(1)}, bf16[2,2,48,1920]{3,2,1,0:T(8,128)(2,1)S(1)}, u32[]{:S(2)}, u32[]{:S(2)}) collective-permute-start(bf16[2,2,48,1920]{3,2,1,0:T(8,128)(2,1)S(1)} %get-tuple-element.87), channel_id=1, source_target_pairs={{0,1},{1,0},{2,3},{3,2},{4,5},{5,4},{6,7},{7,6},{8,9},{9,8},{10,11... | collective-permute-start | bytes 2211848 | tf_op jit(solution)/shard_map/ppermute | solution.py:25
  741.7 46.3 %collective-permute-start.68 = (bf16[48,1664]{1,0:T(8,128)(2,1)S(1)}, bf16[48,1664]{1,0:T(8,128)(2,1)S(1)}, u32[]{:S(2)}, u32[]{:S(2)}) collective-permute-start(bf16[48,1664]{1,0:T(8,128)(2,1)S(1)} %fusion.90), channel_id=1, source_target_pairs={{0,4},{1,5},{2,6},{3,7},{4,0},{5,1},{6,2},{7,3},{8,12},{9,13},{10,... | collective-permute-start | bytes 479240 | tf_op jit(solution)/shard_map/ppermute | solution.py:25
  743.6 52.0 %collective-permute-start.72 = (bf16[48,1664]{1,0:T(8,128)(2,1)S(1)}, bf16[48,1664]{1,0:T(8,128)(2,1)S(1)}, u32[]{:S(2)}, u32[]{:S(2)}) collective-permute-start(bf16[48,1664]{1,0:T(8,128)(2,1)S(1)} %fusion.91), channel_id=1, source_target_pairs={{0,4},{1,5},{2,6},{3,7},{4,0},{5,1},{6,2},{7,3},{8,12},{9,13},{10,... | collective-permute-start | bytes 479240 | tf_op jit(solution)/shard_map/ppermute | solution.py:25
  749.3 15.6 %collective-permute-start.48 = (bf16[2,48,1920]{2,1,0:T(8,128)(2,1)S(1)}, bf16[2,48,1920]{2,1,0:T(8,128)(2,1)S(1)}, u32[]{:S(2)}, u32[]{:S(2)}) collective-permute-start(bf16[2,48,1920]{2,1,0:T(8,128)(2,1)S(1)} %fusion.61), channel_id=1, source_target_pairs={{0,2},{1,3},{2,0},{3,1},{4,6},{5,7},{6,4},{7,5},{8,10},{9,11},{10,... | collective-permute-start | bytes 1105928 | tf_op jit(solution)/shard_map/ppermute | solution.py:25
  753.9 17.8 %collective-permute-start.52 = (bf16[2,48,1920]{2,1,0:T(8,128)(2,1)S(1)}, bf16[2,48,1920]{2,1,0:T(8,128)(2,1)S(1)}, u32[]{:S(2)}, u32[]{:S(2)}) collective-permute-start(bf16[2,48,1920]{2,1,0:T(8,128)(2,1)S(1)} %fusion.62), channel_id=1, source_target_pairs={{0,2},{1,3},{2,0},{3,1},{4,6},{5,7},{6,4},{7,5},{8,10},{9,11},{10,... | collective-permute-start | bytes 1105928 | tf_op jit(solution)/shard_map/ppermute | solution.py:25
  757.0 18.7 %collective-permute-start.56 = (bf16[2,48,1920]{2,1,0:T(8,128)(2,1)S(1)}, bf16[2,48,1920]{2,1,0:T(8,128)(2,1)S(1)}, u32[]{:S(2)}, u32[]{:S(2)}) collective-permute-start(bf16[2,48,1920]{2,1,0:T(8,128)(2,1)S(1)} %fusion.63), channel_id=1, source_target_pairs={{0,2},{1,3},{2,0},{3,1},{4,6},{5,7},{6,4},{7,5},{8,10},{9,11},{10,... | collective-permute-start | bytes 1105928 | tf_op jit(solution)/shard_map/ppermute | solution.py:25
  764.9 23.2 %collective-permute-start.65 = (bf16[48,1664]{1,0:T(8,128)(2,1)S(1)}, bf16[48,1664]{1,0:T(8,128)(2,1)S(1)}, u32[]{:S(2)}, u32[]{:S(2)}) collective-permute-start(bf16[48,1664]{1,0:T(8,128)(2,1)S(1)} %fusion.78), channel_id=1, source_target_pairs={{0,8},{1,9},{2,10},{3,11},{4,12},{5,13},{6,14},{7,15},{8,16},{9,17... | collective-permute-start | bytes 479240 | tf_op jit(solution)/shard_map/ppermute | solution.py:30
  (91 other events, 1240.8 us)

commit v2 on v1

--- a/solution.py
+++ b/solution.py
@@ -18,6 +18,7 @@
 LOW = jnp.bfloat16
 FULL = jnp.float32
 MIB = 1024 * 1024
+LIGHT = pl.CostEstimate(flops=1024, bytes_accessed=1024, transcendentals=0)
 
 
 def flip(array, bit):
@@ -101,73 +102,428 @@
     return by_near.reshape(4, rows, columns)
 
 
+def gather_kernel(
+    ring, bands, attn_ref, ffn_ref, attn_out, ffn_out, local_sem, send_sem, recv_sem
+):
+    size = ring * RING
+    me = lax.axis_index("tok")
+    core, near, side, z = me % 2, (me // 2) % 2, (me // 4) % 2, me // RING
+    core_mate, near_mate, side_mate = me + 1 - 2 * core, me + 2 - 4 * near, me + 4 - 8 * side
+    far_mate = near_mate + 1 - 2 * core
+    up, down = (me + RING) % size, (me + size - RING) % size
+
+    barrier = pltpu.get_barrier_semaphore()
+    partners = (core_mate, near_mate, side_mate, far_mate, up, down)
+    for partner in partners:
+        pl.semaphore_signal(
+            barrier, inc=1, device_id=(partner,), device_id_type=pl.DeviceIdType.MESH
+        )
+    pl.semaphore_wait(barrier, len(partners))
+
+    own = pltpu.make_async_copy(attn_ref, attn_out.at[z, side, near, core], local_sem.at[0])
+    own.start()
+    own_slice = pltpu.make_async_copy(
+        ffn_ref.at[2 * near + core], ffn_out.at[2 * near + core], local_sem.at[1]
+    )
+    own_slice.start()
+
+    copies = []
+
+    def send(src, dst, to):
+        index = len(copies)
+        copy = pltpu.make_async_remote_copy(
+            src_ref=src,
+            dst_ref=dst,
+            send_sem=send_sem.at[index],
+            recv_sem=recv_sem.at[index],
+            device_id=(to,),
+            device_id_type=pl.DeviceIdType.MESH,
+        )
+        copy.start()
+        copies.append(copy)
+        return copy
+
+    def forward(ref, to):
+        return send(ref, ref, to)
+
+    def chunk_of(step):
+        return (z - step + ring) % ring
+
+    def piece(step, band):
+        return attn_out.at[chunk_of(step), side, near, core, bands[band]]
+
+    hops, first, second, last = {}, {}, {}, {}
+    over = []
+
+    def finish(step):
+        first[0, step].wait_recv()
+        second[0, step] = forward(attn_out.at[chunk_of(step), side, :, core, bands[0]], side_mate)
+        first[1, step].wait_recv()
+        second[1, step] = forward(attn_out.at[chunk_of(step), :, near, core, bands[1]], near_mate)
+
+    def hand_over(step):
+        second[0, step].wait_recv()
+        second[1, step].wait_recv()
+        over.append(forward(attn_out.at[chunk_of(step), :, :, core], core_mate))
+
+    for step in range(ring):
+        for band in (0, 1):
+            if step > 0:
+                hops[band, step].wait_recv()
+            source = attn_ref.at[bands[band]] if step == 0 else piece(step, band)
+            if step < ring - 1:
+                hops[band, step + 1] = send(source, piece(step, band), up)
+            mate = near_mate if band == 0 else side_mate
+            first[band, step] = send(source, piece(step, band), mate)
+        if step == 0:
+            begun = send(attn_ref.at[bands[2]], piece(0, 2), near_mate)
+            slices = [
+                send(ffn_ref.at[index], ffn_out.at[2 * near + core], mate)
+                for mate, index in (
+                    (near_mate, 2 * (1 - near) + core),
+                    (far_mate, 2 * (1 - near) + 1 - core),
+                    (core_mate, 2 * near + 1 - core),
+                )
+            ]
+            own.wait()
+            begun.wait_recv()
+            last[0] = forward(attn_out.at[z, side, :, core, bands[2]], side_mate)
+        else:
+            last[step - 1].wait_recv()
+            last[step] = forward(attn_out.at[chunk_of(step - 1), :, :, core, bands[2]], up)
+            finish(step - 1)
+        if step >= 2:
+            hand_over(step - 2)
+    finish(ring - 1)
+    hand_over(ring - 2)
+    last[ring - 1].wait_recv()
+    hand_over(ring - 1)
+    own_slice.wait()
+    for copy in slices + over:
+        copy.wait_recv()
+    for copy in copies:
+        copy.wait_send()
+
+
+def gather(attn_pack, ffn_pack):
+    size = lax.axis_size("tok")
+    ring = size // RING
+    rows, columns = attn_pack.shape
+    if ring > LONGEST_RING or ring < 2 or rows % 48:
+        return lax.all_gather(attn_pack, "tok", axis=0, tiled=True), slices_to_group(ffn_pack)
+    third = rows // 3
+    bands = [pl.ds(third * band, third) for band in range(3)]
+    count = 3 + 2 * (ring - 1) + 2 * ring + 2 * ring + 1 + ring + ring
+    anywhere = pl.BlockSpec(memory_space=pl.ANY)
+    attn_all, ffn_rows = pl.pallas_call(
+        functools.partial(gather_kernel, ring, bands),
+        in_specs=[anywhere] * 2,
+        out_specs=[anywhere] * 2,
+        out_shape=[
+            jax.ShapeDtypeStruct((ring, 2, 2, 2, rows, columns), attn_pack.dtype),
+            jax.ShapeDtypeStruct(ffn_pack.shape, ffn_pack.dtype),
+        ],
+        scratch_shapes=[
+            pltpu.SemaphoreType.DMA((2,)),
+            pltpu.SemaphoreType.DMA((count,)),
+            pltpu.SemaphoreType.DMA((count,)),
+        ],
+        compiler_params=pltpu.CompilerParams(collective_id=0, has_side_effects=True),
+    )(attn_pack, ffn_pack)
+    return attn_all.reshape(size * rows, columns), ffn_rows.reshape(GROUP * rows, -1)
+
+
+def scatter_kernel(
+    ring, bands, edges, *refs
+):
+    count = len(edges) - 1
+    grad_refs, ffn_ref, attn_out, ffn_out = refs[:count], refs[count], refs[count + 1], refs[count + 2]
+    pack, core_in, a_side, a_near, a_ring, b_near, b_side, b_ring, c_ring, c_side, c_near = refs[
+        count + 3 : count + 14
+    ]
+    local_sem, send_sem, recv_sem = refs[count + 14 :]
+    size = ring * RING
+    me = lax.axis_index("tok")
+    core, near, side, z = me % 2, (me // 2) % 2, (me // 4) % 2, me // RING
+    core_mate, near_mate, side_mate = me + 1 - 2 * core, me + 2 - 4 * near, me + 4 - 8 * side
+    far_mate = near_mate + 1 - 2 * core
+    up, down = (me + RING) % size, (me + size - RING) % size
+
+    def chunk_of(step):
+        return (z - 1 - step + 2 * ring) % ring
+
+    loads = []
+    for step in range(ring):
+        row = []
+        for k in range(count):
+            load = pltpu.make_async_copy(
+                grad_refs[k].at[chunk_of(step)],
+                pack.at[chunk_of(step), :, :, :, :, pl.ds(edges[k], edges[k + 1] - edges[k])],
+                local_sem.at[step * count + k],
+            )
+            load.start()
+            row.append(load)
+        loads.append(row)
+    own_slice = pltpu.make_async_copy(
+        ffn_ref.at[2 * near + core], ffn_out.at[2 * near + core], local_sem.at[ring * count]
+    )
+    own_slice.start()
+
+    barrier = pltpu.get_barrier_semaphore()
+    partners = (core_mate, near_mate, side_mate, far_mate, up, down)
+    for partner in partners:
+        pl.semaphore_signal(
+            barrier, inc=1, device_id=(partner,), device_id_type=pl.DeviceIdType.MESH
+        )
+    pl.semaphore_wait(barrier, len(partners))
+
+    copies = []
+
+    def send(src, dst, to):
+        index = len(copies)
+        copy = pltpu.make_async_remote_copy(
+            src_ref=src,
+            dst_ref=dst,
+            send_sem=send_sem.at[index],
+            recv_sem=recv_sem.at[index],
+            device_id=(to,),
+            device_id_type=pl.DeviceIdType.MESH,
+        )
+        copy.start()
+        copies.append(copy)
+        return copy
+
+    def add(held, arrived):
+        held[...] = (held[...].astype(FULL) + arrived[...].astype(FULL)).astype(LOW)
+
+    def part(step, y, x, band):
+        return pack.at[chunk_of(step), y, x, core, bands[band]]
+
+    def own(step, band):
+        return part(step, side, near, band)
+
+    across, first, second, hops = {}, {}, {}, {}
+
+    def begin(step):
+        chunk = chunk_of(step)
+        across[step].wait_recv()
+
+        def one(k, _):
+            add(pack.at[chunk, k // 2, k % 2, core], core_in.at[chunk, k // 2, k % 2])
+            return 0
+
+        lax.fori_loop(0, 4, one, 0)
+        first[0, step] = send(
+            pack.at[chunk, 1 - side, :, core, bands[0]], a_side.at[step], side_mate
+        )
+        first[1, step] = send(
+            pack.at[chunk, :, 1 - near, core, bands[1]], b_near.at[step], near_mate
+        )
+        if step > 0:
+            hops[2, step].wait_recv()
+            for k in range(4):
+                add(part(step, k // 2, k % 2, 2), c_ring.at[step - 1, k // 2, k % 2])
+        if step < ring - 1:
+            hops[2, step + 1] = send(
+                pack.at[chunk, :, :, core, bands[2]], c_ring.at[step], up
+            )
+
+    def middle(step):
+        first[0, step].wait_recv()
+        for x in range(2):
+            add(part(step, side, x, 0), a_side.at[step, x])
+        second[0, step] = send(part(step, side, 1 - near, 0), a_near.at[step], near_mate)
+        first[1, step].wait_recv()
+        for y in range(2):
+            add(part(step, y, near, 1), b_near.at[step, y])
+        second[1, step] = send(part(step, 1 - side, near, 1), b_side.at[step], side_mate)
+
+    def end(step):
+        for band, arrived, passing in ((0, a_near, a_ring), (1, b_side, b_ring)):
+            second[band, step].wait_recv()
+            add(own(step, band), arrived.at[step])
+            if step > 0:
+                hops[band, step].wait_recv()
+                add(own(step, band), passing.at[step - 1])
+            if step < ring - 1:
+                hops[band, step + 1] = send(own(step, band), passing.at[step], up)
+
+    for step in range(ring):
+        for load in loads[step]:
+            load.wait()
+        across[step] = send(
+            pack.at[chunk_of(step), :, :, 1 - core], core_in.at[chunk_of(step)], core_mate
+        )
+    slices = []
+    for step in range(ring + 2):
+        if step < ring:
+            begin(step)
+        if step == 0:
+            slices += [
+                send(ffn_ref.at[index], ffn_out.at[2 * near + core], mate)
+                for mate, index in (
+                    (near_mate, 2 * (1 - near) + core),
+                    (far_mate, 2 * (1 - near) + 1 - core),
+                    (core_mate, 2 * near + 1 - core),
+                )
+            ]
+        if 1 <= step <= ring:
+            middle(step - 1)
+        if step == ring:
+            last = ring - 1
+            to_side = send(pack.at[z, 1 - side, :, core, bands[2]], c_side, side_mate)
+        if step >= 2:
+            end(step - 2)
+        if step == ring:
+            to_side.wait_recv()
+            for x in range(2):
+                add(part(last, side, x, 2), c_side.at[x])
+            to_near = send(part(last, side, 1 - near, 2), c_near, near_mate)
+    to_near.wait_recv()
+    add(own(last, 2), c_near)
+    attn_out[...] = pack[z, side, near, core].astype(FULL)
+    own_slice.wait()
+    for copy in slices:
+        copy.wait_recv()
+    for copy in copies:
+        copy.wait_send()
+
+
+def scatter(grads, ffn_sum):
+    size = lax.axis_size("tok")
+    ring = size // RING
+    rows = grads[0].shape[0] // size
+    if ring > LONGEST_RING or ring < 2 or rows % 48:
+        joined = jnp.concatenate(grads, axis=1).astype(FULL)
+        return (
+            lax.psum_scatter(joined, "tok", scatter_dimension=0, tiled=True),
+            slices_from_group(ffn_sum),
+        )
+    third = rows // 3
+    bands = [pl.ds(third * band, third) for band in range(3)]
+    edges = [0]
+    for grad in grads:
+        edges.append(edges[-1] + grad.shape[1])
+    columns = edges[-1]
+    count = ring + 2 * ring + (ring - 1) + 3 + 2 * ring + 1 + 2 * (ring - 1) + 1
+    anywhere = pl.BlockSpec(memory_space=pl.ANY)
+    band = (third, columns)
+    low = lambda *shape: pltpu.VMEM((*shape, *band), LOW)
+    return pl.pallas_call(
+        functools.partial(scatter_kernel, ring, bands, edges),
+        in_specs=[anywhere] * (len(grads) + 1),
+        out_specs=[pl.BlockSpec(memory_space=pltpu.VMEM), anywhere],
+        out_shape=[
+            jax.ShapeDtypeStruct((rows, columns), FULL),
+            jax.ShapeDtypeStruct((GROUP, rows, ffn_sum.shape[1]), LOW),
+        ],
+        scratch_shapes=[
+            pltpu.VMEM((ring, 2, 2, 2, rows, columns), LOW),
+            pltpu.VMEM((ring, 2, 2, rows, columns), LOW),
+            low(ring, 2),
+            low(ring),
+            low(ring - 1),
+            low(ring, 2),
+            low(ring),
+            low(ring - 1),
+            low(ring - 1, 2, 2),
+            low(2),
+            low(),
+            pltpu.SemaphoreType.DMA((ring * len(grads) + 1,)),
+            pltpu.SemaphoreType.DMA((count,)),
+            pltpu.SemaphoreType.DMA((count,)),
+        ],
+        compiler_params=pltpu.CompilerParams(
+            collective_id=1, has_side_effects=True, vmem_limit_bytes=44 * MIB
+        ),
+    )(
+        *[grad.reshape(ring, 2, 2, 2, rows, -1) for grad in grads],
+        ffn_sum.astype(LOW).reshape(GROUP, rows, -1),
+    )
+
+
+def after(value, *marks):
+    return lax.optimization_barrier((value, *marks))[0]
+
+
 def groups_of(stride):
     size = lax.axis_size("tok")
     return [[s + stride * k for k in range(size // stride)] for s in range(stride)]
 
 
-def spread(block, stages):
+def spread(block):
     size = lax.axis_size("tok")
     ring = size // RING
     if ring > LONGEST_RING:
-        return lax.all_gather(
-            block, "tok", axis=0, tiled=True, axis_index_groups=groups_of(stages[-1])
-        )
-    device, _, _, _, z = place()
+        gathered = lax.all_gather(
+            block, "tok", axis=0, tiled=True, axis_index_groups=groups_of(GROUP)
+        )
+        return gathered, []
+    _, _, _, side, z = place()
     rows, columns = block.shape
-    steps = RING // stages[-1]
-    total = jnp.zeros((ring * steps, rows, columns), block.dtype)
-    own = block
+    total = jnp.zeros((ring, 2, rows, columns), block.dtype)
+    own, arrivals = block, []
     for step in range(ring):
         chunk = lax.rem(z - step + ring, ring)
-        blocks = [own]
-        for bit in stages:
-            stacked = jnp.stack(blocks) if len(blocks) > 1 else blocks[0][None]
-            got = flip(stacked, bit)
-            blocks = blocks + [got[k] for k in range(len(blocks))]
-        low_bits = lax.rem(device, RING) // stages[-1]
-        for k, piece in enumerate(blocks):
-            mask = 0
-            for j, bit in enumerate(stages):
-                if (k >> j) & 1:
-                    mask |= bit // stages[-1]
-            index = chunk * steps + lax.bitwise_xor(low_bits, mask)
-            total = lax.dynamic_update_index_in_dim(total, piece, index, 0)
+        for piece, y in ((own, side), (flip(own, SIDE), 1 - side)):
+            total = lax.dynamic_update_slice(total, piece[None, None], (chunk, y, 0, 0))
         if step < ring - 1:
             own = around(own)
-    return total.reshape(ring * steps * rows, columns)
-
-
-def collect(partial, stages):
-    size = lax.axis_size("tok")
-    ring = size // RING
-    if ring > LONGEST_RING:
+            arrivals.append(own)
+    return total.reshape(ring * 2 * rows, columns), arrivals
+
+
+class Reduction:
+    def __init__(self, normed, cotangent, array):
+        self.given = (normed, cotangent, array)
+        self.size = lax.axis_size("tok")
+        self.ring = self.size // RING
+        _, _, _, self.side, self.z = place()
+        self.rows = normed.shape[1] // (self.ring * 2)
+        self.short = 2 <= self.ring <= LONGEST_RING and self.rows % 64 == 0
+        self.blocks, self.crossing, self.total = {}, None, None
+
+    def multiply(self, step, mark=None):
+        if not self.short:
+            return ()
+        chunk = lax.rem(self.z - 1 - step + 2 * self.ring, self.ring)
+        normed, cotangent, array = self.given
+        array = after(array, *jax.tree.leaves(mark))
+        product = outer_products(normed, cotangent, array, chunk, 2 * self.rows)
+        self.blocks[step] = product.reshape(2, self.rows, -1)
+        return self.blocks[step]
+
+    def begin(self):
+        if self.short:
+            self.crossing = flip(pick(self.blocks[0], 1 - self.side), SIDE)
+
+    def advance(self, step, *marks):
+        if not self.short:
+            return ()
+        arrived = (self.crossing,) if self.total is None else (self.crossing, self.total)
+        block = self.blocks[min(step + 1, self.ring - 1)]
+        block, *arrived = lax.optimization_barrier((block, *arrived, *marks))[: len(arrived) + 1]
+        total = pick(self.blocks[step], self.side).astype(FULL)
+        for part in arrived:
+            total = total + part.astype(FULL)
+        if step == self.ring - 1:
+            self.sum = total.astype(LOW)
+            return (self.sum,)
+        low, give = total.astype(LOW), pick(block, 1 - self.side)
+        self.total, self.crossing = around(low), flip(give, SIDE)
+        return (low, give)
+
+    def result(self):
+        if self.short:
+            return self.sum
+        normed, cotangent, array = self.given
+        joined = jnp.concatenate(
+            [outer_sum(normed, array[0]), outer_sum(normed, array[1]), outer_sum(cotangent, array[2])],
+            axis=1,
+        )
         return lax.psum_scatter(
-            partial.astype(FULL),
-            "tok",
-            scatter_dimension=0,
-            tiled=True,
-            axis_index_groups=groups_of(stages[-1]),
-        )
-    device, _, _, _, z = place()
-    steps = RING // stages[-1]
-    rows, columns = partial.shape[0] // (ring * steps), partial.shape[1]
-    parts = partial.astype(LOW).reshape((ring, *([2] * len(stages)), rows, columns))
-
-    def piece(chunk):
-        held = pick(parts, chunk)
-        for bit in reversed(stages):
-            axis = stages.index(bit)
-            own_bit = (device // bit) % 2
-            keep = lax.dynamic_index_in_dim(held, own_bit, axis, keepdims=False)
-            give = lax.dynamic_index_in_dim(held, 1 - own_bit, axis, keepdims=False)
-            held = keep.astype(FULL) + flip(give.astype(LOW), bit).astype(FULL)
-        return held
-
-    total = piece(lax.rem(z - 1 + ring, ring))
-    for step in range(1, ring):
-        total = around(total.astype(LOW)).astype(FULL) + piece(lax.rem(z - 1 - step + 2 * ring, ring))
-    return total
+            joined, "tok", scatter_dimension=0, tiled=True, axis_index_groups=groups_of(GROUP)
+        )
 
 
 def turn(values, cosine, sine):
@@ -209,19 +565,17 @@
         log_ref[0, :, rows] = top + jnp.log2(total)
 
 
-def attend(raw_query, key_value, key_segments, query_segments, cosine, sine):
-    queries, width = raw_query.shape
+def attend(raw_query, key_value, key_segments, query_segments, cosine, sine, first, heads):
+    queries, width = raw_query.shape[0], heads * HD
     keys = key_value.shape[0]
-    heads = width // HD
     block = min(256, queries)
     head = pl.BlockSpec((queries, HD), lambda h: (0, h))
     whole = lambda shape: pl.BlockSpec(shape, lambda h: (0,) * len(shape))
-    cost = 4 * width * queries * (WINDOW + block)
     return pl.pallas_call(
         functools.partial(attend_kernel, block, HD**-0.5 * LOG2E),
         grid=(heads,),
         in_specs=[
-            head,
+            pl.BlockSpec((queries, HD), lambda h: (0, first + h)),
             whole((keys, HD)),
             whole((HD, keys)),
             whole((keys, 1)),
@@ -237,9 +591,7 @@
         ],
         scratch_shapes=[pltpu.VMEM((keys, queries), FULL)],
         compiler_params=pltpu.CompilerParams(vmem_limit_bytes=40 * MIB),
-        cost_estimate=pl.CostEstimate(
-            flops=4 * cost, bytes_accessed=8 * queries * width, transcendentals=0
-        ),
+        cost_estimate=LIGHT,
     )(
         raw_query,
         key_value[:, :HD],
@@ -284,7 +636,6 @@
     block = min(256, queries)
     head = pl.BlockSpec((queries, HD), lambda h: (0, h))
     whole = lambda shape: pl.BlockSpec(shape, lambda h: (0,) * len(shape))
-    cost = 10 * width * queries * (WINDOW + block)
     return pl.pallas_call(
         functools.partial(attend_back_kernel, block, HD**-0.5 * LOG2E),
         grid=(heads,),
@@ -309,9 +660,7 @@
         ],
         scratch_shapes=[pltpu.VMEM((keys, queries), FULL)],
         compiler_params=pltpu.CompilerParams(vmem_limit_bytes=40 * MIB),
-        cost_estimate=pl.CostEstimate(
-            flops=3 * cost, bytes_accessed=8 * queries * width, transcendentals=0
-        ),
+        cost_estimate=LIGHT,
     )(
         rot,
         grad,
@@ -331,7 +680,7 @@
 GELU_B = 0.044715
 
 
-def hidden_kernel(normed_ref, cot_ref, gate_ref, up_ref, down_ref, hidden_ref, gate_out, up_out):
+def hidden_kernel(normed_ref, cot_ref, gate_ref, up_ref, down_ref, out_ref):
     gate = matmul(normed_ref[...], gate_ref[...])
     up = matmul(normed_ref[...], up_ref[...])
     grad_hidden = matmul(cot_ref[...], down_ref[...])
@@ -340,35 +689,149 @@
     half = 0.5 * (1.0 + bent)
     value = gate * half
     slope = half + 0.5 * gate * (1.0 - bent * bent) * (GELU_A + 3.0 * GELU_A * GELU_B * square)
-    hidden_ref[...] = (value * up).astype(LOW)
-    gate_out[...] = (grad_hidden * up * slope).astype(LOW)
-    up_out[...] = (grad_hidden * value).astype(LOW)
-
-
-def hidden_and_grads(normed, cotangent, gate_w, up_w, down_w):
+    out_ref[0] = (grad_hidden * up * slope).astype(LOW)
+    out_ref[1] = (grad_hidden * value).astype(LOW)
+    out_ref[2] = (value * up).astype(LOW)
+
+
+def hidden_and_grads(normed, cotangent, pack):
     tokens, width = normed.shape
-    columns = gate_w.shape[1]
-    rows, wide = min(512, tokens), 384
+    columns = pack.shape[1] // 3
+    rows, wide = min(256, tokens), columns
+    steps = columns // wide
     token_block = pl.BlockSpec((rows, width), lambda j, i: (i, 0))
-    weight_block = pl.BlockSpec((width, wide), lambda j, i: (0, j))
-    out_block = pl.BlockSpec((rows, wide), lambda j, i: (i, j))
+    weight_blocks = [
+        pl.BlockSpec(
+            (width, wide),
+            lambda j, i, part=part: (0, part * steps + j),
+            pipeline_mode=pl.Buffered(1),
+        )
+        for part in range(3)
+    ]
     return pl.pallas_call(
         hidden_kernel,
-        grid=(columns // wide, tokens // rows),
-        in_specs=[token_block, token_block, weight_block, weight_block, weight_block],
-        out_specs=[out_block] * 3,
-        out_shape=[jax.ShapeDtypeStruct((tokens, columns), LOW)] * 3,
+        grid=(steps, tokens // rows),
+        in_specs=[token_block, token_block, *weight_blocks],
+        out_specs=pl.BlockSpec((3, rows, wide), lambda j, i: (0, i, j)),
+        out_shape=jax.ShapeDtypeStruct((3, tokens, columns), LOW),
         compiler_params=pltpu.CompilerParams(vmem_limit_bytes=48 * MIB),
-        cost_estimate=pl.CostEstimate(
-            flops=6 * tokens * width * columns,
-            bytes_accessed=12 * tokens * width,
-            transcendentals=tokens * columns,
+        cost_estimate=LIGHT,
+    )(normed, cotangent, pack, pack, pack)
+
+
+def project_sum_kernel(count, blocks, array_ref, *refs):
+    weight_refs, out_ref = refs[:count], refs[count]
+    away, arrived, send_sem, recv_sem = refs[count + 1 :]
+    step, column = pl.program_id(0), pl.program_id(1)
+    columns, rows = pl.num_programs(1), out_ref.shape[0]
+    me = lax.axis_index("tok")
+    mate = me + 1 - 2 * (me % 2)
+
+    def crossing(block):
+        return pltpu.make_async_remote_copy(
+            src_ref=away.at[block],
+            dst_ref=arrived.at[block],
+            send_sem=send_sem.at[block],
+            recv_sem=recv_sem.at[block],
+            device_id=(mate,),
+            device_id_type=pl.DeviceIdType.MESH,
+        )
+
+    @pl.when((step == 0) & (column == 0))
+    def _():
+        barrier = pltpu.get_barrier_semaphore()
+        pl.semaphore_signal(
+            barrier, inc=1, device_id=(mate,), device_id_type=pl.DeviceIdType.MESH
+        )
+        pl.semaphore_wait(barrier, 1)
+
+    total = by_rows(array_ref[0], weight_refs[0][...])
+    for k in range(1, count):
+        total += by_rows(array_ref[k], weight_refs[k][...])
+    for block in range(blocks):
+
+        @pl.when(step == block)
+        def _():
+            away[block, column] = total.astype(LOW)
+
+            @pl.when(column == columns - 1)
+            def _():
+                crossing(block).start()
+
+        @pl.when(step == blocks + block)
+        def _():
+            @pl.when(column == 0)
+            def _():
+                crossing(block).wait()
+
+            out_ref[...] = (total + arrived[block, column].astype(FULL)).astype(LOW)
+
+
+def project_sum(array, pack, first, count, identity, marks=()):
+    array = after(array, *jax.tree.leaves(marks))
+    tokens, columns = array.shape[1:]
+    width = pack.shape[0]
+    rows, wide = tokens // 4, 512
+    blocks = tokens // rows // 2
+    return pl.pallas_call(
+        functools.partial(project_sum_kernel, count, blocks),
+        grid=(2 * blocks, width // wide),
+        in_specs=[
+            pl.BlockSpec(
+                (count, rows, columns), lambda i, j: (first // count, (i + blocks) % (2 * blocks), 0)
+            )
+        ]
+        + [pl.BlockSpec((wide, columns), lambda i, j, k=k: (j, first + k)) for k in range(count)],
+        out_specs=pl.BlockSpec(
+            (rows, wide),
+            lambda i, j: (jnp.maximum(i - blocks, 0), jnp.where(i >= blocks, j, 0)),
         ),
-    )(normed, cotangent, gate_w, up_w, down_w)
-
-
-def as_column(vector):
-    return jnp.pad(vector[:, None], ((0, 0), (0, HD - 1)))
+        out_shape=jax.ShapeDtypeStruct((tokens // 2, width), LOW),
+        scratch_shapes=[
+            pltpu.VMEM((blocks, width // wide, rows, wide), LOW),
+            pltpu.VMEM((blocks, width // wide, rows, wide), LOW),
+            pltpu.SemaphoreType.DMA((blocks,)),
+            pltpu.SemaphoreType.DMA((blocks,)),
+        ],
+        compiler_params=pltpu.CompilerParams(
+            collective_id=identity, has_side_effects=True, vmem_limit_bytes=44 * MIB
+        ),
+        cost_estimate=LIGHT,
+    )(array, *([pack] * count))
+
+
+def outer_kernel(steps, chunk_ref, normed_ref, cot_ref, right_ref, out_ref, left):
+    for start, ref in ((0, normed_ref), (2 * steps, cot_ref)):
+
+        @pl.when(pl.program_id(0) == start)
+        def _():
+            left[...] = ref[...].T
+
+    out_ref[...] = matmul(left[...], right_ref[0]).astype(LOW)
+
+
+def outer_products(normed, cotangent, array, chunk, rows):
+    tokens, columns = array.shape[1:]
+    wide = columns
+    steps = columns // wide
+    left = pl.BlockSpec((tokens, rows), lambda j, chunk_ref: (0, chunk_ref[0]))
+    return pl.pallas_call(
+        functools.partial(outer_kernel, steps),
+        grid_spec=pltpu.PrefetchScalarGridSpec(
+            num_scalar_prefetch=1,
+            grid=(3 * steps,),
+            in_specs=[
+                left,
+                left,
+                pl.BlockSpec((1, tokens, wide), lambda j, chunk_ref: (j // steps, 0, j % steps)),
+            ],
+            out_specs=pl.BlockSpec((rows, wide), lambda j, chunk_ref: (0, j)),
+            scratch_shapes=[pltpu.VMEM((rows, tokens), LOW)],
+        ),
+        out_shape=jax.ShapeDtypeStruct((rows, 3 * columns), LOW),
+        compiler_params=pltpu.CompilerParams(vmem_limit_bytes=40 * MIB),
+        cost_estimate=LIGHT,
+    )(chunk[None].astype(jnp.int32), normed, cotangent, array)
 
 
 def on_device(
@@ -407,22 +870,21 @@
         ],
         axis=1,
     )
-    attn_all = spread(attn_pack, (SIDE, NEAR, CORE))
     edge = heads_width + 2 * HD
+    def sliced(weight):
+        return weight.reshape(own_rows, GROUP, slice_width).transpose(1, 0, 2)
+
+    ffn_pack = jnp.concatenate([sliced(w_gate), sliced(w_up), sliced(w_down)], axis=2)
+    attn_all, ffn_rows = gather(attn_pack, ffn_pack)
     query_w, kv_w = attn_all[:, :heads_width], attn_all[:, heads_width:edge]
     out_w = attn_all[:, edge : edge + heads_width]
     gains = attn_all[:, edge + heads_width : edge + heads_width + 2].astype(FULL)
     gain_one, gain_two = gains[:, 0], gains[:, 1]
 
-    def sliced(weight):
-        return weight.reshape(own_rows, GROUP, slice_width).transpose(1, 0, 2)
-
-    ffn_pack = jnp.concatenate([sliced(w_gate), sliced(w_up), sliced(w_down)], axis=2)
-    ffn_rows = slices_to_group(ffn_pack)
-    gate_up_w = spread(ffn_rows[:, : 2 * slice_width], (SIDE,))
-    down_w = spread(ffn_rows[:, 2 * slice_width :], (SIDE,))
+    ffn_w, arrivals = spread(ffn_rows)
+    gate_up_w, down_w = ffn_w[:, : 2 * slice_width], ffn_w[:, 2 * slice_width :]
     gate_w, up_w = gate_up_w[:, :slice_width], gate_up_w[:, slice_width:]
-    cot_group = rows_to_group(cotangent)
+    cot_group = rows_to_group(after(cotangent, attn_all))
 
     inverse_one = lax.rsqrt(jnp.mean(inputs * inputs, axis=-1, keepdims=True) + EPSILON)
     normed = (inputs * inverse_one * gain_one).astype(LOW)
@@ -437,22 +899,33 @@
     received = [passed_along(key_value, hop) for hop in range(hop_count, 0, -1)]
     all_keys = jnp.concatenate(received + [key_value], axis=0)
     raw_query = matmul(normed, query_w)
-    rot, mixed, logs = attend(raw_query, all_keys, key_segments, query_segments, cosine, sine)
+    heads = heads_width // HD
+    given = (all_keys, key_segments, query_segments, cosine, sine)
+    early = attend(raw_query, *given, 0, heads // 2)
+    late = attend(
+        after(raw_query, early[1], *arrivals[:1]), *given, heads // 2, heads - heads // 2
+    )
+    rot, mixed = (jnp.concatenate([early[k], late[k]], axis=1) for k in range(2))
+    logs = jnp.concatenate([early[2], late[2]], axis=0)
     middle = inputs + by_rows(mixed, out_w)
     inverse_two = lax.rsqrt(jnp.mean(middle * middle, axis=-1, keepdims=True) + EPSILON)
     normed_two = (middle * inverse_two * gain_two).astype(LOW)
 
-    normed_group = rows_to_group(normed_two)
-    hidden, gate_low, up_low = hidden_and_grads(normed_group, cot_group, gate_w, up_w, down_w)
-    grad_down_w = outer_sum(cot_group, hidden).astype(LOW)
-    down_sum = collect(grad_down_w, (SIDE,))
-    grad_normed_part = by_rows(gate_low, gate_w) + by_rows(up_low, up_w)
-    grad_normed_two = rows_from_group(grad_normed_part.astype(LOW))
-    gate_up_low = jnp.concatenate([gate_low, up_low], axis=1)
-    grad_gate_up_w = outer_sum(normed_group, gate_up_low).astype(LOW)
-    gate_up_sum = collect(grad_gate_up_w, (SIDE,))
-    result = middle + rows_from_group(by_rows(hidden, down_w).astype(LOW))
-    output = result.astype(LOW)
+    normed_group = rows_to_group(after(normed_two, *arrivals[1:2]))
+    hidden_pack = hidden_and_grads(normed_group, cot_group, ffn_w)
+    reduction = Reduction(normed_group, cot_group, hidden_pack)
+    pairs_done = reduction.multiply(0)
+    reduction.begin()
+    pairs_done = reduction.multiply(1, pairs_done)
+    group_sum = project_sum(hidden_pack, ffn_w, 0, 2, 2, pairs_done)
+    near_sent = flip(group_sum[token_count:], NEAR)
+    marks = reduction.advance(0, group_sum)
+    pairs_done = reduction.multiply(2, marks)
+    pairs_done = reduction.multiply(3, pairs_done)
+    marks = reduction.advance(1, pairs_done)
+    output_sum = project_sum(hidden_pack, ffn_w, 2, 1, 3, marks)
+    output_near = flip(after(output_sum, near_sent)[token_count:], NEAR)
+    grad_normed_two = group_sum[:token_count].astype(FULL) + after(near_sent, output_sum).astype(FULL)
 
     scaled = grad_normed_two * gain_two
     grad_middle = (
@@ -460,18 +933,16 @@
         + inverse_two * scaled
         - middle * inverse_two**3 * jnp.mean(scaled * middle, axis=-1, keepdims=True)
     )
-    gain_two_part = jnp.sum(grad_normed_two * middle * inverse_two, axis=0)
     branch = grad_middle.astype(LOW)
     grad_mixed = matmul(branch, out_w).astype(LOW)
-    grad_out_w = outer_sum(branch, mixed)
-    out_sum = collect(
-        jnp.concatenate([grad_out_w.astype(LOW), as_column(gain_two_part.astype(LOW))], axis=1),
-        (SIDE, NEAR, CORE),
-    )
-
+    grad_out_w = outer_sum(branch, mixed).astype(LOW)
+    marks = reduction.advance(2, grad_mixed)
     query_low, key_grads, value_grads = attend_back(
-        rot, grad_mixed, mixed, logs, all_keys, key_segments, query_segments, cosine, sine
-    )
+        rot, after(grad_mixed, *marks), mixed, logs, all_keys, key_segments, query_segments, cosine, sine
+    )
+    output = (
+        middle + output_sum[:token_count].astype(FULL) + after(output_near, query_low).astype(FULL)
+    ).astype(LOW)
     grads = jnp.concatenate([key_grads * HD**-0.5, value_grads], axis=1)
     shares = grads[WINDOW:]
     for hop in range(1, hop_count + 1):
@@ -487,14 +958,15 @@
         scaled_one * inputs, axis=-1, keepdims=True
     )
     grad_tokens = (grad_middle + grad_inputs).astype(LOW)
-    gain_one_part = jnp.sum(grad_normed * inputs * inverse_one, axis=0)
-    query_sum = collect(
-        jnp.concatenate([grad_query_w, grad_kv_w, as_column(gain_one_part.astype(LOW))], axis=1),
-        (SIDE, NEAR, CORE),
-    )
-
-    down_parts = slices_from_group(down_sum)
-    gate_up_parts = slices_from_group(gate_up_sum)
+    lane = lax.broadcasted_iota(jnp.int32, (token_count, HD), 1)
+    grad_gains = (
+        outer_sum((grad_normed * inputs * inverse_one).astype(LOW), (lane == 0).astype(LOW))
+        + outer_sum((grad_normed_two * middle * inverse_two).astype(LOW), (lane == 1).astype(LOW))
+    ).astype(LOW)
+    reduction.advance(3, grad_query_w)
+    attn_sum, ffn_parts = scatter(
+        [grad_query_w, grad_kv_w, grad_out_w, grad_gains], reduction.result()
+    )
 
     def joined(parts):
         return parts.transpose(1, 0, 2).reshape(own_rows, hidden_width).astype(FULL)
@@ -502,15 +974,15 @@
     return (
         output,
         grad_tokens,
-        query_sum[:, edge],
-        out_sum[:, heads_width],
-        query_sum[:, :heads_width],
-        query_sum[:, heads_width : heads_width + HD],
-        query_sum[:, heads_width + HD : edge],
-        out_sum[:, :heads_width],
-        joined(gate_up_parts[:, :, :slice_width]),
-        joined(gate_up_parts[:, :, slice_width:]),
-        joined(down_parts),
+        attn_sum[:, edge + heads_width],
+        attn_sum[:, edge + heads_width + 1],
+        attn_sum[:, :heads_width],
+        attn_sum[:, heads_width : heads_width + HD],
+        attn_sum[:, heads_width + HD : edge],
+        attn_sum[:, edge : edge + heads_width],
+        joined(ffn_parts[:, :, :slice_width]),
+        joined(ffn_parts[:, :, slice_width : 2 * slice_width]),
+        joined(ffn_parts[:, :, 2 * slice_width :]),
     )
 
 

time: 817 us -> 549 us (0.67)
  waiting for transfers between devices: 292 us -> 70.9 us
  Pallas kernels: 86.7 us -> 294 us
  local copies, waits for them, and re-layouts: 145 us -> 64.9 us
  matrix products: 105 us -> 35.3 us
  starting transfers between devices: 103 us -> 45.1 us
  other arithmetic: 70 us -> 31.3 us
    pallas_call x1 -> x9, Pallas kernels: 36.5 us -> 245 us  [the longest x1 63.5 us: scatter(): pl.pallas_call(functools.partial(scatter_kernel, ring, bands, edges), in_...]
    ppermute x66 -> x14, waiting for transfers between devices: 187 us -> 26.4 us  [flip(): return lax.ppermute(array, 'tok', [(i, i ^ bit) for i in range(size)])]
    ppermute x21 -> x6, waiting for transfers between devices: 101 us -> 44.6 us  [around(): lax.ppermute(array, 'tok', [(i, (i + RING) % size) for i in range(size)])]
    ppermute x66 -> x14, starting transfers between devices: 64.9 us -> 15.6 us  [flip(): return lax.ppermute(array, 'tok', [(i, i ^ bit) for i in range(size)])]
    dot_general x6 -> x3, matrix products: 49.7 us -> 11.6 us  [by_rows(): lax.dot_general(left_side, right_side, (((1,), (1,)), ((), ())), preferre...]
    dynamic_update_slice x48 -> x8, local copies, waits for them, and re-layouts: 48.6 us -> 12.7 us  [spread(): total = lax.dynamic_update_slice(total, piece[None, None], (chunk, y, 0, 0))]
    dot_general x5, matrix products: 40.9 us -> 10.3 us  [outer_sum(): lax.dot_general(left_side, right_side, (((0,), (0,)), ((), ())), preferre...]
    dynamic_slice x15 -> x0, local copies, waits for them, and re-layouts: 18.2 us -> none  [the longest x6 7.06 us: pick(): return lax.dynamic_index_in_dim(array, index, 0, keepdims=False)]
  transfers between devices with their start and end apart: 91 -> 24, of which waited for: 38 -> 7; matrix products, arithmetic and copies ran while one was open for 32% -> 17% of each run, Pallas kernels for 6% -> 23%
where the time goes in v2:
time: 549 us; the launch traced here: 544 us
  Pallas kernels  294 us (54%)
  waiting for transfers between devices  70.9 us (13%)
  local copies, waits for them, and re-layouts  64.9 us (12%)
  starting transfers between devices  45.1 us (8%)
  matrix products  35.3 us (6%)
  other arithmetic  31.3 us (6%)
    pallas_call x1, Pallas kernels, scatter(): pl.pallas_call(functools.partial(scatter_kernel, ring, bands, edges), in_...  63.5 us
    pallas_call x1, Pallas kernels, gather(): pl.pallas_call(functools.partial(gather_kernel, ring, bands), in_specs=[a...  63.1 us
    ppermute x6, waiting for transfers between devices, around(): lax.ppermute(array, 'tok', [(i, (i + RING) % size) for i in range(size)])  44.6 us
    pallas_call x4, Pallas kernels, outer_products(): pl.pallas_call(functools.partial(outer_kernel, steps), grid_spec=pltpu.Pr...  42.9 us
    pallas_call x2, Pallas kernels, project_sum(): pl.pallas_call(functools.partial(project_sum_kernel, count, blocks), grid...  42 us
    pallas_call x1, Pallas kernels, hidden_and_grads(): pl.pallas_call(hidden_kernel, grid=(steps, tokens // rows), in_specs=[tok...  33.1 us
    unnamed x94, local copies, waits for them, and re-layouts  27.5 us
    ppermute x14, waiting for transfers between devices, flip(): return lax.ppermute(array, 'tok', [(i, i ^ bit) for i in range(size)])  26.4 us
  transfers between devices with their start and end apart: 24, of which 7 were waited for; matrix products, arithmetic and copies ran while one was open for 17% of the time, Pallas kernels for 23%

profile of v2, /device:TPU:0, one launch (start us, length us, event | category | flops | bytes accessed | tf_op | source)
XLA Modules:
  0.0 543.6 jit_solution(2007839007069415110)
XLA Ops:
  3.4 1.2 bitcast_bitcast_fusion
  7.1 1.2 pad_maximum_fusion.4.ffn_ref
  8.3 63.1 %shard_map.222 = (bf16[4,2,2,2,48,3456]{5,4,3,2,1,0:T(8,128)(2,1)}, bf16[4,48,3456]{2,1,0:T(8,128)(2,1)}) custom-call(bf16[48,3456]{1,0:T(8,128)(2,1)} %copy-done.36, bf16[4,48,3456]{2,1,0:T(8,128)(2,1)} %pad_maximum_fusion.4.ffn_ref), custom_call_target="tpu_custom_call" | custom-call | tf_op jit(solution)/shard_map/pallas_call | solution.py:218
  71.4 1.6 collective-permute-start.8
  75.7 1.8 fusion.41
  79.7 2.1 collective-permute-start
  81.8 1.8 collective-permute-start.1
  83.6 3.1 collective-permute-start.6
  86.7 6.7 %fusion.6.q_ref = f32[512,1536]{1,0:T(8,128)} fusion(bf16[1536,3456]{1,0:T(8,128)(2,1)} %bitcast.121, bf16[512,1536]{1,0:T(8,128)(2,1)S(1)} %copy-done.26, f32[1536]{0:T(1024)S(1)} %get-tuple-element.124, f32[512]{0:T(512)S(1)} %get-tuple-element.149), kind=kOutput, calls=%fused_computation.14 | convolution fusion | flops 2419064832 | bytes 9445376 | tf_op jit(solution)/shard_map/dot_general | solution.py:57
  93.4 4.7 broadcast_in_dim.55
  99.6 2.9 constant_dynamic-update-slice_fusion.12
  103.9 1.9 copy-done.6
  105.8 12.8 %shard_map.223 = (bf16[512,768]{1,0:T(8,128)(2,1)S(1)}, bf16[512,768]{1,0:T(8,128)(2,1)S(1)}, f32[6,1,512]{2,1,0:T(1,128)S(1)}) custom-call(f32[512,1536]{1,0:T(8,128)S(1)} %copy-done.6, bf16[1536,128]{1,0:T(8,128)(2,1)S(1)} %get-tuple-element.135.key_ref, bf16[128,1536]{1,0:T(8,128)(2,1)S(1)} %copy.61.value_t_ref, s32[1536,1]{1,0:T(8,128)S(1)} %broadcast_in_dim.67.ks_ref, ...), custom_call_target="tpu_custom_call" | custom-call | flops 1024 | bytes 1024 | tf_op jit(solution)/shard_map/pallas_call | solution.py:574
  119.5 12.8 %shard_map.224 = (bf16[512,768]{1,0:T(8,128)(2,1)S(1)}, bf16[512,768]{1,0:T(8,128)(2,1)S(1)}, f32[6,1,512]{2,1,0:T(1,128)S(1)}) custom-call(f32[512,1536]{1,0:T(8,128)S(1)} %copy-done.6, bf16[1536,128]{1,0:T(8,128)(2,1)S(1)} %get-tuple-element.135.key_ref, bf16[128,1536]{1,0:T(8,128)(2,1)S(1)} %copy.61.value_t_ref, s32[1536,1]{1,0:T(8,128)S(1)} %broadcast_in_dim.67.ks_ref, ...), custom_call_target="tpu_custom_call" | custom-call | flops 1024 | bytes 1024 | tf_op jit(solution)/shard_map/pallas_call | solution.py:574
  132.5 21.7 %collective-permute-start.3 = (bf16[192,3456]{1,0:T(8,128)(2,1)}, bf16[192,3456]{1,0:T(8,128)(2,1)S(1)}, u32[]{:S(2)}, u32[]{:S(2)}) collective-permute-start(bf16[192,3456]{1,0:T(8,128)(2,1)} %collective-permute-done.2), channel_id=1, source_target_pairs={{0,8},{1,9},{2,10},{3,11},{4,12},{5,13},{6,14},{7,15},{8,16},{9,17... | collective-permute-start | bytes 3981320 | tf_op jit(solution)/shard_map/ppermute | solution.py:31
  154.2 3.1 bitcast_dynamic-update-slice_fusion.6
  157.3 2.6 bitcast_dynamic-update-slice_fusion.5
  160.0 4.8 multiply_reduce_fusion.1
  165.2 2.8 pad_maximum_fusion.1
  168.2 1.5 constant_dynamic-update-slice_fusion.11
  169.7 10.1 %collective-permute-done.3 = bf16[192,3456]{1,0:T(8,128)(2,1)S(1)} collective-permute-done((bf16[192,3456]{1,0:T(8,128)(2,1)}, bf16[192,3456]{1,0:T(8,128)(2,1)S(1)}, u32[]{:S(2)}, u32[]{:S(2)}) %collective-permute-start.3) | collective-permute-done | bytes 1327136 | tf_op jit(solution)/shard_map/ppermute | solution.py:31
  179.7 3.7 collective-permute-start.4
  185.9 30.9 %collective-permute-done.11 = bf16[192,3456]{1,0:T(8,128)(2,1)S(1)} collective-permute-done((bf16[192,3456]{1,0:T(8,128)(2,1)S(1)}, bf16[192,3456]{1,0:T(8,128)(2,1)S(1)}, u32[]{:S(2)}, u32[]{:S(2)}) %collective-permute-start.11) | collective-permute-done | bytes 1327136 | tf_op jit(solution)/shard_map/ppermute | solution.py:31
  216.8 1.7 collective-permute-start.12
  220.3 1.2 bitcast_dynamic-update-slice_fusion.1
  221.8 25.7 %collective-permute-done.12 = bf16[192,3456]{1,0:T(8,128)(2,1)S(1)} collective-permute-done((bf16[192,3456]{1,0:T(8,128)(2,1)S(1)}, bf16[192,3456]{1,0:T(8,128)(2,1)S(1)}, u32[]{:S(2)}, u32[]{:S(2)}) %collective-permute-start.12) | collective-permute-done | bytes 1327136 | tf_op jit(solution)/shard_map/ppermute | solution.py:26
  247.5 1.2 bitcast_dynamic-update-slice_fusion
  248.9 2.7 copy-done
  251.6 33.1 %shard_map.225.right_ref.array_ref = bf16[3,2048,1152]{2,1,0:T(8,128)(2,1)} custom-call(bf16[2048,1536]{1,0:T(8,128)(2,1)} %copy-done, bf16[2048,1536]{1,0:T(8,128)(2,1)} %copy-done.22, bf16[1536,3456]{1,0:T(8,128)(2,1)} %bitcast.17.gate_ref.up_ref.down_ref.refs_0_.refs_1_, bf16[1536,3456]{1,0:T(8,128)(2,1)} %bitcast.17.gate_ref.up_ref.down_ref.refs_0_.refs_1_, ...), custom_call_target="tpu_custom_call" | custom-call | flops 1024 | bytes 1024 | tf_op jit(solution)/shard_map/pallas_call | solution.py:711
  284.8 2.8 copy-done.1
  287.5 10.7 %shard_map.226 = bf16[384,3456]{1,0:T(8,128)(2,1)S(1)} custom-call(s32[1]{0:T(128)} %bitcast.19.chunk_ref, bf16[2048,1536]{1,0:T(8,128)(2,1)S(1)} %copy-done.1, bf16[2048,1536]{1,0:T(8,128)(2,1)} %copy-done.22, bf16[3,2048,1152]{2,1,0:T(8,128)(2,1)} %shard_map.225.right_ref.array_ref), custom_call_target="tpu_custom_call" | custom-call | flops 1024 | bytes 1024 | tf_op jit(solution)/shard_map/pallas_call | solution.py:818
  298.3 1.5 copy-done.9
  300.9 1.4 collective-permute-start.13
  302.3 2.8 copy-done.2
  305.1 10.7 %shard_map.227 = bf16[384,3456]{1,0:T(8,128)(2,1)S(1)} custom-call(s32[1]{0:T(128)} %bitcast.18.chunk_ref, bf16[2048,1536]{1,0:T(8,128)(2,1)S(1)} %copy-done.2, bf16[2048,1536]{1,0:T(8,128)(2,1)} %copy-done.22, bf16[3,2048,1152]{2,1,0:T(8,128)(2,1)} %shard_map.225.right_ref.array_ref), custom_call_target="tpu_custom_call" | custom-call | flops 1024 | bytes 1024 | tf_op jit(solution)/shard_map/pallas_call | solution.py:818
  315.8 25.6 %shard_map.228 = bf16[1024,1536]{1,0:T(8,128)(2,1)S(1)} custom-call(bf16[3,2048,1152]{2,1,0:T(8,128)(2,1)} %shard_map.225.right_ref.array_ref, bf16[1536,3456]{1,0:T(8,128)(2,1)} %bitcast.17.gate_ref.up_ref.down_ref.refs_0_.refs_1_, bf16[1536,3456]{1,0:T(8,128)(2,1)} %bitcast.17.gate_ref.up_ref.down_ref.refs_0_.refs_1_), custom_call_target="tpu_custom_call" | custom-call | flops 1024 | bytes 1024 | tf_op jit(solution)/shard_map/pallas_call | solution.py:776
  343.7 2.7 fusion.28
  347.3 1.9 copy.65.key_t_ref
  349.2 2.6 pad_maximum_fusion.3.rot_ref
  351.8 1.2 slice.150
  353.6 2.8 copy-done.3
  356.4 10.7 %shard_map.229 = bf16[384,3456]{1,0:T(8,128)(2,1)S(1)} custom-call(s32[1]{0:T(128)} %bitcast.23.chunk_ref, bf16[2048,1536]{1,0:T(8,128)(2,1)S(1)} %copy-done.3, bf16[2048,1536]{1,0:T(8,128)(2,1)} %copy-done.22, bf16[3,2048,1152]{2,1,0:T(8,128)(2,1)} %shard_map.225.right_ref.array_ref), custom_call_target="tpu_custom_call" | custom-call | flops 1024 | bytes 1024 | tf_op jit(solution)/shard_map/pallas_call | solution.py:818
  367.1 10.7 %shard_map.230 = bf16[384,3456]{1,0:T(8,128)(2,1)S(1)} custom-call(s32[1]{0:T(128)} %bitcast.28.chunk_ref, bf16[2048,1536]{1,0:T(8,128)(2,1)S(1)} %copy-done.3, bf16[2048,1536]{1,0:T(8,128)(2,1)} %copy-done.22, bf16[3,2048,1152]{2,1,0:T(8,128)(2,1)} %shard_map.225.right_ref.array_ref), custom_call_target="tpu_custom_call" | custom-call | flops 1024 | bytes 1024 | tf_op jit(solution)/shard_map/pallas_call | solution.py:818
  378.2 2.4 collective-permute-done.15
  380.6 1.2 dynamic-slice_bitcast_fusion.1
  381.7 1.4 collective-permute-start.18
  383.1 3.3 fusion.30
  386.8 16.4 %shard_map.231 = bf16[1024,1536]{1,0:T(8,128)(2,1)S(1)} custom-call(bf16[3,2048,1152]{2,1,0:T(8,128)(2,1)} %shard_map.225.right_ref.array_ref, bf16[1536,3456]{1,0:T(8,128)(2,1)} %bitcast.17.gate_ref.up_ref.down_ref.refs_0_.refs_1_), custom_call_target="tpu_custom_call" | custom-call | flops 1024 | bytes 1024 | tf_op jit(solution)/shard_map/pallas_call | solution.py:776
  404.0 1.2 slice.151
  405.8 2.7 multiply_subtract_fusion
  408.5 4.3 convolution_convert_fusion
  412.9 4.9 fusion.20.grad_ref
  417.8 1.2 collective-permute-done.19
  420.9 3.6 fusion.27
  424.6 24.1 %shard_map.232 = (bf16[512,1536]{1,0:T(8,128)(2,1)S(1)}, f32[1536,128]{1,0:T(8,128)S(1)}, f32[1536,128]{1,0:T(8,128)S(1)}) custom-call(bf16[512,1536]{1,0:T(8,128)(2,1)S(1)} %copy-done.13, bf16[512,1536]{1,0:T(8,128)(2,1)S(1)} %fusion.20.grad_ref, bf16[512,1536]{1,0:T(8,128)(2,1)S(1)} %copy-done.17, f32[12,1,512]{2,1,0:T(1,128)S(1)} %pad_maximum_fusion.11.log_ref, ...), custom_call_target="tpu_custom_call" | custom-call | flops 1024 | bytes 1024 | tf_op jit(solution)/shard_map/pallas_call | solution.py:639
  449.0 1.4 collective-permute-start.20
  450.4 1.5 collective-permute-start.21
  451.9 3.1 convolution_convert_fusion.1
  455.0 4.7 fusion.4
  459.8 3.2 add_convert_fusion
  465.0 2.1 fusion.15
  470.3 2.0 fusion.14
  472.4 2.2 fusion.25
  474.6 63.5 %shard_map.233 = (f32[48,3456]{1,0:T(8,128)S(1)}, bf16[4,48,3456]{2,1,0:T(8,128)(2,1)S(1)}) custom-call(bf16[4,2,2,2,48,1536]{5,4,3,2,1,0:T(8,128)(2,1)S(1)} %bitcast.100, bf16[4,2,2,2,48,256]{5,4,3,2,1,0:T(8,128)(2,1)S(1)} %bitcast.102, bf16[4,2,2,2,48,1536]{5,4,3,2,1,0:T(8,128)(2,1)} %bitcast.108, bf16[4,2,2,2,48,128]{5,4,3,2,1,0:T(8,128)(2,1)S(1)} %bitcast.101, ...), custom_call_target="tpu_custom_call" | custom-call | tf_op jit(solution)/shard_map/pallas_call | solution.py:412
  (177 shorter events, 38.8 us)
Async XLA Ops:
  4.6 70.1 %copy-start.26 = (bf16[512,1536]{1,0:T(8,128)(2,1)S(1)}, bf16[512,1536]{1,0:T(8,128)(2,1)}, u32[]{:S(2)}) copy-start(bf16[512,1536]{1,0:T(8,128)(2,1)} %param.21) | copy-start | bytes 4718596
  7.1 1.2 copy-start.36
  71.4 82.8 %collective-permute-start.8 = (bf16[192,3456]{1,0:T(8,128)(2,1)}, bf16[192,3456]{1,0:T(8,128)(2,1)}, u32[]{:S(2)}, u32[]{:S(2)}) collective-permute-start(bf16[192,3456]{1,0:T(8,128)(2,1)} %bitcast.110), channel_id=1, source_target_pairs={{0,4},{1,5},{2,6},{3,7},{4,0},{5,1},{6,2},{7,3},{8,12},{9,13},{10,... | collective-permute-start | bytes 3981320 | tf_op jit(solution)/shard_map/ppermute | solution.py:26
  73.0 46.5 %collective-permute-start.2 = (bf16[192,3456]{1,0:T(8,128)(2,1)}, bf16[192,3456]{1,0:T(8,128)(2,1)}, u32[]{:S(2)}, u32[]{:S(2)}) collective-permute-start(bf16[192,3456]{1,0:T(8,128)(2,1)} %bitcast.111), channel_id=1, source_target_pairs={{0,8},{1,9},{2,10},{3,11},{4,12},{5,13},{6,14},{7,15},{8,16},{9,17... | collective-permute-start | bytes 3981320 | tf_op jit(solution)/shard_map/ppermute | solution.py:31
  75.1 2.5 copy-start.39
  79.6 39.9 %copy-start.14 = (f32[512,128]{1,0:T(8,128)}, f32[512,128]{1,0:T(8,128)S(1)}, u32[]{:S(2)}) copy-start(f32[512,128]{1,0:T(8,128)S(1)} %get-tuple-element.144.cos_ref) | copy-start | bytes 786436
  79.7 22.9 %collective-permute-start = (bf16[512,256]{1,0:T(8,128)(2,1)S(1)}, bf16[512,256]{1,0:T(8,128)(2,1)S(1)}, u32[]{:S(2)}, u32[]{:S(2)}) collective-permute-start(bf16[512,256]{1,0:T(8,128)(2,1)S(1)} %pad_maximum_fusion.7), channel_id=1, source_target_pairs={{0,2},{1,3},{2,4},{3,5},{4,6},{5,7},{6,8},{7,9},{8,10},{9,11},{10,... | collective-permute-start | bytes 786440 | tf_op jit(solution)/shard_map/ppermute | solution.py:37
  81.8 20.8 %collective-permute-start.1 = (bf16[512,256]{1,0:T(8,128)(2,1)S(1)}, bf16[512,256]{1,0:T(8,128)(2,1)S(1)}, u32[]{:S(2)}, u32[]{:S(2)}) collective-permute-start(bf16[512,256]{1,0:T(8,128)(2,1)S(1)} %pad_maximum_fusion.7), channel_id=1, source_target_pairs={{0,1},{1,2},{2,3},{3,4},{4,5},{5,6},{6,7},{7,8},{8,9},{9,10},{10,1... | collective-permute-start | bytes 786440 | tf_op jit(solution)/shard_map/ppermute | solution.py:37
  83.6 81.6 %collective-permute-start.6 = (bf16[512,1536]{1,0:T(8,128)(2,1)}, bf16[512,1536]{1,0:T(8,128)(2,1)}, u32[]{:S(2)}, u32[]{:S(2)}) collective-permute-start(bf16[512,1536]{1,0:T(8,128)(2,1)} %param.22), channel_id=1, source_target_pairs={{0,2},{1,3},{2,0},{3,1},{4,6},{5,7},{6,4},{7,5},{8,10},{9,11},{10,... | collective-permute-start | bytes 4718600 | tf_op jit(solution)/shard_map/ppermute | solution.py:26
  93.3 4.7 copy-start.35
  93.4 5.9 %copy-start.37 = (s32[16384]{0:T(1024)S(1)}, s32[16384]{0:T(1024)}, u32[]{:S(2)}) copy-start(s32[16384]{0:T(1024)} %param.32) | copy-start | bytes 196612
  99.6 20.0 %copy-start.4 = (s32[1536,1]{1,0:T(8,128)}, s32[1536,1]{1,0:T(8,128)S(1)}, u32[]{:S(2)}) copy-start(s32[1536,1]{1,0:T(8,128)S(1)} %broadcast_in_dim.67.ks_ref) | copy-start | bytes 18436
  103.7 15.8 %copy-start.11 = (bf16[1536,128]{1,0:T(8,128)(2,1)}, bf16[1536,128]{1,0:T(8,128)(2,1)S(1)}, u32[]{:S(2)}) copy-start(bf16[1536,128]{1,0:T(8,128)(2,1)S(1)} %get-tuple-element.135.key_ref) | copy-start | bytes 1179652
  103.9 1.9 copy-start.6
  132.4 27.6 %copy-start.21 = (bf16[512,768]{1,0:T(8,128)(2,1)}, bf16[512,768]{1,0:T(8,128)(2,1)S(1)}, u32[]{:S(2)}) copy-start(bf16[512,768]{1,0:T(8,128)(2,1)S(1)} %get-tuple-element.105) | copy-start | bytes 2359300
  132.4 51.1 %collective-permute-start.9 = (bf16[192,3456]{1,0:T(8,128)(2,1)}, bf16[192,3456]{1,0:T(8,128)(2,1)S(1)}, u32[]{:S(2)}, u32[]{:S(2)}) collective-permute-start(bf16[192,3456]{1,0:T(8,128)(2,1)} %collective-permute-done.2), channel_id=1, source_target_pairs={{0,4},{1,5},{2,6},{3,7},{4,0},{5,1},{6,2},{7,3},{8,12},{9,13},{10,... | collective-permute-start | bytes 3981320 | tf_op jit(solution)/shard_map/ppermute | solution.py:26
  132.5 47.3 %collective-permute-start.3 = (bf16[192,3456]{1,0:T(8,128)(2,1)}, bf16[192,3456]{1,0:T(8,128)(2,1)S(1)}, u32[]{:S(2)}, u32[]{:S(2)}) collective-permute-start(bf16[192,3456]{1,0:T(8,128)(2,1)} %collective-permute-done.2), channel_id=1, source_target_pairs={{0,8},{1,9},{2,10},{3,11},{4,12},{5,13},{6,14},{7,15},{8,16},{9,17... | collective-permute-start | bytes 3981320 | tf_op jit(solution)/shard_map/ppermute | solution.py:31
  154.2 5.8 %copy-start.27 = (bf16[512,1536]{1,0:T(8,128)(2,1)S(1)}, bf16[512,1536]{1,0:T(8,128)(2,1)}, u32[]{:S(2)}) copy-start(bf16[512,1536]{1,0:T(8,128)(2,1)} %param.21) | copy-start | bytes 4718596
  154.2 10.6 %copy-start.16 = (bf16[512,1536]{1,0:T(8,128)(2,1)}, bf16[512,1536]{1,0:T(8,128)(2,1)S(1)}, u32[]{:S(2)}) copy-start(bf16[512,1536]{1,0:T(8,128)(2,1)S(1)} %constant_dynamic-update-slice_fusion.5.mixed_ref) | copy-start | bytes 4718596
  157.3 10.8 %slice-start = ((s8[6291456]{0:T(1024)(128)(4,1)}), s8[4194304]{0:T(1024)(128)(4,1)S(1)}, s32[]{:S(2)}) async-start(s8[6291456]{0:T(1024)(128)(4,1)} %bitcast.106), calls=%async_computation | async-start | bytes 8388608
  160.0 8.2 %slice-start.1 = ((s8[6291456]{0:T(1024)(128)(4,1)}), s8[2097152]{0:T(1024)(128)(4,1)S(1)}, s32[]{:S(2)}) async-start(s8[6291456]{0:T(1024)(128)(4,1)} %bitcast.106), calls=%async_computation.1 | async-start | bytes 4194304
  164.8 3.2 copy-start.23
  168.1 53.5 %collective-permute-start.7 = (bf16[1024,1536]{1,0:T(8,128)(2,1)S(1)}, bf16[1024,1536]{1,0:T(8,128)(2,1)S(1)}, u32[]{:S(2)}, u32[]{:S(2)}) collective-permute-start(bf16[1024,1536]{1,0:T(8,128)(2,1)S(1)} %pad_maximum_fusion.1), channel_id=1, source_target_pairs={{0,1},{1,0},{2,3},{3,2},{4,5},{5,4},{6,7},{7,6},{8,9},{9,8},{10,11... | collective-permute-start | bytes 9437192 | tf_op jit(solution)/shard_map/ppermute | solution.py:26
  179.7 39.0 %collective-permute-start.4 = (bf16[512,1536]{1,0:T(8,128)(2,1)S(1)}, bf16[512,1536]{1,0:T(8,128)(2,1)S(1)}, u32[]{:S(2)}, u32[]{:S(2)}) collective-permute-start(bf16[512,1536]{1,0:T(8,128)(2,1)S(1)} %multiply_convert_fusion.1), channel_id=1, source_target_pairs={{0,2},{1,3},{2,0},{3,1},{4,6},{5,7},{6,4},{7,5},{8,10},{9,11},{10,... | collective-permute-start | bytes 4718600 | tf_op jit(solution)/shard_map/ppermute | solution.py:26
  183.5 35.6 %collective-permute-start.10 = (bf16[192,3456]{1,0:T(8,128)(2,1)S(1)}, bf16[192,3456]{1,0:T(8,128)(2,1)S(1)}, u32[]{:S(2)}, u32[]{:S(2)}) collective-permute-start(bf16[192,3456]{1,0:T(8,128)(2,1)S(1)} %collective-permute-done.3), channel_id=1, source_target_pairs={{0,4},{1,5},{2,6},{3,7},{4,0},{5,1},{6,2},{7,3},{8,12},{9,13},{10,... | collective-permute-start | bytes 3981320 | tf_op jit(solution)/shard_map/ppermute | solution.py:26
  183.5 33.3 %collective-permute-start.11 = (bf16[192,3456]{1,0:T(8,128)(2,1)S(1)}, bf16[192,3456]{1,0:T(8,128)(2,1)S(1)}, u32[]{:S(2)}, u32[]{:S(2)}) collective-permute-start(bf16[192,3456]{1,0:T(8,128)(2,1)S(1)} %collective-permute-done.3), channel_id=1, source_target_pairs={{0,8},{1,9},{2,10},{3,11},{4,12},{5,13},{6,14},{7,15},{8,16},{9,17... | collective-permute-start | bytes 3981320 | tf_op jit(solution)/shard_map/ppermute | solution.py:31
  216.8 30.7 %collective-permute-start.12 = (bf16[192,3456]{1,0:T(8,128)(2,1)S(1)}, bf16[192,3456]{1,0:T(8,128)(2,1)S(1)}, u32[]{:S(2)}, u32[]{:S(2)}) collective-permute-start(bf16[192,3456]{1,0:T(8,128)(2,1)S(1)} %collective-permute-done.11), channel_id=1, source_target_pairs={{0,4},{1,5},{2,6},{3,7},{4,0},{5,1},{6,2},{7,3},{8,12},{9,13},{10,... | collective-permute-start | bytes 3981320 | tf_op jit(solution)/shard_map/ppermute | solution.py:26
  218.9 29.8 %collective-permute-start.5 = (bf16[1024,1536]{1,0:T(8,128)(2,1)S(1)}, bf16[1024,1536]{1,0:T(8,128)(2,1)S(1)}, u32[]{:S(2)}, u32[]{:S(2)}) collective-permute-start(bf16[1024,1536]{1,0:T(8,128)(2,1)S(1)} %pad_maximum_fusion), channel_id=1, source_target_pairs={{0,1},{1,0},{2,3},{3,2},{4,5},{5,4},{6,7},{7,6},{8,9},{9,8},{10,11... | collective-permute-start | bytes 9437192 | tf_op jit(solution)/shard_map/ppermute | solution.py:26
  221.8 27.1 %copy-start.22 = (bf16[2048,1536]{1,0:T(8,128)(2,1)}, bf16[2048,1536]{1,0:T(8,128)(2,1)S(1)}, u32[]{:S(2)}) copy-start(bf16[2048,1536]{1,0:T(8,128)(2,1)S(1)} %constant_dynamic-update-slice_fusion.10.cot_ref) | copy-start | bytes 18874372
  248.9 2.7 copy-start
  284.8 2.8 copy-start.1
  298.3 1.5 copy-start.9
  300.9 40.5 %collective-permute-start.13 = (bf16[192,3456]{1,0:T(8,128)(2,1)}, bf16[192,3456]{1,0:T(8,128)(2,1)}, u32[]{:S(2)}, u32[]{:S(2)}) collective-permute-start(bf16[192,3456]{1,0:T(8,128)(2,1)} %dynamic-slice_bitcast_fusion.3), channel_id=1, source_target_pairs={{0,4},{1,5},{2,6},{3,7},{4,0},{5,1},{6,2},{7,3},{8,12},{9,13},{10,... | collective-permute-start | bytes 3981320 | tf_op jit(solution)/shard_map/ppermute | solution.py:26
  302.3 2.8 copy-start.2
  315.8 25.7 %copy-start.7 = (bf16[384,3456]{1,0:T(8,128)(2,1)}, bf16[384,3456]{1,0:T(8,128)(2,1)S(1)}, u32[]{:S(2)}) copy-start(bf16[384,3456]{1,0:T(8,128)(2,1)S(1)} %shard_map.227) | copy-start | bytes 7962628
  341.4 2.2 copy-start.10
  346.4 31.9 %collective-permute-start.14 = (bf16[192,3456]{1,0:T(8,128)(2,1)}, bf16[192,3456]{1,0:T(8,128)(2,1)}, u32[]{:S(2)}, u32[]{:S(2)}) collective-permute-start(bf16[192,3456]{1,0:T(8,128)(2,1)} %dynamic-slice_bitcast_fusion.2), channel_id=1, source_target_pairs={{0,4},{1,5},{2,6},{3,7},{4,0},{5,1},{6,2},{7,3},{8,12},{9,13},{10,... | collective-permute-start | bytes 3981320 | tf_op jit(solution)/shard_map/ppermute | solution.py:26
  347.0 33.6 %collective-permute-start.15 = (bf16[192,3456]{1,0:T(8,128)(2,1)}, bf16[192,3456]{1,0:T(8,128)(2,1)}, u32[]{:S(2)}, u32[]{:S(2)}) collective-permute-start(bf16[192,3456]{1,0:T(8,128)(2,1)} %fusion.28), channel_id=1, source_target_pairs={{0,8},{1,9},{2,10},{3,11},{4,12},{5,13},{6,14},{7,15},{8,16},{9,17... | collective-permute-start | bytes 3981320 | tf_op jit(solution)/shard_map/ppermute | solution.py:31
  353.1 50.2 %collective-permute-start.16 = (bf16[512,1536]{1,0:T(8,128)(2,1)}, bf16[512,1536]{1,0:T(8,128)(2,1)S(1)}, u32[]{:S(2)}, u32[]{:S(2)}) collective-permute-start(bf16[512,1536]{1,0:T(8,128)(2,1)} %slice.150), channel_id=1, source_target_pairs={{0,2},{1,3},{2,0},{3,1},{4,6},{5,7},{6,4},{7,5},{8,10},{9,11},{10,... | collective-permute-start | bytes 4718600 | tf_op jit(solution)/shard_map/ppermute | solution.py:26
  353.6 2.8 copy-start.3
  377.8 5.3 copy-start.8
  381.7 36.0 %collective-permute-start.18 = (bf16[192,3456]{1,0:T(8,128)(2,1)}, bf16[192,3456]{1,0:T(8,128)(2,1)}, u32[]{:S(2)}, u32[]{:S(2)}) collective-permute-start(bf16[192,3456]{1,0:T(8,128)(2,1)} %dynamic-slice_bitcast_fusion.1), channel_id=1, source_target_pairs={{0,4},{1,5},{2,6},{3,7},{4,0},{5,1},{6,2},{7,3},{8,12},{9,13},{10,... | collective-permute-start | bytes 3981320 | tf_op jit(solution)/shard_map/ppermute | solution.py:26
  386.4 16.8 %copy-start.24 = (f32[512,1536]{1,0:T(8,128)S(1)}, f32[512,1536]{1,0:T(8,128)}, u32[]{:S(2)}) copy-start(f32[512,1536]{1,0:T(8,128)} %copy-done.23) | copy-start | bytes 9437188
  386.4 32.7 %collective-permute-start.19 = (bf16[192,3456]{1,0:T(8,128)(2,1)}, bf16[192,3456]{1,0:T(8,128)(2,1)}, u32[]{:S(2)}, u32[]{:S(2)}) collective-permute-start(bf16[192,3456]{1,0:T(8,128)(2,1)} %fusion.30), channel_id=1, source_target_pairs={{0,8},{1,9},{2,10},{3,11},{4,12},{5,13},{6,14},{7,15},{8,16},{9,17... | collective-permute-start | bytes 3981320 | tf_op jit(solution)/shard_map/ppermute | solution.py:31
  403.2 2.6 copy-start.29
  405.2 54.5 %collective-permute-start.17 = (bf16[512,1536]{1,0:T(8,128)(2,1)}, bf16[512,1536]{1,0:T(8,128)(2,1)}, u32[]{:S(2)}, u32[]{:S(2)}) collective-permute-start(bf16[512,1536]{1,0:T(8,128)(2,1)} %slice.151), channel_id=1, source_target_pairs={{0,2},{1,3},{2,0},{3,1},{4,6},{5,7},{6,4},{7,5},{8,10},{9,11},{10,... | collective-permute-start | bytes 4718600 | tf_op jit(solution)/shard_map/ppermute | solution.py:26
  405.8 2.7 copy-start.17
  408.5 4.4 copy-start.31
  420.2 4.4 copy-start.5
  420.2 4.4 copy-start.12
  420.2 4.4 copy-start.13
  420.2 4.4 copy-start.15
  420.2 4.4 copy-start.18
  420.2 4.4 copy-start.19
  420.2 52.1 %collective-permute-start.22 = (bf16[192,3456]{1,0:T(8,128)(2,1)}, bf16[192,3456]{1,0:T(8,128)(2,1)}, u32[]{:S(2)}, u32[]{:S(2)}) collective-permute-start(bf16[192,3456]{1,0:T(8,128)(2,1)} %dynamic-slice_bitcast_fusion), channel_id=1, source_target_pairs={{0,4},{1,5},{2,6},{3,7},{4,0},{5,1},{6,2},{7,3},{8,12},{9,13},{10,... | collective-permute-start | bytes 3981320 | tf_op jit(solution)/shard_map/ppermute | solution.py:26
  424.6 47.8 %collective-permute-start.23 = (bf16[192,3456]{1,0:T(8,128)(2,1)}, bf16[192,3456]{1,0:T(8,128)(2,1)}, u32[]{:S(2)}, u32[]{:S(2)}) collective-permute-start(bf16[192,3456]{1,0:T(8,128)(2,1)} %fusion.27), channel_id=1, source_target_pairs={{0,8},{1,9},{2,10},{3,11},{4,12},{5,13},{6,14},{7,15},{8,16},{9,17... | collective-permute-start | bytes 3981320 | tf_op jit(solution)/shard_map/ppermute | solution.py:31
  448.7 3.2 copy-start.28
  449.0 14.0 %collective-permute-start.20 = (bf16[512,256]{1,0:T(8,128)(2,1)S(1)}, bf16[512,256]{1,0:T(8,128)(2,1)S(1)}, u32[]{:S(2)}, u32[]{:S(2)}) collective-permute-start(bf16[512,256]{1,0:T(8,128)(2,1)S(1)} %get-tuple-element.130), channel_id=1, source_target_pairs={{1,0},{2,1},{3,2},{4,3},{5,4},{6,5},{7,6},{8,7},{9,8},{10,9},{11,1... | collective-permute-start | bytes 786440 | tf_op jit(solution)/shard_map/ppermute | solution.py:37
  450.4 12.5 %collective-permute-start.21 = (bf16[512,256]{1,0:T(8,128)(2,1)S(1)}, bf16[512,256]{1,0:T(8,128)(2,1)S(1)}, u32[]{:S(2)}, u32[]{:S(2)}) collective-permute-start(bf16[512,256]{1,0:T(8,128)(2,1)S(1)} %get-tuple-element.131), channel_id=1, source_target_pairs={{2,0},{3,1},{4,2},{5,3},{6,4},{7,5},{8,6},{9,7},{10,8},{11,9},{12,... | collective-permute-start | bytes 786440 | tf_op jit(solution)/shard_map/ppermute | solution.py:37
  455.0 4.8 copy-start.25
  462.9 0.9 copy-start.34
  467.0 1.4 copy-start.30
  468.5 1.9 copy-start.32
  468.5 1.9 copy-start.38
  (2 other events, 1.6 us)

commit v3 on v2

--- a/solution.py
+++ b/solution.py
@@ -66,16 +66,9 @@
     return device, device % 2, (device // 2) % 2, (device // 4) % 2, device // RING
 
 
-def rows_to_group(array):
-    two = jnp.concatenate([array, flip(array, NEAR)], axis=0)
-    return jnp.concatenate([two, flip(two, CORE)], axis=0)
-
-
-def rows_from_group(partial):
-    half = partial.shape[0] // 2
-    two = partial[:half].astype(FULL) + flip(partial[half:].astype(LOW), CORE).astype(FULL)
-    quarter = half // 2
-    return two[:quarter] + flip(two[quarter:].astype(LOW), NEAR).astype(FULL)
+def rows_to_group(array, marks=()):
+    two = jnp.concatenate([array, after(flip(array, NEAR), *marks)], axis=0)
+    return two, flip(two, CORE)
 
 
 def slices_to_group(parts):
@@ -451,26 +444,24 @@
     return [[s + stride * k for k in range(size // stride)] for s in range(stride)]
 
 
-def spread(block):
+def spread(block, marks):
     size = lax.axis_size("tok")
     ring = size // RING
     if ring > LONGEST_RING:
         gathered = lax.all_gather(
             block, "tok", axis=0, tiled=True, axis_index_groups=groups_of(GROUP)
         )
-        return gathered, []
-    _, _, _, side, z = place()
-    rows, columns = block.shape
-    total = jnp.zeros((ring, 2, rows, columns), block.dtype)
-    own, arrivals = block, []
+        return [gathered], [()] * 3
+    own, crossed = [block], []
     for step in range(ring):
-        chunk = lax.rem(z - step + ring, ring)
-        for piece, y in ((own, side), (flip(own, SIDE), 1 - side)):
-            total = lax.dynamic_update_slice(total, piece[None, None], (chunk, y, 0, 0))
+        crossed.append(flip(own[-1], SIDE))
         if step < ring - 1:
-            own = around(own)
-            arrivals.append(own)
-    return total.reshape(ring * 2 * rows, columns), arrivals
+            arrived = around(own[-1])
+            if step == 0:
+                arrived, crossed[0] = lax.optimization_barrier((arrived, crossed[0], *marks))[:2]
+            own.append(arrived)
+    pieces = [piece for pair in zip(own, crossed) for piece in pair]
+    return pieces, [(*own[step + 1 : step + 2], crossed[step]) for step in range(ring)]
 
 
 class Reduction:
@@ -479,7 +470,7 @@
         self.size = lax.axis_size("tok")
         self.ring = self.size // RING
         _, _, _, self.side, self.z = place()
-        self.rows = normed.shape[1] // (self.ring * 2)
+        self.rows = normed[0].shape[1] // (self.ring * 2)
         self.short = 2 <= self.ring <= LONGEST_RING and self.rows % 64 == 0
         self.blocks, self.crossing, self.total = {}, None, None
 
@@ -516,7 +507,8 @@
     def result(self):
         if self.short:
             return self.sum
-        normed, cotangent, array = self.given
+        normed, cotangent = (jnp.concatenate(pair, axis=0) for pair in self.given[:2])
+        array = self.given[2]
         joined = jnp.concatenate(
             [outer_sum(normed, array[0]), outer_sum(normed, array[1]), outer_sum(cotangent, array[2])],
             axis=1,
@@ -680,10 +672,40 @@
 GELU_B = 0.044715
 
 
-def hidden_kernel(normed_ref, cot_ref, gate_ref, up_ref, down_ref, out_ref):
-    gate = matmul(normed_ref[...], gate_ref[...])
-    up = matmul(normed_ref[...], up_ref[...])
-    grad_hidden = matmul(cot_ref[...], down_ref[...])
+def hidden_kernel(count, *refs):
+    normed_refs, cot_refs, pieces = refs[:2], refs[2:4], refs[4 : 4 + count]
+    out_ref, weights_out, weights, sems = refs[4 + count :]
+    step, steps = pl.program_id(0), pl.num_programs(0)
+    me = lax.axis_index("tok")
+    side, z, ring = (me // SIDE) % 2, me // RING, count // 2
+    rows = weights.shape[0] // count
+
+    def load(k):
+        if count == 1:
+            start = 0
+        else:
+            start = 2 * ((z - k // 2 + ring) % ring) + (side if k % 2 == 0 else 1 - side)
+        return pltpu.make_async_copy(
+            pieces[k], weights.at[pl.ds(pl.multiple_of(start * rows, 16), rows)], sems.at[k]
+        )
+
+    keep = pltpu.make_async_copy(weights, weights_out, sems.at[count])
+
+    @pl.when(step == 0)
+    def _():
+        for k in range(count):
+            load(k).start()
+        for k in range(count):
+            load(k).wait()
+        keep.start()
+
+    early = step < steps // 2
+    normed = jnp.where(early, normed_refs[0][...], normed_refs[1][...])
+    cotangent = jnp.where(early, cot_refs[0][...], cot_refs[1][...])
+    columns = out_ref.shape[2]
+    gate = matmul(normed, weights[:, :columns])
+    up = matmul(normed, weights[:, columns : 2 * columns])
+    grad_hidden = matmul(cotangent, weights[:, 2 * columns :])
     square = gate * gate
     bent = jnp.tanh(gate * (GELU_A + GELU_A * GELU_B * square))
     half = 0.5 * (1.0 + bent)
@@ -693,30 +715,38 @@
     out_ref[1] = (grad_hidden * value).astype(LOW)
     out_ref[2] = (value * up).astype(LOW)
 
-
-def hidden_and_grads(normed, cotangent, pack):
-    tokens, width = normed.shape
-    columns = pack.shape[1] // 3
-    rows, wide = min(256, tokens), columns
-    steps = columns // wide
-    token_block = pl.BlockSpec((rows, width), lambda j, i: (i, 0))
-    weight_blocks = [
-        pl.BlockSpec(
-            (width, wide),
-            lambda j, i, part=part: (0, part * steps + j),
-            pipeline_mode=pl.Buffered(1),
-        )
-        for part in range(3)
+    @pl.when(step == steps - 1)
+    def _():
+        keep.wait()
+
+
+def hidden_and_grads(normed, cotangent, pieces):
+    half, width = normed[0].shape
+    columns = pieces[0].shape[1] // 3
+    rows = min(256, half)
+    steps = half // rows
+    count = len(pieces)
+    blocks = [
+        pl.BlockSpec((rows, width), lambda i: (jnp.minimum(i, steps - 1), 0)),
+        pl.BlockSpec((rows, width), lambda i: (jnp.maximum(i - steps, 0), 0)),
     ]
+    anywhere = pl.BlockSpec(memory_space=pl.ANY)
     return pl.pallas_call(
-        hidden_kernel,
-        grid=(steps, tokens // rows),
-        in_specs=[token_block, token_block, *weight_blocks],
-        out_specs=pl.BlockSpec((3, rows, wide), lambda j, i: (0, i, j)),
-        out_shape=jax.ShapeDtypeStruct((3, tokens, columns), LOW),
+        functools.partial(hidden_kernel, count),
+        grid=(2 * steps,),
+        in_specs=blocks * 2 + [anywhere] * count,
+        out_specs=[pl.BlockSpec((3, rows, columns), lambda i: (0, i, 0)), anywhere],
+        out_shape=[
+            jax.ShapeDtypeStruct((3, 2 * half, columns), LOW),
+            jax.ShapeDtypeStruct((width, 3 * columns), LOW),
+        ],
+        scratch_shapes=[
+            pltpu.VMEM((width, 3 * columns), LOW),
+            pltpu.SemaphoreType.DMA((count + 1,)),
+        ],
         compiler_params=pltpu.CompilerParams(vmem_limit_bytes=48 * MIB),
         cost_estimate=LIGHT,
-    )(normed, cotangent, pack, pack, pack)
+    )(*normed, *cotangent, *pieces)
 
 
 def project_sum_kernel(count, blocks, array_ref, *refs):
@@ -771,7 +801,7 @@
     array = after(array, *jax.tree.leaves(marks))
     tokens, columns = array.shape[1:]
     width = pack.shape[0]
-    rows, wide = tokens // 4, 512
+    rows, wide = tokens // 4, width
     blocks = tokens // rows // 2
     return pl.pallas_call(
         functools.partial(project_sum_kernel, count, blocks),
@@ -781,7 +811,12 @@
                 (count, rows, columns), lambda i, j: (first // count, (i + blocks) % (2 * blocks), 0)
             )
         ]
-        + [pl.BlockSpec((wide, columns), lambda i, j, k=k: (j, first + k)) for k in range(count)],
+        + [
+            pl.BlockSpec(
+                (wide, columns), lambda i, j, k=k: (j, first + k), pipeline_mode=pl.Buffered(1)
+            )
+            for k in range(count)
+        ],
         out_specs=pl.BlockSpec(
             (rows, wide),
             lambda i, j: (jnp.maximum(i - blocks, 0), jnp.where(i >= blocks, j, 0)),
@@ -800,38 +835,134 @@
     )(array, *([pack] * count))
 
 
-def outer_kernel(steps, chunk_ref, normed_ref, cot_ref, right_ref, out_ref, left):
-    for start, ref in ((0, normed_ref), (2 * steps, cot_ref)):
-
-        @pl.when(pl.program_id(0) == start)
-        def _():
-            left[...] = ref[...].T
-
-    out_ref[...] = matmul(left[...], right_ref[0]).astype(LOW)
+def outer_kernel(chunk_ref, *refs):
+    normed_refs, cot_refs, right_ref, out_ref, total = refs[:2], refs[2:4], *refs[4:]
+    step, steps = pl.program_id(0), pl.num_programs(0)
+    early = step < steps // 2
+    normed = jnp.where(early, normed_refs[0][...], normed_refs[1][...])
+    cotangent = jnp.where(early, cot_refs[0][...], cot_refs[1][...])
+    columns = right_ref.shape[2]
+
+    @pl.when(step == 0)
+    def _():
+        total[...] = jnp.zeros_like(total)
+
+    for k, left in enumerate((normed, normed, cotangent)):
+        total[:, k * columns : (k + 1) * columns] += outer_sum(left, right_ref[k])
+
+    @pl.when(step == steps - 1)
+    def _():
+        out_ref[...] = total[...].astype(LOW)
 
 
 def outer_products(normed, cotangent, array, chunk, rows):
     tokens, columns = array.shape[1:]
-    wide = columns
-    steps = columns // wide
-    left = pl.BlockSpec((tokens, rows), lambda j, chunk_ref: (0, chunk_ref[0]))
+    deep = min(512, tokens // 2)
+    steps = tokens // 2 // deep
+    lefts = [
+        pl.BlockSpec((deep, rows), lambda i, chunk_ref: (jnp.minimum(i, steps - 1), chunk_ref[0])),
+        pl.BlockSpec((deep, rows), lambda i, chunk_ref: (jnp.maximum(i - steps, 0), chunk_ref[0])),
+    ]
     return pl.pallas_call(
-        functools.partial(outer_kernel, steps),
+        outer_kernel,
         grid_spec=pltpu.PrefetchScalarGridSpec(
             num_scalar_prefetch=1,
-            grid=(3 * steps,),
-            in_specs=[
-                left,
-                left,
-                pl.BlockSpec((1, tokens, wide), lambda j, chunk_ref: (j // steps, 0, j % steps)),
-            ],
-            out_specs=pl.BlockSpec((rows, wide), lambda j, chunk_ref: (0, j)),
-            scratch_shapes=[pltpu.VMEM((rows, tokens), LOW)],
+            grid=(2 * steps,),
+            in_specs=lefts * 2
+            + [pl.BlockSpec((3, deep, columns), lambda i, chunk_ref: (0, i, 0))],
+            out_specs=pl.BlockSpec((rows, 3 * columns), lambda i, chunk_ref: (0, 0)),
+            scratch_shapes=[pltpu.VMEM((rows, 3 * columns), FULL)],
         ),
         out_shape=jax.ShapeDtypeStruct((rows, 3 * columns), LOW),
         compiler_params=pltpu.CompilerParams(vmem_limit_bytes=40 * MIB),
         cost_estimate=LIGHT,
-    )(chunk[None].astype(jnp.int32), normed, cotangent, array)
+    )(chunk[None].astype(jnp.int32), *normed, *cotangent, array)
+
+
+def join_kernel(count, epsilon, *refs):
+    inputs_ref, gain_ref, weight_ref = refs[:3]
+    parts, (middle_ref, normed_ref, inverse_ref) = refs[3 : 3 + count], refs[3 + count :]
+    total, start = inputs_ref[...].astype(FULL), 0
+    for part in parts:
+        columns = part.shape[1]
+        total += by_rows(part[...], weight_ref[:, start : start + columns])
+        start += columns
+    inverse = lax.rsqrt(jnp.mean(total * total, axis=1, keepdims=True) + epsilon)
+    middle_ref[...] = total
+    inverse_ref[...] = jnp.broadcast_to(inverse, inverse_ref.shape)
+    normed_ref[...] = (total * inverse * gain_ref[...]).astype(LOW)
+
+
+def join(tokens, gain, weight, parts):
+    count, width = tokens.shape
+    rows = min(256, count)
+    block = lambda columns: pl.BlockSpec((rows, columns), lambda i: (i, 0))
+    return pl.pallas_call(
+        functools.partial(join_kernel, len(parts), EPSILON),
+        grid=(count // rows,),
+        in_specs=[
+            block(width),
+            pl.BlockSpec((1, width), lambda i: (0, 0)),
+            pl.BlockSpec((width, width), lambda i: (0, 0), pipeline_mode=pl.Buffered(1)),
+        ]
+        + [block(part.shape[1]) for part in parts],
+        out_specs=[block(width), block(width), block(HD)],
+        out_shape=[
+            jax.ShapeDtypeStruct((count, width), FULL),
+            jax.ShapeDtypeStruct((count, width), LOW),
+            jax.ShapeDtypeStruct((count, HD), FULL),
+        ],
+        compiler_params=pltpu.CompilerParams(vmem_limit_bytes=40 * MIB),
+        cost_estimate=LIGHT,
+    )(tokens, gain[None], weight, *parts)
+
+
+def branch_kernel(
+    group_ref, near_ref, cot_ref, middle_ref, inverse_ref, gain_ref, weight_ref,
+    grad_ref, branch_ref, mixed_ref, scaled_ref,
+):
+    grad = group_ref[...].astype(FULL) + near_ref[...].astype(FULL)
+    middle, inverse = middle_ref[...], inverse_ref[:, :1]
+    normal = middle * inverse
+    scaled_ref[...] = (grad * normal).astype(LOW)
+    scaled = grad * gain_ref[...]
+    total = (
+        cot_ref[...].astype(FULL)
+        + inverse * scaled
+        - normal * (inverse * jnp.mean(scaled * normal, axis=1, keepdims=True))
+    )
+    grad_ref[...] = total
+    branch = total.astype(LOW)
+    branch_ref[...] = branch
+    mixed_ref[...] = matmul(branch, weight_ref[...]).astype(LOW)
+
+
+def branch_back(group, near, cotangent, middle, inverse, gain, weight):
+    count, width = middle.shape
+    rows = min(256, count)
+    block = lambda columns: pl.BlockSpec((rows, columns), lambda i: (i, 0))
+    return pl.pallas_call(
+        branch_kernel,
+        grid=(count // rows,),
+        in_specs=[
+            block(width),
+            block(width),
+            block(width),
+            block(width),
+            block(HD),
+            pl.BlockSpec((1, width), lambda i: (0, 0)),
+            pl.BlockSpec((width, width), lambda i: (0, 0), pipeline_mode=pl.Buffered(1)),
+        ],
+        out_specs=[block(width)] * 4,
+        out_shape=[
+            jax.ShapeDtypeStruct((count, width), FULL),
+            jax.ShapeDtypeStruct((count, width), LOW),
+            jax.ShapeDtypeStruct((count, width), LOW),
+            jax.ShapeDtypeStruct((count, width), LOW),
+        ],
+        compiler_params=pltpu.CompilerParams(vmem_limit_bytes=48 * MIB),
+        cost_estimate=LIGHT,
+    )(group, near, cotangent, middle, inverse, gain[None], weight)
 
 
 def on_device(
@@ -863,7 +994,6 @@
             w_query,
             w_key,
             w_value,
-            w_out,
             jnp.pad(
                 jnp.stack([attn_gain, ffn_gain], axis=1), ((0, 0), (0, HD - 2))
             ),
@@ -876,15 +1006,10 @@
 
     ffn_pack = jnp.concatenate([sliced(w_gate), sliced(w_up), sliced(w_down)], axis=2)
     attn_all, ffn_rows = gather(attn_pack, ffn_pack)
+    out_w = lax.all_gather(w_out, "tok", axis=0, tiled=True)
     query_w, kv_w = attn_all[:, :heads_width], attn_all[:, heads_width:edge]
-    out_w = attn_all[:, edge : edge + heads_width]
-    gains = attn_all[:, edge + heads_width : edge + heads_width + 2].astype(FULL)
+    gains = attn_all[:, edge : edge + 2].astype(FULL)
     gain_one, gain_two = gains[:, 0], gains[:, 1]
-
-    ffn_w, arrivals = spread(ffn_rows)
-    gate_up_w, down_w = ffn_w[:, : 2 * slice_width], ffn_w[:, 2 * slice_width :]
-    gate_w, up_w = gate_up_w[:, :slice_width], gate_up_w[:, slice_width:]
-    cot_group = rows_to_group(after(cotangent, attn_all))
 
     inverse_one = lax.rsqrt(jnp.mean(inputs * inputs, axis=-1, keepdims=True) + EPSILON)
     normed = (inputs * inverse_one * gain_one).astype(LOW)
@@ -902,17 +1027,17 @@
     heads = heads_width // HD
     given = (all_keys, key_segments, query_segments, cosine, sine)
     early = attend(raw_query, *given, 0, heads // 2)
+    pieces, steps = spread(ffn_rows, (early[1],))
+    cot_group = rows_to_group(after(cotangent, attn_all), steps[1])
     late = attend(
-        after(raw_query, early[1], *arrivals[:1]), *given, heads // 2, heads - heads // 2
+        after(raw_query, early[1]), *given, heads // 2, heads - heads // 2
     )
     rot, mixed = (jnp.concatenate([early[k], late[k]], axis=1) for k in range(2))
     logs = jnp.concatenate([early[2], late[2]], axis=0)
-    middle = inputs + by_rows(mixed, out_w)
-    inverse_two = lax.rsqrt(jnp.mean(middle * middle, axis=-1, keepdims=True) + EPSILON)
-    normed_two = (middle * inverse_two * gain_two).astype(LOW)
-
-    normed_group = rows_to_group(after(normed_two, *arrivals[1:2]))
-    hidden_pack = hidden_and_grads(normed_group, cot_group, ffn_w)
+    middle, normed_two, inverse_two = join(tokens, gain_two, out_w, (early[1], late[1]))
+
+    normed_group = rows_to_group(after(normed_two, *steps[1]), steps[2])
+    hidden_pack, ffn_w = hidden_and_grads(normed_group, cot_group, pieces)
     reduction = Reduction(normed_group, cot_group, hidden_pack)
     pairs_done = reduction.multiply(0)
     reduction.begin()
@@ -925,17 +1050,12 @@
     marks = reduction.advance(1, pairs_done)
     output_sum = project_sum(hidden_pack, ffn_w, 2, 1, 3, marks)
     output_near = flip(after(output_sum, near_sent)[token_count:], NEAR)
-    grad_normed_two = group_sum[:token_count].astype(FULL) + after(near_sent, output_sum).astype(FULL)
-
-    scaled = grad_normed_two * gain_two
-    grad_middle = (
-        cotangent.astype(FULL)
-        + inverse_two * scaled
-        - middle * inverse_two**3 * jnp.mean(scaled * middle, axis=-1, keepdims=True)
-    )
-    branch = grad_middle.astype(LOW)
-    grad_mixed = matmul(branch, out_w).astype(LOW)
+
+    grad_middle, branch, grad_mixed, gain_two_parts = branch_back(
+        group_sum[:token_count], after(near_sent, output_sum), cotangent, middle, inverse_two, gain_two, out_w
+    )
     grad_out_w = outer_sum(branch, mixed).astype(LOW)
+    out_sum = lax.psum_scatter(grad_out_w, "tok", scatter_dimension=0, tiled=True).astype(FULL)
     marks = reduction.advance(2, grad_mixed)
     query_low, key_grads, value_grads = attend_back(
         rot, after(grad_mixed, *marks), mixed, logs, all_keys, key_segments, query_segments, cosine, sine
@@ -961,11 +1081,11 @@
     lane = lax.broadcasted_iota(jnp.int32, (token_count, HD), 1)
     grad_gains = (
         outer_sum((grad_normed * inputs * inverse_one).astype(LOW), (lane == 0).astype(LOW))
-        + outer_sum((grad_normed_two * middle * inverse_two).astype(LOW), (lane == 1).astype(LOW))
+        + outer_sum(gain_two_parts, (lane == 1).astype(LOW))
     ).astype(LOW)
     reduction.advance(3, grad_query_w)
     attn_sum, ffn_parts = scatter(
-        [grad_query_w, grad_kv_w, grad_out_w, grad_gains], reduction.result()
+        [grad_query_w, grad_kv_w, grad_gains], reduction.result()
     )
 
     def joined(parts):
@@ -974,12 +1094,12 @@
     return (
         output,
         grad_tokens,
-        attn_sum[:, edge + heads_width],
-        attn_sum[:, edge + heads_width + 1],
+        attn_sum[:, edge],
+        attn_sum[:, edge + 1],
         attn_sum[:, :heads_width],
         attn_sum[:, heads_width : heads_width + HD],
         attn_sum[:, heads_width + HD : edge],
-        attn_sum[:, edge : edge + heads_width],
+        out_sum,
         joined(ffn_parts[:, :, :slice_width]),
         joined(ffn_parts[:, :, slice_width : 2 * slice_width]),
         joined(ffn_parts[:, :, 2 * slice_width :]),

time: 549 us -> 513 us (0.934)
  Pallas kernels: 294 us -> 272 us
  waiting for transfers between devices: 70.9 us -> 91.1 us
  starting transfers between devices: 45.1 us -> 27.7 us
  local copies, waits for them, and re-layouts: 64.9 us -> 49.1 us
  between operations: 1.76 us -> 15.1 us
  matrix products: 35.3 us -> 22.9 us
    pallas_call x1, Pallas kernels: 63.1 us -> 42.8 us  [gather(): pl.pallas_call(functools.partial(gather_kernel, ring, bands), in_specs=[a...]
    ppermute x6, starting transfers between devices: 22.7 us -> 2.4 us  [around(): lax.ppermute(array, 'tok', [(i, (i + RING) % size) for i in range(size)])]
    pallas_call x5 -> x7, Pallas kernels: 76 us -> 92 us  [the longest x4 45 us: outer_products(): pl.pallas_call(outer_kernel, grid_spec=pltpu.PrefetchScalarGridSpec(num_s...]
    dynamic_update_slice x8 -> x0, local copies, waits for them, and re-layouts: 12.7 us -> none  [spread(): total = lax.dynamic_update_slice(total, piece[None, None], (chunk, y, 0, 0))]
    pallas_call x1, Pallas kernels: 63.5 us -> 52.1 us  [scatter(): pl.pallas_call(functools.partial(scatter_kernel, ring, bands, edges), in_...]
    ppermute x6, waiting for transfers between devices: 44.6 us -> 55.5 us  [around(): lax.ppermute(array, 'tok', [(i, (i + RING) % size) for i in range(size)])]
    ppermute x14, waiting for transfers between devices: 26.4 us -> 35 us  [flip(): return lax.ppermute(array, 'tok', [(i, i ^ bit) for i in range(size)])]
    dot_general x3 -> x2, matrix products: 13.4 us -> 6.25 us  [matmul(): return jnp.dot(left_side, right_side, preferred_element_type=FULL)]
  transfers between devices with their start and end apart: 24 -> 26, of which waited for: 7 -> 6; matrix products, arithmetic and copies ran while one was open for 17% -> 15% of each run, Pallas kernels for 23% -> 45%
where the time goes in v3:
time: 513 us; the launch traced here: 506 us
  Pallas kernels  272 us (53%)
  waiting for transfers between devices  91.1 us (18%)
  local copies, waits for them, and re-layouts  49.1 us (10%)
  starting transfers between devices  27.7 us (5%)
  other arithmetic  27.6 us (5%)
  matrix products  22.9 us (4%)
  between operations  15.1 us (3%)
    ppermute x6, waiting for transfers between devices, around(): lax.ppermute(array, 'tok', [(i, (i + RING) % size) for i in range(size)])  55.5 us
    pallas_call x1, Pallas kernels, scatter(): pl.pallas_call(functools.partial(scatter_kernel, ring, bands, edges), in_...  52.1 us
    pallas_call x4, Pallas kernels, outer_products(): pl.pallas_call(outer_kernel, grid_spec=pltpu.PrefetchScalarGridSpec(num_s...  45 us
    pallas_call x1, Pallas kernels, gather(): pl.pallas_call(functools.partial(gather_kernel, ring, bands), in_specs=[a...  42.8 us
    pallas_call x1, Pallas kernels, hidden_and_grads(): pl.pallas_call(functools.partial(hidden_kernel, count), grid=(2 * steps,)...  35.1 us
    pallas_call x2, Pallas kernels, project_sum(): pl.pallas_call(functools.partial(project_sum_kernel, count, blocks), grid...  35.1 us
    ppermute x14, waiting for transfers between devices, flip(): return lax.ppermute(array, 'tok', [(i, i ^ bit) for i in range(size)])  35 us
    pallas_call x2, Pallas kernels, attend(): pl.pallas_call(functools.partial(attend_kernel, block, HD ** (-0.5) * LOG...  25.6 us
  transfers between devices with their start and end apart: 26, of which 6 were waited for; matrix products, arithmetic and copies ran while one was open for 15% of the time, Pallas kernels for 45%

profile of v3, /device:TPU:0, one launch (start us, length us, event | category | flops | bytes accessed | tf_op | source)
XLA Modules:
  0.0 505.5 jit_solution(5518322283493025412)
XLA Ops:
  9.8 1.6 fusion.37.attn_ref
  11.4 1.2 bitcast_bitcast_fusion
  12.7 1.2 pad_maximum_fusion.2.ffn_ref
  13.8 42.8 %shard_map.222 = (bf16[4,2,2,2,48,1920]{5,4,3,2,1,0:T(8,128)(2,1)}, bf16[4,48,3456]{2,1,0:T(8,128)(2,1)}) custom-call(bf16[48,1920]{1,0:T(8,128)(2,1)} %fusion.37.attn_ref, bf16[4,48,3456]{2,1,0:T(8,128)(2,1)} %pad_maximum_fusion.2.ffn_ref), custom_call_target="tpu_custom_call" | custom-call | tf_op jit(solution)/shard_map/pallas_call | solution.py:211
  58.4 2.0 fusion.27
  61.9 3.4 collective-permute-start
  65.3 2.7 collective-permute-start.1
  68.2 4.3 fusion.2.q_ref
  72.9 1.3 maximum_maximum_fusion
  75.3 2.1 copy.61.value_t_ref
  77.4 1.9 copy-done.9
  80.3 12.8 %shard_map.223 = (bf16[512,768]{1,0:T(8,128)(2,1)S(1)}, bf16[512,768]{1,0:T(8,128)(2,1)S(1)}, f32[6,1,512]{2,1,0:T(1,128)S(1)}) custom-call(f32[512,1536]{1,0:T(8,128)S(1)} %copy-done.9, bf16[1536,128]{1,0:T(8,128)(2,1)S(1)} %get-tuple-element.161.key_ref, bf16[128,1536]{1,0:T(8,128)(2,1)S(1)} %copy-done.25, s32[1536,1]{1,0:T(8,128)S(1)} %broadcast_in_dim.33.ks_ref, ...), custom_call_target="tpu_custom_call" | custom-call | flops 1024 | bytes 1024 | tf_op jit(solution)/shard_map/pallas_call | solution.py:566
  94.8 19.6 %collective-permute-done.2.refs_6_ = bf16[192,3456]{1,0:T(8,128)(2,1)} collective-permute-done((bf16[192,3456]{1,0:T(8,128)(2,1)}, bf16[192,3456]{1,0:T(8,128)(2,1)}, u32[]{:S(2)}, u32[]{:S(2)}) %collective-permute-start.2) | collective-permute-done | bytes 1327136 | tf_op jit(solution)/shard_map/ppermute | solution.py:31
  115.5 2.9 collective-permute-start.10
  118.4 12.8 %shard_map.224 = (bf16[512,768]{1,0:T(8,128)(2,1)S(1)}, bf16[512,768]{1,0:T(8,128)(2,1)S(1)}, f32[6,1,512]{2,1,0:T(1,128)S(1)}) custom-call(f32[512,1536]{1,0:T(8,128)S(1)} %copy-done.9, bf16[1536,128]{1,0:T(8,128)(2,1)S(1)} %get-tuple-element.161.key_ref, bf16[128,1536]{1,0:T(8,128)(2,1)S(1)} %copy-done.25, s32[1536,1]{1,0:T(8,128)S(1)} %broadcast_in_dim.33.ks_ref, ...), custom_call_target="tpu_custom_call" | custom-call | flops 1024 | bytes 1024 | tf_op jit(solution)/shard_map/pallas_call | solution.py:566
  133.0 2.3 copy-done.5
  137.6 3.2 shard_map.225
  140.8 6.9 %collective-permute-done.4.refs_8_ = bf16[192,3456]{1,0:T(8,128)(2,1)} collective-permute-done((bf16[192,3456]{1,0:T(8,128)(2,1)}, bf16[192,3456]{1,0:T(8,128)(2,1)}, u32[]{:S(2)}, u32[]{:S(2)}) %collective-permute-start.4) | collective-permute-done | bytes 1327136 | tf_op jit(solution)/shard_map/ppermute | solution.py:31
  148.8 1.9 collective-permute-start.8
  150.6 2.7 constant_dynamic-update-slice_fusion.3
  153.4 2.7 constant_dynamic-update-slice_fusion.2.refs_2_
  156.1 1.8 collective-permute-start.11
  157.9 23.8 %collective-permute-done.7.refs_10_ = bf16[192,3456]{1,0:T(8,128)(2,1)} collective-permute-done((bf16[192,3456]{1,0:T(8,128)(2,1)}, bf16[192,3456]{1,0:T(8,128)(2,1)}, u32[]{:S(2)}, u32[]{:S(2)}) %collective-permute-start.7) | collective-permute-done | bytes 1327136 | tf_op jit(solution)/shard_map/ppermute | solution.py:31
  181.7 4.8 collective-permute-done.6
  187.6 1.3 collective-permute-start.12
  188.8 30.2 %collective-permute-done.12.refs_11_ = bf16[192,3456]{1,0:T(8,128)(2,1)} collective-permute-done((bf16[192,3456]{1,0:T(8,128)(2,1)}, bf16[192,3456]{1,0:T(8,128)(2,1)}, u32[]{:S(2)}, u32[]{:S(2)}) %collective-permute-start.12) | collective-permute-done | bytes 1327136 | tf_op jit(solution)/shard_map/ppermute | solution.py:26
  219.0 35.1 %shard_map.226 = (bf16[3,2048,1152]{2,1,0:T(8,128)(2,1)}, bf16[1536,3456]{1,0:T(8,128)(2,1)}) custom-call(bf16[1024,1536]{1,0:T(8,128)(2,1)} %copy-done, bf16[1024,1536]{1,0:T(8,128)(2,1)} %collective-permute-done.9.refs_1_, bf16[1024,1536]{1,0:T(8,128)(2,1)} %constant_dynamic-update-slice_fusion.2.refs_2_, ...), custom_call_target="tpu_custom_call" | custom-call | flops 1024 | bytes 1024 | tf_op jit(solution)/shard_map/pallas_call | solution.py:734
  254.1 1.9 copy-done.1
  256.0 11.1 %shard_map.227 = bf16[384,3456]{1,0:T(8,128)(2,1)S(1)} custom-call(s32[1]{0:T(128)} %bitcast.11.chunk_ref, bf16[1024,1536]{1,0:T(8,128)(2,1)S(1)} %copy-done.1, bf16[1024,1536]{1,0:T(8,128)(2,1)} %collective-permute-done.9.refs_1_, bf16[1024,1536]{1,0:T(8,128)(2,1)} %constant_dynamic-update-slice_fusion.2.refs_2_, ...), custom_call_target="tpu_custom_call" | custom-call | flops 1024 | bytes 1024 | tf_op jit(solution)/shard_map/pallas_call | solution.py:866
  267.2 1.5 copy-done.18
  268.6 1.2 dynamic-slice_bitcast_fusion.3
  269.8 1.6 collective-permute-start.13
  271.3 11.0 %shard_map.228 = bf16[384,3456]{1,0:T(8,128)(2,1)S(1)} custom-call(s32[1]{0:T(128)} %bitcast.10.chunk_ref, bf16[1024,1536]{1,0:T(8,128)(2,1)S(1)} %copy-done.2, bf16[1024,1536]{1,0:T(8,128)(2,1)} %collective-permute-done.9.refs_1_, bf16[1024,1536]{1,0:T(8,128)(2,1)} %constant_dynamic-update-slice_fusion.2.refs_2_, ...), custom_call_target="tpu_custom_call" | custom-call | flops 1024 | bytes 1024 | tf_op jit(solution)/shard_map/pallas_call | solution.py:866
  282.3 22.8 %shard_map.229 = bf16[1024,1536]{1,0:T(8,128)(2,1)S(1)} custom-call(bf16[3,2048,1152]{2,1,0:T(8,128)(2,1)} %get-tuple-element.123.refs_4_.array_ref, bf16[1536,3456]{1,0:T(8,128)(2,1)} %get-tuple-element.115.refs_0_.refs_1_, bf16[1536,3456]{1,0:T(8,128)(2,1)} %get-tuple-element.115.refs_0_.refs_1_), custom_call_target="tpu_custom_call" | custom-call | flops 1024 | bytes 1024 | tf_op jit(solution)/shard_map/pallas_call | solution.py:806
  305.2 1.1 dynamic-slice_bitcast_fusion.2
  306.8 1.7 copy-done.19
  308.5 2.7 fusion.18
  311.2 1.3 collective-permute-start.15
  312.5 3.7 fusion.47
  316.9 11.0 %shard_map.230 = bf16[384,3456]{1,0:T(8,128)(2,1)S(1)} custom-call(s32[1]{0:T(128)} %bitcast.15.chunk_ref, bf16[1024,1536]{1,0:T(8,128)(2,1)S(1)} %copy-done.2, bf16[1024,1536]{1,0:T(8,128)(2,1)} %collective-permute-done.9.refs_1_, bf16[1024,1536]{1,0:T(8,128)(2,1)} %constant_dynamic-update-slice_fusion.2.refs_2_, ...), custom_call_target="tpu_custom_call" | custom-call | flops 1024 | bytes 1024 | tf_op jit(solution)/shard_map/pallas_call | solution.py:866
  327.9 11.9 %shard_map.231 = bf16[384,3456]{1,0:T(8,128)(2,1)S(1)} custom-call(s32[1]{0:T(128)} %bitcast.20.chunk_ref, bf16[1024,1536]{1,0:T(8,128)(2,1)S(1)} %copy-done.2, bf16[1024,1536]{1,0:T(8,128)(2,1)} %collective-permute-done.9.refs_1_, bf16[1024,1536]{1,0:T(8,128)(2,1)} %constant_dynamic-update-slice_fusion.2.refs_2_, ...), custom_call_target="tpu_custom_call" | custom-call | flops 1024 | bytes 1024 | tf_op jit(solution)/shard_map/pallas_call | solution.py:866
  339.8 5.2 %collective-permute-done.15 = bf16[192,3456]{1,0:T(8,128)(2,1)} collective-permute-done((bf16[192,3456]{1,0:T(8,128)(2,1)}, bf16[192,3456]{1,0:T(8,128)(2,1)}, u32[]{:S(2)}, u32[]{:S(2)}) %collective-permute-start.15) | collective-permute-done | bytes 1327136 | tf_op jit(solution)/shard_map/ppermute | solution.py:31
  345.0 1.2 dynamic-slice_bitcast_fusion.1
  346.7 3.3 fusion.20
  350.1 2.0 copy.65.key_t_ref
  352.3 1.4 pad_maximum_fusion.1.rot_ref
  353.7 12.3 %shard_map.232 = bf16[1024,1536]{1,0:T(8,128)(2,1)S(1)} custom-call(bf16[3,2048,1152]{2,1,0:T(8,128)(2,1)} %get-tuple-element.123.refs_4_.array_ref, bf16[1536,3456]{1,0:T(8,128)(2,1)} %get-tuple-element.115.refs_0_.refs_1_), custom_call_target="tpu_custom_call" | custom-call | flops 1024 | bytes 1024 | tf_op jit(solution)/shard_map/pallas_call | solution.py:806
  366.1 8.7 %shard_map.233 = (f32[512,1536]{1,0:T(8,128)}, bf16[512,1536]{1,0:T(8,128)(2,1)S(1)}, bf16[512,1536]{1,0:T(8,128)(2,1)S(1)}, bf16[512,1536]{1,0:T(8,128)(2,1)S(1)}) custom-call(bf16[512,1536]{1,0:T(8,128)(2,1)} %get-tuple-element.151.group_ref, bf16[512,1536]{1,0:T(8,128)(2,1)} %collective-permute-done.16.near_ref, bf16[512,1536]{1,0:T(8,128)(2,1)} %cot_ref.1, ...), custom_call_target="tpu_custom_call" | custom-call | flops 1024 | bytes 1024 | tf_op jit(solution)/shard_map/pallas_call | solution.py:944
  375.9 1.1 copy-done.38
  377.0 4.3 convolution_convert_fusion
  381.5 2.1 collective-permute-start.17
  384.9 3.7 fusion.17
  388.7 1.4 copy-done.39
  390.1 24.3 %shard_map.234 = (bf16[512,1536]{1,0:T(8,128)(2,1)S(1)}, f32[1536,128]{1,0:T(8,128)S(1)}, f32[1536,128]{1,0:T(8,128)S(1)}) custom-call(bf16[512,1536]{1,0:T(8,128)(2,1)S(1)} %copy-done.22, bf16[512,1536]{1,0:T(8,128)(2,1)S(1)} %copy-done.39, bf16[512,1536]{1,0:T(8,128)(2,1)S(1)} %copy-done.27, f32[12,1,512]{2,1,0:T(1,128)S(1)} %pad_maximum_fusion.9.log_ref, ...), custom_call_target="tpu_custom_call" | custom-call | flops 1024 | bytes 1024 | tf_op jit(solution)/shard_map/pallas_call | solution.py:631
  414.6 1.3 collective-permute-start.20
  415.9 1.5 collective-permute-start.21
  417.5 4.7 fusion
  422.2 3.1 convolution_convert_fusion.1
  425.4 3.4 add_convert_fusion
  429.9 2.1 fusion.11
  435.2 2.0 fusion.10
  437.2 2.3 fusion.15
  439.5 52.1 %shard_map.235 = (f32[48,1920]{1,0:T(8,128)S(1)}, bf16[4,48,3456]{2,1,0:T(8,128)(2,1)S(1)}) custom-call(bf16[4,2,2,2,48,1536]{5,4,3,2,1,0:T(8,128)(2,1)S(1)} %bitcast.86, bf16[4,2,2,2,48,256]{5,4,3,2,1,0:T(8,128)(2,1)S(1)} %bitcast.88, bf16[4,2,2,2,48,128]{5,4,3,2,1,0:T(8,128)(2,1)S(1)} %bitcast.87, bf16[4,48,3456]{2,1,0:T(8,128)(2,1)S(1)} %bitcast.85), custom_call_target="tpu_custom_call" | custom-call | tf_op jit(solution)/shard_map/pallas_call | solution.py:405
  496.8 1.6 convert_element_type.174
  (186 shorter events, 31.6 us)
Async XLA Ops:
  7.2 125.8 %all-gather.2.cloned.1.call-start = ((), (), s32[]{:S(2)}) async-start(), calls=%async_computation.1 | async-start | bytes 4866048 | tf_op jit(solution)/shard_map/all_gather | solution.py:1009
  7.9 488.9 %reduce-scatter.2.cloned.1.call-start = ((), (), s32[]{:S(2)}) async-start(), calls=%async_computation.2 | async-start | bytes 4866048 | tf_op jit(solution)/shard_map/reduce_scatter | solution.py:1058
  12.7 45.2 %copy-start.51 = (s32[512]{0:T(512)S(1)}, s32[512]{0:T(512)}, u32[]{:S(2)}) copy-start(s32[512]{0:T(512)} %param.33) | copy-start | bytes 6148
  12.7 45.2 %copy-start.3 = (bf16[512,1536]{1,0:T(8,128)(2,1)S(1)}, bf16[512,1536]{1,0:T(8,128)(2,1)}, u32[]{:S(2)}) copy-start(bf16[512,1536]{1,0:T(8,128)(2,1)} %refs_0_.1) | copy-start | bytes 4718596
  57.9 10.3 %slice-start = ((s8[5898240]{0:T(1024)(128)(4,1)}), s8[4194304]{0:T(1024)(128)(4,1)S(1)}, s32[]{:S(2)}) async-start(s8[5898240]{0:T(1024)(128)(4,1)} %bitcast.103), calls=%async_computation.3 | async-start | bytes 8388608
  58.3 9.8 %slice-start.1 = ((s8[5898240]{0:T(1024)(128)(4,1)}), s8[1703936]{0:T(1024)(128)(4,1)S(1)}, s32[]{:S(2)}) async-start(s8[5898240]{0:T(1024)(128)(4,1)} %bitcast.103), calls=%async_computation.4 | async-start | bytes 3407872
  61.5 10.9 %copy-start.47 = (f32[512,64]{1,0:T(8,128)}, f32[512,64]{1,0:T(8,128)S(1)}, u32[]{:S(2)}) copy-start(f32[512,64]{1,0:T(8,128)S(1)} %get-tuple-element.173) | copy-start | bytes 393220
  61.8 56.6 %copy-start.23 = (f32[512,128]{1,0:T(8,128)}, f32[512,128]{1,0:T(8,128)S(1)}, u32[]{:S(2)}) copy-start(f32[512,128]{1,0:T(8,128)S(1)} %get-tuple-element.168.cos_ref) | copy-start | bytes 786436
  61.9 11.0 %collective-permute-start = (bf16[512,256]{1,0:T(8,128)(2,1)S(1)}, bf16[512,256]{1,0:T(8,128)(2,1)}, u32[]{:S(2)}, u32[]{:S(2)}) collective-permute-start(bf16[512,256]{1,0:T(8,128)(2,1)S(1)} %pad_maximum_fusion.5), channel_id=1, source_target_pairs={{0,2},{1,3},{2,4},{3,5},{4,6},{5,7},{6,8},{7,9},{8,10},{9,11},{10,... | collective-permute-start | bytes 786440 | tf_op jit(solution)/shard_map/ppermute | solution.py:37
  65.3 7.6 %collective-permute-start.1 = (bf16[512,256]{1,0:T(8,128)(2,1)S(1)}, bf16[512,256]{1,0:T(8,128)(2,1)}, u32[]{:S(2)}, u32[]{:S(2)}) collective-permute-start(bf16[512,256]{1,0:T(8,128)(2,1)S(1)} %pad_maximum_fusion.5), channel_id=1, source_target_pairs={{0,1},{1,2},{2,3},{3,4},{4,5},{5,6},{6,7},{7,8},{8,9},{9,10},{10,1... | collective-permute-start | bytes 786440 | tf_op jit(solution)/shard_map/ppermute | solution.py:37
  68.0 4.4 copy-start.50
  68.0 46.4 %collective-permute-start.2 = (bf16[192,3456]{1,0:T(8,128)(2,1)}, bf16[192,3456]{1,0:T(8,128)(2,1)}, u32[]{:S(2)}, u32[]{:S(2)}) collective-permute-start(bf16[192,3456]{1,0:T(8,128)(2,1)} %bitcast.9.refs_4_), channel_id=1, source_target_pairs={{0,8},{1,9},{2,10},{3,11},{4,12},{5,13},{6,14},{7,15},{8,16},{9,17... | collective-permute-start | bytes 3981320 | tf_op jit(solution)/shard_map/ppermute | solution.py:31
  68.0 46.4 %collective-permute-start.3 = (bf16[192,3456]{1,0:T(8,128)(2,1)}, bf16[192,3456]{1,0:T(8,128)(2,1)}, u32[]{:S(2)}, u32[]{:S(2)}) collective-permute-start(bf16[192,3456]{1,0:T(8,128)(2,1)} %bitcast.9.refs_4_), channel_id=1, source_target_pairs={{0,4},{1,5},{2,6},{3,7},{4,0},{5,1},{6,2},{7,3},{8,12},{9,13},{10,... | collective-permute-start | bytes 3981320 | tf_op jit(solution)/shard_map/ppermute | solution.py:26
  72.8 45.6 %copy-start.6 = (s32[1536,1]{1,0:T(8,128)}, s32[1536,1]{1,0:T(8,128)S(1)}, u32[]{:S(2)}) copy-start(s32[1536,1]{1,0:T(8,128)S(1)} %broadcast_in_dim.33.ks_ref) | copy-start | bytes 18436
  75.3 43.1 %copy-start.20 = (bf16[1536,128]{1,0:T(8,128)(2,1)}, bf16[1536,128]{1,0:T(8,128)(2,1)S(1)}, u32[]{:S(2)}) copy-start(bf16[1536,128]{1,0:T(8,128)(2,1)S(1)} %get-tuple-element.161.key_ref) | copy-start | bytes 1179652
  114.4 33.3 %collective-permute-start.4 = (bf16[192,3456]{1,0:T(8,128)(2,1)}, bf16[192,3456]{1,0:T(8,128)(2,1)}, u32[]{:S(2)}, u32[]{:S(2)}) collective-permute-start(bf16[192,3456]{1,0:T(8,128)(2,1)} %collective-permute-done.2.refs_6_), channel_id=1, source_target_pairs={{0,8},{1,9},{2,10},{3,11},{4,12},{5,13},{6,14},{7,15},{8,16},{9,17... | collective-permute-start | bytes 3981320 | tf_op jit(solution)/shard_map/ppermute | solution.py:31
  115.5 32.3 %collective-permute-start.5 = (bf16[192,3456]{1,0:T(8,128)(2,1)}, bf16[192,3456]{1,0:T(8,128)(2,1)}, u32[]{:S(2)}, u32[]{:S(2)}) collective-permute-start(bf16[192,3456]{1,0:T(8,128)(2,1)} %collective-permute-done.2.refs_6_), channel_id=1, source_target_pairs={{0,4},{1,5},{2,6},{3,7},{4,0},{5,1},{6,2},{7,3},{8,12},{9,13},{10,... | collective-permute-start | bytes 3981320 | tf_op jit(solution)/shard_map/ppermute | solution.py:26
  115.5 37.9 %collective-permute-start.10 = (bf16[512,1536]{1,0:T(8,128)(2,1)}, bf16[512,1536]{1,0:T(8,128)(2,1)}, u32[]{:S(2)}, u32[]{:S(2)}) collective-permute-start(bf16[512,1536]{1,0:T(8,128)(2,1)} %cot_ref.1), channel_id=1, source_target_pairs={{0,2},{1,3},{2,0},{3,1},{4,6},{5,7},{6,4},{7,5},{8,10},{9,11},{10,... | collective-permute-start | bytes 4718600 | tf_op jit(solution)/shard_map/ppermute | solution.py:26
  133.0 2.3 copy-start.5
  140.8 15.3 %copy-start.10 = (f32[512,1536]{1,0:T(8,128)}, f32[512,1536]{1,0:T(8,128)S(1)}, u32[]{:S(2)}) copy-start(f32[512,1536]{1,0:T(8,128)S(1)} %get-tuple-element.103.middle_ref) | copy-start | bytes 9437188
  140.8 15.3 %copy-start.44 = (f32[512,128]{1,0:T(8,128)}, f32[512,128]{1,0:T(8,128)S(1)}, u32[]{:S(2)}) copy-start(f32[512,128]{1,0:T(8,128)S(1)} %get-tuple-element.128.inverse_ref) | copy-start | bytes 786436
  147.7 38.7 %collective-permute-start.6 = (bf16[512,1536]{1,0:T(8,128)(2,1)S(1)}, bf16[512,1536]{1,0:T(8,128)(2,1)S(1)}, u32[]{:S(2)}, u32[]{:S(2)}) collective-permute-start(bf16[512,1536]{1,0:T(8,128)(2,1)S(1)} %get-tuple-element.107), channel_id=1, source_target_pairs={{0,2},{1,3},{2,0},{3,1},{4,6},{5,7},{6,4},{7,5},{8,10},{9,11},{10,... | collective-permute-start | bytes 4718600 | tf_op jit(solution)/shard_map/ppermute | solution.py:26
  148.8 32.9 %collective-permute-start.7 = (bf16[192,3456]{1,0:T(8,128)(2,1)}, bf16[192,3456]{1,0:T(8,128)(2,1)}, u32[]{:S(2)}, u32[]{:S(2)}) collective-permute-start(bf16[192,3456]{1,0:T(8,128)(2,1)} %collective-permute-done.4.refs_8_), channel_id=1, source_target_pairs={{0,8},{1,9},{2,10},{3,11},{4,12},{5,13},{6,14},{7,15},{8,16},{9,17... | collective-permute-start | bytes 3981320 | tf_op jit(solution)/shard_map/ppermute | solution.py:31
  148.8 32.9 %collective-permute-start.8 = (bf16[192,3456]{1,0:T(8,128)(2,1)}, bf16[192,3456]{1,0:T(8,128)(2,1)S(1)}, u32[]{:S(2)}, u32[]{:S(2)}) collective-permute-start(bf16[192,3456]{1,0:T(8,128)(2,1)} %collective-permute-done.4.refs_8_), channel_id=1, source_target_pairs={{0,4},{1,5},{2,6},{3,7},{4,0},{5,1},{6,2},{7,3},{8,12},{9,13},{10,... | collective-permute-start | bytes 3981320 | tf_op jit(solution)/shard_map/ppermute | solution.py:26
  156.1 62.9 %collective-permute-start.11 = (bf16[1024,1536]{1,0:T(8,128)(2,1)}, bf16[1024,1536]{1,0:T(8,128)(2,1)}, u32[]{:S(2)}, u32[]{:S(2)}) collective-permute-start(bf16[1024,1536]{1,0:T(8,128)(2,1)} %constant_dynamic-update-slice_fusion.2.refs_2_), channel_id=1, source_target_pairs={{0,1},{1,0},{2,3},{3,2},{4,5},{5,4},{6,7},{7,6},{8,9},{9,8},{10,11... | collective-permute-start | bytes 9437192 | tf_op jit(solution)/shard_map/ppermute | solution.py:26
  181.7 4.9 copy-start.49
  186.6 32.4 %copy-start = (bf16[1024,1536]{1,0:T(8,128)(2,1)}, bf16[1024,1536]{1,0:T(8,128)(2,1)S(1)}, u32[]{:S(2)}) copy-start(bf16[1024,1536]{1,0:T(8,128)(2,1)S(1)} %constant_dynamic-update-slice_fusion.refs_0_) | copy-start | bytes 9437188
  186.6 32.4 %collective-permute-start.9 = (bf16[1024,1536]{1,0:T(8,128)(2,1)S(1)}, bf16[1024,1536]{1,0:T(8,128)(2,1)}, u32[]{:S(2)}, u32[]{:S(2)}) collective-permute-start(bf16[1024,1536]{1,0:T(8,128)(2,1)S(1)} %constant_dynamic-update-slice_fusion.refs_0_), channel_id=1, source_target_pairs={{0,1},{1,0},{2,3},{3,2},{4,5},{5,4},{6,7},{7,6},{8,9},{9,8},{10,11... | collective-permute-start | bytes 9437192 | tf_op jit(solution)/shard_map/ppermute | solution.py:26
  187.6 31.4 %collective-permute-start.12 = (bf16[192,3456]{1,0:T(8,128)(2,1)}, bf16[192,3456]{1,0:T(8,128)(2,1)}, u32[]{:S(2)}, u32[]{:S(2)}) collective-permute-start(bf16[192,3456]{1,0:T(8,128)(2,1)} %collective-permute-done.7.refs_10_), channel_id=1, source_target_pairs={{0,4},{1,5},{2,6},{3,7},{4,0},{5,1},{6,2},{7,3},{8,12},{9,13},{10,... | collective-permute-start | bytes 3981320 | tf_op jit(solution)/shard_map/ppermute | solution.py:26
  256.0 15.3 %copy-start.2 = (bf16[1024,1536]{1,0:T(8,128)(2,1)S(1)}, bf16[1024,1536]{1,0:T(8,128)(2,1)}, u32[]{:S(2)}) copy-start(bf16[1024,1536]{1,0:T(8,128)(2,1)} %copy-done) | copy-start | bytes 9437188
  269.8 35.4 %collective-permute-start.13 = (bf16[192,3456]{1,0:T(8,128)(2,1)}, bf16[192,3456]{1,0:T(8,128)(2,1)}, u32[]{:S(2)}, u32[]{:S(2)}) collective-permute-start(bf16[192,3456]{1,0:T(8,128)(2,1)} %dynamic-slice_bitcast_fusion.3), channel_id=1, source_target_pairs={{0,4},{1,5},{2,6},{3,7},{4,0},{5,1},{6,2},{7,3},{8,12},{9,13},{10,... | collective-permute-start | bytes 3981320 | tf_op jit(solution)/shard_map/ppermute | solution.py:26
  282.3 22.8 %copy-start.16 = (bf16[384,3456]{1,0:T(8,128)(2,1)}, bf16[384,3456]{1,0:T(8,128)(2,1)S(1)}, u32[]{:S(2)}) copy-start(bf16[384,3456]{1,0:T(8,128)(2,1)S(1)} %shard_map.228) | copy-start | bytes 7962628
  305.1 6.1 %copy-start.8 = (bf16[1024,1536]{1,0:T(8,128)(2,1)}, bf16[1024,1536]{1,0:T(8,128)(2,1)S(1)}, u32[]{:S(2)}) copy-start(bf16[1024,1536]{1,0:T(8,128)(2,1)S(1)} %shard_map.229) | copy-start | bytes 9437188
  305.1 3.4 copy-start.19
  306.3 33.5 %collective-permute-start.14 = (bf16[192,3456]{1,0:T(8,128)(2,1)}, bf16[192,3456]{1,0:T(8,128)(2,1)}, u32[]{:S(2)}, u32[]{:S(2)}) collective-permute-start(bf16[192,3456]{1,0:T(8,128)(2,1)} %dynamic-slice_bitcast_fusion.2), channel_id=1, source_target_pairs={{0,4},{1,5},{2,6},{3,7},{4,0},{5,1},{6,2},{7,3},{8,12},{9,13},{10,... | collective-permute-start | bytes 3981320 | tf_op jit(solution)/shard_map/ppermute | solution.py:26
  311.2 33.8 %collective-permute-start.15 = (bf16[192,3456]{1,0:T(8,128)(2,1)}, bf16[192,3456]{1,0:T(8,128)(2,1)}, u32[]{:S(2)}, u32[]{:S(2)}) collective-permute-start(bf16[192,3456]{1,0:T(8,128)(2,1)} %fusion.18), channel_id=1, source_target_pairs={{0,8},{1,9},{2,10},{3,11},{4,12},{5,13},{6,14},{7,15},{8,16},{9,17... | collective-permute-start | bytes 3981320 | tf_op jit(solution)/shard_map/ppermute | solution.py:31
  316.3 49.8 %collective-permute-start.16 = (bf16[512,1536]{1,0:T(8,128)(2,1)}, bf16[512,1536]{1,0:T(8,128)(2,1)}, u32[]{:S(2)}, u32[]{:S(2)}) collective-permute-start(bf16[512,1536]{1,0:T(8,128)(2,1)} %get-tuple-element.152), channel_id=1, source_target_pairs={{0,2},{1,3},{2,0},{3,1},{4,6},{5,7},{6,4},{7,5},{8,10},{9,11},{10,... | collective-permute-start | bytes 4718600 | tf_op jit(solution)/shard_map/ppermute | solution.py:26
  327.9 17.1 %copy-start.14 = (bf16[384,3456]{1,0:T(8,128)(2,1)}, bf16[384,3456]{1,0:T(8,128)(2,1)S(1)}, u32[]{:S(2)}) copy-start(bf16[384,3456]{1,0:T(8,128)(2,1)S(1)} %shard_map.230) | copy-start | bytes 7962628
  339.8 10.2 %copy-start.12 = (bf16[384,3456]{1,0:T(8,128)(2,1)}, bf16[384,3456]{1,0:T(8,128)(2,1)S(1)}, u32[]{:S(2)}) copy-start(bf16[384,3456]{1,0:T(8,128)(2,1)S(1)} %shard_map.231) | copy-start | bytes 7962628
  339.8 6.9 %copy-start.17 = (bf16[384,3456]{1,0:T(8,128)(2,1)S(1)}, bf16[384,3456]{1,0:T(8,128)(2,1)}, u32[]{:S(2)}) copy-start(bf16[384,3456]{1,0:T(8,128)(2,1)} %copy-done.16) | copy-start | bytes 7962628
  346.2 6.0 %copy-start.30 = (bf16[512,768]{1,0:T(8,128)(2,1)S(1)}, bf16[512,768]{1,0:T(8,128)(2,1)}, u32[]{:S(2)}) copy-start(bf16[512,768]{1,0:T(8,128)(2,1)} %copy-done.28) | copy-start | bytes 2359300
  346.2 6.0 %copy-start.33 = (bf16[512,768]{1,0:T(8,128)(2,1)S(1)}, bf16[512,768]{1,0:T(8,128)(2,1)}, u32[]{:S(2)}) copy-start(bf16[512,768]{1,0:T(8,128)(2,1)} %copy-done.31) | copy-start | bytes 2359300
  346.2 37.4 %collective-permute-start.18 = (bf16[192,3456]{1,0:T(8,128)(2,1)}, bf16[192,3456]{1,0:T(8,128)(2,1)}, u32[]{:S(2)}, u32[]{:S(2)}) collective-permute-start(bf16[192,3456]{1,0:T(8,128)(2,1)} %dynamic-slice_bitcast_fusion.1), channel_id=1, source_target_pairs={{0,4},{1,5},{2,6},{3,7},{4,0},{5,1},{6,2},{7,3},{8,12},{9,13},{10,... | collective-permute-start | bytes 3981320 | tf_op jit(solution)/shard_map/ppermute | solution.py:26
  350.0 2.3 copy-start.41
  350.0 2.3 copy-start.43
  350.0 33.6 %collective-permute-start.19 = (bf16[192,3456]{1,0:T(8,128)(2,1)}, bf16[192,3456]{1,0:T(8,128)(2,1)}, u32[]{:S(2)}, u32[]{:S(2)}) collective-permute-start(bf16[192,3456]{1,0:T(8,128)(2,1)} %fusion.20), channel_id=1, source_target_pairs={{0,8},{1,9},{2,10},{3,11},{4,12},{5,13},{6,14},{7,15},{8,16},{9,17... | collective-permute-start | bytes 3981320 | tf_op jit(solution)/shard_map/ppermute | solution.py:31
  352.3 24.7 %copy-start.26 = (bf16[512,1536]{1,0:T(8,128)(2,1)}, bf16[512,1536]{1,0:T(8,128)(2,1)S(1)}, u32[]{:S(2)}) copy-start(bf16[512,1536]{1,0:T(8,128)(2,1)S(1)} %constant_dynamic-update-slice_fusion.4.mixed_ref) | copy-start | bytes 4718596
  353.7 12.4 %copy-start.45 = (f32[512,128]{1,0:T(8,128)S(1)}, f32[512,128]{1,0:T(8,128)}, u32[]{:S(2)}) copy-start(f32[512,128]{1,0:T(8,128)} %copy-done.44) | copy-start | bytes 786436
  381.4 3.5 copy-start.15
  381.5 43.8 %collective-permute-start.17 = (bf16[512,1536]{1,0:T(8,128)(2,1)S(1)}, bf16[512,1536]{1,0:T(8,128)(2,1)}, u32[]{:S(2)}, u32[]{:S(2)}) collective-permute-start(bf16[512,1536]{1,0:T(8,128)(2,1)S(1)} %slice.144), channel_id=1, source_target_pairs={{0,2},{1,3},{2,0},{3,1},{4,6},{5,7},{6,4},{7,5},{8,10},{9,11},{10,... | collective-permute-start | bytes 4718600 | tf_op jit(solution)/shard_map/ppermute | solution.py:26
  383.6 5.0 copy-start.37
  383.7 4.9 copy-start.7
  383.7 4.9 copy-start.21
  383.7 4.9 copy-start.22
  383.8 4.9 copy-start.24
  383.8 4.9 copy-start.27
  383.8 4.9 copy-start.34
  383.8 53.4 %collective-permute-start.22 = (bf16[192,3456]{1,0:T(8,128)(2,1)S(1)}, bf16[192,3456]{1,0:T(8,128)(2,1)}, u32[]{:S(2)}, u32[]{:S(2)}) collective-permute-start(bf16[192,3456]{1,0:T(8,128)(2,1)S(1)} %dynamic-slice_bitcast_fusion), channel_id=1, source_target_pairs={{0,4},{1,5},{2,6},{3,7},{4,0},{5,1},{6,2},{7,3},{8,12},{9,13},{10,... | collective-permute-start | bytes 3981320 | tf_op jit(solution)/shard_map/ppermute | solution.py:26
  388.6 48.7 %collective-permute-start.23 = (bf16[192,3456]{1,0:T(8,128)(2,1)}, bf16[192,3456]{1,0:T(8,128)(2,1)}, u32[]{:S(2)}, u32[]{:S(2)}) collective-permute-start(bf16[192,3456]{1,0:T(8,128)(2,1)} %fusion.17), channel_id=1, source_target_pairs={{0,8},{1,9},{2,10},{3,11},{4,12},{5,13},{6,14},{7,15},{8,16},{9,17... | collective-permute-start | bytes 3981320 | tf_op jit(solution)/shard_map/ppermute | solution.py:31
  414.6 14.1 %collective-permute-start.20 = (bf16[512,256]{1,0:T(8,128)(2,1)S(1)}, bf16[512,256]{1,0:T(8,128)(2,1)S(1)}, u32[]{:S(2)}, u32[]{:S(2)}) collective-permute-start(bf16[512,256]{1,0:T(8,128)(2,1)S(1)} %get-tuple-element.156), channel_id=1, source_target_pairs={{1,0},{2,1},{3,2},{4,3},{5,4},{6,5},{7,6},{8,7},{9,8},{10,9},{11,1... | collective-permute-start | bytes 786440 | tf_op jit(solution)/shard_map/ppermute | solution.py:37
  415.9 12.8 %collective-permute-start.21 = (bf16[512,256]{1,0:T(8,128)(2,1)S(1)}, bf16[512,256]{1,0:T(8,128)(2,1)S(1)}, u32[]{:S(2)}, u32[]{:S(2)}) collective-permute-start(bf16[512,256]{1,0:T(8,128)(2,1)S(1)} %get-tuple-element.157), channel_id=1, source_target_pairs={{2,0},{3,1},{4,2},{5,3},{6,4},{7,5},{8,6},{9,7},{10,8},{11,9},{12,... | collective-permute-start | bytes 786440 | tf_op jit(solution)/shard_map/ppermute | solution.py:37
  417.4 4.7 copy-start.4
  422.2 3.2 copy-start.11
  432.9 2.4 copy-start.46
  (16 other events, 20.4 us)
Sparse Core Ops, SparseCore 0:
  10.9 98.2 all-gather.1
  381.5 112.6 reduce-scatter.1

commit v4 on v3

--- a/solution.py
+++ b/solution.py
@@ -706,14 +706,7 @@
     gate = matmul(normed, weights[:, :columns])
     up = matmul(normed, weights[:, columns : 2 * columns])
     grad_hidden = matmul(cotangent, weights[:, 2 * columns :])
-    square = gate * gate
-    bent = jnp.tanh(gate * (GELU_A + GELU_A * GELU_B * square))
-    half = 0.5 * (1.0 + bent)
-    value = gate * half
-    slope = half + 0.5 * gate * (1.0 - bent * bent) * (GELU_A + 3.0 * GELU_A * GELU_B * square)
-    out_ref[0] = (grad_hidden * up * slope).astype(LOW)
-    out_ref[1] = (grad_hidden * value).astype(LOW)
-    out_ref[2] = (value * up).astype(LOW)
+    activation_grads(out_ref, gate, up, grad_hidden)
 
     @pl.when(step == steps - 1)
     def _():
@@ -726,6 +719,8 @@
     rows = min(256, half)
     steps = half // rows
     count = len(pieces)
+    if count >= 4 and pieces[0].shape[0] % 64 == 0:
+        return hidden_by_depth(normed, cotangent, pieces)
     blocks = [
         pl.BlockSpec((rows, width), lambda i: (jnp.minimum(i, steps - 1), 0)),
         pl.BlockSpec((rows, width), lambda i: (jnp.maximum(i - steps, 0), 0)),
@@ -747,6 +742,117 @@
         compiler_params=pltpu.CompilerParams(vmem_limit_bytes=48 * MIB),
         cost_estimate=LIGHT,
     )(*normed, *cotangent, *pieces)
+
+
+def activation_grads(out_ref, gate, up, grad_hidden):
+    square = gate * gate
+    bent = jnp.tanh(gate * (GELU_A + GELU_A * GELU_B * square))
+    half = 0.5 * (1.0 + bent)
+    value = gate * half
+    slope = half + 0.5 * gate * (1.0 - bent * bent) * (GELU_A + 3.0 * GELU_A * GELU_B * square)
+    out_ref[0] = (grad_hidden * up * slope).astype(LOW)
+    out_ref[1] = (grad_hidden * value).astype(LOW)
+    out_ref[2] = (value * up).astype(LOW)
+
+
+def depth_kernel(ring, first, count, last, *refs):
+    normed_refs, cot_refs, pieces, refs = refs[:2], refs[2:4], refs[4 : 4 + count], refs[4 + count :]
+    if last:
+        partial_ref, _, out_ref, weights_out, weights, sems = refs
+    else:
+        out_ref, weights_out, weights, sems = refs
+    step, steps = pl.program_id(0), pl.num_programs(0)
+    me = lax.axis_index("tok")
+    side, z = (me // SIDE) % 2, me // RING
+    rows = weights.shape[0] // count
+    wide = 2 * rows
+
+    def chunk(k):
+        return (z - first - k + 2 * ring) % ring
+
+    def load(k):
+        start = wide * (k // 2) + rows * (side if k % 2 == 0 else 1 - side)
+        return pltpu.make_async_copy(
+            pieces[k], weights.at[pl.ds(pl.multiple_of(start, 16), rows)], sems.at[k]
+        )
+
+    def keep(k):
+        return pltpu.make_async_copy(
+            weights.at[pl.ds(wide * k, wide)],
+            weights_out.at[pl.ds(pl.multiple_of(chunk(k) * wide, 16), wide)],
+            sems.at[count + k],
+        )
+
+    @pl.when(step == 0)
+    def _():
+        for k in range(count):
+            load(k).start()
+        for k in range(count):
+            load(k).wait()
+        for k in range(count // 2):
+            keep(k).start()
+
+    early = step < steps // 2
+
+    def columns_of(pair):
+        parts = []
+        for k in range(count // 2):
+            lanes = pl.ds(pl.multiple_of(chunk(k) * wide, HD), wide)
+            parts.append(jnp.where(early, pair[0][:, lanes], pair[1][:, lanes]))
+        return parts[0] if len(parts) == 1 else jnp.concatenate(parts, axis=1)
+
+    normed, cotangent = columns_of(normed_refs), columns_of(cot_refs)
+    columns = out_ref.shape[2]
+    products = [
+        matmul(left, weights[:, k * columns : (k + 1) * columns])
+        for k, left in enumerate((normed, normed, cotangent))
+    ]
+    if last:
+        activation_grads(out_ref, *(products[k] + partial_ref[k].astype(FULL) for k in range(3)))
+    else:
+        for k in range(3):
+            out_ref[k] = products[k].astype(LOW)
+
+    @pl.when(step == steps - 1)
+    def _():
+        for k in range(count // 2):
+            keep(k).wait()
+
+
+def hidden_by_depth(normed, cotangent, pieces):
+    half, width = normed[0].shape
+    columns = pieces[0].shape[1] // 3
+    rows = min(256, half)
+    steps = half // rows
+    ring = len(pieces) // 2
+    deep = width // ring
+    blocks = [
+        pl.BlockSpec((rows, width), lambda i: (jnp.minimum(i, steps - 1), 0)),
+        pl.BlockSpec((rows, width), lambda i: (jnp.maximum(i - steps, 0), 0)),
+    ]
+    anywhere = pl.BlockSpec(memory_space=pl.ANY)
+    block = pl.BlockSpec((3, rows, columns), lambda i: (0, i, 0))
+    weights_shape = jax.ShapeDtypeStruct((width, 3 * columns), LOW)
+
+    def part(first, given, more):
+        count = len(given)
+        return pl.pallas_call(
+            functools.partial(depth_kernel, ring, first, count, len(more) > 0),
+            grid=(2 * steps,),
+            in_specs=blocks * 2 + [anywhere] * count + [block, anywhere][: len(more)],
+            out_specs=[block, anywhere],
+            out_shape=[jax.ShapeDtypeStruct((3, 2 * half, columns), LOW), weights_shape],
+            input_output_aliases={5 + count: 1} if more else {},
+            scratch_shapes=[
+                pltpu.VMEM((deep * (count // 2), 3 * columns), LOW),
+                pltpu.SemaphoreType.DMA((count + count // 2,)),
+            ],
+            compiler_params=pltpu.CompilerParams(vmem_limit_bytes=48 * MIB),
+            cost_estimate=LIGHT,
+        )(*normed, *cotangent, *given, *more)
+
+    partial = part(0, pieces[:-2], [])
+    return part(ring - 1, pieces[-2:], partial)
 
 
 def project_sum_kernel(count, blocks, array_ref, *refs):

time: 513 us -> 502 us (0.979)
  waiting for transfers between devices: 91.1 us -> 65 us
  Pallas kernels: 272 us -> 287 us
    ppermute x14, waiting for transfers between devices: 35 us -> 8.95 us  [flip(): return lax.ppermute(array, 'tok', [(i, i ^ bit) for i in range(size)])]
    pallas_call x1 -> x2, Pallas kernels: 35.1 us -> 49.8 us  [part(): pl.pallas_call(functools.partial(depth_kernel, ring, first, count, len(mo...]
  transfers between devices with their start and end apart: 26 -> 26, of which waited for: 6 -> 6; matrix products, arithmetic and copies ran while one was open for 15% -> 15% of each run, Pallas kernels for 45% -> 51%
where the time goes in v4:
time: 502 us; the launch traced here: 495 us
  Pallas kernels  287 us (57%)
  waiting for transfers between devices  65 us (13%)
  local copies, waits for them, and re-layouts  49 us (10%)
  starting transfers between devices  27.7 us (6%)
  other arithmetic  27.7 us (6%)
  matrix products  23.2 us (5%)
  between operations  15.4 us (3%)
    ppermute x6, waiting for transfers between devices, around(): lax.ppermute(array, 'tok', [(i, (i + RING) % size) for i in range(size)])  55.3 us
    pallas_call x1, Pallas kernels, scatter(): pl.pallas_call(functools.partial(scatter_kernel, ring, bands, edges), in_...  52 us
    pallas_call x2, Pallas kernels, part(): pl.pallas_call(functools.partial(depth_kernel, ring, first, count, len(mo...  49.8 us
    pallas_call x4, Pallas kernels, outer_products(): pl.pallas_call(outer_kernel, grid_spec=pltpu.PrefetchScalarGridSpec(num_s...  44.9 us
    pallas_call x1, Pallas kernels, gather(): pl.pallas_call(functools.partial(gather_kernel, ring, bands), in_specs=[a...  42.8 us
    pallas_call x2, Pallas kernels, project_sum(): pl.pallas_call(functools.partial(project_sum_kernel, count, blocks), grid...  35.2 us
    pallas_call x2, Pallas kernels, attend(): pl.pallas_call(functools.partial(attend_kernel, block, HD ** (-0.5) * LOG...  25.6 us
    unnamed x112, local copies, waits for them, and re-layouts  24.3 us
  transfers between devices with their start and end apart: 26, of which 6 were waited for; matrix products, arithmetic and copies ran while one was open for 15% of the time, Pallas kernels for 51%

profile of v4, /device:TPU:0, one launch (start us, length us, event | category | flops | bytes accessed | tf_op | source)
XLA Modules:
  0.0 494.5 jit_solution(17333456898565812350)
XLA Ops:
  9.8 1.6 fusion.37.attn_ref
  11.4 1.2 bitcast_bitcast_fusion
  12.7 1.2 pad_maximum_fusion.2.ffn_ref
  13.8 42.8 %shard_map.222 = (bf16[4,2,2,2,48,1920]{5,4,3,2,1,0:T(8,128)(2,1)}, bf16[4,48,3456]{2,1,0:T(8,128)(2,1)}) custom-call(bf16[48,1920]{1,0:T(8,128)(2,1)} %fusion.37.attn_ref, bf16[4,48,3456]{2,1,0:T(8,128)(2,1)} %pad_maximum_fusion.2.ffn_ref), custom_call_target="tpu_custom_call" | custom-call | tf_op jit(solution)/shard_map/pallas_call | solution.py:211
  58.4 2.0 fusion.27
  61.9 3.4 collective-permute-start
  65.3 2.8 collective-permute-start.1
  68.2 4.3 fusion.2.q_ref
  72.9 1.3 maximum_maximum_fusion
  75.3 2.1 copy.62.value_t_ref
  77.4 1.9 copy-done.9
  80.3 12.8 %shard_map.223 = (bf16[512,768]{1,0:T(8,128)(2,1)S(1)}, bf16[512,768]{1,0:T(8,128)(2,1)S(1)}, f32[6,1,512]{2,1,0:T(1,128)S(1)}) custom-call(f32[512,1536]{1,0:T(8,128)S(1)} %copy-done.9, bf16[1536,128]{1,0:T(8,128)(2,1)S(1)} %get-tuple-element.165.key_ref, bf16[128,1536]{1,0:T(8,128)(2,1)S(1)} %copy-done.25, s32[1536,1]{1,0:T(8,128)S(1)} %broadcast_in_dim.33.ks_ref, ...), custom_call_target="tpu_custom_call" | custom-call | flops 1024 | bytes 1024 | tf_op jit(solution)/shard_map/pallas_call | solution.py:566
  94.8 19.6 %collective-permute-done.2.refs_6_ = bf16[192,3456]{1,0:T(8,128)(2,1)} collective-permute-done((bf16[192,3456]{1,0:T(8,128)(2,1)}, bf16[192,3456]{1,0:T(8,128)(2,1)}, u32[]{:S(2)}, u32[]{:S(2)}) %collective-permute-start.2) | collective-permute-done | bytes 1327136 | tf_op jit(solution)/shard_map/ppermute | solution.py:31
  115.5 2.9 collective-permute-start.10
  118.4 12.8 %shard_map.224 = (bf16[512,768]{1,0:T(8,128)(2,1)S(1)}, bf16[512,768]{1,0:T(8,128)(2,1)S(1)}, f32[6,1,512]{2,1,0:T(1,128)S(1)}) custom-call(f32[512,1536]{1,0:T(8,128)S(1)} %copy-done.9, bf16[1536,128]{1,0:T(8,128)(2,1)S(1)} %get-tuple-element.165.key_ref, bf16[128,1536]{1,0:T(8,128)(2,1)S(1)} %copy-done.25, s32[1536,1]{1,0:T(8,128)S(1)} %broadcast_in_dim.33.ks_ref, ...), custom_call_target="tpu_custom_call" | custom-call | flops 1024 | bytes 1024 | tf_op jit(solution)/shard_map/pallas_call | solution.py:566
  133.0 2.3 copy-done.5
  137.6 3.2 shard_map.225
  140.8 6.9 %collective-permute-done.4.refs_8_ = bf16[192,3456]{1,0:T(8,128)(2,1)} collective-permute-done((bf16[192,3456]{1,0:T(8,128)(2,1)}, bf16[192,3456]{1,0:T(8,128)(2,1)}, u32[]{:S(2)}, u32[]{:S(2)}) %collective-permute-start.4) | collective-permute-done | bytes 1327136 | tf_op jit(solution)/shard_map/ppermute | solution.py:31
  148.8 1.9 collective-permute-start.8
  150.6 2.7 constant_dynamic-update-slice_fusion.3
  153.3 2.7 constant_dynamic-update-slice_fusion.2.refs_2_
  156.0 1.8 collective-permute-start.11
  157.9 23.8 %collective-permute-done.7.refs_4_ = bf16[192,3456]{1,0:T(8,128)(2,1)} collective-permute-done((bf16[192,3456]{1,0:T(8,128)(2,1)}, bf16[192,3456]{1,0:T(8,128)(2,1)}, u32[]{:S(2)}, u32[]{:S(2)}) %collective-permute-start.7) | collective-permute-done | bytes 1327136 | tf_op jit(solution)/shard_map/ppermute | solution.py:31
  181.7 4.8 collective-permute-done.6
  187.6 1.3 collective-permute-start.12
  188.8 4.1 collective-permute-done.9.refs_1_
  193.0 28.6 %shard_map.226 = (bf16[3,2048,1152]{2,1,0:T(8,128)(2,1)}, bf16[1536,3456]{1,0:T(8,128)(2,1)}) custom-call(bf16[1024,1536]{1,0:T(8,128)(2,1)} %copy-done, bf16[1024,1536]{1,0:T(8,128)(2,1)} %collective-permute-done.9.refs_1_, bf16[1024,1536]{1,0:T(8,128)(2,1)} %constant_dynamic-update-slice_fusion.2.refs_2_, ...), custom_call_target="tpu_custom_call" | custom-call | flops 1024 | bytes 1024 | tf_op jit(solution)/shard_map/pallas_call | solution.py:839
  221.6 1.9 copy-done.1
  223.5 21.1 %shard_map.227 = (bf16[3,2048,1152]{2,1,0:T(8,128)(2,1)}, bf16[1536,3456]{1,0:T(8,128)(2,1)}) custom-call(bf16[1024,1536]{1,0:T(8,128)(2,1)S(1)} %copy-done.1, bf16[1024,1536]{1,0:T(8,128)(2,1)} %collective-permute-done.9.refs_1_, bf16[1024,1536]{1,0:T(8,128)(2,1)} %constant_dynamic-update-slice_fusion.2.refs_2_, ...), custom_call_target="tpu_custom_call", output_to_operand_aliasing={{1}: (7, {})} | custom-call | flops 1024 | bytes 1024 | tf_op jit(solution)/shard_map/pallas_call | solution.py:839
  244.7 11.0 %shard_map.228 = bf16[384,3456]{1,0:T(8,128)(2,1)S(1)} custom-call(s32[1]{0:T(128)} %bitcast.11.chunk_ref, bf16[1024,1536]{1,0:T(8,128)(2,1)S(1)} %copy-done.2, bf16[1024,1536]{1,0:T(8,128)(2,1)} %collective-permute-done.9.refs_1_, bf16[1024,1536]{1,0:T(8,128)(2,1)} %constant_dynamic-update-slice_fusion.2.refs_2_, ...), custom_call_target="tpu_custom_call" | custom-call | flops 1024 | bytes 1024 | tf_op jit(solution)/shard_map/pallas_call | solution.py:972
  255.7 1.5 copy-done.18
  258.4 1.5 collective-permute-start.13
  259.8 11.0 %shard_map.229 = bf16[384,3456]{1,0:T(8,128)(2,1)S(1)} custom-call(s32[1]{0:T(128)} %bitcast.10.chunk_ref, bf16[1024,1536]{1,0:T(8,128)(2,1)S(1)} %copy-done.2, bf16[1024,1536]{1,0:T(8,128)(2,1)} %collective-permute-done.9.refs_1_, bf16[1024,1536]{1,0:T(8,128)(2,1)} %constant_dynamic-update-slice_fusion.2.refs_2_, ...), custom_call_target="tpu_custom_call" | custom-call | flops 1024 | bytes 1024 | tf_op jit(solution)/shard_map/pallas_call | solution.py:972
  270.8 22.8 %shard_map.230 = bf16[1024,1536]{1,0:T(8,128)(2,1)S(1)} custom-call(bf16[3,2048,1152]{2,1,0:T(8,128)(2,1)} %get-tuple-element.127.refs_4_.array_ref, bf16[1536,3456]{1,0:T(8,128)(2,1)} %get-tuple-element.119.refs_0_.refs_1_, bf16[1536,3456]{1,0:T(8,128)(2,1)} %get-tuple-element.119.refs_0_.refs_1_), custom_call_target="tpu_custom_call" | custom-call | flops 1024 | bytes 1024 | tf_op jit(solution)/shard_map/pallas_call | solution.py:912
  293.7 1.2 dynamic-slice_bitcast_fusion.2
  295.5 1.5 copy-done.19
  297.0 2.8 fusion.18
  299.8 1.2 collective-permute-start.15
  300.9 3.7 fusion.47
  305.5 11.0 %shard_map.231 = bf16[384,3456]{1,0:T(8,128)(2,1)S(1)} custom-call(s32[1]{0:T(128)} %bitcast.15.chunk_ref, bf16[1024,1536]{1,0:T(8,128)(2,1)S(1)} %copy-done.2, bf16[1024,1536]{1,0:T(8,128)(2,1)} %collective-permute-done.9.refs_1_, bf16[1024,1536]{1,0:T(8,128)(2,1)} %constant_dynamic-update-slice_fusion.2.refs_2_, ...), custom_call_target="tpu_custom_call" | custom-call | flops 1024 | bytes 1024 | tf_op jit(solution)/shard_map/pallas_call | solution.py:972
  316.5 11.9 %shard_map.232 = bf16[384,3456]{1,0:T(8,128)(2,1)S(1)} custom-call(s32[1]{0:T(128)} %bitcast.20.chunk_ref, bf16[1024,1536]{1,0:T(8,128)(2,1)S(1)} %copy-done.2, bf16[1024,1536]{1,0:T(8,128)(2,1)} %collective-permute-done.9.refs_1_, bf16[1024,1536]{1,0:T(8,128)(2,1)} %constant_dynamic-update-slice_fusion.2.refs_2_, ...), custom_call_target="tpu_custom_call" | custom-call | flops 1024 | bytes 1024 | tf_op jit(solution)/shard_map/pallas_call | solution.py:972
  328.4 5.0 %collective-permute-done.15 = bf16[192,3456]{1,0:T(8,128)(2,1)} collective-permute-done((bf16[192,3456]{1,0:T(8,128)(2,1)}, bf16[192,3456]{1,0:T(8,128)(2,1)}, u32[]{:S(2)}, u32[]{:S(2)}) %collective-permute-start.15) | collective-permute-done | bytes 1327136 | tf_op jit(solution)/shard_map/ppermute | solution.py:31
  333.4 1.2 dynamic-slice_bitcast_fusion.1
  335.2 3.3 fusion.20
  338.6 2.0 copy.66.key_t_ref
  340.8 1.4 pad_maximum_fusion.1.rot_ref
  342.2 12.5 %shard_map.233 = bf16[1024,1536]{1,0:T(8,128)(2,1)S(1)} custom-call(bf16[3,2048,1152]{2,1,0:T(8,128)(2,1)} %get-tuple-element.127.refs_4_.array_ref, bf16[1536,3456]{1,0:T(8,128)(2,1)} %get-tuple-element.119.refs_0_.refs_1_), custom_call_target="tpu_custom_call" | custom-call | flops 1024 | bytes 1024 | tf_op jit(solution)/shard_map/pallas_call | solution.py:912
  354.7 8.7 %shard_map.234 = (f32[512,1536]{1,0:T(8,128)}, bf16[512,1536]{1,0:T(8,128)(2,1)S(1)}, bf16[512,1536]{1,0:T(8,128)(2,1)S(1)}, bf16[512,1536]{1,0:T(8,128)(2,1)S(1)}) custom-call(bf16[512,1536]{1,0:T(8,128)(2,1)} %get-tuple-element.155.group_ref, bf16[512,1536]{1,0:T(8,128)(2,1)} %collective-permute-done.16.near_ref, bf16[512,1536]{1,0:T(8,128)(2,1)} %cot_ref.1, ...), custom_call_target="tpu_custom_call" | custom-call | flops 1024 | bytes 1024 | tf_op jit(solution)/shard_map/pallas_call | solution.py:1050
  363.4 1.2 copy-done.35
  365.7 4.4 convolution_convert_fusion
  370.3 2.1 collective-permute-start.17
  373.6 3.7 fusion.17
  377.4 1.4 copy-done.39
  378.8 24.3 %shard_map.235 = (bf16[512,1536]{1,0:T(8,128)(2,1)S(1)}, f32[1536,128]{1,0:T(8,128)S(1)}, f32[1536,128]{1,0:T(8,128)S(1)}) custom-call(bf16[512,1536]{1,0:T(8,128)(2,1)S(1)} %copy-done.22, bf16[512,1536]{1,0:T(8,128)(2,1)S(1)} %copy-done.39, bf16[512,1536]{1,0:T(8,128)(2,1)S(1)} %copy-done.27, f32[12,1,512]{2,1,0:T(1,128)S(1)} %pad_maximum_fusion.9.log_ref, ...), custom_call_target="tpu_custom_call" | custom-call | flops 1024 | bytes 1024 | tf_op jit(solution)/shard_map/pallas_call | solution.py:631
  403.4 1.3 collective-permute-start.20
  404.7 1.3 collective-permute-start.21
  406.0 5.0 %fusion = f32[512,1536]{1,0:T(8,128)S(1)} fusion(bf16[512,1536]{1,0:T(8,128)(2,1)S(1)} %get-tuple-element.140, bf16[1536,1920]{1,0:T(8,128)(2,1)} %bitcast.101), kind=kOutput, calls=%fused_computation.7 | convolution fusion | flops 2415919104 | bytes 9437184 | tf_op jit(solution)/shard_map/dot_general | solution.py:51
  411.0 3.1 convolution_convert_fusion.1
  414.2 3.4 add_convert_fusion
  418.7 2.1 fusion.11
  424.0 2.0 fusion.10
  426.1 2.3 fusion.15
  428.4 52.0 %shard_map.236 = (f32[48,1920]{1,0:T(8,128)S(1)}, bf16[4,48,3456]{2,1,0:T(8,128)(2,1)S(1)}) custom-call(bf16[4,2,2,2,48,1536]{5,4,3,2,1,0:T(8,128)(2,1)S(1)} %bitcast.86, bf16[4,2,2,2,48,256]{5,4,3,2,1,0:T(8,128)(2,1)S(1)} %bitcast.88, bf16[4,2,2,2,48,128]{5,4,3,2,1,0:T(8,128)(2,1)S(1)} %bitcast.87, bf16[4,48,3456]{2,1,0:T(8,128)(2,1)S(1)} %bitcast.85), custom_call_target="tpu_custom_call" | custom-call | tf_op jit(solution)/shard_map/pallas_call | solution.py:405
  485.6 1.6 convert_element_type.174
  (187 shorter events, 33.1 us)
Async XLA Ops:
  7.2 125.8 %all-gather.2.cloned.1.call-start = ((), (), s32[]{:S(2)}) async-start(), calls=%async_computation.1 | async-start | bytes 4866048 | tf_op jit(solution)/shard_map/all_gather | solution.py:1115
  7.9 477.7 %reduce-scatter.2.cloned.1.call-start = ((), (), s32[]{:S(2)}) async-start(), calls=%async_computation.2 | async-start | bytes 4866048 | tf_op jit(solution)/shard_map/reduce_scatter | solution.py:1164
  12.7 45.2 %copy-start.51 = (s32[512]{0:T(512)S(1)}, s32[512]{0:T(512)}, u32[]{:S(2)}) copy-start(s32[512]{0:T(512)} %param.33) | copy-start | bytes 6148
  12.7 45.2 %copy-start.3 = (bf16[512,1536]{1,0:T(8,128)(2,1)S(1)}, bf16[512,1536]{1,0:T(8,128)(2,1)}, u32[]{:S(2)}) copy-start(bf16[512,1536]{1,0:T(8,128)(2,1)} %refs_0_.1) | copy-start | bytes 4718596
  57.9 10.3 %slice-start = ((s8[5898240]{0:T(1024)(128)(4,1)}), s8[4194304]{0:T(1024)(128)(4,1)S(1)}, s32[]{:S(2)}) async-start(s8[5898240]{0:T(1024)(128)(4,1)} %bitcast.103), calls=%async_computation.3 | async-start | bytes 8388608
  58.3 9.8 %slice-start.1 = ((s8[5898240]{0:T(1024)(128)(4,1)}), s8[1703936]{0:T(1024)(128)(4,1)S(1)}, s32[]{:S(2)}) async-start(s8[5898240]{0:T(1024)(128)(4,1)} %bitcast.103), calls=%async_computation.4 | async-start | bytes 3407872
  61.5 10.9 %copy-start.47 = (f32[512,64]{1,0:T(8,128)}, f32[512,64]{1,0:T(8,128)S(1)}, u32[]{:S(2)}) copy-start(f32[512,64]{1,0:T(8,128)S(1)} %get-tuple-element.177) | copy-start | bytes 393220
  61.8 56.6 %copy-start.23 = (f32[512,128]{1,0:T(8,128)}, f32[512,128]{1,0:T(8,128)S(1)}, u32[]{:S(2)}) copy-start(f32[512,128]{1,0:T(8,128)S(1)} %get-tuple-element.172.cos_ref) | copy-start | bytes 786436
  61.9 11.0 %collective-permute-start = (bf16[512,256]{1,0:T(8,128)(2,1)S(1)}, bf16[512,256]{1,0:T(8,128)(2,1)}, u32[]{:S(2)}, u32[]{:S(2)}) collective-permute-start(bf16[512,256]{1,0:T(8,128)(2,1)S(1)} %pad_maximum_fusion.5), channel_id=1, source_target_pairs={{0,2},{1,3},{2,4},{3,5},{4,6},{5,7},{6,8},{7,9},{8,10},{9,11},{10,... | collective-permute-start | bytes 786440 | tf_op jit(solution)/shard_map/ppermute | solution.py:37
  65.3 7.6 %collective-permute-start.1 = (bf16[512,256]{1,0:T(8,128)(2,1)S(1)}, bf16[512,256]{1,0:T(8,128)(2,1)}, u32[]{:S(2)}, u32[]{:S(2)}) collective-permute-start(bf16[512,256]{1,0:T(8,128)(2,1)S(1)} %pad_maximum_fusion.5), channel_id=1, source_target_pairs={{0,1},{1,2},{2,3},{3,4},{4,5},{5,6},{6,7},{7,8},{8,9},{9,10},{10,1... | collective-permute-start | bytes 786440 | tf_op jit(solution)/shard_map/ppermute | solution.py:37
  68.0 4.4 copy-start.50
  68.0 46.4 %collective-permute-start.2 = (bf16[192,3456]{1,0:T(8,128)(2,1)}, bf16[192,3456]{1,0:T(8,128)(2,1)}, u32[]{:S(2)}, u32[]{:S(2)}) collective-permute-start(bf16[192,3456]{1,0:T(8,128)(2,1)} %bitcast.9.refs_4_), channel_id=1, source_target_pairs={{0,8},{1,9},{2,10},{3,11},{4,12},{5,13},{6,14},{7,15},{8,16},{9,17... | collective-permute-start | bytes 3981320 | tf_op jit(solution)/shard_map/ppermute | solution.py:31
  68.1 46.4 %collective-permute-start.3 = (bf16[192,3456]{1,0:T(8,128)(2,1)}, bf16[192,3456]{1,0:T(8,128)(2,1)}, u32[]{:S(2)}, u32[]{:S(2)}) collective-permute-start(bf16[192,3456]{1,0:T(8,128)(2,1)} %bitcast.9.refs_4_), channel_id=1, source_target_pairs={{0,4},{1,5},{2,6},{3,7},{4,0},{5,1},{6,2},{7,3},{8,12},{9,13},{10,... | collective-permute-start | bytes 3981320 | tf_op jit(solution)/shard_map/ppermute | solution.py:26
  72.8 45.6 %copy-start.6 = (s32[1536,1]{1,0:T(8,128)}, s32[1536,1]{1,0:T(8,128)S(1)}, u32[]{:S(2)}) copy-start(s32[1536,1]{1,0:T(8,128)S(1)} %broadcast_in_dim.33.ks_ref) | copy-start | bytes 18436
  75.3 43.1 %copy-start.20 = (bf16[1536,128]{1,0:T(8,128)(2,1)}, bf16[1536,128]{1,0:T(8,128)(2,1)S(1)}, u32[]{:S(2)}) copy-start(bf16[1536,128]{1,0:T(8,128)(2,1)S(1)} %get-tuple-element.165.key_ref) | copy-start | bytes 1179652
  114.4 33.3 %collective-permute-start.4 = (bf16[192,3456]{1,0:T(8,128)(2,1)}, bf16[192,3456]{1,0:T(8,128)(2,1)}, u32[]{:S(2)}, u32[]{:S(2)}) collective-permute-start(bf16[192,3456]{1,0:T(8,128)(2,1)} %collective-permute-done.2.refs_6_), channel_id=1, source_target_pairs={{0,8},{1,9},{2,10},{3,11},{4,12},{5,13},{6,14},{7,15},{8,16},{9,17... | collective-permute-start | bytes 3981320 | tf_op jit(solution)/shard_map/ppermute | solution.py:31
  115.5 32.2 %collective-permute-start.5 = (bf16[192,3456]{1,0:T(8,128)(2,1)}, bf16[192,3456]{1,0:T(8,128)(2,1)}, u32[]{:S(2)}, u32[]{:S(2)}) collective-permute-start(bf16[192,3456]{1,0:T(8,128)(2,1)} %collective-permute-done.2.refs_6_), channel_id=1, source_target_pairs={{0,4},{1,5},{2,6},{3,7},{4,0},{5,1},{6,2},{7,3},{8,12},{9,13},{10,... | collective-permute-start | bytes 3981320 | tf_op jit(solution)/shard_map/ppermute | solution.py:26
  115.5 37.9 %collective-permute-start.10 = (bf16[512,1536]{1,0:T(8,128)(2,1)}, bf16[512,1536]{1,0:T(8,128)(2,1)}, u32[]{:S(2)}, u32[]{:S(2)}) collective-permute-start(bf16[512,1536]{1,0:T(8,128)(2,1)} %cot_ref.1), channel_id=1, source_target_pairs={{0,2},{1,3},{2,0},{3,1},{4,6},{5,7},{6,4},{7,5},{8,10},{9,11},{10,... | collective-permute-start | bytes 4718600 | tf_op jit(solution)/shard_map/ppermute | solution.py:26
  133.0 2.3 copy-start.5
  140.8 15.2 %copy-start.10 = (f32[512,1536]{1,0:T(8,128)}, f32[512,1536]{1,0:T(8,128)S(1)}, u32[]{:S(2)}) copy-start(f32[512,1536]{1,0:T(8,128)S(1)} %get-tuple-element.105.middle_ref) | copy-start | bytes 9437188
  140.8 15.2 %copy-start.44 = (f32[512,128]{1,0:T(8,128)}, f32[512,128]{1,0:T(8,128)S(1)}, u32[]{:S(2)}) copy-start(f32[512,128]{1,0:T(8,128)S(1)} %get-tuple-element.132.inverse_ref) | copy-start | bytes 786436
  147.7 38.7 %collective-permute-start.6 = (bf16[512,1536]{1,0:T(8,128)(2,1)S(1)}, bf16[512,1536]{1,0:T(8,128)(2,1)S(1)}, u32[]{:S(2)}, u32[]{:S(2)}) collective-permute-start(bf16[512,1536]{1,0:T(8,128)(2,1)S(1)} %get-tuple-element.109), channel_id=1, source_target_pairs={{0,2},{1,3},{2,0},{3,1},{4,6},{5,7},{6,4},{7,5},{8,10},{9,11},{10,... | collective-permute-start | bytes 4718600 | tf_op jit(solution)/shard_map/ppermute | solution.py:26
  148.8 32.9 %collective-permute-start.7 = (bf16[192,3456]{1,0:T(8,128)(2,1)}, bf16[192,3456]{1,0:T(8,128)(2,1)}, u32[]{:S(2)}, u32[]{:S(2)}) collective-permute-start(bf16[192,3456]{1,0:T(8,128)(2,1)} %collective-permute-done.4.refs_8_), channel_id=1, source_target_pairs={{0,8},{1,9},{2,10},{3,11},{4,12},{5,13},{6,14},{7,15},{8,16},{9,17... | collective-permute-start | bytes 3981320 | tf_op jit(solution)/shard_map/ppermute | solution.py:31
  148.8 32.9 %collective-permute-start.8 = (bf16[192,3456]{1,0:T(8,128)(2,1)}, bf16[192,3456]{1,0:T(8,128)(2,1)S(1)}, u32[]{:S(2)}, u32[]{:S(2)}) collective-permute-start(bf16[192,3456]{1,0:T(8,128)(2,1)} %collective-permute-done.4.refs_8_), channel_id=1, source_target_pairs={{0,4},{1,5},{2,6},{3,7},{4,0},{5,1},{6,2},{7,3},{8,12},{9,13},{10,... | collective-permute-start | bytes 3981320 | tf_op jit(solution)/shard_map/ppermute | solution.py:26
  156.0 32.8 %collective-permute-start.11 = (bf16[1024,1536]{1,0:T(8,128)(2,1)}, bf16[1024,1536]{1,0:T(8,128)(2,1)}, u32[]{:S(2)}, u32[]{:S(2)}) collective-permute-start(bf16[1024,1536]{1,0:T(8,128)(2,1)} %constant_dynamic-update-slice_fusion.2.refs_2_), channel_id=1, source_target_pairs={{0,1},{1,0},{2,3},{3,2},{4,5},{5,4},{6,7},{7,6},{8,9},{9,8},{10,11... | collective-permute-start | bytes 9437192 | tf_op jit(solution)/shard_map/ppermute | solution.py:26
  181.7 4.9 copy-start.49
  186.6 6.4 %copy-start = (bf16[1024,1536]{1,0:T(8,128)(2,1)}, bf16[1024,1536]{1,0:T(8,128)(2,1)S(1)}, u32[]{:S(2)}) copy-start(bf16[1024,1536]{1,0:T(8,128)(2,1)S(1)} %constant_dynamic-update-slice_fusion.refs_0_) | copy-start | bytes 9437188
  186.6 6.4 %collective-permute-start.9 = (bf16[1024,1536]{1,0:T(8,128)(2,1)S(1)}, bf16[1024,1536]{1,0:T(8,128)(2,1)}, u32[]{:S(2)}, u32[]{:S(2)}) collective-permute-start(bf16[1024,1536]{1,0:T(8,128)(2,1)S(1)} %constant_dynamic-update-slice_fusion.refs_0_), channel_id=1, source_target_pairs={{0,1},{1,0},{2,3},{3,2},{4,5},{5,4},{6,7},{7,6},{8,9},{9,8},{10,11... | collective-permute-start | bytes 9437192 | tf_op jit(solution)/shard_map/ppermute | solution.py:26
  187.6 34.1 %collective-permute-start.12 = (bf16[192,3456]{1,0:T(8,128)(2,1)}, bf16[192,3456]{1,0:T(8,128)(2,1)}, u32[]{:S(2)}, u32[]{:S(2)}) collective-permute-start(bf16[192,3456]{1,0:T(8,128)(2,1)} %collective-permute-done.7.refs_4_), channel_id=1, source_target_pairs={{0,4},{1,5},{2,6},{3,7},{4,0},{5,1},{6,2},{7,3},{8,12},{9,13},{10,... | collective-permute-start | bytes 3981320 | tf_op jit(solution)/shard_map/ppermute | solution.py:26
  223.5 21.2 %copy-start.2 = (bf16[1024,1536]{1,0:T(8,128)(2,1)S(1)}, bf16[1024,1536]{1,0:T(8,128)(2,1)}, u32[]{:S(2)}) copy-start(bf16[1024,1536]{1,0:T(8,128)(2,1)} %copy-done) | copy-start | bytes 9437188
  258.4 35.3 %collective-permute-start.13 = (bf16[192,3456]{1,0:T(8,128)(2,1)}, bf16[192,3456]{1,0:T(8,128)(2,1)}, u32[]{:S(2)}, u32[]{:S(2)}) collective-permute-start(bf16[192,3456]{1,0:T(8,128)(2,1)} %dynamic-slice_bitcast_fusion.3), channel_id=1, source_target_pairs={{0,4},{1,5},{2,6},{3,7},{4,0},{5,1},{6,2},{7,3},{8,12},{9,13},{10,... | collective-permute-start | bytes 3981320 | tf_op jit(solution)/shard_map/ppermute | solution.py:26
  270.8 22.8 %copy-start.16 = (bf16[384,3456]{1,0:T(8,128)(2,1)}, bf16[384,3456]{1,0:T(8,128)(2,1)S(1)}, u32[]{:S(2)}) copy-start(bf16[384,3456]{1,0:T(8,128)(2,1)S(1)} %shard_map.229) | copy-start | bytes 7962628
  293.6 6.2 %copy-start.8 = (bf16[1024,1536]{1,0:T(8,128)(2,1)}, bf16[1024,1536]{1,0:T(8,128)(2,1)S(1)}, u32[]{:S(2)}) copy-start(bf16[1024,1536]{1,0:T(8,128)(2,1)S(1)} %shard_map.230) | copy-start | bytes 9437188
  293.6 3.4 copy-start.19
  294.9 33.5 %collective-permute-start.14 = (bf16[192,3456]{1,0:T(8,128)(2,1)}, bf16[192,3456]{1,0:T(8,128)(2,1)}, u32[]{:S(2)}, u32[]{:S(2)}) collective-permute-start(bf16[192,3456]{1,0:T(8,128)(2,1)} %dynamic-slice_bitcast_fusion.2), channel_id=1, source_target_pairs={{0,4},{1,5},{2,6},{3,7},{4,0},{5,1},{6,2},{7,3},{8,12},{9,13},{10,... | collective-permute-start | bytes 3981320 | tf_op jit(solution)/shard_map/ppermute | solution.py:26
  299.8 33.7 %collective-permute-start.15 = (bf16[192,3456]{1,0:T(8,128)(2,1)}, bf16[192,3456]{1,0:T(8,128)(2,1)}, u32[]{:S(2)}, u32[]{:S(2)}) collective-permute-start(bf16[192,3456]{1,0:T(8,128)(2,1)} %fusion.18), channel_id=1, source_target_pairs={{0,8},{1,9},{2,10},{3,11},{4,12},{5,13},{6,14},{7,15},{8,16},{9,17... | collective-permute-start | bytes 3981320 | tf_op jit(solution)/shard_map/ppermute | solution.py:31
  304.7 50.0 %collective-permute-start.16 = (bf16[512,1536]{1,0:T(8,128)(2,1)}, bf16[512,1536]{1,0:T(8,128)(2,1)}, u32[]{:S(2)}, u32[]{:S(2)}) collective-permute-start(bf16[512,1536]{1,0:T(8,128)(2,1)} %get-tuple-element.156), channel_id=1, source_target_pairs={{0,2},{1,3},{2,0},{3,1},{4,6},{5,7},{6,4},{7,5},{8,10},{9,11},{10,... | collective-permute-start | bytes 4718600 | tf_op jit(solution)/shard_map/ppermute | solution.py:26
  316.5 17.0 %copy-start.14 = (bf16[384,3456]{1,0:T(8,128)(2,1)}, bf16[384,3456]{1,0:T(8,128)(2,1)S(1)}, u32[]{:S(2)}) copy-start(bf16[384,3456]{1,0:T(8,128)(2,1)S(1)} %shard_map.231) | copy-start | bytes 7962628
  328.4 10.1 %copy-start.12 = (bf16[384,3456]{1,0:T(8,128)(2,1)}, bf16[384,3456]{1,0:T(8,128)(2,1)S(1)}, u32[]{:S(2)}) copy-start(bf16[384,3456]{1,0:T(8,128)(2,1)S(1)} %shard_map.232) | copy-start | bytes 7962628
  328.4 6.8 %copy-start.17 = (bf16[384,3456]{1,0:T(8,128)(2,1)S(1)}, bf16[384,3456]{1,0:T(8,128)(2,1)}, u32[]{:S(2)}) copy-start(bf16[384,3456]{1,0:T(8,128)(2,1)} %copy-done.16) | copy-start | bytes 7962628
  334.6 6.0 %copy-start.30 = (bf16[512,768]{1,0:T(8,128)(2,1)S(1)}, bf16[512,768]{1,0:T(8,128)(2,1)}, u32[]{:S(2)}) copy-start(bf16[512,768]{1,0:T(8,128)(2,1)} %copy-done.28) | copy-start | bytes 2359300
  334.6 6.1 %copy-start.33 = (bf16[512,768]{1,0:T(8,128)(2,1)S(1)}, bf16[512,768]{1,0:T(8,128)(2,1)}, u32[]{:S(2)}) copy-start(bf16[512,768]{1,0:T(8,128)(2,1)} %copy-done.31) | copy-start | bytes 2359300
  334.6 37.7 %collective-permute-start.18 = (bf16[192,3456]{1,0:T(8,128)(2,1)}, bf16[192,3456]{1,0:T(8,128)(2,1)}, u32[]{:S(2)}, u32[]{:S(2)}) collective-permute-start(bf16[192,3456]{1,0:T(8,128)(2,1)} %dynamic-slice_bitcast_fusion.1), channel_id=1, source_target_pairs={{0,4},{1,5},{2,6},{3,7},{4,0},{5,1},{6,2},{7,3},{8,12},{9,13},{10,... | collective-permute-start | bytes 3981320 | tf_op jit(solution)/shard_map/ppermute | solution.py:26
  338.5 2.3 copy-start.41
  338.5 2.3 copy-start.43
  338.5 33.9 %collective-permute-start.19 = (bf16[192,3456]{1,0:T(8,128)(2,1)}, bf16[192,3456]{1,0:T(8,128)(2,1)}, u32[]{:S(2)}, u32[]{:S(2)}) collective-permute-start(bf16[192,3456]{1,0:T(8,128)(2,1)} %fusion.20), channel_id=1, source_target_pairs={{0,8},{1,9},{2,10},{3,11},{4,12},{5,13},{6,14},{7,15},{8,16},{9,17... | collective-permute-start | bytes 3981320 | tf_op jit(solution)/shard_map/ppermute | solution.py:31
  340.8 24.9 %copy-start.26 = (bf16[512,1536]{1,0:T(8,128)(2,1)}, bf16[512,1536]{1,0:T(8,128)(2,1)S(1)}, u32[]{:S(2)}) copy-start(bf16[512,1536]{1,0:T(8,128)(2,1)S(1)} %constant_dynamic-update-slice_fusion.4.mixed_ref) | copy-start | bytes 4718596
  342.2 12.5 %copy-start.45 = (f32[512,128]{1,0:T(8,128)S(1)}, f32[512,128]{1,0:T(8,128)}, u32[]{:S(2)}) copy-start(f32[512,128]{1,0:T(8,128)} %copy-done.44) | copy-start | bytes 786436
  370.1 3.4 copy-start.15
  370.3 43.9 %collective-permute-start.17 = (bf16[512,1536]{1,0:T(8,128)(2,1)S(1)}, bf16[512,1536]{1,0:T(8,128)(2,1)}, u32[]{:S(2)}, u32[]{:S(2)}) collective-permute-start(bf16[512,1536]{1,0:T(8,128)(2,1)S(1)} %slice.144), channel_id=1, source_target_pairs={{0,2},{1,3},{2,0},{3,1},{4,6},{5,7},{6,4},{7,5},{8,10},{9,11},{10,... | collective-permute-start | bytes 4718600 | tf_op jit(solution)/shard_map/ppermute | solution.py:26
  372.4 4.9 copy-start.37
  372.5 4.8 copy-start.7
  372.5 4.8 copy-start.21
  372.5 4.8 copy-start.22
  372.5 4.8 copy-start.24
  372.6 4.8 copy-start.27
  372.6 4.8 copy-start.34
  372.6 53.5 %collective-permute-start.22 = (bf16[192,3456]{1,0:T(8,128)(2,1)S(1)}, bf16[192,3456]{1,0:T(8,128)(2,1)}, u32[]{:S(2)}, u32[]{:S(2)}) collective-permute-start(bf16[192,3456]{1,0:T(8,128)(2,1)S(1)} %dynamic-slice_bitcast_fusion), channel_id=1, source_target_pairs={{0,4},{1,5},{2,6},{3,7},{4,0},{5,1},{6,2},{7,3},{8,12},{9,13},{10,... | collective-permute-start | bytes 3981320 | tf_op jit(solution)/shard_map/ppermute | solution.py:26
  377.3 48.8 %collective-permute-start.23 = (bf16[192,3456]{1,0:T(8,128)(2,1)}, bf16[192,3456]{1,0:T(8,128)(2,1)}, u32[]{:S(2)}, u32[]{:S(2)}) collective-permute-start(bf16[192,3456]{1,0:T(8,128)(2,1)} %fusion.17), channel_id=1, source_target_pairs={{0,8},{1,9},{2,10},{3,11},{4,12},{5,13},{6,14},{7,15},{8,16},{9,17... | collective-permute-start | bytes 3981320 | tf_op jit(solution)/shard_map/ppermute | solution.py:31
  403.4 14.2 %collective-permute-start.20 = (bf16[512,256]{1,0:T(8,128)(2,1)S(1)}, bf16[512,256]{1,0:T(8,128)(2,1)S(1)}, u32[]{:S(2)}, u32[]{:S(2)}) collective-permute-start(bf16[512,256]{1,0:T(8,128)(2,1)S(1)} %get-tuple-element.160), channel_id=1, source_target_pairs={{1,0},{2,1},{3,2},{4,3},{5,4},{6,5},{7,6},{8,7},{9,8},{10,9},{11,1... | collective-permute-start | bytes 786440 | tf_op jit(solution)/shard_map/ppermute | solution.py:37
  404.7 12.9 %collective-permute-start.21 = (bf16[512,256]{1,0:T(8,128)(2,1)S(1)}, bf16[512,256]{1,0:T(8,128)(2,1)S(1)}, u32[]{:S(2)}, u32[]{:S(2)}) collective-permute-start(bf16[512,256]{1,0:T(8,128)(2,1)S(1)} %get-tuple-element.161), channel_id=1, source_target_pairs={{2,0},{3,1},{4,2},{5,3},{6,4},{7,5},{8,6},{9,7},{10,8},{11,9},{12,... | collective-permute-start | bytes 786440 | tf_op jit(solution)/shard_map/ppermute | solution.py:37
  406.0 5.1 %copy-start.4 = (bf16[512,1536]{1,0:T(8,128)(2,1)S(1)}, bf16[512,1536]{1,0:T(8,128)(2,1)}, u32[]{:S(2)}) copy-start(bf16[512,1536]{1,0:T(8,128)(2,1)} %refs_0_.1) | copy-start | bytes 4718596
  411.0 3.2 copy-start.11
  421.7 2.4 copy-start.46
  (16 other events, 20.4 us)
Sparse Core Ops, SparseCore 0:
  10.9 98.2 all-gather.1
  370.3 112.5 reduce-scatter.1

commit v5 on v4

--- a/solution.py
+++ b/solution.py
@@ -469,7 +469,7 @@
         self.given = (normed, cotangent, array)
         self.size = lax.axis_size("tok")
         self.ring = self.size // RING
-        _, _, _, self.side, self.z = place()
+        _, _, _, _, self.z = place()
         self.rows = normed[0].shape[1] // (self.ring * 2)
         self.short = 2 <= self.ring <= LONGEST_RING and self.rows % 64 == 0
         self.blocks, self.crossing, self.total = {}, None, None
@@ -480,27 +480,26 @@
         chunk = lax.rem(self.z - 1 - step + 2 * self.ring, self.ring)
         normed, cotangent, array = self.given
         array = after(array, *jax.tree.leaves(mark))
-        product = outer_products(normed, cotangent, array, chunk, 2 * self.rows)
-        self.blocks[step] = product.reshape(2, self.rows, -1)
-        return self.blocks[step]
+        self.blocks[step] = outer_products(normed, cotangent, array, chunk, 2 * self.rows)
+        return self.blocks[step][0]
 
     def begin(self):
         if self.short:
-            self.crossing = flip(pick(self.blocks[0], 1 - self.side), SIDE)
+            self.crossing = flip(self.blocks[0][0], SIDE)
 
     def advance(self, step, *marks):
         if not self.short:
             return ()
         arrived = (self.crossing,) if self.total is None else (self.crossing, self.total)
-        block = self.blocks[min(step + 1, self.ring - 1)]
-        block, *arrived = lax.optimization_barrier((block, *arrived, *marks))[: len(arrived) + 1]
-        total = pick(self.blocks[step], self.side).astype(FULL)
+        give = self.blocks[min(step + 1, self.ring - 1)][0]
+        give, *arrived = lax.optimization_barrier((give, *arrived, *marks))[: len(arrived) + 1]
+        total = self.blocks[step][1].astype(FULL)
         for part in arrived:
             total = total + part.astype(FULL)
         if step == self.ring - 1:
             self.sum = total.astype(LOW)
             return (self.sum,)
-        low, give = total.astype(LOW), pick(block, 1 - self.side)
+        low = total.astype(LOW)
         self.total, self.crossing = around(low), flip(give, SIDE)
         return (low, give)
 
@@ -596,12 +595,13 @@
 
 
 def attend_back_kernel(
-    block, factor, rot_ref, grad_ref, mixed_ref, log_ref, key_ref, value_ref, key_t_ref, ks_ref, qs_ref,
-    cos_ref, sin_ref, query_out, key_out, value_out, bias,
+    block, factor, rot_ref, grad_ref, mixed_ref, log_ref, key_ref, value_ref, ks_ref, qs_ref,
+    cos_ref, sin_ref, query_out, key_out, value_out, bias, key_t_ref,
 ):
     @pl.when(pl.program_id(0) == 0)
     def _():
         mask_into(bias, ks_ref, qs_ref, block)
+        key_t_ref[...] = key_ref[...].T
         key_out[...] = jnp.zeros_like(key_out)
         value_out[...] = jnp.zeros_like(value_out)
 
@@ -636,9 +636,8 @@
             head,
             head,
             pl.BlockSpec((1, 1, queries), lambda h: (h, 0, 0)),
-            whole((keys, HD)),
-            whole((keys, HD)),
-            whole((HD, keys)),
+            pl.BlockSpec((keys, HD), lambda h: (0, 0)),
+            pl.BlockSpec((keys, HD), lambda h: (0, 1)),
             whole((keys, 1)),
             whole((1, queries)),
             whole((queries, HD)),
@@ -650,7 +649,7 @@
             jax.ShapeDtypeStruct((keys, HD), FULL),
             jax.ShapeDtypeStruct((keys, HD), FULL),
         ],
-        scratch_shapes=[pltpu.VMEM((keys, queries), FULL)],
+        scratch_shapes=[pltpu.VMEM((keys, queries), FULL), pltpu.VMEM((HD, keys), LOW)],
         compiler_params=pltpu.CompilerParams(vmem_limit_bytes=40 * MIB),
         cost_estimate=LIGHT,
     )(
@@ -658,9 +657,8 @@
         grad,
         mixed,
         logs,
-        key_value[:, :HD],
-        key_value[:, HD:],
-        key_value[:, :HD].T,
+        key_value,
+        key_value,
         key_segments[:, None],
         query_segments[None, :],
         cosine,
@@ -855,11 +853,10 @@
     return part(ring - 1, pieces[-2:], partial)
 
 
-def project_sum_kernel(count, blocks, array_ref, *refs):
-    weight_refs, out_ref = refs[:count], refs[count]
-    away, arrived, send_sem, recv_sem = refs[count + 1 :]
-    step, column = pl.program_id(0), pl.program_id(1)
-    columns, rows = pl.num_programs(1), out_ref.shape[0]
+def project_sum_kernel(count, array_ref, *refs):
+    weight_refs, out_refs = refs[:count], refs[count : count + 2]
+    away, arrived, send_sem, recv_sem = refs[count + 2 :]
+    step = pl.program_id(0)
     me = lax.axis_index("tok")
     mate = me + 1 - 2 * (me % 2)
 
@@ -873,7 +870,7 @@
             device_id_type=pl.DeviceIdType.MESH,
         )
 
-    @pl.when((step == 0) & (column == 0))
+    @pl.when(step == 0)
     def _():
         barrier = pltpu.get_barrier_semaphore()
         pl.semaphore_signal(
@@ -884,55 +881,42 @@
     total = by_rows(array_ref[0], weight_refs[0][...])
     for k in range(1, count):
         total += by_rows(array_ref[k], weight_refs[k][...])
-    for block in range(blocks):
+    for block in range(2):
 
         @pl.when(step == block)
         def _():
-            away[block, column] = total.astype(LOW)
-
-            @pl.when(column == columns - 1)
-            def _():
-                crossing(block).start()
-
-        @pl.when(step == blocks + block)
+            away[block] = total.astype(LOW)
+            crossing(block).start()
+
+        @pl.when(step == 2 + block)
         def _():
-            @pl.when(column == 0)
-            def _():
-                crossing(block).wait()
-
-            out_ref[...] = (total + arrived[block, column].astype(FULL)).astype(LOW)
+            crossing(block).wait()
+            out_refs[block][...] = (total + arrived[block].astype(FULL)).astype(LOW)
 
 
 def project_sum(array, pack, first, count, identity, marks=()):
     array = after(array, *jax.tree.leaves(marks))
     tokens, columns = array.shape[1:]
     width = pack.shape[0]
-    rows, wide = tokens // 4, width
-    blocks = tokens // rows // 2
+    rows = tokens // 4
+    whole = pl.BlockSpec((rows, width), lambda i: (0, 0))
     return pl.pallas_call(
-        functools.partial(project_sum_kernel, count, blocks),
-        grid=(2 * blocks, width // wide),
-        in_specs=[
-            pl.BlockSpec(
-                (count, rows, columns), lambda i, j: (first // count, (i + blocks) % (2 * blocks), 0)
-            )
-        ]
+        functools.partial(project_sum_kernel, count),
+        grid=(4,),
+        in_specs=[pl.BlockSpec((count, rows, columns), lambda i: (first // count, (i + 2) % 4, 0))]
         + [
             pl.BlockSpec(
-                (wide, columns), lambda i, j, k=k: (j, first + k), pipeline_mode=pl.Buffered(1)
+                (width, columns), lambda i, k=k: (0, first + k), pipeline_mode=pl.Buffered(1)
             )
             for k in range(count)
         ],
-        out_specs=pl.BlockSpec(
-            (rows, wide),
-            lambda i, j: (jnp.maximum(i - blocks, 0), jnp.where(i >= blocks, j, 0)),
-        ),
-        out_shape=jax.ShapeDtypeStruct((tokens // 2, width), LOW),
+        out_specs=[whole] * 2,
+        out_shape=[jax.ShapeDtypeStruct((rows, width), LOW)] * 2,
         scratch_shapes=[
-            pltpu.VMEM((blocks, width // wide, rows, wide), LOW),
-            pltpu.VMEM((blocks, width // wide, rows, wide), LOW),
-            pltpu.SemaphoreType.DMA((blocks,)),
-            pltpu.SemaphoreType.DMA((blocks,)),
+            pltpu.VMEM((2, rows, width), LOW),
+            pltpu.VMEM((2, rows, width), LOW),
+            pltpu.SemaphoreType.DMA((2,)),
+            pltpu.SemaphoreType.DMA((2,)),
         ],
         compiler_params=pltpu.CompilerParams(
             collective_id=identity, has_side_effects=True, vmem_limit_bytes=44 * MIB
@@ -942,7 +926,7 @@
 
 
 def outer_kernel(chunk_ref, *refs):
-    normed_refs, cot_refs, right_ref, out_ref, total = refs[:2], refs[2:4], *refs[4:]
+    normed_refs, cot_refs, right_ref, give_ref, keep_ref, total = refs[:2], refs[2:4], *refs[4:]
     step, steps = pl.program_id(0), pl.num_programs(0)
     early = step < steps // 2
     normed = jnp.where(early, normed_refs[0][...], normed_refs[1][...])
@@ -958,7 +942,10 @@
 
     @pl.when(step == steps - 1)
     def _():
-        out_ref[...] = total[...].astype(LOW)
+        rows = keep_ref.shape[0]
+        side = (lax.axis_index("tok") // SIDE) % 2
+        for ref, place_of in ((give_ref, 1 - side), (keep_ref, side)):
+            ref[...] = total[pl.ds(pl.multiple_of(place_of * rows, 16), rows), :].astype(LOW)
 
 
 def outer_products(normed, cotangent, array, chunk, rows):
@@ -976,10 +963,10 @@
             grid=(2 * steps,),
             in_specs=lefts * 2
             + [pl.BlockSpec((3, deep, columns), lambda i, chunk_ref: (0, i, 0))],
-            out_specs=pl.BlockSpec((rows, 3 * columns), lambda i, chunk_ref: (0, 0)),
+            out_specs=[pl.BlockSpec((rows // 2, 3 * columns), lambda i, chunk_ref: (0, 0))] * 2,
             scratch_shapes=[pltpu.VMEM((rows, 3 * columns), FULL)],
         ),
-        out_shape=jax.ShapeDtypeStruct((rows, 3 * columns), LOW),
+        out_shape=[jax.ShapeDtypeStruct((rows // 2, 3 * columns), LOW)] * 2,
         compiler_params=pltpu.CompilerParams(vmem_limit_bytes=40 * MIB),
         cost_estimate=LIGHT,
     )(chunk[None].astype(jnp.int32), *normed, *cotangent, array)
@@ -1148,17 +1135,17 @@
     pairs_done = reduction.multiply(0)
     reduction.begin()
     pairs_done = reduction.multiply(1, pairs_done)
-    group_sum = project_sum(hidden_pack, ffn_w, 0, 2, 2, pairs_done)
-    near_sent = flip(group_sum[token_count:], NEAR)
-    marks = reduction.advance(0, group_sum)
+    own_sum, near_sum = project_sum(hidden_pack, ffn_w, 0, 2, 2, pairs_done)
+    near_sent = flip(near_sum, NEAR)
+    marks = reduction.advance(0, near_sum)
     pairs_done = reduction.multiply(2, marks)
     pairs_done = reduction.multiply(3, pairs_done)
     marks = reduction.advance(1, pairs_done)
-    output_sum = project_sum(hidden_pack, ffn_w, 2, 1, 3, marks)
-    output_near = flip(after(output_sum, near_sent)[token_count:], NEAR)
+    output_own, output_near = project_sum(hidden_pack, ffn_w, 2, 1, 3, marks)
+    output_near = flip(after(output_near, near_sent), NEAR)
 
     grad_middle, branch, grad_mixed, gain_two_parts = branch_back(
-        group_sum[:token_count], after(near_sent, output_sum), cotangent, middle, inverse_two, gain_two, out_w
+        own_sum, after(near_sent, output_own), cotangent, middle, inverse_two, gain_two, out_w
     )
     grad_out_w = outer_sum(branch, mixed).astype(LOW)
     out_sum = lax.psum_scatter(grad_out_w, "tok", scatter_dimension=0, tiled=True).astype(FULL)
@@ -1167,7 +1154,7 @@
         rot, after(grad_mixed, *marks), mixed, logs, all_keys, key_segments, query_segments, cosine, sine
     )
     output = (
-        middle + output_sum[:token_count].astype(FULL) + after(output_near, query_low).astype(FULL)
+        middle + output_own.astype(FULL) + after(output_near, query_low).astype(FULL)
     ).astype(LOW)
     grads = jnp.concatenate([key_grads * HD**-0.5, value_grads], axis=1)
     shares = grads[WINDOW:]

time: 502 us -> 505 us (level)
  starting transfers between devices: 27.7 us -> 35.5 us
  Pallas kernels: 287 us -> 294 us
  local copies, waits for them, and re-layouts: 49 us -> 42 us
    ppermute x6, waiting for transfers between devices: 55.3 us -> 40.8 us  [around(): lax.ppermute(array, 'tok', [(i, (i + RING) % size) for i in range(size)])]
    ppermute x4, waiting for transfers between devices: 0.01 us -> 6.16 us  [passed_along(): return lax.ppermute(array, 'tok', pairs)]
    unnamed x112 -> x118, local copies, waits for them, and re-layouts: 24.3 us -> 29 us
  transfers between devices with their start and end apart: 26 -> 26, of which waited for: 6 -> 11; matrix products, arithmetic and copies ran while one was open for 15% -> 12% of each run, Pallas kernels for 51% -> 53%
where the time goes in v5:
time: 505 us; the launch traced here: 496 us
  Pallas kernels  294 us (58%)
  waiting for transfers between devices  62.6 us (12%)
  local copies, waits for them, and re-layouts  42 us (8%)
  starting transfers between devices  35.5 us (7%)
  matrix products  23.4 us (5%)
  other arithmetic  23.2 us (5%)
  between operations  15.3 us (3%)
    pallas_call x1, Pallas kernels, scatter(): pl.pallas_call(functools.partial(scatter_kernel, ring, bands, edges), in_...  52.3 us
    pallas_call x2, Pallas kernels, part(): pl.pallas_call(functools.partial(depth_kernel, ring, first, count, len(mo...  49.9 us
    pallas_call x4, Pallas kernels, outer_products(): pl.pallas_call(outer_kernel, grid_spec=pltpu.PrefetchScalarGridSpec(num_s...  47.2 us
    pallas_call x1, Pallas kernels, gather(): pl.pallas_call(functools.partial(gather_kernel, ring, bands), in_specs=[a...  46.3 us
    ppermute x6, waiting for transfers between devices, around(): lax.ppermute(array, 'tok', [(i, (i + RING) % size) for i in range(size)])  40.8 us
    pallas_call x2, Pallas kernels, project_sum(): pl.pallas_call(functools.partial(project_sum_kernel, count), grid=(4,), i...  35.2 us
    unnamed x118, local copies, waits for them, and re-layouts  29 us
    pallas_call x2, Pallas kernels, attend(): pl.pallas_call(functools.partial(attend_kernel, block, HD ** (-0.5) * LOG...  26 us
  transfers between devices with their start and end apart: 26, of which 11 were waited for; matrix products, arithmetic and copies ran while one was open for 12% of the time, Pallas kernels for 53%

profile of v5, /device:TPU:0, one launch (start us, length us, event | category | flops | bytes accessed | tf_op | source)
XLA Modules:
  0.0 495.7 jit_solution(1229302100043607015)
XLA Ops:
  9.8 1.6 fusion.30.attn_ref
  11.5 1.2 pad_maximum_fusion.2.ffn_ref
  12.7 46.3 %shard_map.222 = (bf16[4,2,2,2,48,1920]{5,4,3,2,1,0:T(8,128)(2,1)}, bf16[4,48,3456]{2,1,0:T(8,128)(2,1)}) custom-call(bf16[48,1920]{1,0:T(8,128)(2,1)} %fusion.30.attn_ref, bf16[4,48,3456]{2,1,0:T(8,128)(2,1)} %pad_maximum_fusion.2.ffn_ref), custom_call_target="tpu_custom_call" | custom-call | tf_op jit(solution)/shard_map/pallas_call | solution.py:211
  60.8 2.0 fusion.20
  65.0 5.9 %collective-permute-start = (bf16[512,256]{1,0:T(8,128)(2,1)S(1)}, bf16[512,256]{1,0:T(8,128)(2,1)}, u32[]{:S(2)}, u32[]{:S(2)}) collective-permute-start(bf16[512,256]{1,0:T(8,128)(2,1)S(1)} %pad_maximum_fusion.5), channel_id=1, source_target_pairs={{0,2},{1,3},{2,4},{3,5},{4,6},{5,7},{6,8},{7,9},{8,10},{9,11},{10,... | collective-permute-start | bytes 786440 | tf_op jit(solution)/shard_map/ppermute | solution.py:37
  70.9 2.8 collective-permute-start.1
  73.7 4.3 fusion.2.q_ref
  78.4 4.0 collective-permute-done
  85.3 1.2 copy.60.value_t_ref
  86.5 1.9 copy-done.10
  89.4 13.0 %shard_map.223 = (bf16[512,768]{1,0:T(8,128)(2,1)S(1)}, bf16[512,768]{1,0:T(8,128)(2,1)S(1)}, f32[6,1,512]{2,1,0:T(1,128)S(1)}) custom-call(f32[512,1536]{1,0:T(8,128)S(1)} %copy-done.10, bf16[1536,128]{1,0:T(8,128)(2,1)S(1)} %copy-done.15, bf16[128,1536]{1,0:T(8,128)(2,1)S(1)} %copy.60.value_t_ref, s32[1536,1]{1,0:T(8,128)S(1)} %broadcast_in_dim.33.ks_ref, ...), custom_call_target="tpu_custom_call" | custom-call | flops 1024 | bytes 1024 | tf_op jit(solution)/shard_map/pallas_call | solution.py:565
  104.1 9.4 %collective-permute-done.2.refs_6_ = bf16[192,3456]{1,0:T(8,128)(2,1)} collective-permute-done((bf16[192,3456]{1,0:T(8,128)(2,1)}, bf16[192,3456]{1,0:T(8,128)(2,1)}, u32[]{:S(2)}, u32[]{:S(2)}) %collective-permute-start.2) | collective-permute-done | bytes 1327136 | tf_op jit(solution)/shard_map/ppermute | solution.py:31
  113.6 3.5 collective-permute-start.4
  117.7 3.0 collective-permute-start.10
  120.7 13.0 %shard_map.224 = (bf16[512,768]{1,0:T(8,128)(2,1)S(1)}, bf16[512,768]{1,0:T(8,128)(2,1)S(1)}, f32[6,1,512]{2,1,0:T(1,128)S(1)}) custom-call(f32[512,1536]{1,0:T(8,128)S(1)} %copy-done.10, bf16[1536,128]{1,0:T(8,128)(2,1)S(1)} %copy-done.15, bf16[128,1536]{1,0:T(8,128)(2,1)S(1)} %copy.60.value_t_ref, s32[1536,1]{1,0:T(8,128)S(1)} %broadcast_in_dim.33.ks_ref, ...), custom_call_target="tpu_custom_call" | custom-call | flops 1024 | bytes 1024 | tf_op jit(solution)/shard_map/pallas_call | solution.py:565
  135.5 2.3 copy-done.5
  137.8 1.1 copy-done.17
  139.0 1.1 copy-done.20
  140.1 3.2 shard_map.225
  144.0 2.8 collective-permute-done.4.refs_8_
  146.8 1.5 collective-permute-done.5.refs_7_
  149.8 2.4 collective-permute-start.8
  152.2 2.7 constant_dynamic-update-slice_fusion.3
  154.9 2.7 constant_dynamic-update-slice_fusion.2.refs_2_
  157.6 2.9 collective-permute-start.11
  160.6 22.9 %collective-permute-done.7.refs_4_ = bf16[192,3456]{1,0:T(8,128)(2,1)} collective-permute-done((bf16[192,3456]{1,0:T(8,128)(2,1)}, bf16[192,3456]{1,0:T(8,128)(2,1)}, u32[]{:S(2)}, u32[]{:S(2)}) %collective-permute-start.7) | collective-permute-done | bytes 1327136 | tf_op jit(solution)/shard_map/ppermute | solution.py:31
  183.4 5.0 %collective-permute-done.6 = bf16[512,1536]{1,0:T(8,128)(2,1)S(1)} collective-permute-done((bf16[512,1536]{1,0:T(8,128)(2,1)S(1)}, bf16[512,1536]{1,0:T(8,128)(2,1)S(1)}, u32[]{:S(2)}, u32[]{:S(2)}) %collective-permute-start.6) | collective-permute-done | bytes 1572896 | tf_op jit(solution)/shard_map/ppermute | solution.py:26
  188.6 1.3 collective-permute-start.9
  190.4 4.9 collective-permute-done.9.refs_1_
  195.3 28.8 %shard_map.226 = (bf16[3,2048,1152]{2,1,0:T(8,128)(2,1)}, bf16[1536,3456]{1,0:T(8,128)(2,1)}) custom-call(bf16[1024,1536]{1,0:T(8,128)(2,1)} %copy-done, bf16[1024,1536]{1,0:T(8,128)(2,1)} %collective-permute-done.9.refs_1_, bf16[1024,1536]{1,0:T(8,128)(2,1)} %constant_dynamic-update-slice_fusion.2.refs_2_, ...), custom_call_target="tpu_custom_call" | custom-call | flops 1024 | bytes 1024 | tf_op jit(solution)/shard_map/pallas_call | solution.py:837
  224.1 1.9 copy-done.1
  226.0 21.1 %shard_map.227 = (bf16[3,2048,1152]{2,1,0:T(8,128)(2,1)}, bf16[1536,3456]{1,0:T(8,128)(2,1)}) custom-call(bf16[1024,1536]{1,0:T(8,128)(2,1)S(1)} %copy-done.1, bf16[1024,1536]{1,0:T(8,128)(2,1)} %collective-permute-done.9.refs_1_, bf16[1024,1536]{1,0:T(8,128)(2,1)} %constant_dynamic-update-slice_fusion.2.refs_2_, ...), custom_call_target="tpu_custom_call", output_to_operand_aliasing={{1}: (7, {})} | custom-call | flops 1024 | bytes 1024 | tf_op jit(solution)/shard_map/pallas_call | solution.py:837
  247.1 12.1 %shard_map.228 = (bf16[192,3456]{1,0:T(8,128)(2,1)}, bf16[192,3456]{1,0:T(8,128)(2,1)S(1)}) custom-call(s32[1]{0:T(128)} %bitcast.11.chunk_ref, bf16[1024,1536]{1,0:T(8,128)(2,1)S(1)} %copy-done.2, bf16[1024,1536]{1,0:T(8,128)(2,1)} %collective-permute-done.9.refs_1_, bf16[1024,1536]{1,0:T(8,128)(2,1)} %constant_dynamic-update-slice_fusion.2.refs_2_, ...), custom_call_target="tpu_custom_call" | custom-call | flops 1024 | bytes 1024 | tf_op jit(solution)/shard_map/pallas_call | solution.py:959
  260.8 12.0 %shard_map.229 = (bf16[192,3456]{1,0:T(8,128)(2,1)}, bf16[192,3456]{1,0:T(8,128)(2,1)S(1)}) custom-call(s32[1]{0:T(128)} %bitcast.10.chunk_ref, bf16[1024,1536]{1,0:T(8,128)(2,1)S(1)} %copy-done.2, bf16[1024,1536]{1,0:T(8,128)(2,1)} %collective-permute-done.9.refs_1_, bf16[1024,1536]{1,0:T(8,128)(2,1)} %constant_dynamic-update-slice_fusion.2.refs_2_, ...), custom_call_target="tpu_custom_call" | custom-call | flops 1024 | bytes 1024 | tf_op jit(solution)/shard_map/pallas_call | solution.py:959
  272.8 22.6 %shard_map.230 = (bf16[512,1536]{1,0:T(8,128)(2,1)S(1)}, bf16[512,1536]{1,0:T(8,128)(2,1)S(1)}) custom-call(bf16[3,2048,1152]{2,1,0:T(8,128)(2,1)} %get-tuple-element.146.refs_4_.array_ref, bf16[1536,3456]{1,0:T(8,128)(2,1)} %get-tuple-element.135.refs_0_.refs_1_, bf16[1536,3456]{1,0:T(8,128)(2,1)} %get-tuple-element.135.refs_0_.refs_1_), custom_call_target="tpu_custom_call" | custom-call | flops 1024 | bytes 1024 | tf_op jit(solution)/shard_map/pallas_call | solution.py:903
  295.5 3.7 add_convert_fusion.4
  299.3 1.6 collective-permute-start.14
  300.9 2.0 collective-permute-start.16
  302.9 12.0 %shard_map.231 = (bf16[192,3456]{1,0:T(8,128)(2,1)}, bf16[192,3456]{1,0:T(8,128)(2,1)S(1)}) custom-call(s32[1]{0:T(128)} %bitcast.12.chunk_ref, bf16[1024,1536]{1,0:T(8,128)(2,1)S(1)} %copy-done.2, bf16[1024,1536]{1,0:T(8,128)(2,1)} %collective-permute-done.9.refs_1_, bf16[1024,1536]{1,0:T(8,128)(2,1)} %constant_dynamic-update-slice_fusion.2.refs_2_, ...), custom_call_target="tpu_custom_call" | custom-call | flops 1024 | bytes 1024 | tf_op jit(solution)/shard_map/pallas_call | solution.py:959
  316.0 11.1 %shard_map.232 = (bf16[192,3456]{1,0:T(8,128)(2,1)S(1)}, bf16[192,3456]{1,0:T(8,128)(2,1)S(1)}) custom-call(s32[1]{0:T(128)} %bitcast.13.chunk_ref, bf16[1024,1536]{1,0:T(8,128)(2,1)S(1)} %copy-done.2, bf16[1024,1536]{1,0:T(8,128)(2,1)} %collective-permute-done.9.refs_1_, bf16[1024,1536]{1,0:T(8,128)(2,1)} %constant_dynamic-update-slice_fusion.2.refs_2_, ...), custom_call_target="tpu_custom_call" | custom-call | flops 1024 | bytes 1024 | tf_op jit(solution)/shard_map/pallas_call | solution.py:959
  327.1 5.7 %collective-permute-done.15 = bf16[192,3456]{1,0:T(8,128)(2,1)} collective-permute-done((bf16[192,3456]{1,0:T(8,128)(2,1)}, bf16[192,3456]{1,0:T(8,128)(2,1)}, u32[]{:S(2)}, u32[]{:S(2)}) %collective-permute-start.15) | collective-permute-done | bytes 1327136 | tf_op jit(solution)/shard_map/ppermute | solution.py:31
  332.9 3.4 add_convert_fusion.3
  336.4 1.6 collective-permute-start.18
  339.5 12.5 %shard_map.233 = (bf16[512,1536]{1,0:T(8,128)(2,1)S(1)}, bf16[512,1536]{1,0:T(8,128)(2,1)S(1)}) custom-call(bf16[3,2048,1152]{2,1,0:T(8,128)(2,1)} %get-tuple-element.146.refs_4_.array_ref, bf16[1536,3456]{1,0:T(8,128)(2,1)} %get-tuple-element.135.refs_0_.refs_1_), custom_call_target="tpu_custom_call" | custom-call | flops 1024 | bytes 1024 | tf_op jit(solution)/shard_map/pallas_call | solution.py:903
  352.1 1.1 copy-done.27
  353.2 1.1 copy-done.43
  354.3 1.2 copy-done.49
  355.5 8.7 %shard_map.234 = (f32[512,1536]{1,0:T(8,128)}, bf16[512,1536]{1,0:T(8,128)(2,1)S(1)}, bf16[512,1536]{1,0:T(8,128)(2,1)S(1)}, bf16[512,1536]{1,0:T(8,128)(2,1)S(1)}) custom-call(bf16[512,1536]{1,0:T(8,128)(2,1)} %copy-done.22, bf16[512,1536]{1,0:T(8,128)(2,1)} %copy-done.49, bf16[512,1536]{1,0:T(8,128)(2,1)} %cot_ref.1, f32[512,1536]{1,0:T(8,128)} %copy-done.11, ...), custom_call_target="tpu_custom_call" | custom-call | flops 1024 | bytes 1024 | tf_op jit(solution)/shard_map/pallas_call | solution.py:1037
  365.3 1.2 copy-done.25
  366.5 4.4 convolution_convert_fusion
  370.9 2.1 collective-permute-start.17
  373.0 2.7 add_convert_fusion.2
  376.6 25.0 %shard_map.235 = (bf16[512,1536]{1,0:T(8,128)(2,1)S(1)}, f32[1536,128]{1,0:T(8,128)S(1)}, f32[1536,128]{1,0:T(8,128)S(1)}) custom-call(bf16[512,1536]{1,0:T(8,128)(2,1)S(1)} %pad_maximum_fusion.1.rot_ref, bf16[512,1536]{1,0:T(8,128)(2,1)S(1)} %copy-done.24, bf16[512,1536]{1,0:T(8,128)(2,1)S(1)} %constant_dynamic-update-slice_fusion.4.mixed_ref, ...), custom_call_target="tpu_custom_call" | custom-call | flops 1024 | bytes 1024 | tf_op jit(solution)/shard_map/pallas_call | solution.py:631
  401.9 1.3 collective-permute-start.20
  403.2 1.3 collective-permute-start.21
  404.5 5.0 %fusion = f32[512,1536]{1,0:T(8,128)S(1)} fusion(bf16[512,1536]{1,0:T(8,128)(2,1)S(1)} %get-tuple-element.163, bf16[1536,1920]{1,0:T(8,128)(2,1)} %bitcast.67), kind=kOutput, calls=%fused_computation.7 | convolution fusion | flops 2415919104 | bytes 9437184 | tf_op jit(solution)/shard_map/dot_general | solution.py:51
  409.5 3.1 convolution_convert_fusion.1
  412.7 1.9 add_convert_fusion
  414.5 2.1 collective-permute-done.21
  417.2 2.1 fusion.11
  423.3 2.0 fusion.10
  425.9 52.3 %shard_map.236 = (f32[48,1920]{1,0:T(8,128)S(1)}, bf16[4,48,3456]{2,1,0:T(8,128)(2,1)S(1)}) custom-call(bf16[4,2,2,2,48,1536]{5,4,3,2,1,0:T(8,128)(2,1)S(1)} %bitcast.52, bf16[4,2,2,2,48,256]{5,4,3,2,1,0:T(8,128)(2,1)S(1)} %bitcast.54, bf16[4,2,2,2,48,128]{5,4,3,2,1,0:T(8,128)(2,1)S(1)} %bitcast.53, bf16[4,48,3456]{2,1,0:T(8,128)(2,1)S(1)} %bitcast.51), custom_call_target="tpu_custom_call" | custom-call | tf_op jit(solution)/shard_map/pallas_call | solution.py:405
  483.4 3.4 reduce-scatter.2.cloned.1.call-done
  486.7 1.6 convert_element_type.158
  (186 shorter events, 34.6 us)
Async XLA Ops:
  7.2 4.3 copy-start.52
  7.2 4.3 copy-start.51
  7.2 128.3 %all-gather.2.cloned.1.call-start = ((), (), s32[]{:S(2)}) async-start(), calls=%async_computation.1 | async-start | bytes 4866048 | tf_op jit(solution)/shard_map/all_gather | solution.py:1102
  7.9 478.8 %reduce-scatter.2.cloned.1.call-start = ((), (), s32[]{:S(2)}) async-start(), calls=%async_computation.2 | async-start | bytes 4866048 | tf_op jit(solution)/shard_map/reduce_scatter | solution.py:1151
  12.7 47.6 %copy-start.54 = (s32[512]{0:T(512)S(1)}, s32[512]{0:T(512)}, u32[]{:S(2)}) copy-start(s32[512]{0:T(512)} %param.33) | copy-start | bytes 6148
  12.7 47.6 %copy-start.3 = (bf16[512,1536]{1,0:T(8,128)(2,1)S(1)}, bf16[512,1536]{1,0:T(8,128)(2,1)}, u32[]{:S(2)}) copy-start(bf16[512,1536]{1,0:T(8,128)(2,1)} %refs_0_.1) | copy-start | bytes 4718596
  60.3 13.3 %slice-start = ((s8[5898240]{0:T(1024)(128)(4,1)}), s8[4194304]{0:T(1024)(128)(4,1)S(1)}, s32[]{:S(2)}) async-start(s8[5898240]{0:T(1024)(128)(4,1)} %bitcast.69), calls=%async_computation.3 | async-start | bytes 8388608
  60.7 12.9 %slice-start.1 = ((s8[5898240]{0:T(1024)(128)(4,1)}), s8[1703936]{0:T(1024)(128)(4,1)S(1)}, s32[]{:S(2)}) async-start(s8[5898240]{0:T(1024)(128)(4,1)} %bitcast.69), calls=%async_computation.4 | async-start | bytes 3407872
  64.9 55.8 %copy-start.13 = (f32[512,128]{1,0:T(8,128)}, f32[512,128]{1,0:T(8,128)S(1)}, u32[]{:S(2)}) copy-start(f32[512,128]{1,0:T(8,128)S(1)} %get-tuple-element.192.cos_ref) | copy-start | bytes 786436
  65.0 17.4 %collective-permute-start = (bf16[512,256]{1,0:T(8,128)(2,1)S(1)}, bf16[512,256]{1,0:T(8,128)(2,1)}, u32[]{:S(2)}, u32[]{:S(2)}) collective-permute-start(bf16[512,256]{1,0:T(8,128)(2,1)S(1)} %pad_maximum_fusion.5), channel_id=1, source_target_pairs={{0,2},{1,3},{2,4},{3,5},{4,6},{5,7},{6,8},{7,9},{8,10},{9,11},{10,... | collective-permute-start | bytes 786440 | tf_op jit(solution)/shard_map/ppermute | solution.py:37
  70.9 11.5 %collective-permute-start.1 = (bf16[512,256]{1,0:T(8,128)(2,1)S(1)}, bf16[512,256]{1,0:T(8,128)(2,1)}, u32[]{:S(2)}, u32[]{:S(2)}) collective-permute-start(bf16[512,256]{1,0:T(8,128)(2,1)S(1)} %pad_maximum_fusion.5), channel_id=1, source_target_pairs={{0,1},{1,2},{2,3},{3,4},{4,5},{5,6},{6,7},{7,8},{8,9},{9,10},{10,1... | collective-permute-start | bytes 786440 | tf_op jit(solution)/shard_map/ppermute | solution.py:37
  73.6 4.3 copy-start.53
  73.6 40.0 %collective-permute-start.2 = (bf16[192,3456]{1,0:T(8,128)(2,1)}, bf16[192,3456]{1,0:T(8,128)(2,1)}, u32[]{:S(2)}, u32[]{:S(2)}) collective-permute-start(bf16[192,3456]{1,0:T(8,128)(2,1)} %bitcast.9.refs_4_), channel_id=1, source_target_pairs={{0,8},{1,9},{2,10},{3,11},{4,12},{5,13},{6,14},{7,15},{8,16},{9,17... | collective-permute-start | bytes 3981320 | tf_op jit(solution)/shard_map/ppermute | solution.py:31
  73.6 40.0 %collective-permute-start.3 = (bf16[192,3456]{1,0:T(8,128)(2,1)}, bf16[192,3456]{1,0:T(8,128)(2,1)}, u32[]{:S(2)}, u32[]{:S(2)}) collective-permute-start(bf16[192,3456]{1,0:T(8,128)(2,1)} %bitcast.9.refs_4_), channel_id=1, source_target_pairs={{0,4},{1,5},{2,6},{3,7},{4,0},{5,1},{6,2},{7,3},{8,12},{9,13},{10,... | collective-permute-start | bytes 3981320 | tf_op jit(solution)/shard_map/ppermute | solution.py:26
  78.3 42.4 %copy-start.6 = (s32[1536,1]{1,0:T(8,128)}, s32[1536,1]{1,0:T(8,128)S(1)}, u32[]{:S(2)}) copy-start(s32[1536,1]{1,0:T(8,128)S(1)} %broadcast_in_dim.33.ks_ref) | copy-start | bytes 18436
  86.5 1.9 copy-start.10
  113.6 33.2 %collective-permute-start.4 = (bf16[192,3456]{1,0:T(8,128)(2,1)}, bf16[192,3456]{1,0:T(8,128)(2,1)}, u32[]{:S(2)}, u32[]{:S(2)}) collective-permute-start(bf16[192,3456]{1,0:T(8,128)(2,1)} %collective-permute-done.2.refs_6_), channel_id=1, source_target_pairs={{0,8},{1,9},{2,10},{3,11},{4,12},{5,13},{6,14},{7,15},{8,16},{9,17... | collective-permute-start | bytes 3981320 | tf_op jit(solution)/shard_map/ppermute | solution.py:31
  117.1 31.2 %collective-permute-start.5 = (bf16[192,3456]{1,0:T(8,128)(2,1)}, bf16[192,3456]{1,0:T(8,128)(2,1)}, u32[]{:S(2)}, u32[]{:S(2)}) collective-permute-start(bf16[192,3456]{1,0:T(8,128)(2,1)} %collective-permute-done.2.refs_6_), channel_id=1, source_target_pairs={{0,4},{1,5},{2,6},{3,7},{4,0},{5,1},{6,2},{7,3},{8,12},{9,13},{10,... | collective-permute-start | bytes 3981320 | tf_op jit(solution)/shard_map/ppermute | solution.py:26
  117.7 37.1 %collective-permute-start.10 = (bf16[512,1536]{1,0:T(8,128)(2,1)}, bf16[512,1536]{1,0:T(8,128)(2,1)}, u32[]{:S(2)}, u32[]{:S(2)}) collective-permute-start(bf16[512,1536]{1,0:T(8,128)(2,1)} %cot_ref.1), channel_id=1, source_target_pairs={{0,2},{1,3},{2,0},{3,1},{4,6},{5,7},{6,4},{7,5},{8,10},{9,11},{10,... | collective-permute-start | bytes 4718600 | tf_op jit(solution)/shard_map/ppermute | solution.py:26
  135.5 2.3 copy-start.5
  144.0 10.9 %copy-start.11 = (f32[512,1536]{1,0:T(8,128)}, f32[512,1536]{1,0:T(8,128)S(1)}, u32[]{:S(2)}) copy-start(f32[512,1536]{1,0:T(8,128)S(1)} %get-tuple-element.117.middle_ref) | copy-start | bytes 9437188
  148.3 40.2 %collective-permute-start.6 = (bf16[512,1536]{1,0:T(8,128)(2,1)S(1)}, bf16[512,1536]{1,0:T(8,128)(2,1)S(1)}, u32[]{:S(2)}, u32[]{:S(2)}) collective-permute-start(bf16[512,1536]{1,0:T(8,128)(2,1)S(1)} %get-tuple-element.121), channel_id=1, source_target_pairs={{0,2},{1,3},{2,0},{3,1},{4,6},{5,7},{6,4},{7,5},{8,10},{9,11},{10,... | collective-permute-start | bytes 4718600 | tf_op jit(solution)/shard_map/ppermute | solution.py:26
  149.3 34.1 %collective-permute-start.7 = (bf16[192,3456]{1,0:T(8,128)(2,1)}, bf16[192,3456]{1,0:T(8,128)(2,1)}, u32[]{:S(2)}, u32[]{:S(2)}) collective-permute-start(bf16[192,3456]{1,0:T(8,128)(2,1)} %collective-permute-done.4.refs_8_), channel_id=1, source_target_pairs={{0,8},{1,9},{2,10},{3,11},{4,12},{5,13},{6,14},{7,15},{8,16},{9,17... | collective-permute-start | bytes 3981320 | tf_op jit(solution)/shard_map/ppermute | solution.py:31
  149.8 33.6 %collective-permute-start.8 = (bf16[192,3456]{1,0:T(8,128)(2,1)}, bf16[192,3456]{1,0:T(8,128)(2,1)S(1)}, u32[]{:S(2)}, u32[]{:S(2)}) collective-permute-start(bf16[192,3456]{1,0:T(8,128)(2,1)} %collective-permute-done.4.refs_8_), channel_id=1, source_target_pairs={{0,4},{1,5},{2,6},{3,7},{4,0},{5,1},{6,2},{7,3},{8,12},{9,13},{10,... | collective-permute-start | bytes 3981320 | tf_op jit(solution)/shard_map/ppermute | solution.py:26
  157.6 32.8 %collective-permute-start.11 = (bf16[1024,1536]{1,0:T(8,128)(2,1)}, bf16[1024,1536]{1,0:T(8,128)(2,1)}, u32[]{:S(2)}, u32[]{:S(2)}) collective-permute-start(bf16[1024,1536]{1,0:T(8,128)(2,1)} %constant_dynamic-update-slice_fusion.2.refs_2_), channel_id=1, source_target_pairs={{0,1},{1,0},{2,3},{3,2},{4,5},{5,4},{6,7},{7,6},{8,9},{9,8},{10,11... | collective-permute-start | bytes 9437192 | tf_op jit(solution)/shard_map/ppermute | solution.py:26
  183.4 5.1 %copy-start.50 = (bf16[192,3456]{1,0:T(8,128)(2,1)}, bf16[192,3456]{1,0:T(8,128)(2,1)S(1)}, u32[]{:S(2)}) copy-start(bf16[192,3456]{1,0:T(8,128)(2,1)S(1)} %collective-permute-done.8.refs_9_) | copy-start | bytes 3981316
  188.6 6.7 %copy-start = (bf16[1024,1536]{1,0:T(8,128)(2,1)}, bf16[1024,1536]{1,0:T(8,128)(2,1)S(1)}, u32[]{:S(2)}) copy-start(bf16[1024,1536]{1,0:T(8,128)(2,1)S(1)} %constant_dynamic-update-slice_fusion.refs_0_) | copy-start | bytes 9437188
  188.6 6.7 %collective-permute-start.9 = (bf16[1024,1536]{1,0:T(8,128)(2,1)S(1)}, bf16[1024,1536]{1,0:T(8,128)(2,1)}, u32[]{:S(2)}, u32[]{:S(2)}) collective-permute-start(bf16[1024,1536]{1,0:T(8,128)(2,1)S(1)} %constant_dynamic-update-slice_fusion.refs_0_), channel_id=1, source_target_pairs={{0,1},{1,0},{2,3},{3,2},{4,5},{5,4},{6,7},{7,6},{8,9},{9,8},{10,11... | collective-permute-start | bytes 9437192 | tf_op jit(solution)/shard_map/ppermute | solution.py:26
  189.9 34.2 %collective-permute-start.12 = (bf16[192,3456]{1,0:T(8,128)(2,1)}, bf16[192,3456]{1,0:T(8,128)(2,1)}, u32[]{:S(2)}, u32[]{:S(2)}) collective-permute-start(bf16[192,3456]{1,0:T(8,128)(2,1)} %collective-permute-done.7.refs_4_), channel_id=1, source_target_pairs={{0,4},{1,5},{2,6},{3,7},{4,0},{5,1},{6,2},{7,3},{8,12},{9,13},{10,... | collective-permute-start | bytes 3981320 | tf_op jit(solution)/shard_map/ppermute | solution.py:26
  224.1 1.9 copy-start.1
  226.0 21.1 %copy-start.2 = (bf16[1024,1536]{1,0:T(8,128)(2,1)S(1)}, bf16[1024,1536]{1,0:T(8,128)(2,1)}, u32[]{:S(2)}) copy-start(bf16[1024,1536]{1,0:T(8,128)(2,1)} %copy-done) | copy-start | bytes 9437188
  260.3 35.2 %collective-permute-start.13 = (bf16[192,3456]{1,0:T(8,128)(2,1)}, bf16[192,3456]{1,0:T(8,128)(2,1)}, u32[]{:S(2)}, u32[]{:S(2)}) collective-permute-start(bf16[192,3456]{1,0:T(8,128)(2,1)} %get-tuple-element.129), channel_id=1, source_target_pairs={{0,4},{1,5},{2,6},{3,7},{4,0},{5,1},{6,2},{7,3},{8,12},{9,13},{10,... | collective-permute-start | bytes 3981320 | tf_op jit(solution)/shard_map/ppermute | solution.py:26
  272.8 22.7 %copy-start.32 = (bf16[192,3456]{1,0:T(8,128)(2,1)}, bf16[192,3456]{1,0:T(8,128)(2,1)S(1)}, u32[]{:S(2)}) copy-start(bf16[192,3456]{1,0:T(8,128)(2,1)S(1)} %get-tuple-element.131) | copy-start | bytes 3981316
  272.8 22.7 %copy-start.35 = (bf16[192,3456]{1,0:T(8,128)(2,1)S(1)}, bf16[192,3456]{1,0:T(8,128)(2,1)}, u32[]{:S(2)}) copy-start(bf16[192,3456]{1,0:T(8,128)(2,1)} %copy-done.34) | copy-start | bytes 3981316
  295.5 3.8 copy-start.22
  295.5 3.8 copy-start.42
  299.3 33.6 %collective-permute-start.15 = (bf16[192,3456]{1,0:T(8,128)(2,1)}, bf16[192,3456]{1,0:T(8,128)(2,1)}, u32[]{:S(2)}, u32[]{:S(2)}) collective-permute-start(bf16[192,3456]{1,0:T(8,128)(2,1)} %add_convert_fusion.4), channel_id=1, source_target_pairs={{0,8},{1,9},{2,10},{3,11},{4,12},{5,13},{6,14},{7,15},{8,16},{9,17... | collective-permute-start | bytes 3981320 | tf_op jit(solution)/shard_map/ppermute | solution.py:31
  299.3 33.6 %collective-permute-start.14 = (bf16[192,3456]{1,0:T(8,128)(2,1)}, bf16[192,3456]{1,0:T(8,128)(2,1)}, u32[]{:S(2)}, u32[]{:S(2)}) collective-permute-start(bf16[192,3456]{1,0:T(8,128)(2,1)} %get-tuple-element.138), channel_id=1, source_target_pairs={{0,4},{1,5},{2,6},{3,7},{4,0},{5,1},{6,2},{7,3},{8,12},{9,13},{10,... | collective-permute-start | bytes 3981320 | tf_op jit(solution)/shard_map/ppermute | solution.py:26
  300.9 53.5 %collective-permute-start.16 = (bf16[512,1536]{1,0:T(8,128)(2,1)}, bf16[512,1536]{1,0:T(8,128)(2,1)S(1)}, u32[]{:S(2)}, u32[]{:S(2)}) collective-permute-start(bf16[512,1536]{1,0:T(8,128)(2,1)} %copy-done.42), channel_id=1, source_target_pairs={{0,2},{1,3},{2,0},{3,1},{4,6},{5,7},{6,4},{7,5},{8,10},{9,11},{10,... | collective-permute-start | bytes 4718600 | tf_op jit(solution)/shard_map/ppermute | solution.py:26
  316.0 16.8 %copy-start.33 = (bf16[192,3456]{1,0:T(8,128)(2,1)S(1)}, bf16[192,3456]{1,0:T(8,128)(2,1)}, u32[]{:S(2)}) copy-start(bf16[192,3456]{1,0:T(8,128)(2,1)} %copy-done.32) | copy-start | bytes 3981316
  327.1 9.2 %copy-start.29 = (bf16[192,3456]{1,0:T(8,128)(2,1)}, bf16[192,3456]{1,0:T(8,128)(2,1)S(1)}, u32[]{:S(2)}) copy-start(bf16[192,3456]{1,0:T(8,128)(2,1)S(1)} %get-tuple-element.169) | copy-start | bytes 3981316
  327.1 9.2 %copy-start.44 = (bf16[192,3456]{1,0:T(8,128)(2,1)}, bf16[192,3456]{1,0:T(8,128)(2,1)S(1)}, u32[]{:S(2)}) copy-start(bf16[192,3456]{1,0:T(8,128)(2,1)S(1)} %get-tuple-element.159) | copy-start | bytes 3981316
  332.9 5.2 %copy-start.18 = (bf16[512,768]{1,0:T(8,128)(2,1)S(1)}, bf16[512,768]{1,0:T(8,128)(2,1)}, u32[]{:S(2)}) copy-start(bf16[512,768]{1,0:T(8,128)(2,1)} %copy-done.16) | copy-start | bytes 2359300
  336.3 1.8 copy-start.21
  336.3 36.7 %collective-permute-start.19 = (bf16[192,3456]{1,0:T(8,128)(2,1)}, bf16[192,3456]{1,0:T(8,128)(2,1)}, u32[]{:S(2)}, u32[]{:S(2)}) collective-permute-start(bf16[192,3456]{1,0:T(8,128)(2,1)} %add_convert_fusion.3), channel_id=1, source_target_pairs={{0,8},{1,9},{2,10},{3,11},{4,12},{5,13},{6,14},{7,15},{8,16},{9,17... | collective-permute-start | bytes 3981320 | tf_op jit(solution)/shard_map/ppermute | solution.py:31
  336.4 36.6 %collective-permute-start.18 = (bf16[192,3456]{1,0:T(8,128)(2,1)}, bf16[192,3456]{1,0:T(8,128)(2,1)}, u32[]{:S(2)}, u32[]{:S(2)}) collective-permute-start(bf16[192,3456]{1,0:T(8,128)(2,1)} %get-tuple-element.145), channel_id=1, source_target_pairs={{0,4},{1,5},{2,6},{3,7},{4,0},{5,1},{6,2},{7,3},{8,12},{9,13},{10,... | collective-permute-start | bytes 3981320 | tf_op jit(solution)/shard_map/ppermute | solution.py:26
  339.5 16.0 %copy-start.41 = (f32[512,128]{1,0:T(8,128)S(1)}, f32[512,128]{1,0:T(8,128)}, u32[]{:S(2)}) copy-start(f32[512,128]{1,0:T(8,128)} %copy-done.40) | copy-start | bytes 786436
  370.9 41.7 %collective-permute-start.17 = (bf16[512,1536]{1,0:T(8,128)(2,1)}, bf16[512,1536]{1,0:T(8,128)(2,1)S(1)}, u32[]{:S(2)}, u32[]{:S(2)}) collective-permute-start(bf16[512,1536]{1,0:T(8,128)(2,1)} %copy-done.43), channel_id=1, source_target_pairs={{0,2},{1,3},{2,0},{3,1},{4,6},{5,7},{6,4},{7,5},{8,10},{9,11},{10,... | collective-permute-start | bytes 4718600 | tf_op jit(solution)/shard_map/ppermute | solution.py:26
  373.0 3.2 copy-start.45
  373.0 3.5 copy-start.7
  373.0 3.5 copy-start.9
  373.0 3.5 copy-start.14
  373.0 3.5 copy-start.24
  375.8 49.5 %collective-permute-start.23 = (bf16[192,3456]{1,0:T(8,128)(2,1)S(1)}, bf16[192,3456]{1,0:T(8,128)(2,1)S(1)}, u32[]{:S(2)}, u32[]{:S(2)}) collective-permute-start(bf16[192,3456]{1,0:T(8,128)(2,1)S(1)} %add_convert_fusion.2), channel_id=1, source_target_pairs={{0,8},{1,9},{2,10},{3,11},{4,12},{5,13},{6,14},{7,15},{8,16},{9,17... | collective-permute-start | bytes 3981320 | tf_op jit(solution)/shard_map/ppermute | solution.py:31
  376.2 49.1 %collective-permute-start.22 = (bf16[192,3456]{1,0:T(8,128)(2,1)S(1)}, bf16[192,3456]{1,0:T(8,128)(2,1)S(1)}, u32[]{:S(2)}, u32[]{:S(2)}) collective-permute-start(bf16[192,3456]{1,0:T(8,128)(2,1)S(1)} %copy-done.45), channel_id=1, source_target_pairs={{0,4},{1,5},{2,6},{3,7},{4,0},{5,1},{6,2},{7,3},{8,12},{9,13},{10,... | collective-permute-start | bytes 3981320 | tf_op jit(solution)/shard_map/ppermute | solution.py:26
  401.9 12.7 %collective-permute-start.20 = (bf16[512,256]{1,0:T(8,128)(2,1)S(1)}, bf16[512,256]{1,0:T(8,128)(2,1)S(1)}, u32[]{:S(2)}, u32[]{:S(2)}) collective-permute-start(bf16[512,256]{1,0:T(8,128)(2,1)S(1)} %get-tuple-element.182), channel_id=1, source_target_pairs={{1,0},{2,1},{3,2},{4,3},{5,4},{6,5},{7,6},{8,7},{9,8},{10,9},{11,1... | collective-permute-start | bytes 786440 | tf_op jit(solution)/shard_map/ppermute | solution.py:37
  403.2 13.5 %collective-permute-start.21 = (bf16[512,256]{1,0:T(8,128)(2,1)S(1)}, bf16[512,256]{1,0:T(8,128)(2,1)S(1)}, u32[]{:S(2)}, u32[]{:S(2)}) collective-permute-start(bf16[512,256]{1,0:T(8,128)(2,1)S(1)} %get-tuple-element.183), channel_id=1, source_target_pairs={{2,0},{3,1},{4,2},{5,3},{6,4},{7,5},{8,6},{9,7},{10,8},{11,9},{12,... | collective-permute-start | bytes 786440 | tf_op jit(solution)/shard_map/ppermute | solution.py:37
  404.5 5.0 %copy-start.4 = (bf16[512,1536]{1,0:T(8,128)(2,1)S(1)}, bf16[512,1536]{1,0:T(8,128)(2,1)}, u32[]{:S(2)}) copy-start(bf16[512,1536]{1,0:T(8,128)(2,1)} %refs_0_.1) | copy-start | bytes 4718596
  409.5 3.2 copy-start.12
  409.5 3.2 copy-start.28
  414.5 2.4 copy-start.48
  420.3 1.8 copy-start.26
  420.3 3.0 copy-start.46
  423.3 2.0 copy-start.30
  (19 other events, 19.5 us)
Sparse Core Ops, SparseCore 0:
  10.9 105.4 all-gather.1
  371.0 115.6 reduce-scatter.1

commit v6 on v5

--- a/solution.py
+++ b/solution.py
@@ -1148,7 +1148,8 @@
         own_sum, after(near_sent, output_own), cotangent, middle, inverse_two, gain_two, out_w
     )
     grad_out_w = outer_sum(branch, mixed).astype(LOW)
-    out_sum = lax.psum_scatter(grad_out_w, "tok", scatter_dimension=0, tiled=True).astype(FULL)
+    cut = heads_width // 2
+    out_sum = lax.psum_scatter(grad_out_w[:, :cut], "tok", scatter_dimension=0, tiled=True)
     marks = reduction.advance(2, grad_mixed)
     query_low, key_grads, value_grads = attend_back(
         rot, after(grad_mixed, *marks), mixed, logs, all_keys, key_segments, query_segments, cosine, sine
@@ -1178,7 +1179,7 @@
     ).astype(LOW)
     reduction.advance(3, grad_query_w)
     attn_sum, ffn_parts = scatter(
-        [grad_query_w, grad_kv_w, grad_gains], reduction.result()
+        [grad_query_w, grad_kv_w, grad_gains, grad_out_w[:, cut:]], reduction.result()
     )
 
     def joined(parts):
@@ -1192,7 +1193,7 @@
         attn_sum[:, :heads_width],
         attn_sum[:, heads_width : heads_width + HD],
         attn_sum[:, heads_width + HD : edge],
-        out_sum,
+        jnp.concatenate([out_sum.astype(FULL), attn_sum[:, edge + HD :]], axis=1),
         joined(ffn_parts[:, :, :slice_width]),
         joined(ffn_parts[:, :, slice_width : 2 * slice_width]),
         joined(ffn_parts[:, :, 2 * slice_width :]),

time: 505 us -> 502 us (level)
  waiting for transfers between devices: 62.6 us -> 56.2 us
    unnamed x118 -> x124, local copies, waits for them, and re-layouts: 29 us -> 27.7 us
  transfers between devices with their start and end apart: 26 -> 26, of which waited for: 11 -> 9; matrix products, arithmetic and copies ran while one was open for 12% -> 12% of each run, Pallas kernels for 53% -> 54%
where the time goes in v6:
time: 502 us; the launch traced here: 492 us
  Pallas kernels  298 us (59%)
  waiting for transfers between devices  56.2 us (11%)
  local copies, waits for them, and re-layouts  42.4 us (8%)
  starting transfers between devices  36.3 us (7%)
  other arithmetic  24.2 us (5%)
  matrix products  19.9 us (4%)
  between operations  15.3 us (3%)
    pallas_call x1, Pallas kernels, scatter(): pl.pallas_call(functools.partial(scatter_kernel, ring, bands, edges), in_...  57.3 us
    pallas_call x2, Pallas kernels, part(): pl.pallas_call(functools.partial(depth_kernel, ring, first, count, len(mo...  49.8 us
    pallas_call x4, Pallas kernels, outer_products(): pl.pallas_call(outer_kernel, grid_spec=pltpu.PrefetchScalarGridSpec(num_s...  47.3 us
    pallas_call x1, Pallas kernels, gather(): pl.pallas_call(functools.partial(gather_kernel, ring, bands), in_specs=[a...  46.3 us
    ppermute x6, waiting for transfers between devices, around(): lax.ppermute(array, 'tok', [(i, (i + RING) % size) for i in range(size)])  38 us
    pallas_call x2, Pallas kernels, project_sum(): pl.pallas_call(functools.partial(project_sum_kernel, count), grid=(4,), i...  35.1 us
    unnamed x124, local copies, waits for them, and re-layouts  27.7 us
    pallas_call x2, Pallas kernels, attend(): pl.pallas_call(functools.partial(attend_kernel, block, HD ** (-0.5) * LOG...  25.9 us
  transfers between devices with their start and end apart: 26, of which 9 were waited for; matrix products, arithmetic and copies ran while one was open for 12% of the time, Pallas kernels for 54%

profile of v6, /device:TPU:0, one launch (start us, length us, event | category | flops | bytes accessed | tf_op | source)
XLA Modules:
  0.0 492.2 jit_solution(3531488578982667843)
XLA Ops:
  9.8 1.6 fusion.30.attn_ref
  11.5 1.2 pad_maximum_fusion.2.ffn_ref
  12.7 46.3 %shard_map.222 = (bf16[4,2,2,2,48,1920]{5,4,3,2,1,0:T(8,128)(2,1)}, bf16[4,48,3456]{2,1,0:T(8,128)(2,1)}) custom-call(bf16[48,1920]{1,0:T(8,128)(2,1)} %fusion.30.attn_ref, bf16[4,48,3456]{2,1,0:T(8,128)(2,1)} %pad_maximum_fusion.2.ffn_ref), custom_call_target="tpu_custom_call" | custom-call | tf_op jit(solution)/shard_map/pallas_call | solution.py:211
  60.8 2.0 fusion.20
  65.0 5.9 %collective-permute-start = (bf16[512,256]{1,0:T(8,128)(2,1)S(1)}, bf16[512,256]{1,0:T(8,128)(2,1)}, u32[]{:S(2)}, u32[]{:S(2)}) collective-permute-start(bf16[512,256]{1,0:T(8,128)(2,1)S(1)} %pad_maximum_fusion.6), channel_id=1, source_target_pairs={{0,2},{1,3},{2,4},{3,5},{4,6},{5,7},{6,8},{7,9},{8,10},{9,11},{10,... | collective-permute-start | bytes 786440 | tf_op jit(solution)/shard_map/ppermute | solution.py:37
  70.9 2.8 collective-permute-start.1
  73.7 4.3 fusion.2.q_ref
  78.5 4.0 collective-permute-done
  85.3 1.2 copy.60.value_t_ref
  86.5 1.9 copy-done.10
  89.4 13.0 %shard_map.223 = (bf16[512,768]{1,0:T(8,128)(2,1)S(1)}, bf16[512,768]{1,0:T(8,128)(2,1)S(1)}, f32[6,1,512]{2,1,0:T(1,128)S(1)}) custom-call(f32[512,1536]{1,0:T(8,128)S(1)} %copy-done.10, bf16[1536,128]{1,0:T(8,128)(2,1)S(1)} %copy-done.18, bf16[128,1536]{1,0:T(8,128)(2,1)S(1)} %copy.60.value_t_ref, s32[1536,1]{1,0:T(8,128)S(1)} %broadcast_in_dim.33.ks_ref, ...), custom_call_target="tpu_custom_call" | custom-call | flops 1024 | bytes 1024 | tf_op jit(solution)/shard_map/pallas_call | solution.py:565
  104.1 9.5 %collective-permute-done.2.refs_6_ = bf16[192,3456]{1,0:T(8,128)(2,1)} collective-permute-done((bf16[192,3456]{1,0:T(8,128)(2,1)}, bf16[192,3456]{1,0:T(8,128)(2,1)}, u32[]{:S(2)}, u32[]{:S(2)}) %collective-permute-start.2) | collective-permute-done | bytes 1327136 | tf_op jit(solution)/shard_map/ppermute | solution.py:31
  113.6 3.5 collective-permute-start.4
  117.8 3.0 collective-permute-start.10
  120.7 13.0 %shard_map.224 = (bf16[512,768]{1,0:T(8,128)(2,1)S(1)}, bf16[512,768]{1,0:T(8,128)(2,1)S(1)}, f32[6,1,512]{2,1,0:T(1,128)S(1)}) custom-call(f32[512,1536]{1,0:T(8,128)S(1)} %copy-done.10, bf16[1536,128]{1,0:T(8,128)(2,1)S(1)} %copy-done.18, bf16[128,1536]{1,0:T(8,128)(2,1)S(1)} %copy.60.value_t_ref, s32[1536,1]{1,0:T(8,128)S(1)} %broadcast_in_dim.33.ks_ref, ...), custom_call_target="tpu_custom_call" | custom-call | flops 1024 | bytes 1024 | tf_op jit(solution)/shard_map/pallas_call | solution.py:565
  135.5 2.3 copy-done.5
  137.8 1.1 copy-done.20
  139.0 1.1 copy-done.22
  140.1 3.2 shard_map.225
  144.0 2.8 collective-permute-done.4.refs_8_
  146.8 1.5 collective-permute-done.5.refs_7_
  149.9 2.4 collective-permute-start.8
  152.2 2.7 constant_dynamic-update-slice_fusion.3
  154.9 2.7 constant_dynamic-update-slice_fusion.2.refs_2_
  157.6 2.9 collective-permute-start.11
  160.5 22.9 %collective-permute-done.7.refs_4_ = bf16[192,3456]{1,0:T(8,128)(2,1)} collective-permute-done((bf16[192,3456]{1,0:T(8,128)(2,1)}, bf16[192,3456]{1,0:T(8,128)(2,1)}, u32[]{:S(2)}, u32[]{:S(2)}) %collective-permute-start.7) | collective-permute-done | bytes 1327136 | tf_op jit(solution)/shard_map/ppermute | solution.py:31
  183.5 5.0 %collective-permute-done.6 = bf16[512,1536]{1,0:T(8,128)(2,1)S(1)} collective-permute-done((bf16[512,1536]{1,0:T(8,128)(2,1)S(1)}, bf16[512,1536]{1,0:T(8,128)(2,1)S(1)}, u32[]{:S(2)}, u32[]{:S(2)}) %collective-permute-start.6) | collective-permute-done | bytes 1572896 | tf_op jit(solution)/shard_map/ppermute | solution.py:26
  188.6 1.3 collective-permute-start.9
  190.4 4.9 %collective-permute-done.9.refs_1_ = bf16[1024,1536]{1,0:T(8,128)(2,1)} collective-permute-done((bf16[1024,1536]{1,0:T(8,128)(2,1)S(1)}, bf16[1024,1536]{1,0:T(8,128)(2,1)}, u32[]{:S(2)}, u32[]{:S(2)}) %collective-permute-start.9) | collective-permute-done | bytes 3145760 | tf_op jit(solution)/shard_map/ppermute | solution.py:26
  195.3 28.6 %shard_map.226 = (bf16[3,2048,1152]{2,1,0:T(8,128)(2,1)}, bf16[1536,3456]{1,0:T(8,128)(2,1)}) custom-call(bf16[1024,1536]{1,0:T(8,128)(2,1)} %copy-done, bf16[1024,1536]{1,0:T(8,128)(2,1)} %collective-permute-done.9.refs_1_, bf16[1024,1536]{1,0:T(8,128)(2,1)} %constant_dynamic-update-slice_fusion.2.refs_2_, ...), custom_call_target="tpu_custom_call" | custom-call | flops 1024 | bytes 1024 | tf_op jit(solution)/shard_map/pallas_call | solution.py:837
  224.0 1.9 copy-done.1
  225.8 21.1 %shard_map.227 = (bf16[3,2048,1152]{2,1,0:T(8,128)(2,1)}, bf16[1536,3456]{1,0:T(8,128)(2,1)}) custom-call(bf16[1024,1536]{1,0:T(8,128)(2,1)S(1)} %copy-done.1, bf16[1024,1536]{1,0:T(8,128)(2,1)} %collective-permute-done.9.refs_1_, bf16[1024,1536]{1,0:T(8,128)(2,1)} %constant_dynamic-update-slice_fusion.2.refs_2_, ...), custom_call_target="tpu_custom_call", output_to_operand_aliasing={{1}: (7, {})} | custom-call | flops 1024 | bytes 1024 | tf_op jit(solution)/shard_map/pallas_call | solution.py:837
  247.0 12.1 %shard_map.228 = (bf16[192,3456]{1,0:T(8,128)(2,1)}, bf16[192,3456]{1,0:T(8,128)(2,1)S(1)}) custom-call(s32[1]{0:T(128)} %bitcast.11.chunk_ref, bf16[1024,1536]{1,0:T(8,128)(2,1)S(1)} %copy-done.2, bf16[1024,1536]{1,0:T(8,128)(2,1)} %collective-permute-done.9.refs_1_, bf16[1024,1536]{1,0:T(8,128)(2,1)} %constant_dynamic-update-slice_fusion.2.refs_2_, ...), custom_call_target="tpu_custom_call" | custom-call | flops 1024 | bytes 1024 | tf_op jit(solution)/shard_map/pallas_call | solution.py:959
  260.6 12.1 %shard_map.229 = (bf16[192,3456]{1,0:T(8,128)(2,1)}, bf16[192,3456]{1,0:T(8,128)(2,1)S(1)}) custom-call(s32[1]{0:T(128)} %bitcast.10.chunk_ref, bf16[1024,1536]{1,0:T(8,128)(2,1)S(1)} %copy-done.2, bf16[1024,1536]{1,0:T(8,128)(2,1)} %collective-permute-done.9.refs_1_, bf16[1024,1536]{1,0:T(8,128)(2,1)} %constant_dynamic-update-slice_fusion.2.refs_2_, ...), custom_call_target="tpu_custom_call" | custom-call | flops 1024 | bytes 1024 | tf_op jit(solution)/shard_map/pallas_call | solution.py:959
  272.7 22.6 %shard_map.230 = (bf16[512,1536]{1,0:T(8,128)(2,1)S(1)}, bf16[512,1536]{1,0:T(8,128)(2,1)S(1)}) custom-call(bf16[3,2048,1152]{2,1,0:T(8,128)(2,1)} %get-tuple-element.146.refs_4_.array_ref, bf16[1536,3456]{1,0:T(8,128)(2,1)} %get-tuple-element.135.refs_0_.refs_1_, bf16[1536,3456]{1,0:T(8,128)(2,1)} %get-tuple-element.135.refs_0_.refs_1_), custom_call_target="tpu_custom_call" | custom-call | flops 1024 | bytes 1024 | tf_op jit(solution)/shard_map/pallas_call | solution.py:903
  295.4 3.7 add_convert_fusion.4
  299.1 1.6 collective-permute-start.14
  300.8 1.3 constant_dynamic-update-slice_fusion.5
  302.1 2.1 collective-permute-start.16
  304.3 1.4 pad_maximum_fusion.1.rot_ref
  305.7 12.1 %shard_map.231 = (bf16[192,3456]{1,0:T(8,128)(2,1)}, bf16[192,3456]{1,0:T(8,128)(2,1)S(1)}) custom-call(s32[1]{0:T(128)} %bitcast.12.chunk_ref, bf16[1024,1536]{1,0:T(8,128)(2,1)S(1)} %copy-done.2, bf16[1024,1536]{1,0:T(8,128)(2,1)} %collective-permute-done.9.refs_1_, bf16[1024,1536]{1,0:T(8,128)(2,1)} %constant_dynamic-update-slice_fusion.2.refs_2_, ...), custom_call_target="tpu_custom_call" | custom-call | flops 1024 | bytes 1024 | tf_op jit(solution)/shard_map/pallas_call | solution.py:959
  318.8 11.1 %shard_map.232 = (bf16[192,3456]{1,0:T(8,128)(2,1)S(1)}, bf16[192,3456]{1,0:T(8,128)(2,1)S(1)}) custom-call(s32[1]{0:T(128)} %bitcast.13.chunk_ref, bf16[1024,1536]{1,0:T(8,128)(2,1)S(1)} %copy-done.2, bf16[1024,1536]{1,0:T(8,128)(2,1)} %collective-permute-done.9.refs_1_, bf16[1024,1536]{1,0:T(8,128)(2,1)} %constant_dynamic-update-slice_fusion.2.refs_2_, ...), custom_call_target="tpu_custom_call" | custom-call | flops 1024 | bytes 1024 | tf_op jit(solution)/shard_map/pallas_call | solution.py:959
  329.9 2.8 collective-permute-done.15
  332.7 3.2 add_convert_fusion.3
  336.0 1.6 collective-permute-start.18
  337.6 12.5 %shard_map.233 = (bf16[512,1536]{1,0:T(8,128)(2,1)S(1)}, bf16[512,1536]{1,0:T(8,128)(2,1)S(1)}) custom-call(bf16[3,2048,1152]{2,1,0:T(8,128)(2,1)} %get-tuple-element.146.refs_4_.array_ref, bf16[1536,3456]{1,0:T(8,128)(2,1)} %get-tuple-element.135.refs_0_.refs_1_), custom_call_target="tpu_custom_call" | custom-call | flops 1024 | bytes 1024 | tf_op jit(solution)/shard_map/pallas_call | solution.py:903
  350.1 1.1 copy-done.29
  351.3 1.1 copy-done.45
  352.4 1.1 copy-done.50
  353.6 8.7 %shard_map.234 = (f32[512,1536]{1,0:T(8,128)}, bf16[512,1536]{1,0:T(8,128)(2,1)S(1)}, bf16[512,1536]{1,0:T(8,128)(2,1)S(1)}, bf16[512,1536]{1,0:T(8,128)(2,1)S(1)}) custom-call(bf16[512,1536]{1,0:T(8,128)(2,1)} %copy-done.24, bf16[512,1536]{1,0:T(8,128)(2,1)} %copy-done.50, bf16[512,1536]{1,0:T(8,128)(2,1)} %cot_ref.1, f32[512,1536]{1,0:T(8,128)} %copy-done.11, ...), custom_call_target="tpu_custom_call" | custom-call | flops 1024 | bytes 1024 | tf_op jit(solution)/shard_map/pallas_call | solution.py:1037
  362.3 2.9 convolution_convert_fusion
  365.2 1.7 fusion.40
  367.0 2.1 collective-permute-start.17
  369.1 2.7 add_convert_fusion.2
  373.2 1.4 copy-done.26
  374.7 24.3 %shard_map.235 = (bf16[512,1536]{1,0:T(8,128)(2,1)S(1)}, f32[1536,128]{1,0:T(8,128)S(1)}, f32[1536,128]{1,0:T(8,128)S(1)}) custom-call(bf16[512,1536]{1,0:T(8,128)(2,1)S(1)} %copy-done.13, bf16[512,1536]{1,0:T(8,128)(2,1)S(1)} %copy-done.26, bf16[512,1536]{1,0:T(8,128)(2,1)S(1)} %copy-done.17, f32[12,1,512]{2,1,0:T(1,128)S(1)} %pad_maximum_fusion.10.log_ref, ...), custom_call_target="tpu_custom_call" | custom-call | flops 1024 | bytes 1024 | tf_op jit(solution)/shard_map/pallas_call | solution.py:631
  399.2 1.4 collective-permute-start.20
  400.6 1.3 collective-permute-start.21
  401.9 4.7 convolution_convert_fusion.1
  406.7 2.6 fusion
  409.4 1.9 add_convert_fusion
  411.2 2.0 collective-permute-done.21
  418.2 2.0 fusion.10
  420.8 57.3 %shard_map.236 = (f32[48,2688]{1,0:T(8,128)S(1)}, bf16[4,48,3456]{2,1,0:T(8,128)(2,1)S(1)}) custom-call(bf16[4,2,2,2,48,1536]{5,4,3,2,1,0:T(8,128)(2,1)} %bitcast.59, bf16[4,2,2,2,48,256]{5,4,3,2,1,0:T(8,128)(2,1)S(1)} %bitcast.55, bf16[4,2,2,2,48,128]{5,4,3,2,1,0:T(8,128)(2,1)S(1)} %bitcast.54, bf16[4,2,2,2,48,768]{5,4,3,2,1,0:T(8,128)(2,1)S(1)} %bitcast.52, ...), custom_call_target="tpu_custom_call" | custom-call | tf_op jit(solution)/shard_map/pallas_call | solution.py:405
  (196 shorter events, 34.7 us)
Async XLA Ops:
  7.2 4.3 copy-start.53
  7.2 4.3 copy-start.52
  7.2 128.3 %all-gather.2.cloned.1.call-start = ((), (), s32[]{:S(2)}) async-start(), calls=%async_computation.1 | async-start | bytes 4866048 | tf_op jit(solution)/shard_map/all_gather | solution.py:1102
  7.9 475.3 %reduce-scatter.2.cloned.1.call-start = ((), (), s32[]{:S(2)}) async-start(), calls=%async_computation.2 | async-start | bytes 2433024 | tf_op jit(solution)/shard_map/reduce_scatter | solution.py:1152
  12.7 47.6 %copy-start.55 = (s32[512]{0:T(512)S(1)}, s32[512]{0:T(512)}, u32[]{:S(2)}) copy-start(s32[512]{0:T(512)} %param.33) | copy-start | bytes 6148
  12.7 47.6 %copy-start.3 = (bf16[512,1536]{1,0:T(8,128)(2,1)S(1)}, bf16[512,1536]{1,0:T(8,128)(2,1)}, u32[]{:S(2)}) copy-start(bf16[512,1536]{1,0:T(8,128)(2,1)} %refs_0_.1) | copy-start | bytes 4718596
  60.3 13.4 %slice-start = ((s8[5898240]{0:T(1024)(128)(4,1)}), s8[4194304]{0:T(1024)(128)(4,1)S(1)}, s32[]{:S(2)}) async-start(s8[5898240]{0:T(1024)(128)(4,1)} %bitcast.69), calls=%async_computation.3 | async-start | bytes 8388608
  60.7 12.9 %slice-start.1 = ((s8[5898240]{0:T(1024)(128)(4,1)}), s8[1703936]{0:T(1024)(128)(4,1)S(1)}, s32[]{:S(2)}) async-start(s8[5898240]{0:T(1024)(128)(4,1)} %bitcast.69), calls=%async_computation.4 | async-start | bytes 3407872
  64.9 55.8 %copy-start.14 = (f32[512,128]{1,0:T(8,128)}, f32[512,128]{1,0:T(8,128)S(1)}, u32[]{:S(2)}) copy-start(f32[512,128]{1,0:T(8,128)S(1)} %get-tuple-element.194.cos_ref) | copy-start | bytes 786436
  65.0 17.4 %collective-permute-start = (bf16[512,256]{1,0:T(8,128)(2,1)S(1)}, bf16[512,256]{1,0:T(8,128)(2,1)}, u32[]{:S(2)}, u32[]{:S(2)}) collective-permute-start(bf16[512,256]{1,0:T(8,128)(2,1)S(1)} %pad_maximum_fusion.6), channel_id=1, source_target_pairs={{0,2},{1,3},{2,4},{3,5},{4,6},{5,7},{6,8},{7,9},{8,10},{9,11},{10,... | collective-permute-start | bytes 786440 | tf_op jit(solution)/shard_map/ppermute | solution.py:37
  70.9 11.5 %collective-permute-start.1 = (bf16[512,256]{1,0:T(8,128)(2,1)S(1)}, bf16[512,256]{1,0:T(8,128)(2,1)}, u32[]{:S(2)}, u32[]{:S(2)}) collective-permute-start(bf16[512,256]{1,0:T(8,128)(2,1)S(1)} %pad_maximum_fusion.6), channel_id=1, source_target_pairs={{0,1},{1,2},{2,3},{3,4},{4,5},{5,6},{6,7},{7,8},{8,9},{9,10},{10,1... | collective-permute-start | bytes 786440 | tf_op jit(solution)/shard_map/ppermute | solution.py:37
  73.7 4.4 copy-start.54
  73.7 40.0 %collective-permute-start.2 = (bf16[192,3456]{1,0:T(8,128)(2,1)}, bf16[192,3456]{1,0:T(8,128)(2,1)}, u32[]{:S(2)}, u32[]{:S(2)}) collective-permute-start(bf16[192,3456]{1,0:T(8,128)(2,1)} %bitcast.9.refs_4_), channel_id=1, source_target_pairs={{0,8},{1,9},{2,10},{3,11},{4,12},{5,13},{6,14},{7,15},{8,16},{9,17... | collective-permute-start | bytes 3981320 | tf_op jit(solution)/shard_map/ppermute | solution.py:31
  73.7 40.0 %collective-permute-start.3 = (bf16[192,3456]{1,0:T(8,128)(2,1)}, bf16[192,3456]{1,0:T(8,128)(2,1)}, u32[]{:S(2)}, u32[]{:S(2)}) collective-permute-start(bf16[192,3456]{1,0:T(8,128)(2,1)} %bitcast.9.refs_4_), channel_id=1, source_target_pairs={{0,4},{1,5},{2,6},{3,7},{4,0},{5,1},{6,2},{7,3},{8,12},{9,13},{10,... | collective-permute-start | bytes 3981320 | tf_op jit(solution)/shard_map/ppermute | solution.py:26
  78.4 42.4 %copy-start.6 = (s32[1536,1]{1,0:T(8,128)}, s32[1536,1]{1,0:T(8,128)S(1)}, u32[]{:S(2)}) copy-start(s32[1536,1]{1,0:T(8,128)S(1)} %broadcast_in_dim.33.ks_ref) | copy-start | bytes 18436
  113.6 33.2 %collective-permute-start.4 = (bf16[192,3456]{1,0:T(8,128)(2,1)}, bf16[192,3456]{1,0:T(8,128)(2,1)}, u32[]{:S(2)}, u32[]{:S(2)}) collective-permute-start(bf16[192,3456]{1,0:T(8,128)(2,1)} %collective-permute-done.2.refs_6_), channel_id=1, source_target_pairs={{0,8},{1,9},{2,10},{3,11},{4,12},{5,13},{6,14},{7,15},{8,16},{9,17... | collective-permute-start | bytes 3981320 | tf_op jit(solution)/shard_map/ppermute | solution.py:31
  117.1 31.2 %collective-permute-start.5 = (bf16[192,3456]{1,0:T(8,128)(2,1)}, bf16[192,3456]{1,0:T(8,128)(2,1)}, u32[]{:S(2)}, u32[]{:S(2)}) collective-permute-start(bf16[192,3456]{1,0:T(8,128)(2,1)} %collective-permute-done.2.refs_6_), channel_id=1, source_target_pairs={{0,4},{1,5},{2,6},{3,7},{4,0},{5,1},{6,2},{7,3},{8,12},{9,13},{10,... | collective-permute-start | bytes 3981320 | tf_op jit(solution)/shard_map/ppermute | solution.py:26
  117.8 37.1 %collective-permute-start.10 = (bf16[512,1536]{1,0:T(8,128)(2,1)}, bf16[512,1536]{1,0:T(8,128)(2,1)}, u32[]{:S(2)}, u32[]{:S(2)}) collective-permute-start(bf16[512,1536]{1,0:T(8,128)(2,1)} %cot_ref.1), channel_id=1, source_target_pairs={{0,2},{1,3},{2,0},{3,1},{4,6},{5,7},{6,4},{7,5},{8,10},{9,11},{10,... | collective-permute-start | bytes 4718600 | tf_op jit(solution)/shard_map/ppermute | solution.py:26
  144.0 10.9 %copy-start.11 = (f32[512,1536]{1,0:T(8,128)}, f32[512,1536]{1,0:T(8,128)S(1)}, u32[]{:S(2)}) copy-start(f32[512,1536]{1,0:T(8,128)S(1)} %get-tuple-element.117.middle_ref) | copy-start | bytes 9437188
  148.3 40.2 %collective-permute-start.6 = (bf16[512,1536]{1,0:T(8,128)(2,1)S(1)}, bf16[512,1536]{1,0:T(8,128)(2,1)S(1)}, u32[]{:S(2)}, u32[]{:S(2)}) collective-permute-start(bf16[512,1536]{1,0:T(8,128)(2,1)S(1)} %get-tuple-element.121), channel_id=1, source_target_pairs={{0,2},{1,3},{2,0},{3,1},{4,6},{5,7},{6,4},{7,5},{8,10},{9,11},{10,... | collective-permute-start | bytes 4718600 | tf_op jit(solution)/shard_map/ppermute | solution.py:26
  149.4 34.1 %collective-permute-start.7 = (bf16[192,3456]{1,0:T(8,128)(2,1)}, bf16[192,3456]{1,0:T(8,128)(2,1)}, u32[]{:S(2)}, u32[]{:S(2)}) collective-permute-start(bf16[192,3456]{1,0:T(8,128)(2,1)} %collective-permute-done.4.refs_8_), channel_id=1, source_target_pairs={{0,8},{1,9},{2,10},{3,11},{4,12},{5,13},{6,14},{7,15},{8,16},{9,17... | collective-permute-start | bytes 3981320 | tf_op jit(solution)/shard_map/ppermute | solution.py:31
  149.9 33.6 %collective-permute-start.8 = (bf16[192,3456]{1,0:T(8,128)(2,1)}, bf16[192,3456]{1,0:T(8,128)(2,1)S(1)}, u32[]{:S(2)}, u32[]{:S(2)}) collective-permute-start(bf16[192,3456]{1,0:T(8,128)(2,1)} %collective-permute-done.4.refs_8_), channel_id=1, source_target_pairs={{0,4},{1,5},{2,6},{3,7},{4,0},{5,1},{6,2},{7,3},{8,12},{9,13},{10,... | collective-permute-start | bytes 3981320 | tf_op jit(solution)/shard_map/ppermute | solution.py:26
  157.6 32.8 %collective-permute-start.11 = (bf16[1024,1536]{1,0:T(8,128)(2,1)}, bf16[1024,1536]{1,0:T(8,128)(2,1)}, u32[]{:S(2)}, u32[]{:S(2)}) collective-permute-start(bf16[1024,1536]{1,0:T(8,128)(2,1)} %constant_dynamic-update-slice_fusion.2.refs_2_), channel_id=1, source_target_pairs={{0,1},{1,0},{2,3},{3,2},{4,5},{5,4},{6,7},{7,6},{8,9},{9,8},{10,11... | collective-permute-start | bytes 9437192 | tf_op jit(solution)/shard_map/ppermute | solution.py:26
  183.5 5.1 %copy-start.51 = (bf16[192,3456]{1,0:T(8,128)(2,1)}, bf16[192,3456]{1,0:T(8,128)(2,1)S(1)}, u32[]{:S(2)}) copy-start(bf16[192,3456]{1,0:T(8,128)(2,1)S(1)} %collective-permute-done.8.refs_9_) | copy-start | bytes 3981316
  188.6 6.7 %copy-start = (bf16[1024,1536]{1,0:T(8,128)(2,1)}, bf16[1024,1536]{1,0:T(8,128)(2,1)S(1)}, u32[]{:S(2)}) copy-start(bf16[1024,1536]{1,0:T(8,128)(2,1)S(1)} %constant_dynamic-update-slice_fusion.refs_0_) | copy-start | bytes 9437188
  188.6 6.7 %collective-permute-start.9 = (bf16[1024,1536]{1,0:T(8,128)(2,1)S(1)}, bf16[1024,1536]{1,0:T(8,128)(2,1)}, u32[]{:S(2)}, u32[]{:S(2)}) collective-permute-start(bf16[1024,1536]{1,0:T(8,128)(2,1)S(1)} %constant_dynamic-update-slice_fusion.refs_0_), channel_id=1, source_target_pairs={{0,1},{1,0},{2,3},{3,2},{4,5},{5,4},{6,7},{7,6},{8,9},{9,8},{10,11... | collective-permute-start | bytes 9437192 | tf_op jit(solution)/shard_map/ppermute | solution.py:26
  189.9 34.0 %collective-permute-start.12 = (bf16[192,3456]{1,0:T(8,128)(2,1)}, bf16[192,3456]{1,0:T(8,128)(2,1)}, u32[]{:S(2)}, u32[]{:S(2)}) collective-permute-start(bf16[192,3456]{1,0:T(8,128)(2,1)} %collective-permute-done.7.refs_4_), channel_id=1, source_target_pairs={{0,4},{1,5},{2,6},{3,7},{4,0},{5,1},{6,2},{7,3},{8,12},{9,13},{10,... | collective-permute-start | bytes 3981320 | tf_op jit(solution)/shard_map/ppermute | solution.py:26
  225.8 21.1 %copy-start.2 = (bf16[1024,1536]{1,0:T(8,128)(2,1)S(1)}, bf16[1024,1536]{1,0:T(8,128)(2,1)}, u32[]{:S(2)}) copy-start(bf16[1024,1536]{1,0:T(8,128)(2,1)} %copy-done) | copy-start | bytes 9437188
  260.1 35.2 %collective-permute-start.13 = (bf16[192,3456]{1,0:T(8,128)(2,1)}, bf16[192,3456]{1,0:T(8,128)(2,1)}, u32[]{:S(2)}, u32[]{:S(2)}) collective-permute-start(bf16[192,3456]{1,0:T(8,128)(2,1)} %get-tuple-element.129), channel_id=1, source_target_pairs={{0,4},{1,5},{2,6},{3,7},{4,0},{5,1},{6,2},{7,3},{8,12},{9,13},{10,... | collective-permute-start | bytes 3981320 | tf_op jit(solution)/shard_map/ppermute | solution.py:26
  272.7 22.7 %copy-start.33 = (bf16[192,3456]{1,0:T(8,128)(2,1)}, bf16[192,3456]{1,0:T(8,128)(2,1)S(1)}, u32[]{:S(2)}) copy-start(bf16[192,3456]{1,0:T(8,128)(2,1)S(1)} %get-tuple-element.131) | copy-start | bytes 3981316
  272.7 22.7 %copy-start.37 = (bf16[192,3456]{1,0:T(8,128)(2,1)S(1)}, bf16[192,3456]{1,0:T(8,128)(2,1)}, u32[]{:S(2)}) copy-start(bf16[192,3456]{1,0:T(8,128)(2,1)} %copy-done.36) | copy-start | bytes 3981316
  295.4 3.7 copy-start.24
  295.4 3.7 copy-start.44
  299.1 33.6 %collective-permute-start.15 = (bf16[192,3456]{1,0:T(8,128)(2,1)}, bf16[192,3456]{1,0:T(8,128)(2,1)}, u32[]{:S(2)}, u32[]{:S(2)}) collective-permute-start(bf16[192,3456]{1,0:T(8,128)(2,1)} %add_convert_fusion.4), channel_id=1, source_target_pairs={{0,8},{1,9},{2,10},{3,11},{4,12},{5,13},{6,14},{7,15},{8,16},{9,17... | collective-permute-start | bytes 3981320 | tf_op jit(solution)/shard_map/ppermute | solution.py:31
  299.1 33.6 %collective-permute-start.14 = (bf16[192,3456]{1,0:T(8,128)(2,1)}, bf16[192,3456]{1,0:T(8,128)(2,1)}, u32[]{:S(2)}, u32[]{:S(2)}) collective-permute-start(bf16[192,3456]{1,0:T(8,128)(2,1)} %get-tuple-element.138), channel_id=1, source_target_pairs={{0,4},{1,5},{2,6},{3,7},{4,0},{5,1},{6,2},{7,3},{8,12},{9,13},{10,... | collective-permute-start | bytes 3981320 | tf_op jit(solution)/shard_map/ppermute | solution.py:26
  300.7 3.5 copy-start.23
  300.7 3.5 copy-start.39
  300.7 3.5 copy-start.41
  302.1 50.3 %collective-permute-start.16 = (bf16[512,1536]{1,0:T(8,128)(2,1)}, bf16[512,1536]{1,0:T(8,128)(2,1)S(1)}, u32[]{:S(2)}, u32[]{:S(2)}) collective-permute-start(bf16[512,1536]{1,0:T(8,128)(2,1)} %copy-done.44), channel_id=1, source_target_pairs={{0,2},{1,3},{2,0},{3,1},{4,6},{5,7},{6,4},{7,5},{8,10},{9,11},{10,... | collective-permute-start | bytes 4718600 | tf_op jit(solution)/shard_map/ppermute | solution.py:26
  304.3 58.0 %copy-start.16 = (bf16[512,1536]{1,0:T(8,128)(2,1)}, bf16[512,1536]{1,0:T(8,128)(2,1)S(1)}, u32[]{:S(2)}) copy-start(bf16[512,1536]{1,0:T(8,128)(2,1)S(1)} %constant_dynamic-update-slice_fusion.4.mixed_ref) | copy-start | bytes 4718596
  318.8 13.9 %copy-start.34 = (bf16[192,3456]{1,0:T(8,128)(2,1)S(1)}, bf16[192,3456]{1,0:T(8,128)(2,1)}, u32[]{:S(2)}) copy-start(bf16[192,3456]{1,0:T(8,128)(2,1)} %copy-done.33) | copy-start | bytes 3981316
  329.9 6.1 %copy-start.31 = (bf16[192,3456]{1,0:T(8,128)(2,1)}, bf16[192,3456]{1,0:T(8,128)(2,1)S(1)}, u32[]{:S(2)}) copy-start(bf16[192,3456]{1,0:T(8,128)(2,1)S(1)} %get-tuple-element.170) | copy-start | bytes 3981316
  329.9 6.0 %copy-start.46 = (bf16[192,3456]{1,0:T(8,128)(2,1)}, bf16[192,3456]{1,0:T(8,128)(2,1)S(1)}, u32[]{:S(2)}) copy-start(bf16[192,3456]{1,0:T(8,128)(2,1)S(1)} %get-tuple-element.159) | copy-start | bytes 3981316
  335.9 33.1 %collective-permute-start.19 = (bf16[192,3456]{1,0:T(8,128)(2,1)}, bf16[192,3456]{1,0:T(8,128)(2,1)}, u32[]{:S(2)}, u32[]{:S(2)}) collective-permute-start(bf16[192,3456]{1,0:T(8,128)(2,1)} %add_convert_fusion.3), channel_id=1, source_target_pairs={{0,8},{1,9},{2,10},{3,11},{4,12},{5,13},{6,14},{7,15},{8,16},{9,17... | collective-permute-start | bytes 3981320 | tf_op jit(solution)/shard_map/ppermute | solution.py:31
  336.0 33.1 %collective-permute-start.18 = (bf16[192,3456]{1,0:T(8,128)(2,1)}, bf16[192,3456]{1,0:T(8,128)(2,1)}, u32[]{:S(2)}, u32[]{:S(2)}) collective-permute-start(bf16[192,3456]{1,0:T(8,128)(2,1)} %get-tuple-element.145), channel_id=1, source_target_pairs={{0,4},{1,5},{2,6},{3,7},{4,0},{5,1},{6,2},{7,3},{8,12},{9,13},{10,... | collective-permute-start | bytes 3981320 | tf_op jit(solution)/shard_map/ppermute | solution.py:26
  337.6 16.0 %copy-start.43 = (f32[512,128]{1,0:T(8,128)S(1)}, f32[512,128]{1,0:T(8,128)}, u32[]{:S(2)}) copy-start(f32[512,128]{1,0:T(8,128)} %copy-done.42) | copy-start | bytes 786436
  362.2 2.9 copy-start.25
  362.2 2.9 copy-start.27
  367.0 42.4 %collective-permute-start.17 = (bf16[512,1536]{1,0:T(8,128)(2,1)}, bf16[512,1536]{1,0:T(8,128)(2,1)S(1)}, u32[]{:S(2)}, u32[]{:S(2)}) collective-permute-start(bf16[512,1536]{1,0:T(8,128)(2,1)} %copy-done.45), channel_id=1, source_target_pairs={{0,2},{1,3},{2,0},{3,1},{4,6},{5,7},{6,4},{7,5},{8,10},{9,11},{10,... | collective-permute-start | bytes 4718600 | tf_op jit(solution)/shard_map/ppermute | solution.py:26
  369.1 4.1 copy-start.7
  369.1 4.1 copy-start.9
  369.1 4.1 copy-start.13
  369.1 4.1 copy-start.15
  369.1 4.1 copy-start.17
  371.9 48.3 %collective-permute-start.23 = (bf16[192,3456]{1,0:T(8,128)(2,1)S(1)}, bf16[192,3456]{1,0:T(8,128)(2,1)S(1)}, u32[]{:S(2)}, u32[]{:S(2)}) collective-permute-start(bf16[192,3456]{1,0:T(8,128)(2,1)S(1)} %add_convert_fusion.2), channel_id=1, source_target_pairs={{0,8},{1,9},{2,10},{3,11},{4,12},{5,13},{6,14},{7,15},{8,16},{9,17... | collective-permute-start | bytes 3981320 | tf_op jit(solution)/shard_map/ppermute | solution.py:31
  372.2 48.0 %collective-permute-start.22 = (bf16[192,3456]{1,0:T(8,128)(2,1)}, bf16[192,3456]{1,0:T(8,128)(2,1)S(1)}, u32[]{:S(2)}, u32[]{:S(2)}) collective-permute-start(bf16[192,3456]{1,0:T(8,128)(2,1)} %copy-done.46), channel_id=1, source_target_pairs={{0,4},{1,5},{2,6},{3,7},{4,0},{5,1},{6,2},{7,3},{8,12},{9,13},{10,... | collective-permute-start | bytes 3981320 | tf_op jit(solution)/shard_map/ppermute | solution.py:26
  374.7 32.0 %slice-start.2 = ((s8[5898240]{0:T(1024)(128)(4,1)}), s8[4194304]{0:T(1024)(128)(4,1)S(1)}, s32[]{:S(2)}) async-start(s8[5898240]{0:T(1024)(128)(4,1)} %bitcast.72), calls=%async_computation.5 | async-start | bytes 8388608
  399.0 2.9 copy-start.4
  399.2 12.1 %collective-permute-start.20 = (bf16[512,256]{1,0:T(8,128)(2,1)S(1)}, bf16[512,256]{1,0:T(8,128)(2,1)S(1)}, u32[]{:S(2)}, u32[]{:S(2)}) collective-permute-start(bf16[512,256]{1,0:T(8,128)(2,1)S(1)} %get-tuple-element.184), channel_id=1, source_target_pairs={{1,0},{2,1},{3,2},{4,3},{5,4},{6,5},{7,6},{8,7},{9,8},{10,9},{11,1... | collective-permute-start | bytes 786440 | tf_op jit(solution)/shard_map/ppermute | solution.py:37
  400.6 12.6 %collective-permute-start.21 = (bf16[512,256]{1,0:T(8,128)(2,1)S(1)}, bf16[512,256]{1,0:T(8,128)(2,1)S(1)}, u32[]{:S(2)}, u32[]{:S(2)}) collective-permute-start(bf16[512,256]{1,0:T(8,128)(2,1)S(1)} %get-tuple-element.185), channel_id=1, source_target_pairs={{2,0},{3,1},{4,2},{5,3},{6,4},{7,5},{8,6},{9,7},{10,8},{11,9},{12,... | collective-permute-start | bytes 786440 | tf_op jit(solution)/shard_map/ppermute | solution.py:37
  401.9 4.7 slice-start.3
  406.7 2.7 copy-start.12
  406.7 2.7 copy-start.30
  415.5 2.7 copy-start.47
  (22 other events, 28.2 us)
Sparse Core Ops, SparseCore 0:
  10.9 105.4 all-gather.1
  367.1 105.1 reduce-scatter.1

commit v7 on v6

--- a/solution.py
+++ b/solution.py
@@ -143,16 +143,16 @@
         return (z - step + ring) % ring
 
     def piece(step, band):
-        return attn_out.at[chunk_of(step), side, near, core, bands[band]]
+        return attn_out.at[chunk_of(step), side, near, core, :, bands[band]]
 
     hops, first, second, last = {}, {}, {}, {}
     over = []
 
     def finish(step):
         first[0, step].wait_recv()
-        second[0, step] = forward(attn_out.at[chunk_of(step), side, :, core, bands[0]], side_mate)
+        second[0, step] = forward(attn_out.at[chunk_of(step), side, :, core, :, bands[0]], side_mate)
         first[1, step].wait_recv()
-        second[1, step] = forward(attn_out.at[chunk_of(step), :, near, core, bands[1]], near_mate)
+        second[1, step] = forward(attn_out.at[chunk_of(step), :, near, core, :, bands[1]], near_mate)
 
     def hand_over(step):
         second[0, step].wait_recv()
@@ -163,13 +163,13 @@
         for band in (0, 1):
             if step > 0:
                 hops[band, step].wait_recv()
-            source = attn_ref.at[bands[band]] if step == 0 else piece(step, band)
+            source = attn_ref.at[:, bands[band]] if step == 0 else piece(step, band)
             if step < ring - 1:
                 hops[band, step + 1] = send(source, piece(step, band), up)
             mate = near_mate if band == 0 else side_mate
             first[band, step] = send(source, piece(step, band), mate)
         if step == 0:
-            begun = send(attn_ref.at[bands[2]], piece(0, 2), near_mate)
+            begun = send(attn_ref.at[:, bands[2]], piece(0, 2), near_mate)
             slices = [
                 send(ffn_ref.at[index], ffn_out.at[2 * near + core], mate)
                 for mate, index in (
@@ -180,10 +180,10 @@
             ]
             own.wait()
             begun.wait_recv()
-            last[0] = forward(attn_out.at[z, side, :, core, bands[2]], side_mate)
+            last[0] = forward(attn_out.at[z, side, :, core, :, bands[2]], side_mate)
         else:
             last[step - 1].wait_recv()
-            last[step] = forward(attn_out.at[chunk_of(step - 1), :, :, core, bands[2]], up)
+            last[step] = forward(attn_out.at[chunk_of(step - 1), :, :, core, :, bands[2]], up)
             finish(step - 1)
         if step >= 2:
             hand_over(step - 2)
@@ -204,8 +204,11 @@
     rows, columns = attn_pack.shape
     if ring > LONGEST_RING or ring < 2 or rows % 48:
         return lax.all_gather(attn_pack, "tok", axis=0, tiled=True), slices_to_group(ffn_pack)
-    third = rows // 3
-    bands = [pl.ds(third * band, third) for band in range(3)]
+    lanes = columns // HD
+    crossed = lanes * 4 // 15
+    first = (lanes - crossed + 1) // 2
+    ends = (0, first * HD, (lanes - crossed) * HD, columns)
+    bands = [pl.ds(ends[band], ends[band + 1] - ends[band]) for band in range(3)]
     count = 3 + 2 * (ring - 1) + 2 * ring + 2 * ring + 1 + ring + ring
     anywhere = pl.BlockSpec(memory_space=pl.ANY)
     attn_all, ffn_rows = pl.pallas_call(

time: 502 us -> 499 us (level)
  no operation moved by 1% of the time
where the time goes in v7:
time: 499 us; the launch traced here: 492 us
  Pallas kernels  299 us (60%)
  waiting for transfers between devices  57 us (11%)
  local copies, waits for them, and re-layouts  42.5 us (9%)
  starting transfers between devices  34.3 us (7%)
  other arithmetic  24.2 us (5%)
  matrix products  19.8 us (4%)
  between operations  15.3 us (3%)
    pallas_call x1, Pallas kernels, scatter(): pl.pallas_call(functools.partial(scatter_kernel, ring, bands, edges), in_...  57.3 us
    pallas_call x2, Pallas kernels, part(): pl.pallas_call(functools.partial(depth_kernel, ring, first, count, len(mo...  49.8 us
    pallas_call x1, Pallas kernels, gather(): pl.pallas_call(functools.partial(gather_kernel, ring, bands), in_specs=[a...  47.5 us
    pallas_call x4, Pallas kernels, outer_products(): pl.pallas_call(outer_kernel, grid_spec=pltpu.PrefetchScalarGridSpec(num_s...  47.3 us
    ppermute x6, waiting for transfers between devices, around(): lax.ppermute(array, 'tok', [(i, (i + RING) % size) for i in range(size)])  40.1 us
    pallas_call x2, Pallas kernels, project_sum(): pl.pallas_call(functools.partial(project_sum_kernel, count), grid=(4,), i...  35.2 us
    unnamed x124, local copies, waits for them, and re-layouts  27.8 us
    pallas_call x2, Pallas kernels, attend(): pl.pallas_call(functools.partial(attend_kernel, block, HD ** (-0.5) * LOG...  25.9 us
  transfers between devices with their start and end apart: 26, of which 9 were waited for; matrix products, arithmetic and copies ran while one was open for 12% of the time, Pallas kernels for 54%

profile of v7, /device:TPU:0, one launch (start us, length us, event | category | flops | bytes accessed | tf_op | source)
XLA Modules:
  0.0 492.2 jit_solution(8012015067465808079)
XLA Ops:
  9.8 1.6 fusion.30.attn_ref
  11.5 1.2 pad_maximum_fusion.2.ffn_ref
  12.7 47.5 %shard_map.222 = (bf16[4,2,2,2,48,1920]{5,4,3,2,1,0:T(8,128)(2,1)}, bf16[4,48,3456]{2,1,0:T(8,128)(2,1)}) custom-call(bf16[48,1920]{1,0:T(8,128)(2,1)} %fusion.30.attn_ref, bf16[4,48,3456]{2,1,0:T(8,128)(2,1)} %pad_maximum_fusion.2.ffn_ref), custom_call_target="tpu_custom_call" | custom-call | tf_op jit(solution)/shard_map/pallas_call | solution.py:214
  61.9 2.0 fusion.20
  66.1 3.2 collective-permute-start
  69.3 2.8 collective-permute-start.1
  72.4 4.3 fusion.2.q_ref
  77.1 3.7 collective-permute-done
  80.8 1.1 maximum_maximum_fusion.key_ref.value_ref
  83.8 1.2 copy.60.value_t_ref
  84.9 1.9 copy-done.10
  87.9 13.0 %shard_map.223 = (bf16[512,768]{1,0:T(8,128)(2,1)S(1)}, bf16[512,768]{1,0:T(8,128)(2,1)S(1)}, f32[6,1,512]{2,1,0:T(1,128)S(1)}) custom-call(f32[512,1536]{1,0:T(8,128)S(1)} %copy-done.10, bf16[1536,128]{1,0:T(8,128)(2,1)S(1)} %copy-done.18, bf16[128,1536]{1,0:T(8,128)(2,1)S(1)} %copy.60.value_t_ref, s32[1536,1]{1,0:T(8,128)S(1)} %broadcast_in_dim.33.ks_ref, ...), custom_call_target="tpu_custom_call" | custom-call | flops 1024 | bytes 1024 | tf_op jit(solution)/shard_map/pallas_call | solution.py:568
  102.6 10.9 %collective-permute-done.2.refs_6_ = bf16[192,3456]{1,0:T(8,128)(2,1)} collective-permute-done((bf16[192,3456]{1,0:T(8,128)(2,1)}, bf16[192,3456]{1,0:T(8,128)(2,1)}, u32[]{:S(2)}, u32[]{:S(2)}) %collective-permute-start.2) | collective-permute-done | bytes 1327136 | tf_op jit(solution)/shard_map/ppermute | solution.py:31
  113.5 3.8 collective-permute-start.4
  117.3 3.4 collective-permute-start.10
  120.7 13.0 %shard_map.224 = (bf16[512,768]{1,0:T(8,128)(2,1)S(1)}, bf16[512,768]{1,0:T(8,128)(2,1)S(1)}, f32[6,1,512]{2,1,0:T(1,128)S(1)}) custom-call(f32[512,1536]{1,0:T(8,128)S(1)} %copy-done.10, bf16[1536,128]{1,0:T(8,128)(2,1)S(1)} %copy-done.18, bf16[128,1536]{1,0:T(8,128)(2,1)S(1)} %copy.60.value_t_ref, s32[1536,1]{1,0:T(8,128)S(1)} %broadcast_in_dim.33.ks_ref, ...), custom_call_target="tpu_custom_call" | custom-call | flops 1024 | bytes 1024 | tf_op jit(solution)/shard_map/pallas_call | solution.py:568
  135.5 2.3 copy-done.5
  137.8 1.1 copy-done.20
  139.0 1.1 copy-done.22
  140.1 3.2 shard_map.225
  144.0 4.2 collective-permute-done.4.refs_8_
  150.0 2.3 collective-permute-start.8
  152.3 2.7 constant_dynamic-update-slice_fusion.3
  155.0 2.7 constant_dynamic-update-slice_fusion.2.refs_2_
  157.6 2.8 collective-permute-start.11
  160.5 22.5 %collective-permute-done.7.refs_4_ = bf16[192,3456]{1,0:T(8,128)(2,1)} collective-permute-done((bf16[192,3456]{1,0:T(8,128)(2,1)}, bf16[192,3456]{1,0:T(8,128)(2,1)}, u32[]{:S(2)}, u32[]{:S(2)}) %collective-permute-start.7) | collective-permute-done | bytes 1327136 | tf_op jit(solution)/shard_map/ppermute | solution.py:31
  183.0 5.5 %collective-permute-done.6 = bf16[512,1536]{1,0:T(8,128)(2,1)S(1)} collective-permute-done((bf16[512,1536]{1,0:T(8,128)(2,1)S(1)}, bf16[512,1536]{1,0:T(8,128)(2,1)S(1)}, u32[]{:S(2)}, u32[]{:S(2)}) %collective-permute-start.6) | collective-permute-done | bytes 1572896 | tf_op jit(solution)/shard_map/ppermute | solution.py:26
  188.6 1.3 collective-permute-start.9
  190.5 4.8 collective-permute-done.9.refs_1_
  195.3 28.6 %shard_map.226 = (bf16[3,2048,1152]{2,1,0:T(8,128)(2,1)}, bf16[1536,3456]{1,0:T(8,128)(2,1)}) custom-call(bf16[1024,1536]{1,0:T(8,128)(2,1)} %copy-done, bf16[1024,1536]{1,0:T(8,128)(2,1)} %collective-permute-done.9.refs_1_, bf16[1024,1536]{1,0:T(8,128)(2,1)} %constant_dynamic-update-slice_fusion.2.refs_2_, ...), custom_call_target="tpu_custom_call" | custom-call | flops 1024 | bytes 1024 | tf_op jit(solution)/shard_map/pallas_call | solution.py:840
  224.0 1.9 copy-done.1
  225.9 21.1 %shard_map.227 = (bf16[3,2048,1152]{2,1,0:T(8,128)(2,1)}, bf16[1536,3456]{1,0:T(8,128)(2,1)}) custom-call(bf16[1024,1536]{1,0:T(8,128)(2,1)S(1)} %copy-done.1, bf16[1024,1536]{1,0:T(8,128)(2,1)} %collective-permute-done.9.refs_1_, bf16[1024,1536]{1,0:T(8,128)(2,1)} %constant_dynamic-update-slice_fusion.2.refs_2_, ...), custom_call_target="tpu_custom_call", output_to_operand_aliasing={{1}: (7, {})} | custom-call | flops 1024 | bytes 1024 | tf_op jit(solution)/shard_map/pallas_call | solution.py:840
  247.0 12.1 %shard_map.228 = (bf16[192,3456]{1,0:T(8,128)(2,1)}, bf16[192,3456]{1,0:T(8,128)(2,1)S(1)}) custom-call(s32[1]{0:T(128)} %bitcast.11.chunk_ref, bf16[1024,1536]{1,0:T(8,128)(2,1)S(1)} %copy-done.2, bf16[1024,1536]{1,0:T(8,128)(2,1)} %collective-permute-done.9.refs_1_, bf16[1024,1536]{1,0:T(8,128)(2,1)} %constant_dynamic-update-slice_fusion.2.refs_2_, ...), custom_call_target="tpu_custom_call" | custom-call | flops 1024 | bytes 1024 | tf_op jit(solution)/shard_map/pallas_call | solution.py:962
  259.1 1.1 copy-done.36
  260.8 12.1 %shard_map.229 = (bf16[192,3456]{1,0:T(8,128)(2,1)}, bf16[192,3456]{1,0:T(8,128)(2,1)S(1)}) custom-call(s32[1]{0:T(128)} %bitcast.10.chunk_ref, bf16[1024,1536]{1,0:T(8,128)(2,1)S(1)} %copy-done.2, bf16[1024,1536]{1,0:T(8,128)(2,1)} %collective-permute-done.9.refs_1_, bf16[1024,1536]{1,0:T(8,128)(2,1)} %constant_dynamic-update-slice_fusion.2.refs_2_, ...), custom_call_target="tpu_custom_call" | custom-call | flops 1024 | bytes 1024 | tf_op jit(solution)/shard_map/pallas_call | solution.py:962
  272.9 22.6 %shard_map.230 = (bf16[512,1536]{1,0:T(8,128)(2,1)S(1)}, bf16[512,1536]{1,0:T(8,128)(2,1)S(1)}) custom-call(bf16[3,2048,1152]{2,1,0:T(8,128)(2,1)} %get-tuple-element.146.refs_4_.array_ref, bf16[1536,3456]{1,0:T(8,128)(2,1)} %get-tuple-element.135.refs_0_.refs_1_, bf16[1536,3456]{1,0:T(8,128)(2,1)} %get-tuple-element.135.refs_0_.refs_1_), custom_call_target="tpu_custom_call" | custom-call | flops 1024 | bytes 1024 | tf_op jit(solution)/shard_map/pallas_call | solution.py:906
  295.6 3.7 add_convert_fusion.4
  301.2 1.3 constant_dynamic-update-slice_fusion.5
  302.6 2.1 collective-permute-start.16
  304.7 1.4 pad_maximum_fusion.1.rot_ref
  306.1 12.1 %shard_map.231 = (bf16[192,3456]{1,0:T(8,128)(2,1)}, bf16[192,3456]{1,0:T(8,128)(2,1)S(1)}) custom-call(s32[1]{0:T(128)} %bitcast.12.chunk_ref, bf16[1024,1536]{1,0:T(8,128)(2,1)S(1)} %copy-done.2, bf16[1024,1536]{1,0:T(8,128)(2,1)} %collective-permute-done.9.refs_1_, bf16[1024,1536]{1,0:T(8,128)(2,1)} %constant_dynamic-update-slice_fusion.2.refs_2_, ...), custom_call_target="tpu_custom_call" | custom-call | flops 1024 | bytes 1024 | tf_op jit(solution)/shard_map/pallas_call | solution.py:962
  318.2 1.1 copy-done.35
  319.2 11.1 %shard_map.232 = (bf16[192,3456]{1,0:T(8,128)(2,1)S(1)}, bf16[192,3456]{1,0:T(8,128)(2,1)S(1)}) custom-call(s32[1]{0:T(128)} %bitcast.13.chunk_ref, bf16[1024,1536]{1,0:T(8,128)(2,1)S(1)} %copy-done.2, bf16[1024,1536]{1,0:T(8,128)(2,1)} %collective-permute-done.9.refs_1_, bf16[1024,1536]{1,0:T(8,128)(2,1)} %constant_dynamic-update-slice_fusion.2.refs_2_, ...), custom_call_target="tpu_custom_call" | custom-call | flops 1024 | bytes 1024 | tf_op jit(solution)/shard_map/pallas_call | solution.py:962
  330.4 2.5 collective-permute-done.15
  332.8 3.2 add_convert_fusion.3
  337.6 12.5 %shard_map.233 = (bf16[512,1536]{1,0:T(8,128)(2,1)S(1)}, bf16[512,1536]{1,0:T(8,128)(2,1)S(1)}) custom-call(bf16[3,2048,1152]{2,1,0:T(8,128)(2,1)} %get-tuple-element.146.refs_4_.array_ref, bf16[1536,3456]{1,0:T(8,128)(2,1)} %get-tuple-element.135.refs_0_.refs_1_), custom_call_target="tpu_custom_call" | custom-call | flops 1024 | bytes 1024 | tf_op jit(solution)/shard_map/pallas_call | solution.py:906
  350.2 1.1 copy-done.29
  351.3 1.1 copy-done.45
  352.4 1.1 copy-done.50
  353.6 8.7 %shard_map.234 = (f32[512,1536]{1,0:T(8,128)}, bf16[512,1536]{1,0:T(8,128)(2,1)S(1)}, bf16[512,1536]{1,0:T(8,128)(2,1)S(1)}, bf16[512,1536]{1,0:T(8,128)(2,1)S(1)}) custom-call(bf16[512,1536]{1,0:T(8,128)(2,1)} %copy-done.24, bf16[512,1536]{1,0:T(8,128)(2,1)} %copy-done.50, bf16[512,1536]{1,0:T(8,128)(2,1)} %cot_ref.1, f32[512,1536]{1,0:T(8,128)} %copy-done.11, ...), custom_call_target="tpu_custom_call" | custom-call | flops 1024 | bytes 1024 | tf_op jit(solution)/shard_map/pallas_call | solution.py:1040
  362.3 2.9 convolution_convert_fusion
  365.2 1.7 fusion.40
  367.0 2.1 collective-permute-start.17
  369.1 2.7 add_convert_fusion.2
  373.3 1.4 copy-done.26
  374.7 24.3 %shard_map.235 = (bf16[512,1536]{1,0:T(8,128)(2,1)S(1)}, f32[1536,128]{1,0:T(8,128)S(1)}, f32[1536,128]{1,0:T(8,128)S(1)}) custom-call(bf16[512,1536]{1,0:T(8,128)(2,1)S(1)} %copy-done.13, bf16[512,1536]{1,0:T(8,128)(2,1)S(1)} %copy-done.26, bf16[512,1536]{1,0:T(8,128)(2,1)S(1)} %copy-done.17, f32[12,1,512]{2,1,0:T(1,128)S(1)} %pad_maximum_fusion.10.log_ref, ...), custom_call_target="tpu_custom_call" | custom-call | flops 1024 | bytes 1024 | tf_op jit(solution)/shard_map/pallas_call | solution.py:634
  399.2 1.4 collective-permute-start.20
  400.6 1.3 collective-permute-start.21
  402.0 4.7 convolution_convert_fusion.1
  406.7 2.6 fusion
  409.4 1.9 add_convert_fusion
  411.3 2.0 collective-permute-done.21
  418.2 2.0 fusion.10
  420.8 57.3 %shard_map.236 = (f32[48,2688]{1,0:T(8,128)S(1)}, bf16[4,48,3456]{2,1,0:T(8,128)(2,1)S(1)}) custom-call(bf16[4,2,2,2,48,1536]{5,4,3,2,1,0:T(8,128)(2,1)} %bitcast.59, bf16[4,2,2,2,48,256]{5,4,3,2,1,0:T(8,128)(2,1)S(1)} %bitcast.55, bf16[4,2,2,2,48,128]{5,4,3,2,1,0:T(8,128)(2,1)S(1)} %bitcast.54, bf16[4,2,2,2,48,768]{5,4,3,2,1,0:T(8,128)(2,1)S(1)} %bitcast.52, ...), custom_call_target="tpu_custom_call" | custom-call | tf_op jit(solution)/shard_map/pallas_call | solution.py:408
  (196 shorter events, 35.0 us)
Async XLA Ops:
  7.2 4.3 copy-start.53
  7.2 4.3 copy-start.52
  7.2 128.3 %all-gather.2.cloned.1.call-start = ((), (), s32[]{:S(2)}) async-start(), calls=%async_computation.1 | async-start | bytes 4866048 | tf_op jit(solution)/shard_map/all_gather | solution.py:1105
  7.9 475.3 %reduce-scatter.2.cloned.1.call-start = ((), (), s32[]{:S(2)}) async-start(), calls=%async_computation.2 | async-start | bytes 2433024 | tf_op jit(solution)/shard_map/reduce_scatter | solution.py:1155
  12.7 48.7 %copy-start.55 = (s32[512]{0:T(512)S(1)}, s32[512]{0:T(512)}, u32[]{:S(2)}) copy-start(s32[512]{0:T(512)} %param.33) | copy-start | bytes 6148
  12.7 48.8 %copy-start.3 = (bf16[512,1536]{1,0:T(8,128)(2,1)S(1)}, bf16[512,1536]{1,0:T(8,128)(2,1)}, u32[]{:S(2)}) copy-start(bf16[512,1536]{1,0:T(8,128)(2,1)} %refs_0_.1) | copy-start | bytes 4718596
  61.5 10.9 %slice-start = ((s8[5898240]{0:T(1024)(128)(4,1)}), s8[4194304]{0:T(1024)(128)(4,1)S(1)}, s32[]{:S(2)}) async-start(s8[5898240]{0:T(1024)(128)(4,1)} %bitcast.69), calls=%async_computation.3 | async-start | bytes 8388608
  61.9 10.4 %slice-start.1 = ((s8[5898240]{0:T(1024)(128)(4,1)}), s8[1703936]{0:T(1024)(128)(4,1)S(1)}, s32[]{:S(2)}) async-start(s8[5898240]{0:T(1024)(128)(4,1)} %bitcast.69), calls=%async_computation.4 | async-start | bytes 3407872
  66.1 54.6 %copy-start.14 = (f32[512,128]{1,0:T(8,128)}, f32[512,128]{1,0:T(8,128)S(1)}, u32[]{:S(2)}) copy-start(f32[512,128]{1,0:T(8,128)S(1)} %get-tuple-element.194.cos_ref) | copy-start | bytes 786436
  66.1 14.7 %collective-permute-start = (bf16[512,256]{1,0:T(8,128)(2,1)S(1)}, bf16[512,256]{1,0:T(8,128)(2,1)}, u32[]{:S(2)}, u32[]{:S(2)}) collective-permute-start(bf16[512,256]{1,0:T(8,128)(2,1)S(1)} %pad_maximum_fusion.6), channel_id=1, source_target_pairs={{0,2},{1,3},{2,4},{3,5},{4,6},{5,7},{6,8},{7,9},{8,10},{9,11},{10,... | collective-permute-start | bytes 786440 | tf_op jit(solution)/shard_map/ppermute | solution.py:37
  69.3 11.5 %collective-permute-start.1 = (bf16[512,256]{1,0:T(8,128)(2,1)S(1)}, bf16[512,256]{1,0:T(8,128)(2,1)}, u32[]{:S(2)}, u32[]{:S(2)}) collective-permute-start(bf16[512,256]{1,0:T(8,128)(2,1)S(1)} %pad_maximum_fusion.6), channel_id=1, source_target_pairs={{0,1},{1,2},{2,3},{3,4},{4,5},{5,6},{6,7},{7,8},{8,9},{9,10},{10,1... | collective-permute-start | bytes 786440 | tf_op jit(solution)/shard_map/ppermute | solution.py:37
  72.1 4.6 copy-start.54
  72.1 41.4 %collective-permute-start.2 = (bf16[192,3456]{1,0:T(8,128)(2,1)}, bf16[192,3456]{1,0:T(8,128)(2,1)}, u32[]{:S(2)}, u32[]{:S(2)}) collective-permute-start(bf16[192,3456]{1,0:T(8,128)(2,1)} %bitcast.9.refs_4_), channel_id=1, source_target_pairs={{0,8},{1,9},{2,10},{3,11},{4,12},{5,13},{6,14},{7,15},{8,16},{9,17... | collective-permute-start | bytes 3981320 | tf_op jit(solution)/shard_map/ppermute | solution.py:31
  72.1 41.4 %collective-permute-start.3 = (bf16[192,3456]{1,0:T(8,128)(2,1)}, bf16[192,3456]{1,0:T(8,128)(2,1)}, u32[]{:S(2)}, u32[]{:S(2)}) collective-permute-start(bf16[192,3456]{1,0:T(8,128)(2,1)} %bitcast.9.refs_4_), channel_id=1, source_target_pairs={{0,4},{1,5},{2,6},{3,7},{4,0},{5,1},{6,2},{7,3},{8,12},{9,13},{10,... | collective-permute-start | bytes 3981320 | tf_op jit(solution)/shard_map/ppermute | solution.py:26
  77.0 43.7 %copy-start.6 = (s32[1536,1]{1,0:T(8,128)}, s32[1536,1]{1,0:T(8,128)S(1)}, u32[]{:S(2)}) copy-start(s32[1536,1]{1,0:T(8,128)S(1)} %broadcast_in_dim.33.ks_ref) | copy-start | bytes 18436
  113.5 34.8 %collective-permute-start.4 = (bf16[192,3456]{1,0:T(8,128)(2,1)}, bf16[192,3456]{1,0:T(8,128)(2,1)}, u32[]{:S(2)}, u32[]{:S(2)}) collective-permute-start(bf16[192,3456]{1,0:T(8,128)(2,1)} %collective-permute-done.2.refs_6_), channel_id=1, source_target_pairs={{0,8},{1,9},{2,10},{3,11},{4,12},{5,13},{6,14},{7,15},{8,16},{9,17... | collective-permute-start | bytes 3981320 | tf_op jit(solution)/shard_map/ppermute | solution.py:31
  117.3 31.2 %collective-permute-start.5 = (bf16[192,3456]{1,0:T(8,128)(2,1)}, bf16[192,3456]{1,0:T(8,128)(2,1)}, u32[]{:S(2)}, u32[]{:S(2)}) collective-permute-start(bf16[192,3456]{1,0:T(8,128)(2,1)} %collective-permute-done.2.refs_6_), channel_id=1, source_target_pairs={{0,4},{1,5},{2,6},{3,7},{4,0},{5,1},{6,2},{7,3},{8,12},{9,13},{10,... | collective-permute-start | bytes 3981320 | tf_op jit(solution)/shard_map/ppermute | solution.py:26
  117.3 37.7 %collective-permute-start.10 = (bf16[512,1536]{1,0:T(8,128)(2,1)}, bf16[512,1536]{1,0:T(8,128)(2,1)}, u32[]{:S(2)}, u32[]{:S(2)}) collective-permute-start(bf16[512,1536]{1,0:T(8,128)(2,1)} %cot_ref.1), channel_id=1, source_target_pairs={{0,2},{1,3},{2,0},{3,1},{4,6},{5,7},{6,4},{7,5},{8,10},{9,11},{10,... | collective-permute-start | bytes 4718600 | tf_op jit(solution)/shard_map/ppermute | solution.py:26
  144.0 10.9 %copy-start.11 = (f32[512,1536]{1,0:T(8,128)}, f32[512,1536]{1,0:T(8,128)S(1)}, u32[]{:S(2)}) copy-start(f32[512,1536]{1,0:T(8,128)S(1)} %get-tuple-element.117.middle_ref) | copy-start | bytes 9437188
  148.5 40.1 %collective-permute-start.6 = (bf16[512,1536]{1,0:T(8,128)(2,1)S(1)}, bf16[512,1536]{1,0:T(8,128)(2,1)S(1)}, u32[]{:S(2)}, u32[]{:S(2)}) collective-permute-start(bf16[512,1536]{1,0:T(8,128)(2,1)S(1)} %get-tuple-element.121), channel_id=1, source_target_pairs={{0,2},{1,3},{2,0},{3,1},{4,6},{5,7},{6,4},{7,5},{8,10},{9,11},{10,... | collective-permute-start | bytes 4718600 | tf_op jit(solution)/shard_map/ppermute | solution.py:26
  149.4 33.6 %collective-permute-start.7 = (bf16[192,3456]{1,0:T(8,128)(2,1)}, bf16[192,3456]{1,0:T(8,128)(2,1)}, u32[]{:S(2)}, u32[]{:S(2)}) collective-permute-start(bf16[192,3456]{1,0:T(8,128)(2,1)} %collective-permute-done.4.refs_8_), channel_id=1, source_target_pairs={{0,8},{1,9},{2,10},{3,11},{4,12},{5,13},{6,14},{7,15},{8,16},{9,17... | collective-permute-start | bytes 3981320 | tf_op jit(solution)/shard_map/ppermute | solution.py:31
  150.0 33.0 %collective-permute-start.8 = (bf16[192,3456]{1,0:T(8,128)(2,1)}, bf16[192,3456]{1,0:T(8,128)(2,1)S(1)}, u32[]{:S(2)}, u32[]{:S(2)}) collective-permute-start(bf16[192,3456]{1,0:T(8,128)(2,1)} %collective-permute-done.4.refs_8_), channel_id=1, source_target_pairs={{0,4},{1,5},{2,6},{3,7},{4,0},{5,1},{6,2},{7,3},{8,12},{9,13},{10,... | collective-permute-start | bytes 3981320 | tf_op jit(solution)/shard_map/ppermute | solution.py:26
  157.6 32.9 %collective-permute-start.11 = (bf16[1024,1536]{1,0:T(8,128)(2,1)}, bf16[1024,1536]{1,0:T(8,128)(2,1)}, u32[]{:S(2)}, u32[]{:S(2)}) collective-permute-start(bf16[1024,1536]{1,0:T(8,128)(2,1)} %constant_dynamic-update-slice_fusion.2.refs_2_), channel_id=1, source_target_pairs={{0,1},{1,0},{2,3},{3,2},{4,5},{5,4},{6,7},{7,6},{8,9},{9,8},{10,11... | collective-permute-start | bytes 9437192 | tf_op jit(solution)/shard_map/ppermute | solution.py:26
  183.0 5.6 %copy-start.51 = (bf16[192,3456]{1,0:T(8,128)(2,1)}, bf16[192,3456]{1,0:T(8,128)(2,1)S(1)}, u32[]{:S(2)}) copy-start(bf16[192,3456]{1,0:T(8,128)(2,1)S(1)} %collective-permute-done.8.refs_9_) | copy-start | bytes 3981316
  188.6 6.7 %copy-start = (bf16[1024,1536]{1,0:T(8,128)(2,1)}, bf16[1024,1536]{1,0:T(8,128)(2,1)S(1)}, u32[]{:S(2)}) copy-start(bf16[1024,1536]{1,0:T(8,128)(2,1)S(1)} %constant_dynamic-update-slice_fusion.refs_0_) | copy-start | bytes 9437188
  188.6 6.7 %collective-permute-start.9 = (bf16[1024,1536]{1,0:T(8,128)(2,1)S(1)}, bf16[1024,1536]{1,0:T(8,128)(2,1)}, u32[]{:S(2)}, u32[]{:S(2)}) collective-permute-start(bf16[1024,1536]{1,0:T(8,128)(2,1)S(1)} %constant_dynamic-update-slice_fusion.refs_0_), channel_id=1, source_target_pairs={{0,1},{1,0},{2,3},{3,2},{4,5},{5,4},{6,7},{7,6},{8,9},{9,8},{10,11... | collective-permute-start | bytes 9437192 | tf_op jit(solution)/shard_map/ppermute | solution.py:26
  189.9 34.1 %collective-permute-start.12 = (bf16[192,3456]{1,0:T(8,128)(2,1)}, bf16[192,3456]{1,0:T(8,128)(2,1)}, u32[]{:S(2)}, u32[]{:S(2)}) collective-permute-start(bf16[192,3456]{1,0:T(8,128)(2,1)} %collective-permute-done.7.refs_4_), channel_id=1, source_target_pairs={{0,4},{1,5},{2,6},{3,7},{4,0},{5,1},{6,2},{7,3},{8,12},{9,13},{10,... | collective-permute-start | bytes 3981320 | tf_op jit(solution)/shard_map/ppermute | solution.py:26
  225.9 21.1 %copy-start.2 = (bf16[1024,1536]{1,0:T(8,128)(2,1)S(1)}, bf16[1024,1536]{1,0:T(8,128)(2,1)}, u32[]{:S(2)}) copy-start(bf16[1024,1536]{1,0:T(8,128)(2,1)} %copy-done) | copy-start | bytes 9437188
  260.2 35.4 %collective-permute-start.13 = (bf16[192,3456]{1,0:T(8,128)(2,1)}, bf16[192,3456]{1,0:T(8,128)(2,1)}, u32[]{:S(2)}, u32[]{:S(2)}) collective-permute-start(bf16[192,3456]{1,0:T(8,128)(2,1)} %get-tuple-element.129), channel_id=1, source_target_pairs={{0,4},{1,5},{2,6},{3,7},{4,0},{5,1},{6,2},{7,3},{8,12},{9,13},{10,... | collective-permute-start | bytes 3981320 | tf_op jit(solution)/shard_map/ppermute | solution.py:26
  272.9 22.7 %copy-start.33 = (bf16[192,3456]{1,0:T(8,128)(2,1)}, bf16[192,3456]{1,0:T(8,128)(2,1)S(1)}, u32[]{:S(2)}) copy-start(bf16[192,3456]{1,0:T(8,128)(2,1)S(1)} %get-tuple-element.131) | copy-start | bytes 3981316
  272.9 22.7 %copy-start.37 = (bf16[192,3456]{1,0:T(8,128)(2,1)S(1)}, bf16[192,3456]{1,0:T(8,128)(2,1)}, u32[]{:S(2)}) copy-start(bf16[192,3456]{1,0:T(8,128)(2,1)} %copy-done.36) | copy-start | bytes 3981316
  295.5 3.7 copy-start.24
  295.5 3.7 copy-start.44
  299.2 33.6 %collective-permute-start.15 = (bf16[192,3456]{1,0:T(8,128)(2,1)}, bf16[192,3456]{1,0:T(8,128)(2,1)}, u32[]{:S(2)}, u32[]{:S(2)}) collective-permute-start(bf16[192,3456]{1,0:T(8,128)(2,1)} %add_convert_fusion.4), channel_id=1, source_target_pairs={{0,8},{1,9},{2,10},{3,11},{4,12},{5,13},{6,14},{7,15},{8,16},{9,17... | collective-permute-start | bytes 3981320 | tf_op jit(solution)/shard_map/ppermute | solution.py:31
  300.2 32.6 %collective-permute-start.14 = (bf16[192,3456]{1,0:T(8,128)(2,1)}, bf16[192,3456]{1,0:T(8,128)(2,1)}, u32[]{:S(2)}, u32[]{:S(2)}) collective-permute-start(bf16[192,3456]{1,0:T(8,128)(2,1)} %get-tuple-element.138), channel_id=1, source_target_pairs={{0,4},{1,5},{2,6},{3,7},{4,0},{5,1},{6,2},{7,3},{8,12},{9,13},{10,... | collective-permute-start | bytes 3981320 | tf_op jit(solution)/shard_map/ppermute | solution.py:26
  301.2 3.5 copy-start.23
  301.2 3.5 copy-start.39
  301.2 3.5 copy-start.41
  302.6 49.9 %collective-permute-start.16 = (bf16[512,1536]{1,0:T(8,128)(2,1)}, bf16[512,1536]{1,0:T(8,128)(2,1)S(1)}, u32[]{:S(2)}, u32[]{:S(2)}) collective-permute-start(bf16[512,1536]{1,0:T(8,128)(2,1)} %copy-done.44), channel_id=1, source_target_pairs={{0,2},{1,3},{2,0},{3,1},{4,6},{5,7},{6,4},{7,5},{8,10},{9,11},{10,... | collective-permute-start | bytes 4718600 | tf_op jit(solution)/shard_map/ppermute | solution.py:26
  304.7 57.6 %copy-start.16 = (bf16[512,1536]{1,0:T(8,128)(2,1)}, bf16[512,1536]{1,0:T(8,128)(2,1)S(1)}, u32[]{:S(2)}) copy-start(bf16[512,1536]{1,0:T(8,128)(2,1)S(1)} %constant_dynamic-update-slice_fusion.4.mixed_ref) | copy-start | bytes 4718596
  319.2 13.6 %copy-start.34 = (bf16[192,3456]{1,0:T(8,128)(2,1)S(1)}, bf16[192,3456]{1,0:T(8,128)(2,1)}, u32[]{:S(2)}) copy-start(bf16[192,3456]{1,0:T(8,128)(2,1)} %copy-done.33) | copy-start | bytes 3981316
  330.3 5.8 %copy-start.31 = (bf16[192,3456]{1,0:T(8,128)(2,1)}, bf16[192,3456]{1,0:T(8,128)(2,1)S(1)}, u32[]{:S(2)}) copy-start(bf16[192,3456]{1,0:T(8,128)(2,1)S(1)} %get-tuple-element.170) | copy-start | bytes 3981316
  330.3 5.8 %copy-start.46 = (bf16[192,3456]{1,0:T(8,128)(2,1)}, bf16[192,3456]{1,0:T(8,128)(2,1)S(1)}, u32[]{:S(2)}) copy-start(bf16[192,3456]{1,0:T(8,128)(2,1)S(1)} %get-tuple-element.159) | copy-start | bytes 3981316
  336.1 33.0 %collective-permute-start.19 = (bf16[192,3456]{1,0:T(8,128)(2,1)}, bf16[192,3456]{1,0:T(8,128)(2,1)}, u32[]{:S(2)}, u32[]{:S(2)}) collective-permute-start(bf16[192,3456]{1,0:T(8,128)(2,1)} %add_convert_fusion.3), channel_id=1, source_target_pairs={{0,8},{1,9},{2,10},{3,11},{4,12},{5,13},{6,14},{7,15},{8,16},{9,17... | collective-permute-start | bytes 3981320 | tf_op jit(solution)/shard_map/ppermute | solution.py:31
  336.9 32.2 %collective-permute-start.18 = (bf16[192,3456]{1,0:T(8,128)(2,1)}, bf16[192,3456]{1,0:T(8,128)(2,1)}, u32[]{:S(2)}, u32[]{:S(2)}) collective-permute-start(bf16[192,3456]{1,0:T(8,128)(2,1)} %get-tuple-element.145), channel_id=1, source_target_pairs={{0,4},{1,5},{2,6},{3,7},{4,0},{5,1},{6,2},{7,3},{8,12},{9,13},{10,... | collective-permute-start | bytes 3981320 | tf_op jit(solution)/shard_map/ppermute | solution.py:26
  337.6 16.0 %copy-start.43 = (f32[512,128]{1,0:T(8,128)S(1)}, f32[512,128]{1,0:T(8,128)}, u32[]{:S(2)}) copy-start(f32[512,128]{1,0:T(8,128)} %copy-done.42) | copy-start | bytes 786436
  362.3 2.9 copy-start.25
  362.3 2.9 copy-start.27
  367.0 42.4 %collective-permute-start.17 = (bf16[512,1536]{1,0:T(8,128)(2,1)}, bf16[512,1536]{1,0:T(8,128)(2,1)S(1)}, u32[]{:S(2)}, u32[]{:S(2)}) collective-permute-start(bf16[512,1536]{1,0:T(8,128)(2,1)} %copy-done.45), channel_id=1, source_target_pairs={{0,2},{1,3},{2,0},{3,1},{4,6},{5,7},{6,4},{7,5},{8,10},{9,11},{10,... | collective-permute-start | bytes 4718600 | tf_op jit(solution)/shard_map/ppermute | solution.py:26
  369.1 4.2 copy-start.7
  369.1 4.2 copy-start.9
  369.1 4.1 copy-start.13
  369.1 4.1 copy-start.15
  369.1 4.1 copy-start.17
  371.9 48.3 %collective-permute-start.23 = (bf16[192,3456]{1,0:T(8,128)(2,1)S(1)}, bf16[192,3456]{1,0:T(8,128)(2,1)S(1)}, u32[]{:S(2)}, u32[]{:S(2)}) collective-permute-start(bf16[192,3456]{1,0:T(8,128)(2,1)S(1)} %add_convert_fusion.2), channel_id=1, source_target_pairs={{0,8},{1,9},{2,10},{3,11},{4,12},{5,13},{6,14},{7,15},{8,16},{9,17... | collective-permute-start | bytes 3981320 | tf_op jit(solution)/shard_map/ppermute | solution.py:31
  372.2 48.0 %collective-permute-start.22 = (bf16[192,3456]{1,0:T(8,128)(2,1)}, bf16[192,3456]{1,0:T(8,128)(2,1)S(1)}, u32[]{:S(2)}, u32[]{:S(2)}) collective-permute-start(bf16[192,3456]{1,0:T(8,128)(2,1)} %copy-done.46), channel_id=1, source_target_pairs={{0,4},{1,5},{2,6},{3,7},{4,0},{5,1},{6,2},{7,3},{8,12},{9,13},{10,... | collective-permute-start | bytes 3981320 | tf_op jit(solution)/shard_map/ppermute | solution.py:26
  374.7 32.0 %slice-start.2 = ((s8[5898240]{0:T(1024)(128)(4,1)}), s8[4194304]{0:T(1024)(128)(4,1)S(1)}, s32[]{:S(2)}) async-start(s8[5898240]{0:T(1024)(128)(4,1)} %bitcast.72), calls=%async_computation.5 | async-start | bytes 8388608
  399.0 2.9 copy-start.4
  399.2 12.1 %collective-permute-start.20 = (bf16[512,256]{1,0:T(8,128)(2,1)S(1)}, bf16[512,256]{1,0:T(8,128)(2,1)S(1)}, u32[]{:S(2)}, u32[]{:S(2)}) collective-permute-start(bf16[512,256]{1,0:T(8,128)(2,1)S(1)} %get-tuple-element.184), channel_id=1, source_target_pairs={{1,0},{2,1},{3,2},{4,3},{5,4},{6,5},{7,6},{8,7},{9,8},{10,9},{11,1... | collective-permute-start | bytes 786440 | tf_op jit(solution)/shard_map/ppermute | solution.py:37
  400.6 12.6 %collective-permute-start.21 = (bf16[512,256]{1,0:T(8,128)(2,1)S(1)}, bf16[512,256]{1,0:T(8,128)(2,1)S(1)}, u32[]{:S(2)}, u32[]{:S(2)}) collective-permute-start(bf16[512,256]{1,0:T(8,128)(2,1)S(1)} %get-tuple-element.185), channel_id=1, source_target_pairs={{2,0},{3,1},{4,2},{5,3},{6,4},{7,5},{8,6},{9,7},{10,8},{11,9},{12,... | collective-permute-start | bytes 786440 | tf_op jit(solution)/shard_map/ppermute | solution.py:37
  401.9 4.7 slice-start.3
  406.7 2.7 copy-start.12
  406.7 2.7 copy-start.30
  415.5 2.7 copy-start.47
  (22 other events, 28.2 us)
Sparse Core Ops, SparseCore 0:
  10.9 105.1 all-gather.1
  367.1 105.1 reduce-scatter.1
